TPU v7x, 32 devices: a whole 2x2x4 slice. The times are simulated.
32 devices in a mesh: grp: 8 (over z, y), ep: 4 (over x, core).
Axes of the slice: x: 2, y: 2, z: 4, core: 2. Of those that a mesh axis runs over, the one named last changes fastest.
Arguments:
- tokens: bfloat16 [8192, 2048], P(('grp', 'ep')), may hold values from -6 to 6
- cotangent: bfloat16 [8192, 2048], P(('grp', 'ep')), may hold values from -6 to 6
- pack_order: int32 [8], replicated, may hold values from 0 to 7, each once
- doc_lengths: int32 [8, 4], P('grp'), may hold values from 1 to 512, 1024 in all within a row
- doc_sets: int32 [8, 4], P('grp'), may hold values from 0 to 7
- routes: int32 [8192, 8], P(('grp', 'ep')), may hold values from 0 to 15, all different within a row; in each aligned block of 256 rows (0 to 255, 256 to 511, ...) at most 144 rows name the same one
- attention_gain: bfloat16 [2048], replicated, may hold values from 0.5 to 1.5
- query_gain: bfloat16 [2048], replicated, may hold values from 0.5 to 1.5
- key_gain: bfloat16 [2048], replicated, may hold values from 0.5 to 1.5
- feed_gain: bfloat16 [2048], replicated, may hold values from 0.5 to 1.5
- qkv_weight: bfloat16 [3, 2048, 2048], P(None, None, 'ep'), may hold values from -0.125 to 0.125
- out_weight: bfloat16 [2048, 2048], P('ep'), may hold values from -0.5 to 0.5
- router_weight: bfloat16 [2048, 16], replicated, may hold values from -0.0625 to 0.0625
- gate_weight: bfloat16 [16, 2048, 1024], P('ep'), may hold values from -0.125 to 0.125
- up_weight: bfloat16 [16, 2048, 1024], P('ep'), may hold values from -0.125 to 0.125
- down_weight: bfloat16 [16, 1024, 2048], P('ep'), may hold values from -1.5 to 1.5
- qkv_enter: bfloat16 [3, 2048, 128], replicated, may hold values from -0.125 to 0.125
- qkv_leave: bfloat16 [3, 128, 2048], P(None, None, 'ep'), may hold values from -0.375 to 0.375
- out_enter: bfloat16 [2048, 128], P('ep'), may hold values from -0.5 to 0.5
- out_leave: bfloat16 [128, 2048], replicated, may hold values from -0.375 to 0.375
- router_enter: bfloat16 [2048, 128], replicated, may hold values from -0.125 to 0.125
- router_leave: bfloat16 [128, 16], replicated, may hold values from -0.1875 to 0.1875
- gate_enter: bfloat16 [16, 2048, 128], P('ep'), may hold values from -0.125 to 0.125
- gate_leave: bfloat16 [16, 128, 1024], P('ep'), may hold values from -0.375 to 0.375
- up_enter: bfloat16 [16, 2048, 128], P('ep'), may hold values from -0.125 to 0.125
- up_leave: bfloat16 [16, 128, 1024], P('ep'), may hold values from -0.375 to 0.375
- down_enter: bfloat16 [16, 1024, 128], P('ep'), may hold values from -0.1875 to 0.1875
- down_leave: bfloat16 [16, 128, 2048], P('ep'), may hold values from -0.375 to 0.375
Outputs:
- layer_output: bfloat16 [8192, 2048], P(('grp', 'ep'))
- input_grad: bfloat16 [8192, 2048], P(('grp', 'ep'))
- qkv_enter_grad: float32 [3, 2048, 128], P(None, 'ep', 'grp')
- qkv_leave_grad: float32 [3, 128, 2048], P(None, 'grp', 'ep')
- out_enter_grad: float32 [2048, 128], P('ep', 'grp')
- out_leave_grad: float32 [128, 2048], P('grp', 'ep')
- router_enter_grad: float32 [2048, 128], P('ep', 'grp')
- router_leave_grad: float32 [128, 16], P('ep', 'grp')
- gate_enter_grad: float32 [16, 2048, 128], P('ep', 'grp')
- gate_leave_grad: float32 [16, 128, 1024], P('ep', None, 'grp')
- up_enter_grad: float32 [16, 2048, 128], P('ep', 'grp')
- up_leave_grad: float32 [16, 128, 1024], P('ep', None, 'grp')
- down_enter_grad: float32 [16, 1024, 128], P('ep', 'grp')
- down_leave_grad: float32 [16, 128, 2048], P('ep', None, 'grp')
Inputs may be any that keep to these rules, and one draw needn't show every extreme that they name: `doc_lengths`: each row holds the 4 document lengths of a slot, summing to 1024. `routes`: each row names 8 different experts; among the rows of one device no expert is named more than 144 times.
All inputs are finite; a program needn't handle non-finite values.
Results may differ from a plain program's by a relative error of at most 0.024.
Values may be sent and summed in bfloat16 or wider, within the bound.
No kernel may reach another device: no remote copies, remote signals or barrier semaphores. Data moves between devices by JAX's collectives and lax.ppermute only.
A program may use at most 384 MiB of HBM per device.

v0:
```python
import jax
import jax.numpy as jnp
from jax import lax
from jax.sharding import PartitionSpec as P

HEAD_DIM = 128
EXPERTS = 16
TOP = 8
SETS = 8
RANK = 16
CAP = 144


EPS = 1e-05
SCALE = 2.0
THETA = 10000.0
NEG = -1e30


def rms_scale(value):
    return lax.rsqrt(jnp.mean(value * value, axis=-1, keepdims=True) + EPS)


def rotate(value, cosine, sine):
    half = value.shape[-1] // 2
    turned = jnp.concatenate([-value[..., half:], value[..., :half]], axis=-1)
    return value * cosine + turned * sine


def rotate_back(grad, cosine, sine):
    half = grad.shape[-1] // 2
    moved = grad * sine
    turned = jnp.concatenate([moved[..., half:], -moved[..., :half]], axis=-1)
    return grad * cosine + turned


def angles(position):
    half = HEAD_DIM // 2
    freq = THETA ** (-(jnp.arange(half, dtype=jnp.float32) * 2.0) / HEAD_DIM)
    phase = position.astype(jnp.float32)[:, None] * freq[None, :]
    cosine = jnp.concatenate([jnp.cos(phase), jnp.cos(phase)], axis=-1)
    sine = jnp.concatenate([jnp.sin(phase), jnp.sin(phase)], axis=-1)
    return (cosine[:, None, :], sine[:, None, :])


def documents(lengths, sets, count):
    ends = jnp.cumsum(lengths)
    starts = ends - lengths
    rows = jnp.arange(count, dtype=jnp.int32)
    doc_index = jnp.sum((rows[:, None] >= ends[None, :]).astype(jnp.int32), axis=1)
    member = doc_index[:, None] == jnp.arange(lengths.shape[0], dtype=jnp.int32)[None, :]
    position = rows - jnp.sum(jnp.where(member, starts[None, :], 0), axis=1)
    chosen = jnp.sum(jnp.where(member, sets[None, :], 0), axis=1)
    columns = jnp.arange(SETS * RANK, dtype=jnp.int32) // RANK
    selector = (columns[None, :] == chosen[:, None]).astype(jnp.float32)
    set_onehot = (jnp.arange(SETS, dtype=jnp.int32)[None, :] == chosen[:, None]).astype(jnp.float32)
    return (doc_index, position, selector, set_onehot)


def chooser(wanted, count, carry, pieces):
    rows = pieces[0].shape[0]
    offset = wanted * count
    inside = (offset >= 0) & (offset + count <= rows)
    clipped = jnp.clip(offset, 0, rows - count)
    taken = tuple((lax.dynamic_slice_in_dim(piece, clipped, count, 0) for piece in pieces))
    return tuple((jnp.where(inside, fresh, older) for fresh, older in zip(taken, carry)))


def expert_forward(
    rows_in, marks, gate_enter, gate_leave, up_enter, up_leave, gate_weight, up_weight
):
    low_gate = jnp.einsum("secd,edr->secr", rows_in, gate_enter, preferred_element_type=jnp.float32)
    low_gate = (low_gate * marks).astype(jnp.bfloat16)
    low_up = jnp.einsum("secd,edr->secr", rows_in, up_enter, preferred_element_type=jnp.float32)
    low_up = (low_up * marks).astype(jnp.bfloat16)
    gate = jnp.einsum("secd,edf->secf", rows_in, gate_weight, preferred_element_type=jnp.float32)
    gate = gate + SCALE * jnp.einsum(
        "secr,erf->secf", low_gate, gate_leave, preferred_element_type=jnp.float32
    )
    up = jnp.einsum("secd,edf->secf", rows_in, up_weight, preferred_element_type=jnp.float32)
    up = up + SCALE * jnp.einsum(
        "secr,erf->secf", low_up, up_leave, preferred_element_type=jnp.float32
    )
    return (low_gate, low_up, gate, up)


def per_device(
    tokens,
    cotangent,
    pack_order,
    doc_lengths,
    doc_sets,
    routes,
    attention_gain,
    query_gain,
    key_gain,
    feed_gain,
    qkv_weight,
    out_weight,
    router_weight,
    gate_weight,
    up_weight,
    down_weight,
    qkv_enter,
    qkv_leave,
    out_enter,
    out_leave,
    router_enter,
    router_leave,
    gate_enter,
    gate_leave,
    up_enter,
    up_leave,
    down_enter,
    down_leave,
):
    member_count = lax.axis_size("ep")
    group_count = lax.axis_size("grp")
    group_index = lax.axis_index("grp")
    member_index = lax.axis_index("ep")
    local = tokens.shape[0]
    width = tokens.shape[1]
    group_len = local * member_count
    slice_width = width // member_count
    heads_here = slice_width // HEAD_DIM
    own_start = member_index * local
    col_start = member_index * slice_width
    source = pack_order[group_index]
    empty = jnp.zeros_like(tokens)
    inputs, upstream = chooser(
        source,
        local,
        (empty, empty),
        (
            lax.all_gather(tokens, "grp", axis=0, tiled=True),
            lax.all_gather(cotangent, "grp", axis=0, tiled=True),
        ),
    )
    doc_index, position, selector, set_onehot = documents(doc_lengths[0], doc_sets[0], group_len)
    own_selector = lax.dynamic_slice_in_dim(selector, own_start, local, 0)
    own_sets = lax.dynamic_slice_in_dim(set_onehot, own_start, local, 0)
    cosine, sine = angles(position)
    resid = inputs.astype(jnp.float32)
    scale_one = rms_scale(resid)
    gain_one = attention_gain.astype(jnp.float32)
    normed_one = (resid * scale_one * gain_one).astype(jnp.bfloat16)
    low_in = jnp.einsum("td,kdc->ktc", normed_one, qkv_enter, preferred_element_type=jnp.float32)
    low_in = (low_in * own_selector[None]).astype(jnp.bfloat16)
    normed_all, low_all = (
        lax.all_gather(normed_one, "ep", axis=0, tiled=True),
        lax.all_gather(low_in, "ep", axis=1, tiled=True),
    )
    projected = jnp.einsum(
        "td,kde->kte", normed_all, qkv_weight, preferred_element_type=jnp.float32
    )
    projected = projected + SCALE * jnp.einsum(
        "ktc,kce->kte", low_all, qkv_leave, preferred_element_type=jnp.float32
    )
    squares = jnp.sum(projected[:2] * projected[:2], axis=-1)
    squares = lax.psum(squares, "ep")
    inverse = lax.rsqrt(squares / width + EPS)[:, :, None]
    gain_query = lax.dynamic_slice_in_dim(query_gain, col_start, slice_width, 0).astype(jnp.float32)
    gain_key = lax.dynamic_slice_in_dim(key_gain, col_start, slice_width, 0).astype(jnp.float32)
    shape = (group_len, heads_here, HEAD_DIM)
    query_norm = (projected[0] * inverse[0] * gain_query).reshape(shape)
    key_norm = (projected[1] * inverse[1] * gain_key).reshape(shape)
    queries = rotate(query_norm, cosine, sine).astype(jnp.bfloat16)
    keys = rotate(key_norm, cosine, sine).astype(jnp.bfloat16)
    values = projected[2].reshape(shape).astype(jnp.bfloat16)
    block = min(512, group_len)
    blocks = group_len // block
    scale_attn = HEAD_DIM ** (-0.5)
    key_rows = jnp.arange(group_len, dtype=jnp.int32)

    def block_scores(index):
        start = index * block
        query_block = lax.dynamic_slice_in_dim(queries, start, block, 0)
        rows = start + jnp.arange(block, dtype=jnp.int32)
        doc_rows = lax.dynamic_slice_in_dim(doc_index, start, block, 0)
        allowed = (doc_rows[:, None] == doc_index[None, :]) & (key_rows[None, :] <= rows[:, None])
        scores = (
            jnp.einsum("qhd,khd->hqk", query_block, keys, preferred_element_type=jnp.float32)
            * scale_attn
        )
        return (query_block, jnp.where(allowed[None], scores, NEG))

    def attend(index):
        scores = block_scores(index)[1]
        peak = jnp.max(scores, axis=-1, keepdims=True)
        expo = jnp.exp(scores - peak)
        total = jnp.sum(expo, axis=-1, keepdims=True)
        probs = (expo / total).astype(jnp.bfloat16)
        mixed = jnp.einsum("hqk,khd->qhd", probs, values, preferred_element_type=jnp.float32)
        return (mixed, (peak + jnp.log(total))[..., 0])

    mixed, logsum = lax.map(attend, jnp.arange(blocks, dtype=jnp.int32))
    attended = mixed.reshape(group_len, slice_width).astype(jnp.bfloat16)
    out_part = jnp.dot(attended, out_weight, preferred_element_type=jnp.float32)
    low_part = jnp.dot(attended, out_enter, preferred_element_type=jnp.float32)
    out_sum, low_sum = (
        lax.psum_scatter(out_part, "ep", scatter_dimension=0, tiled=True),
        lax.psum_scatter(low_part, "ep", scatter_dimension=0, tiled=True),
    )
    low_out = (low_sum * own_selector).astype(jnp.bfloat16)
    hidden_state = (
        resid + out_sum + SCALE * jnp.dot(low_out, out_leave, preferred_element_type=jnp.float32)
    )
    scale_two = rms_scale(hidden_state)
    gain_two = feed_gain.astype(jnp.float32)
    normed_two = (hidden_state * scale_two * gain_two).astype(jnp.bfloat16)
    low_router = jnp.dot(normed_two, router_enter, preferred_element_type=jnp.float32)
    low_router = (low_router * own_selector).astype(jnp.bfloat16)
    logits = jnp.dot(normed_two, router_weight, preferred_element_type=jnp.float32)
    logits = logits + SCALE * jnp.dot(low_router, router_leave, preferred_element_type=jnp.float32)
    probs_router = jax.nn.softmax(logits, axis=-1)
    expert_ids = jnp.arange(EXPERTS, dtype=jnp.int32)
    route_hot = (routes[:, :, None] == expert_ids[None, None, :]).astype(jnp.float32)
    weight = jnp.sum(route_hot * probs_router[:, None, :], axis=-1)
    flat_routes = routes.reshape(-1)
    hot = (flat_routes[:, None] == expert_ids[None, :]).astype(jnp.int32)
    rank = jnp.sum((jnp.cumsum(hot, axis=0) - hot) * hot, axis=1)
    place = flat_routes * CAP + rank
    total = EXPERTS * CAP
    route_count = local * TOP
    route_ids = jnp.arange(route_count, dtype=jnp.int32)
    owner = jnp.zeros((total,), jnp.int32).at[place].set(route_ids // TOP)
    source_route = jnp.zeros((total,), jnp.int32).at[place].set(route_ids)
    filled = jnp.zeros((total,), jnp.int32).at[place].set(1) > 0
    experts_here = gate_weight.shape[0]
    send_rows = jnp.where(filled[:, None], normed_two[owner], 0).reshape(
        member_count, experts_here * CAP, width
    )
    send_sets = jnp.where(filled[:, None], own_sets[owner], 0.0).astype(jnp.bfloat16)
    send_sets = send_sets.reshape(member_count, experts_here * CAP, SETS)
    got_rows, got_sets = (
        lax.all_to_all(send_rows, "ep", split_axis=0, concat_axis=0, tiled=True),
        lax.all_to_all(send_sets, "ep", split_axis=0, concat_axis=0, tiled=True),
    )
    rows_in = got_rows.reshape(member_count, experts_here, CAP, width)
    marks = jnp.repeat(
        got_sets.reshape(member_count, experts_here, CAP, SETS).astype(jnp.float32), RANK, axis=-1
    )
    low_gate, low_up, gate, up = expert_forward(
        rows_in, marks, gate_enter, gate_leave, up_enter, up_leave, gate_weight, up_weight
    )
    sigma = jax.nn.sigmoid(gate)
    hidden = (gate * sigma * up).astype(jnp.bfloat16)
    low_down = jnp.einsum("secf,efr->secr", hidden, down_enter, preferred_element_type=jnp.float32)
    low_down = (low_down * marks).astype(jnp.bfloat16)
    expert_out = jnp.einsum(
        "secf,efd->secd", hidden, down_weight, preferred_element_type=jnp.float32
    )
    expert_out = expert_out + SCALE * jnp.einsum(
        "secr,erd->secd", low_down, down_leave, preferred_element_type=jnp.float32
    )
    expert_out = expert_out.astype(jnp.bfloat16).reshape(member_count, experts_here * CAP, width)
    back_rows = lax.all_to_all(expert_out, "ep", split_axis=0, concat_axis=0, tiled=True).reshape(
        total, width
    )
    route_out = back_rows[place].reshape(local, TOP, width).astype(jnp.float32)
    layer_out = (hidden_state + jnp.sum(route_out * weight[:, :, None], axis=1)).astype(
        jnp.bfloat16
    )
    grad_out = upstream.astype(jnp.float32)
    grad_weight = jnp.sum(route_out * grad_out[:, None, :], axis=-1)
    grad_route = (
        (weight[:, :, None] * grad_out[:, None, :]).astype(jnp.bfloat16).reshape(route_count, width)
    )
    send_grad = jnp.where(filled[:, None], grad_route[source_route], 0)
    send_grad = send_grad.reshape(member_count, experts_here * CAP, width)
    grad_rows = lax.all_to_all(send_grad, "ep", split_axis=0, concat_axis=0, tiled=True)
    grad_rows = grad_rows.reshape(member_count, experts_here, CAP, width)
    grad_low_down = jnp.einsum(
        "secd,erd->secr", grad_rows, down_leave, preferred_element_type=jnp.float32
    )
    grad_low_down = (grad_low_down * SCALE * marks).astype(jnp.bfloat16)
    grad_hidden = jnp.einsum(
        "secd,efd->secf", grad_rows, down_weight, preferred_element_type=jnp.float32
    )
    grad_hidden = grad_hidden + jnp.einsum(
        "secr,efr->secf", grad_low_down, down_enter, preferred_element_type=jnp.float32
    )
    grad_gate = (grad_hidden * up * sigma * (1.0 + gate * (1.0 - sigma))).astype(jnp.bfloat16)
    grad_up = (grad_hidden * gate * sigma).astype(jnp.bfloat16)
    grad_low_gate = jnp.einsum(
        "secf,erf->secr", grad_gate, gate_leave, preferred_element_type=jnp.float32
    )
    grad_low_gate = (grad_low_gate * SCALE * marks).astype(jnp.bfloat16)
    grad_low_up = jnp.einsum(
        "secf,erf->secr", grad_up, up_leave, preferred_element_type=jnp.float32
    )
    grad_low_up = (grad_low_up * SCALE * marks).astype(jnp.bfloat16)
    grad_rows_in = jnp.einsum(
        "secf,edf->secd", grad_gate, gate_weight, preferred_element_type=jnp.float32
    )
    grad_rows_in = grad_rows_in + jnp.einsum(
        "secf,edf->secd", grad_up, up_weight, preferred_element_type=jnp.float32
    )
    grad_rows_in = grad_rows_in + jnp.einsum(
        "secr,edr->secd", grad_low_gate, gate_enter, preferred_element_type=jnp.float32
    )
    grad_rows_in = grad_rows_in + jnp.einsum(
        "secr,edr->secd", grad_low_up, up_enter, preferred_element_type=jnp.float32
    )
    grad_rows_in = grad_rows_in.astype(jnp.bfloat16).reshape(
        member_count, experts_here * CAP, width
    )
    returned = lax.all_to_all(grad_rows_in, "ep", split_axis=0, concat_axis=0, tiled=True).reshape(
        total, width
    )
    grad_normed_two = jnp.sum(
        returned[place].reshape(local, TOP, width).astype(jnp.float32), axis=1
    )
    grad_gate_enter = jnp.einsum(
        "secd,secr->edr", rows_in, grad_low_gate, preferred_element_type=jnp.float32
    )
    grad_gate_leave = SCALE * jnp.einsum(
        "secr,secf->erf", low_gate, grad_gate, preferred_element_type=jnp.float32
    )
    grad_up_enter = jnp.einsum(
        "secd,secr->edr", rows_in, grad_low_up, preferred_element_type=jnp.float32
    )
    grad_up_leave = SCALE * jnp.einsum(
        "secr,secf->erf", low_up, grad_up, preferred_element_type=jnp.float32
    )
    grad_down_enter = jnp.einsum(
        "secf,secr->efr", hidden, grad_low_down, preferred_element_type=jnp.float32
    )
    grad_down_leave = SCALE * jnp.einsum(
        "secr,secd->erd", low_down, grad_rows, preferred_element_type=jnp.float32
    )
    grad_probs = jnp.sum(route_hot * grad_weight[:, :, None], axis=1)
    grad_logits = probs_router * (
        grad_probs - jnp.sum(probs_router * grad_probs, axis=-1, keepdims=True)
    )
    grad_logits = grad_logits.astype(jnp.bfloat16)
    grad_low_router = jnp.einsum(
        "te,ce->tc", grad_logits, router_leave, preferred_element_type=jnp.float32
    )
    grad_low_router = (grad_low_router * SCALE * own_selector).astype(jnp.bfloat16)
    grad_normed_two = grad_normed_two + jnp.einsum(
        "te,de->td", grad_logits, router_weight, preferred_element_type=jnp.float32
    )
    grad_normed_two = grad_normed_two + jnp.einsum(
        "tc,dc->td", grad_low_router, router_enter, preferred_element_type=jnp.float32
    )
    grad_router_enter = jnp.einsum(
        "td,tc->dc", normed_two, grad_low_router, preferred_element_type=jnp.float32
    )
    grad_router_leave = SCALE * jnp.einsum(
        "tc,te->ce", low_router, grad_logits, preferred_element_type=jnp.float32
    )
    weighted_two = gain_two * grad_normed_two
    grad_hidden_state = (
        grad_out
        + scale_two * weighted_two
        - hidden_state
        * scale_two**3
        * jnp.mean(hidden_state * weighted_two, axis=-1, keepdims=True)
    )
    grad_branch = grad_hidden_state.astype(jnp.bfloat16)
    grad_low_out = jnp.einsum(
        "td,cd->tc", grad_branch, out_leave, preferred_element_type=jnp.float32
    )
    grad_low_out = (grad_low_out * SCALE * own_selector).astype(jnp.bfloat16)
    grad_out_leave = SCALE * jnp.einsum(
        "tc,td->cd", low_out, grad_branch, preferred_element_type=jnp.float32
    )
    branch_all, low_grad_all = (
        lax.all_gather(grad_branch, "ep", axis=0, tiled=True),
        lax.all_gather(grad_low_out, "ep", axis=0, tiled=True),
    )
    grad_att = jnp.einsum("td,ed->te", branch_all, out_weight, preferred_element_type=jnp.float32)
    grad_att = grad_att + jnp.einsum(
        "tc,ec->te", low_grad_all, out_enter, preferred_element_type=jnp.float32
    )
    grad_att = grad_att.astype(jnp.bfloat16).reshape(shape)
    grad_out_enter = jnp.einsum(
        "te,tc->ec", attended, low_grad_all, preferred_element_type=jnp.float32
    )

    def back_block(carry, index):
        key_acc, value_acc = carry
        query_block, scores = block_scores(index)
        grad_block = lax.dynamic_slice_in_dim(grad_att, index * block, block, 0)
        probs = jnp.exp(scores - logsum[index][..., None])
        grad_probs_att = jnp.einsum(
            "qhd,khd->hqk", grad_block, values, preferred_element_type=jnp.float32
        )
        inner = jnp.sum(probs * grad_probs_att, axis=-1, keepdims=True)
        grad_scores = (probs * (grad_probs_att - inner) * scale_attn).astype(jnp.bfloat16)
        grad_query = jnp.einsum(
            "hqk,khd->qhd", grad_scores, keys, preferred_element_type=jnp.float32
        )
        key_acc = key_acc + jnp.einsum(
            "hqk,qhd->khd", grad_scores, query_block, preferred_element_type=jnp.float32
        )
        value_acc = value_acc + jnp.einsum(
            "hqk,qhd->khd",
            probs.astype(jnp.bfloat16),
            grad_block,
            preferred_element_type=jnp.float32,
        )
        return ((key_acc, value_acc), grad_query)

    zeros_heads = jnp.zeros(shape, jnp.float32)
    (grad_keys, grad_values), grad_queries = lax.scan(
        back_block, (zeros_heads, zeros_heads), jnp.arange(blocks, dtype=jnp.int32)
    )
    grad_queries = grad_queries.reshape(shape)
    grad_query_norm = rotate_back(grad_queries, cosine, sine).reshape(group_len, slice_width)
    grad_key_norm = rotate_back(grad_keys, cosine, sine).reshape(group_len, slice_width)
    terms = jnp.stack(
        [
            jnp.sum(projected[0] * gain_query * grad_query_norm, axis=-1),
            jnp.sum(projected[1] * gain_key * grad_key_norm, axis=-1),
        ]
    )
    terms = lax.psum(terms, "ep")
    grad_query_proj = (
        inverse[0] * gain_query * grad_query_norm
        - projected[0] * inverse[0] ** 3 * (terms[0] / width)[:, None]
    )
    grad_key_proj = (
        inverse[1] * gain_key * grad_key_norm
        - projected[1] * inverse[1] ** 3 * (terms[1] / width)[:, None]
    )
    grad_proj = jnp.stack(
        [grad_query_proj, grad_key_proj, grad_values.reshape(group_len, slice_width)]
    ).astype(jnp.bfloat16)
    grad_qkv_leave = SCALE * jnp.einsum(
        "ktc,kte->kce", low_all, grad_proj, preferred_element_type=jnp.float32
    )
    part_input = jnp.einsum(
        "kte,kde->td", grad_proj, qkv_weight, preferred_element_type=jnp.float32
    )
    part_low = SCALE * jnp.einsum(
        "kte,kce->ktc", grad_proj, qkv_leave, preferred_element_type=jnp.float32
    )
    input_part, low_part_own, router_enter_part, out_leave_part, router_leave_part = (
        lax.psum_scatter(
            part_input.astype(jnp.bfloat16), "ep", scatter_dimension=0, tiled=True
        ).astype(jnp.float32),
        lax.psum_scatter(
            part_low.astype(jnp.bfloat16), "ep", scatter_dimension=1, tiled=True
        ).astype(jnp.float32),
        lax.psum_scatter(
            grad_router_enter.astype(jnp.bfloat16), "ep", scatter_dimension=0, tiled=True
        ).astype(jnp.float32),
        lax.psum_scatter(
            grad_out_leave.astype(jnp.bfloat16), "ep", scatter_dimension=1, tiled=True
        ).astype(jnp.float32),
        lax.psum_scatter(
            grad_router_leave.astype(jnp.bfloat16), "ep", scatter_dimension=0, tiled=True
        ).astype(jnp.float32),
    )
    grad_low_own = (low_part_own * own_selector[None]).astype(jnp.bfloat16)
    grad_low_all = lax.all_gather(grad_low_own, "ep", axis=1, tiled=True)
    grad_normed_one = input_part + jnp.einsum(
        "ktc,kdc->td", grad_low_own, qkv_enter, preferred_element_type=jnp.float32
    )
    own_cols = lax.dynamic_slice_in_dim(normed_all, col_start, slice_width, 1)
    grad_qkv_enter = jnp.einsum(
        "te,ktc->kec", own_cols, grad_low_all, preferred_element_type=jnp.float32
    )
    weighted_one = gain_one * grad_normed_one
    grad_input = (
        grad_hidden_state
        + scale_one * weighted_one
        - resid * scale_one**3 * jnp.mean(resid * weighted_one, axis=-1, keepdims=True)
    )
    grad_input = grad_input.astype(jnp.bfloat16)
    summed = (
        lax.psum_scatter(
            grad_gate_enter.astype(jnp.bfloat16), "grp", scatter_dimension=1, tiled=True
        ).astype(jnp.float32),
        lax.psum_scatter(
            grad_gate_leave.astype(jnp.bfloat16), "grp", scatter_dimension=2, tiled=True
        ).astype(jnp.float32),
        lax.psum_scatter(
            grad_up_enter.astype(jnp.bfloat16), "grp", scatter_dimension=1, tiled=True
        ).astype(jnp.float32),
        lax.psum_scatter(
            grad_up_leave.astype(jnp.bfloat16), "grp", scatter_dimension=2, tiled=True
        ).astype(jnp.float32),
        lax.psum_scatter(
            grad_down_enter.astype(jnp.bfloat16), "grp", scatter_dimension=1, tiled=True
        ).astype(jnp.float32),
        lax.psum_scatter(
            grad_down_leave.astype(jnp.bfloat16), "grp", scatter_dimension=2, tiled=True
        ).astype(jnp.float32),
        lax.psum_scatter(
            grad_qkv_enter.astype(jnp.bfloat16), "grp", scatter_dimension=2, tiled=True
        ).astype(jnp.float32),
        lax.psum_scatter(
            grad_qkv_leave.astype(jnp.bfloat16), "grp", scatter_dimension=1, tiled=True
        ).astype(jnp.float32),
        lax.psum_scatter(
            grad_out_enter.astype(jnp.bfloat16), "grp", scatter_dimension=1, tiled=True
        ).astype(jnp.float32),
        lax.psum_scatter(
            out_leave_part.astype(jnp.bfloat16), "grp", scatter_dimension=0, tiled=True
        ).astype(jnp.float32),
        lax.psum_scatter(
            router_enter_part.astype(jnp.bfloat16), "grp", scatter_dimension=1, tiled=True
        ).astype(jnp.float32),
        lax.psum_scatter(
            router_leave_part.astype(jnp.bfloat16), "grp", scatter_dimension=1, tiled=True
        ).astype(jnp.float32),
    )
    home = jnp.sum(
        jnp.where(pack_order == group_index, jnp.arange(group_count, dtype=jnp.int32), 0)
    )
    final_out, final_grad = chooser(
        home,
        local,
        (empty, empty),
        (
            lax.all_gather(layer_out, "grp", axis=0, tiled=True),
            lax.all_gather(grad_input, "grp", axis=0, tiled=True),
        ),
    )
    return (
        final_out,
        final_grad,
        summed[6],
        summed[7],
        summed[8],
        summed[9],
        summed[10],
        summed[11],
        summed[0],
        summed[1],
        summed[2],
        summed[3],
        summed[4],
        summed[5],
    )


def solution(mesh):
    in_specs = (
        P(("grp", "ep"), None),
        P(("grp", "ep"), None),
        P(),
        P("grp", None),
        P("grp", None),
        P(("grp", "ep"), None),
        P(),
        P(),
        P(),
        P(),
        P(None, None, "ep"),
        P("ep", None),
        P(),
        P("ep", None, None),
        P("ep", None, None),
        P("ep", None, None),
        P(),
        P(None, None, "ep"),
        P("ep", None),
        P(),
        P(),
        P(),
        P("ep", None, None),
        P("ep", None, None),
        P("ep", None, None),
        P("ep", None, None),
        P("ep", None, None),
        P("ep", None, None),
    )
    out_specs = (
        P(("grp", "ep"), None),
        P(("grp", "ep"), None),
        P(None, "ep", "grp"),
        P(None, "grp", "ep"),
        P("ep", "grp"),
        P("grp", "ep"),
        P("ep", "grp"),
        P("ep", "grp"),
        P("ep", "grp", None),
        P("ep", None, "grp"),
        P("ep", "grp", None),
        P("ep", None, "grp"),
        P("ep", "grp", None),
        P("ep", None, "grp"),
    )
    return jax.shard_map(
        per_device, mesh=mesh, in_specs=in_specs, out_specs=out_specs, check_vma=False
    )
```

profile of v0, /device:TPU:0, one launch (start us, length us, event | category | flops | bytes accessed | tf_op | source)
XLA Modules:
  0.0 2360.0 jit_solution(8616904386638155797)
XLA Ops:
  10.6 127.2 %all-gather.7.cloned.1.call-done = bf16[2048,2048]{1,0:T(8,128)(2,1)} async-done(((bf16[256,2048]{1,0:T(8,128)(2,1)}), bf16[2048,2048]{1,0:T(8,128)(2,1)}) %all-gather.7.cloned.1.call-update) | async-done | bytes 8388624 | tf_op jit(solution)/shard_map/all_gather | solution.py:135
  152.2 13.3 all_gather.29
  170.0 10.6 all-gather.9.cloned.1.call-done
  180.6 11.5 bitcast_add_fusion.2
  209.5 6.7 psum.14
  223.6 23.1 while.30
  251.7 7.6 fusion.232
  266.1 8.1 scatter_custom_fusion.1
  274.2 8.1 scatter_custom_fusion
  291.3 8.5 scatter_custom_fusion.2
  299.9 7.8 all-gather.13.cloned.1.call-done
  310.5 20.0 reduce-scatter.29.cloned.1.call-done
  330.5 74.3 %reduce-scatter.27.cloned.1.call-done = f32[256,2048]{1,0:T(8,128)} async-done(((f32[1024,2048]{1,0:T(8,128)}), f32[256,2048]{1,0:T(8,128)}) %reduce-scatter.27.cloned.1.call-update) | async-done | bytes 2097168 | tf_op jit(solution)/shard_map/reduce_scatter | solution.py:201
  409.4 9.9 gather_fusion
  428.8 22.8 gather_fusion.3
  451.6 14.3 broadcast_select_fusion
  465.9 112.3 %all_to_all.25 = bf16[4,576,2048]{2,1,0:T(8,128)(2,1)} all-to-all(bf16[4,576,2048]{2,1,0:T(8,128)(2,1)} %get-tuple-element.431), channel_id=1, replica_groups=mesh['grp'=8,'ep'=4] {'ep'}, dimensions={0} | all-to-all | bytes 18874368 | tf_op jit(solution)/shard_map/all_to_all | solution.py:236
  588.7 8.1 fusion.205
  600.3 18.4 fusion.85
  618.8 18.6 fusion.89
  637.4 51.2 %all-to-all-done.3 = bf16[4,576,2048]{2,1,0:T(8,128)(2,1)} async-done(((bf16[4,576,2048]{2,1,0:T(8,128)(2,1)}), bf16[4,576,2048]{2,1,0:T(8,128)(2,1)}, u32[]{:S(2)}, u32[]{:S(2)}) %all-to-all-start.3) | async-done | bytes 9437216 | tf_op jit(solution)/shard_map/all_to_all | solution.py:271
  688.6 7.1 fusion.200
  695.7 17.2 fusion.91
  724.5 21.4 fusion.102
  748.0 17.4 fusion.93
  770.1 10.6 fusion.96
  780.7 9.2 copy.236
  796.0 8.9 fusion.155
  809.6 17.9 fusion.87
  827.5 18.0 fusion.83
  845.5 22.8 fusion.97
  868.2 9.3 copy.244
  877.5 22.8 all-to-all-done.2
  906.5 21.4 gather_fusion.2
  927.9 9.5 fusion.82
  939.8 71.0 %all-to-all-done.4 = bf16[4,576,2048]{2,1,0:T(8,128)(2,1)} async-done(((bf16[4,576,2048]{2,1,0:T(8,128)(2,1)}), bf16[4,576,2048]{2,1,0:T(8,128)(2,1)}, u32[]{:S(2)}, u32[]{:S(2)}) %all-to-all-start.4) | async-done | bytes 9437216 | tf_op jit(solution)/shard_map/all_to_all | solution.py:308
  1010.8 21.6 gather_fusion.4
  1032.4 11.4 convert_reduce_fusion
  1062.9 23.4 all-gather.15.cloned.1.call-done
  1093.8 128.2 %while.31 = (s32[]{:T(128)}, f32[1024,4,128]{0,2,1:T(8,128)}, f32[1024,4,128]{0,2,1:T(8,128)}, f32[2,512,4,128]{3,1,2,0:T(8,128)}, s32[2]{0:T(128)S(1)}, /*index...) while((s32[]{:T(128)}, f32[1024,4,128]{0,2,1:T(8,128)}, ...), condition=%wide.region_32.33_spmd.clone.clone, body=%wide.region_30.32_spmd.clone.sunk.clone | while | flops 2742557184 | bytes 166795664 | solution.py:407
  1110.0 24.2 %bitcast_add_fusion.9 = f32[1024,4,128]{0,2,1:T(8,128)} fusion(f32[1024,4,128]{0,2,1:T(8,128)} %get-tuple-element.660, f32[4,512,1024]{2,1,0:T(8,128)} %fusion.403, f32[4,512,1024]{2,1,0:T(8,128)} %copy-done.4, f32[4,512]{1,0:T(4,128)S(1)} %dynamic-slice_bitcast_fusion.3, pred[512,1024]{1,0:T(8,128)(4,1)} %copy-done.22, pred[]{:T(512)S(6)} %compare.10, ...), kind=kOutput, calls=%fused_computation.49.clone.1.clone | convolution fusion | flops 560991232 | bytes 39337988 | tf_op jit(solution)/shard_map/while/body/eval_jaxpr/hqk,qhd->khd/dot_general | solution.py:395
  1134.2 23.3 fusion.406
  1173.6 24.9 %bitcast_add_fusion.9 = f32[1024,4,128]{0,2,1:T(8,128)} fusion(f32[1024,4,128]{0,2,1:T(8,128)} %get-tuple-element.660, f32[4,512,1024]{2,1,0:T(8,128)} %fusion.403, f32[4,512,1024]{2,1,0:T(8,128)} %copy-done.4, f32[4,512]{1,0:T(4,128)S(1)} %dynamic-slice_bitcast_fusion.3, pred[512,1024]{1,0:T(8,128)(4,1)} %copy-done.22, pred[]{:T(512)S(6)} %compare.10, ...), kind=kOutput, calls=%fused_computation.49.clone.1.clone | convolution fusion | flops 560991232 | bytes 39337988 | tf_op jit(solution)/shard_map/while/body/eval_jaxpr/hqk,qhd->khd/dot_general | solution.py:395
  1198.5 23.4 fusion.406
  1271.0 11.3 bitcast_convert_fusion
  1299.8 7.1 fusion.120
  1307.2 8.9 bitcast_convert_fusion.2
  1316.2 9.0 bitcast_convert_fusion.1
  1334.3 11.9 all_gather.35
  1358.7 53.7 %reduce-scatter.61.cloned.1.call-done = bf16[128,512]{1,0:T(8,128)(2,1)} async-done(((bf16[1024,512]{1,0:T(8,128)(2,1)}), bf16[128,512]{1,0:T(8,128)(2,1)}) %reduce-scatter.61.cloned.1.call-update) | async-done | bytes 131088
  1414.2 64.8 %reduce-scatter.59.cloned.1.call-done = bf16[128,512]{1,0:T(8,128)(2,1)} async-done(((bf16[1024,512]{1,0:T(8,128)(2,1)}), bf16[128,512]{1,0:T(8,128)(2,1)}) %reduce-scatter.59.cloned.1.call-update) | async-done | bytes 131088
  1480.9 64.4 %reduce-scatter.51.cloned.1.call-done = bf16[4,128,128]{2,1,0:T(8,128)(2,1)} async-done(((bf16[4,1024,128]{2,1,0:T(8,128)(2,1)}), bf16[4,128,128]{2,1,0:T(8,128)(2,1)}) %reduce-scatter.51.cloned.1.call-update) | async-done | bytes 131088 | tf_op jit(solution)/shard_map/reduce_scatter | solution.py:486
  1546.9 69.3 %reduce-scatter.53.cloned.1.call-done = bf16[4,128,256]{2,1,0:T(8,128)(2,1)} async-done(((bf16[4,128,2048]{2,1,0:T(8,128)(2,1)}), bf16[4,128,256]{2,1,0:T(8,128)(2,1)}) %reduce-scatter.53.cloned.1.call-update) | async-done | bytes 262160 | tf_op jit(solution)/shard_map/reduce_scatter | solution.py:489
  1618.2 68.8 %reduce-scatter.47.cloned.1.call-done = bf16[4,256,128]{2,1,0:T(8,128)(2,1)} async-done(((bf16[4,2048,128]{2,1,0:T(8,128)(2,1)}), bf16[4,256,128]{2,1,0:T(8,128)(2,1)}) %reduce-scatter.47.cloned.1.call-update) | async-done | bytes 262160 | tf_op jit(solution)/shard_map/reduce_scatter | solution.py:474
  1688.8 69.2 %reduce-scatter.49.cloned.1.call-done = bf16[4,256,128]{2,1,0:T(8,128)(2,1)} async-done(((bf16[4,2048,128]{2,1,0:T(8,128)(2,1)}), bf16[4,256,128]{2,1,0:T(8,128)(2,1)}) %reduce-scatter.49.cloned.1.call-update) | async-done | bytes 262160 | tf_op jit(solution)/shard_map/reduce_scatter | solution.py:480
  1759.8 19.5 reduce-scatter.57.cloned.1.call-done
  1780.1 21.4 all-reduce
  1802.0 41.4 %reduce-scatter.39.cloned.1.call-done = bf16[512,16]{0,1:T(8,128)(2,1)} async-done(((bf16[512,128]{0,1:T(8,128)(2,1)}), bf16[512,16]{0,1:T(8,128)(2,1)}) %reduce-scatter.39.cloned.1.call-update) | async-done | bytes 16400 | tf_op jit(solution)/shard_map/reduce_scatter | solution.py:498
  1844.7 61.9 %reduce-scatter.55.cloned.1.call-done = bf16[16,512]{1,0:T(8,128)(2,1)} async-done(((bf16[128,512]{1,0:T(8,128)(2,1)}), bf16[16,512]{1,0:T(8,128)(2,1)}) %reduce-scatter.55.cloned.1.call-update) | async-done | bytes 16400
  1908.2 61.5 %reduce-scatter.43.cloned.1.call-done = bf16[16,512]{1,0:T(8,128)(2,1)} async-done(((bf16[128,512]{1,0:T(8,128)(2,1)}), bf16[16,512]{1,0:T(8,128)(2,1)}) %reduce-scatter.43.cloned.1.call-update) | async-done | bytes 16400 | tf_op jit(solution)/shard_map/reduce_scatter | solution.py:501
  1971.0 63.2 %reduce-scatter.37.cloned.1.call-done = bf16[3,16,512]{2,1,0:T(8,128)(2,1)} async-done(((bf16[3,128,512]{2,1,0:T(8,128)(2,1)}), bf16[3,16,512]{2,1,0:T(8,128)(2,1)}) %reduce-scatter.37.cloned.1.call-update) | async-done | bytes 49168 | tf_op jit(solution)/shard_map/reduce_scatter | solution.py:495
  2035.6 63.0 %reduce-scatter.35.cloned.1.call-done = bf16[3,512,16]{1,2,0:T(8,128)(2,1)} async-done(((bf16[3,512,128]{1,2,0:T(8,128)(2,1)}), bf16[3,512,16]{1,2,0:T(8,128)(2,1)}) %reduce-scatter.35.cloned.1.call-update) | async-done | bytes 49168 | tf_op jit(solution)/shard_map/reduce_scatter | solution.py:492
  2100.1 124.7 %all-gather.11.cloned.1.call-done = bf16[2048,2048]{1,0:T(8,128)(2,1)} async-done(((bf16[256,2048]{1,0:T(8,128)(2,1)}), bf16[2048,2048]{1,0:T(8,128)(2,1)}) %all-gather.11.cloned.1.call-update) | async-done | bytes 8388624 | tf_op jit(solution)/shard_map/all_gather | solution.py:519
  2227.3 123.2 %all-gather.17.cloned.1.call-done = bf16[2048,2048]{1,0:T(8,128)(2,1)} async-done(((bf16[256,2048]{1,0:T(8,128)(2,1)}), bf16[2048,2048]{1,0:T(8,128)(2,1)}) %all-gather.17.cloned.1.call-update) | async-done | bytes 8388624 | tf_op jit(solution)/shard_map/all_gather | solution.py:520
  (538 shorter events, 320.3 us)
Async XLA Ops:
  7.2 681.4 %copy-start = (bf16[4,128,2048]{2,1,0:T(8,128)(2,1)S(1)}, bf16[4,128,2048]{2,1,0:T(8,128)(2,1)}, u32[]{:S(2)}) copy-start(bf16[4,128,2048]{2,1,0:T(8,128)(2,1)} %param.59) | copy-start | bytes 6291460
  7.2 137.1 %copy-start.126 = (s32[1,4]{1,0:T(1,128)S(1)}, s32[1,4]{1,0:T(1,128)}, u32[]{:S(2)}) copy-start(s32[1,4]{1,0:T(1,128)} %param.35) | copy-start | bytes 52
  7.2 137.4 %copy-start.123 = (s32[1,4]{1,0:T(1,128)S(1)}, s32[1,4]{1,0:T(1,128)}, u32[]{:S(2)}) copy-start(s32[1,4]{1,0:T(1,128)} %param.36) | copy-start | bytes 52
  7.2 130.6 %all-gather.7.cloned.1.call-start = ((), (), s32[]{:S(2)}) async-start(), calls=%async_computation.23 | async-start | bytes 9437184 | tf_op jit(solution)/shard_map/all_gather | solution.py:135
  8.0 172.6 %all-gather.9.cloned.1.call-start = ((), (), s32[]{:S(2)}) async-start(), calls=%async_computation.24 | async-start | bytes 5242880 | tf_op jit(solution)/shard_map/all_gather | solution.py:150
  10.6 132.9 %copy-start.92 = (f32[2048]{0:T(1024)}, f32[2048]{0:T(1024)S(1)}, u32[]{:S(2)}) copy-start(f32[2048]{0:T(1024)S(1)} %convert_element_type.277) | copy-start | bytes 24580
  143.5 164.2 %all-gather.13.cloned.1.call-start = ((), (), s32[]{:S(2)}) async-start(), calls=%async_computation.28 | async-start | bytes 9437184 | tf_op jit(solution)/shard_map/all_gather | solution.py:136
  144.2 186.3 %reduce-scatter.29.cloned.1.call-start = ((), (), s32[]{:S(2)}) async-start(), calls=%async_computation.26 | async-start | bytes 655360 | tf_op jit(solution)/shard_map/reduce_scatter | solution.py:202
  144.8 274.9 %copy-start.98 = (s32[256]{0:T(256)}, s32[256]{0:T(256)S(1)}, u32[]{:S(2)}) copy-start(s32[256]{0:T(256)S(1)} %dynamic-slice.2) | copy-start | bytes 3076
  144.8 274.9 %copy-start.111 = (s32[128]{0:T(128)}, s32[128]{0:T(128)S(1)}, u32[]{:S(2)}) copy-start(s32[128]{0:T(128)S(1)} %and_select_fusion) | copy-start | bytes 1540
  146.3 73.8 %copy-start.102 = (f32[4,128]{1,0:T(4,128)}, f32[4,128]{1,0:T(4,128)S(1)}, u32[]{:S(2)}) copy-start(f32[4,128]{1,0:T(4,128)S(1)} %get-tuple-element.427) | copy-start | bytes 6148
  150.2 16.1 copy-start.81
  223.6 26.5 %copy-start.74 = (bf16[512,128]{1,0:T(8,128)(2,1)S(1)}, bf16[512,128]{1,0:T(8,128)(2,1)}, u32[]{:S(2)}) copy-start(bf16[512,128]{1,0:T(8,128)(2,1)} %param.50) | copy-start | bytes 393220
  246.7 12.6 copy-start.5
  246.8 12.6 copy-start.57
  246.8 12.6 copy-start.87
  251.4 153.5 %reduce-scatter.27.cloned.1.call-start = ((), (), s32[]{:S(2)}) async-start(), calls=%async_computation.25 | async-start | bytes 10485760 | tf_op jit(solution)/shard_map/reduce_scatter | solution.py:201
  266.0 25.3 %copy-start.100 = (s32[2048,1]{0,1:T(1,128)}, s32[2048,1]{0,1:T(1,128)S(1)}, u32[]{:S(2)}) copy-start(s32[2048,1]{0,1:T(1,128)S(1)} %compare_select_fusion) | copy-start | bytes 24580
  266.1 25.2 %copy-start.118 = (bf16[2048]{0:T(1024)(128)(2,1)S(1)}, bf16[2048]{0:T(1024)(128)(2,1)}, u32[]{:S(2)}) copy-start(bf16[2048]{0:T(1024)(128)(2,1)} %param.41) | copy-start | bytes 12292
  287.1 117.8 %copy-start.50 = (bf16[128,2048]{1,0:T(8,128)(2,1)S(1)}, bf16[128,2048]{1,0:T(8,128)(2,1)}, u32[]{:S(2)}) copy-start(bf16[128,2048]{1,0:T(8,128)(2,1)} %param.51) | copy-start | bytes 1572868
  288.0 177.9 %all-to-all-start.1 = ((bf16[4,576,8]{1,2,0:T(8,128)(2,1)}), bf16[4,576,8]{1,2,0:T(8,128)(2,1)S(1)}, u32[]{:S(2)}, u32[]{:S(2)}) async-start(bf16[4,576,8]{1,2,0:T(8,128)(2,1)} %select_convert_fusion.1), calls=%async_computation.3 | async-start | bytes 81920 | tf_op jit(solution)/shard_map/all_to_all | solution.py:237
  291.3 117.1 %copy-start.94 = (f32[2048]{0:T(1024)}, f32[2048]{0:T(1024)S(1)}, u32[]{:S(2)}) copy-start(f32[2048]{0:T(1024)S(1)} %convert_element_type.293) | copy-start | bytes 24580
  409.3 10.4 copy-start.2
  409.3 11.8 copy-start.119
  578.2 110.4 %all-to-all-start.3 = ((bf16[4,576,2048]{2,1,0:T(8,128)(2,1)}), bf16[4,576,2048]{2,1,0:T(8,128)(2,1)}, u32[]{:S(2)}, u32[]{:S(2)}) async-start(bf16[4,576,2048]{2,1,0:T(8,128)(2,1)} %get-tuple-element.430), calls=%async_computation.5 | async-start | bytes 18874368 | tf_op jit(solution)/shard_map/all_to_all | solution.py:271
  585.9 11.0 slice-start
  618.8 69.8 %copy-start.31 = (f32[4,4,144,128]{3,2,0,1:T(8,128)S(1)}, f32[4,4,144,128]{3,2,0,1:T(8,128)}, u32[]{:S(2)}) copy-start(f32[4,4,144,128]{3,2,0,1:T(8,128)} %copy.231) | copy-start | bytes 3538948
  724.5 21.4 copy-start.41
  748.0 22.0 copy-start.46
  748.0 17.4 copy-start.125
  789.9 110.5 %all-to-all-start.2 = ((bf16[4,576,2048]{2,1,0:T(8,128)(2,1)}), bf16[4,576,2048]{2,1,0:T(8,128)(2,1)}, u32[]{:S(2)}, u32[]{:S(2)}) async-start(bf16[4,576,2048]{2,1,0:T(8,128)(2,1)} %bitcast.477), calls=%async_computation.4 | async-start | bytes 18874368 | tf_op jit(solution)/shard_map/all_to_all | solution.py:257
  827.5 18.0 copy-start.49
  827.5 18.0 copy-start.69
  900.4 110.4 %all-to-all-start.4 = ((bf16[4,576,2048]{2,1,0:T(8,128)(2,1)}), bf16[4,576,2048]{2,1,0:T(8,128)(2,1)}, u32[]{:S(2)}, u32[]{:S(2)}) async-start(bf16[4,576,2048]{2,1,0:T(8,128)(2,1)} %bitcast.475), calls=%async_computation.6 | async-start | bytes 18874368 | tf_op jit(solution)/shard_map/all_to_all | solution.py:308
  906.4 179.9 %all-gather.15.cloned.1.call-start = ((), (), s32[]{:S(2)}) async-start(), calls=%async_computation.29 | async-start | bytes 5242880 | tf_op jit(solution)/shard_map/all_gather | solution.py:370
  906.4 21.4 copy-start.17
  906.5 21.4 copy-start.60
  937.6 106.2 %copy-start.96 = (bf16[256,16]{0,1:T(8,128)(2,1)}, bf16[256,16]{0,1:T(8,128)(2,1)S(1)}, u32[]{:S(2)}) copy-start(bf16[256,16]{0,1:T(8,128)(2,1)S(1)} %multiply_convert_fusion.4) | copy-start | bytes 24580
  1032.4 11.5 copy-start.14
  1032.4 11.5 copy-start.84
  1032.4 11.4 copy-start.95
  1051.6 275.7 %reduce-scatter.45.cloned.1.call-start = ((), (), s32[]{:S(2)}) async-start(), calls=%async_computation.38 | async-start | bytes 655360 | tf_op jit(solution)/shard_map/reduce_scatter | solution.py:447
  1053.0 276.1 %reduce-scatter.41.cloned.1.call-start = ((), (), s32[]{:S(2)}) async-start(), calls=%async_computation.36 | async-start | bytes 655360 | tf_op jit(solution)/shard_map/reduce_scatter | solution.py:450
  1060.9 30.6 %copy-start.63 = (bf16[1024,128]{1,0:T(8,128)(2,1)}, bf16[1024,128]{1,0:T(8,128)(2,1)S(1)}, u32[]{:S(2)}) copy-start(bf16[1024,128]{1,0:T(8,128)(2,1)S(1)} %all_gather.33) | copy-start | bytes 786436
  1062.8 28.7 %copy-start.75 = (bf16[512,128]{1,0:T(8,128)(2,1)S(1)}, bf16[512,128]{1,0:T(8,128)(2,1)}, u32[]{:S(2)}) copy-start(bf16[512,128]{1,0:T(8,128)(2,1)} %param.50) | copy-start | bytes 393220
  1062.8 270.5 %reduce-scatter.33.cloned.1.call-start = ((), (), s32[]{:S(2)}) async-start(), calls=%async_computation.31 | async-start | bytes 983040 | tf_op jit(solution)/shard_map/reduce_scatter | solution.py:444
  1271.0 78.9 %reduce-scatter.31.cloned.1.call-start = ((), (), s32[]{:S(2)}) async-start(), calls=%async_computation.30 | async-start | bytes 5242880 | tf_op jit(solution)/shard_map/reduce_scatter | solution.py:441
  1282.3 130.1 %reduce-scatter.61.cloned.1.call-start = ((), (), s32[]{:S(2)}) async-start(), calls=%async_computation.46 | async-start | bytes 1179648
  1288.7 190.4 %reduce-scatter.59.cloned.1.call-start = ((), (), s32[]{:S(2)}) async-start(), calls=%async_computation.45 | async-start | bytes 1179648
  1294.3 251.1 %reduce-scatter.51.cloned.1.call-start = ((), (), s32[]{:S(2)}) async-start(), calls=%async_computation.41 | async-start | bytes 1179648 | tf_op jit(solution)/shard_map/reduce_scatter | solution.py:486
  1299.7 316.5 %reduce-scatter.53.cloned.1.call-start = ((), (), s32[]{:S(2)}) async-start(), calls=%async_computation.42 | async-start | bytes 2359296 | tf_op jit(solution)/shard_map/reduce_scatter | solution.py:489
  1306.9 380.0 %reduce-scatter.47.cloned.1.call-start = ((), (), s32[]{:S(2)}) async-start(), calls=%async_computation.39 | async-start | bytes 2359296 | tf_op jit(solution)/shard_map/reduce_scatter | solution.py:474
  1316.1 10.2 copy-start.40
  1316.1 441.9 %reduce-scatter.49.cloned.1.call-start = ((), (), s32[]{:S(2)}) async-start(), calls=%async_computation.40 | async-start | bytes 2359296 | tf_op jit(solution)/shard_map/reduce_scatter | solution.py:480
  1325.2 454.0 %reduce-scatter.57.cloned.1.call-start = ((), (), s32[]{:S(2)}) async-start(), calls=%async_computation.44 | async-start | bytes 40960
  1326.2 517.2 %reduce-scatter.39.cloned.1.call-start = ((), (), s32[]{:S(2)}) async-start(), calls=%async_computation.35 | async-start | bytes 147456 | tf_op jit(solution)/shard_map/reduce_scatter | solution.py:498
  1327.3 579.3 %reduce-scatter.55.cloned.1.call-start = ((), (), s32[]{:S(2)}) async-start(), calls=%async_computation.43 | async-start | bytes 147456
  1329.1 640.6 %reduce-scatter.43.cloned.1.call-start = ((), (), s32[]{:S(2)}) async-start(), calls=%async_computation.37 | async-start | bytes 147456 | tf_op jit(solution)/shard_map/reduce_scatter | solution.py:501
  1329.7 704.5 %reduce-scatter.37.cloned.1.call-start = ((), (), s32[]{:S(2)}) async-start(), calls=%async_computation.34 | async-start | bytes 442368 | tf_op jit(solution)/shard_map/reduce_scatter | solution.py:495
  1333.2 16.7 copy-start.93
  1333.2 765.4 %reduce-scatter.35.cloned.1.call-start = ((), (), s32[]{:S(2)}) async-start(), calls=%async_computation.33 | async-start | bytes 442368 | tf_op jit(solution)/shard_map/reduce_scatter | solution.py:492
  1348.8 875.9 %all-gather.11.cloned.1.call-start = ((), (), s32[]{:S(2)}) async-start(), calls=%async_computation.27 | async-start | bytes 9437184 | tf_op jit(solution)/shard_map/all_gather | solution.py:519
  1349.6 1000.9 %all-gather.17.cloned.1.call-start = ((), (), s32[]{:S(2)}) async-start(), calls=%async_computation.32 | async-start | bytes 9437184 | tf_op jit(solution)/shard_map/all_gather | solution.py:520
  1616.2 736.7 %copy-start.1 = (bf16[4,128,2048]{2,1,0:T(8,128)(2,1)S(1)}, bf16[4,128,2048]{2,1,0:T(8,128)(2,1)}, u32[]{:S(2)}) copy-start(bf16[4,128,2048]{2,1,0:T(8,128)(2,1)} %param.59) | copy-start | bytes 6291460
  (104 other events, 439.6 us)
Sparse Core Ops, SparseCore 0:
  10.2 127.6 all-gather.6
  143.6 36.9 all-gather.8
  182.7 124.9 all-gather.12
  310.6 19.9 reduce-scatter.28
  333.1 71.6 reduce-scatter.26
  1051.7 34.4 all-gather.14
  1088.8 21.6 reduce-scatter.44
  1113.1 21.6 reduce-scatter.40
  1271.1 24.3 reduce-scatter.32
  1298.0 47.6 reduce-scatter.30
  1349.1 63.2 reduce-scatter.60
  1416.6 62.3 reduce-scatter.58
  1482.5 62.7 reduce-scatter.50
  1549.1 67.0 reduce-scatter.52
  1620.0 66.9 reduce-scatter.46
  1690.8 67.1 reduce-scatter.48
  1760.9 18.2 reduce-scatter.56
  1782.5 60.8 reduce-scatter.38
  1846.7 59.8 reduce-scatter.54
  1909.8 59.8 reduce-scatter.42
  1973.0 61.1 reduce-scatter.36
  2037.5 61.1 reduce-scatter.34
  2100.7 123.9 all-gather.10
  2227.3 123.1 all-gather.16
where the time goes:
time: 2370 us; the launch traced here: 2360 us
  waiting for transfers between devices  1360 us (57%)
  matrix products  444 us (19%)
  local copies, waits for them, and re-layouts  203 us (9%)
  blocking collectives  177 us (7%)
  other arithmetic  128 us (5%)
    unnamed x28, waiting for transfers between devices  203 us
    all_gather x1, waiting for transfers between devices, per_device(): lax.all_gather(tokens, 'grp', axis=0, tiled=True)  127 us
    all_gather x1, waiting for transfers between devices, per_device(): lax.all_gather(layer_out, 'grp', axis=0, tiled=True)  125 us
    all_gather x1, waiting for transfers between devices, per_device(): lax.all_gather(grad_input, 'grp', axis=0, tiled=True)  123 us
    all_to_all x1, blocking collectives, per_device(): lax.all_to_all(send_rows, 'ep', split_axis=0, concat_axis=0, tiled=True)  112 us
    reduce_scatter x1, waiting for transfers between devices, per_device(): lax.psum_scatter(out_part, 'ep', scatter_dimension=0, tiled=True)  74.3 us
    all_to_all x1, waiting for transfers between devices, per_device(): lax.all_to_all(grad_rows_in, 'ep', split_axis=0, concat_axis=0, tiled=True)  71 us
    reduce_scatter x1, waiting for transfers between devices, per_device(): lax.psum_scatter(grad_down_leave.astype(jnp.bfloat16), 'grp', scatter_dim...  69.3 us
  transfers between devices with their start and end apart: 28, of which 23 were waited for; matrix products, arithmetic and copies ran while one was open for 26% of the time, Pallas kernels for 0%

commit v1 on v0

v1 whole, which is shorter than its diff:
```python
import functools

import jax
import jax.numpy as jnp
from jax import lax
from jax.experimental import pallas as pl
from jax.experimental.pallas import tpu as pltpu
from jax.sharding import PartitionSpec as P

HEAD_DIM = 128
EXPERTS = 16
TOP = 8
SETS = 8
RANK = 16
CAP = 144


EPS = 1e-05
SCALE = 2.0
THETA = 10000.0
NEG = -1e30


def rms_scale(value):
    return lax.rsqrt(jnp.mean(value * value, axis=-1, keepdims=True) + EPS)


def rotate(value, cosine, sine):
    half = value.shape[-1] // 2
    turned = jnp.concatenate([-value[..., half:], value[..., :half]], axis=-1)
    return value * cosine + turned * sine


def rotate_back(grad, cosine, sine):
    half = grad.shape[-1] // 2
    moved = grad * sine
    turned = jnp.concatenate([moved[..., half:], -moved[..., :half]], axis=-1)
    return grad * cosine + turned


def angles(position):
    half = HEAD_DIM // 2
    freq = THETA ** (-(jnp.arange(half, dtype=jnp.float32) * 2.0) / HEAD_DIM)
    phase = position.astype(jnp.float32)[:, None] * freq[None, :]
    cosine = jnp.concatenate([jnp.cos(phase), jnp.cos(phase)], axis=-1)
    sine = jnp.concatenate([jnp.sin(phase), jnp.sin(phase)], axis=-1)
    return (cosine[:, None, :], sine[:, None, :])


LINE = 4
VMEM = 62 * 1024 * 1024


def swap(value, axis, bit):
    count = lax.axis_size(axis)
    return lax.ppermute(value, axis, [(i, i ^ bit) for i in range(count)])


def gather_parts(value, axis):
    parts, bit = ({0: value}, lax.axis_size(axis) // 2)
    while bit >= 1:
        for j in list(parts):
            parts[j ^ bit] = swap(parts[j], axis, bit)
        bit //= 2
    return [parts[j] for j in range(len(parts))]


def scatter_parts(parts, axis):
    parts, bit, count = (dict(enumerate(parts)), 1, lax.axis_size(axis))
    while bit < count:
        kept = {}
        for j in parts:
            if not j & bit:
                got = swap(parts[j ^ bit], axis, bit)
                kept[j] = parts[j].astype(jnp.float32) + got.astype(jnp.float32)
        bit *= 2
        if bit < count:
            kept = {j: part.astype(jnp.bfloat16) for j, part in kept.items()}
        parts = kept
    return parts[0]


def sum_relative(value, axis, local):
    count, bit = (lax.axis_size(axis), 1)
    while bit < count:
        got = swap(value, axis, bit)
        got = [got[..., (j ^ bit) * local : ((j ^ bit) + 1) * local] for j in range(count)]
        value = value + jnp.concatenate(got, axis=-1)
        bit *= 2
    return value


def line_scatter(parts, axis, length, stride):
    count = lax.axis_size(axis)
    place = lambda i: i // stride % length
    at = place(lax.axis_index(axis))
    up = [(i, i + stride) for i in range(count) if place(i) + 1 < length]
    down = [(i + stride, i) for i in range(count) if place(i) + 1 < length]
    total = [part.astype(jnp.float32) for part in parts]
    if length == 2:
        return total[0] + lax.ppermute(parts[1], axis, up + down).astype(jnp.float32)
    for step in range(1, length):
        from_below = lax.ppermute(total[length - step].astype(jnp.bfloat16), axis, up)
        from_above = lax.ppermute(total[step].astype(jnp.bfloat16), axis, down)
        low, high = (length - step - 1, (step + 1) % length)
        good = (at >= 1) & (at + length - step - 1 < length)
        total[low] = total[low] + jnp.where(good, from_below.astype(jnp.float32), 0.0)
        good = (at + 1 < length) & (at - (length - step - 1) >= 0)
        total[high] = total[high] + jnp.where(good, from_above.astype(jnp.float32), 0.0)
    return total[0]


def by_place(chunks):
    inner = chunks.shape[0] // LINE
    index = lax.axis_index("grp")
    parts = []
    for q in range(inner):
        group = []
        for p in range(LINE):
            chunk = (index // inner + p) % LINE * inner + (index % inner + q) % inner
            group.append(lax.dynamic_index_in_dim(chunks, chunk, 0, keepdims=False))
        parts.append(jnp.stack(group))
    return parts


def sum_packs(parts):
    inner = len(parts)
    mine = line_scatter(parts, "grp", inner, 1).astype(jnp.bfloat16) if inner > 1 else parts[0]
    return line_scatter([mine[p] for p in range(LINE)], "grp", LINE, inner)


def dot_nn(a, b):
    return jnp.dot(a, b, preferred_element_type=jnp.float32)


def dot_nt(a, b):
    return lax.dot_general(a, b, (((1,), (1,)), ((), ())), preferred_element_type=jnp.float32)


def dot_tn(a, b):
    return lax.dot_general(a, b, (((0,), (0,)), ((), ())), preferred_element_type=jnp.float32)


def expert_kernel(
    line,
    rank_ref,
    weight_ref,
    normed_ref,
    upstream_ref,
    mark_ref,
    gate_w,
    up_w,
    down_w,
    gate_enter,
    gate_leave,
    up_enter,
    up_leave,
    down_enter,
    down_leave,
    place_ref,
    mixed_ref,
    grad_ref,
    score_ref,
    *rest,
):
    inner = len(rest) - 9
    sums, (rows_in, grads_in, hidden, grad_gate, grad_up, marks, out_tile, back_tile, done) = (rest[:inner], rest[inner:])
    f32, bf16 = (jnp.float32, jnp.bfloat16)
    blocks, local, width = (rank_ref.shape[1], rank_ref.shape[3], normed_ref.shape[1])
    cap = mixed_ref.shape[2]
    expert, turn = (pl.program_id(0), pl.program_id(1))
    count = blocks * cap
    ff = hidden.shape[1]
    slots = lax.broadcasted_iota(jnp.int32, (cap, local), 0).astype(f32)
    weights = []
    for b in range(blocks):
        hit = rank_ref[0, b] == slots
        pick = hit.astype(bf16)
        weights.append(jnp.sum(jnp.where(hit, weight_ref[0, b], 0.0), axis=1, keepdims=True))
        here, there = (slice(b * cap, (b + 1) * cap), slice(b * local, (b + 1) * local))
        rows_in[here, :] = dot_nn(pick, normed_ref[there, :]).astype(bf16)
        grads_in[here, :] = dot_nn(pick, upstream_ref[there, :]).astype(bf16)
        marks[here, :] = dot_nn(pick, mark_ref[there, :])
    weight = jnp.concatenate(weights, axis=0)
    mark = marks[...]
    rank = mark.shape[1]
    low = dot_nn(rows_in[...], jnp.concatenate([gate_enter[0], up_enter[0]], axis=1))
    low_gate = (low[:, :rank] * mark).astype(bf16) * SCALE
    low_up = (low[:, rank:] * mark).astype(bf16) * SCALE
    grad_low_down = (dot_nt(grads_in[...], down_leave[0]) * (SCALE * weight) * mark).astype(bf16)
    step = min(256, ff)
    for at in range(0, ff, step):
        cut = slice(at, at + step)
        gate = dot_nn(rows_in[...], gate_w[0, :, cut]) + dot_nn(low_gate, gate_leave[0, :, cut])
        up = dot_nn(rows_in[...], up_w[0, :, cut]) + dot_nn(low_up, up_leave[0, :, cut])
        back = dot_nt(grads_in[...], down_w[0, cut, :]) * weight + dot_nt(grad_low_down, down_enter[0, cut, :])
        sigma = 1.0 / (1.0 + jnp.exp(-gate))
        silu = gate * sigma
        hidden[:, cut] = (silu * up).astype(bf16)
        grad_gate[:, cut] = (back * up * sigma * (1.0 + gate * (1.0 - sigma))).astype(bf16)
        grad_up[:, cut] = (back * silu).astype(bf16)
    low_down = (dot_nn(hidden[...], down_enter[0]) * mark).astype(bf16) * SCALE
    grad_low_gate = (dot_nt(grad_gate[...], gate_leave[0]) * SCALE * mark).astype(bf16)
    grad_low_up = (dot_nt(grad_up[...], up_leave[0]) * SCALE * mark).astype(bf16)
    grad_low = jnp.concatenate([grad_low_gate, grad_low_up], axis=1)
    step = out_tile.shape[3]
    sent = []

    def send(slot, cut):
        there = pl.ds(turn * blocks, blocks)
        copies = [
            pltpu.make_async_copy(out_tile.at[slot], mixed_ref.at[there, expert, :, cut], done.at[0, slot]),
            pltpu.make_async_copy(back_tile.at[slot], grad_ref.at[there, expert, :, cut], done.at[1, slot]),
        ]
        for copy in copies:
            copy.start()
        sent.append(copies)

    score = jnp.zeros((count, 1), f32)
    for at in range(0, width, step):
        cut = slice(at, at + step)
        out = dot_nn(hidden[...], down_w[0, :, cut]) + dot_nn(low_down, down_leave[0, :, cut])
        score = score + jnp.sum(out * grads_in[:, cut].astype(f32), axis=1, keepdims=True)
        back = dot_nt(grad_gate[...], gate_w[0, cut, :]) + dot_nt(grad_up[...], up_w[0, cut, :])
        back = back + dot_nt(grad_low, jnp.concatenate([gate_enter[0, cut, :], up_enter[0, cut, :]], axis=1))
        out = (out * weight).astype(bf16)
        back = back.astype(bf16)
        slot = len(sent) % 2
        if len(sent) >= 2:
            for copy in sent[-2]:
                copy.wait()
        for b in range(blocks):
            out_tile[slot, b] = out[b * cap : (b + 1) * cap]
            back_tile[slot, b] = back[b * cap : (b + 1) * cap]
        send(slot, pl.ds(at, step))
    for b in range(blocks):
        hit = rank_ref[0, b] == slots
        score_ref[0, b] = jnp.sum(jnp.where(hit, score[b * cap : (b + 1) * cap], 0.0), axis=0, keepdims=True)

    def keep(value, row, ref_at):
        piece = value.shape[1] // (line * inner)
        value = value.astype(bf16)
        for c in range(line * inner):
            part = value[:, c * piece : (c + 1) * piece]
            for q in range(inner):
                target = sums[q] if ref_at is None else sums[q]
                target = target.at[place_ref[0, c], 0, slice(row, row + value.shape[0]), slice(ref_at, ref_at + piece)]

                @pl.when((place_ref[1, c] == q) & (turn == 0))
                def _():
                    target[...] = part

                @pl.when((place_ref[1, c] == q) & (turn != 0))
                def _():
                    target[...] = (target[...].astype(f32) + part.astype(f32)).astype(bf16)

    wide = width // (line * inner)
    keep(dot_tn(grad_low, rows_in[...]), 0, 0)
    keep(dot_tn((low_down.astype(f32) * weight).astype(bf16), grads_in[...]), 2 * rank, 0)
    keep(dot_tn(low_gate, grad_gate[...]), 0, wide)
    keep(dot_tn(low_up, grad_up[...]), rank, wide)
    keep(dot_tn(grad_low_down, hidden[...]), 2 * rank, wide)
    for copies in sent[-2:]:
        for copy in copies:
            copy.wait()


def run_experts(rank, weight, normed, upstream, marks, place, inner, *params):
    experts, members, _, local = rank.shape
    group_len, width = normed.shape
    ff = params[0].shape[2]
    low = marks.shape[1]
    blocks = min(members, 4)
    turns = members // blocks
    packs = place.shape[1]
    line = packs // inner
    tokens = blocks * local
    bf16 = jnp.bfloat16
    by_turn = lambda e, r: (e, r, 0, 0)
    once = lambda shape: pl.BlockSpec(shape, lambda e, r: (r, 0), pipeline_mode=pl.Buffered(1))
    per_expert = lambda value: pl.BlockSpec((1,) + value.shape[1:], lambda e, r: (e, 0, 0))
    sums = jax.ShapeDtypeStruct((line, experts, 3 * low, (width + ff) // packs), bf16)
    rows_out = jax.ShapeDtypeStruct((members, experts, CAP, width), bf16)
    count = blocks * CAP
    tile = min(512, width)
    return pl.pallas_call(
        functools.partial(expert_kernel, line),
        grid=(experts, turns),
        out_shape=(rows_out, rows_out, jax.ShapeDtypeStruct(rank.shape, jnp.float32)) + (sums,) * inner,
        in_specs=[
            pl.BlockSpec((1, blocks, 1, local), by_turn),
            pl.BlockSpec((1, blocks, 1, local), by_turn),
            once((tokens, width)),
            once((tokens, width)),
            once((tokens, low)),
        ]
        + [per_expert(value) for value in params]
        + [pl.BlockSpec(memory_space=pltpu.SMEM)],
        out_specs=(
            pl.BlockSpec(memory_space=pl.ANY),
            pl.BlockSpec(memory_space=pl.ANY),
            pl.BlockSpec((1, blocks, 1, local), by_turn),
        )
        + (pl.BlockSpec((line, 1) + sums.shape[2:], lambda e, r: (0, e, 0, 0)),) * inner,
        scratch_shapes=[
            pltpu.VMEM((count, width), bf16),
            pltpu.VMEM((count, width), bf16),
            pltpu.VMEM((count, ff), bf16),
            pltpu.VMEM((count, ff), bf16),
            pltpu.VMEM((count, ff), bf16),
            pltpu.VMEM((count, low), jnp.float32),
            pltpu.VMEM((2, blocks, CAP, tile), bf16),
            pltpu.VMEM((2, blocks, CAP, tile), bf16),
            pltpu.SemaphoreType.DMA((2, 2)),
        ],
        compiler_params=pltpu.CompilerParams(vmem_limit_bytes=VMEM),
        cost_estimate=pl.CostEstimate(
            flops=2 * experts * members * CAP * (width * ff * 6 + 9 * low * (width + ff)),
            bytes_accessed=60_000_000,
            transcendentals=experts * members * CAP * ff,
        ),
        name="experts",
    )(rank, weight, normed, upstream, marks, *params, place)


def combine_kernel(rank_ref, rows_ref, out_ref):
    experts, cap, local = (rows_ref.shape[1], rows_ref.shape[2], rank_ref.shape[3])
    slots = lax.broadcasted_iota(jnp.int32, (cap, local), 0).astype(jnp.float32)
    pick = jnp.concatenate([(rank_ref[e, 0] == slots).astype(jnp.bfloat16) for e in range(experts)], axis=0)
    rows = jnp.concatenate([rows_ref[0, e] for e in range(experts)], axis=0)
    out_ref[0] = dot_tn(pick, rows).astype(out_ref.dtype)


def combine(rank, rows, name):
    experts, members, _, local = rank.shape
    width = rows.shape[3]
    half = width // 2
    return pl.pallas_call(
        combine_kernel,
        grid=(members, 2),
        out_shape=jax.ShapeDtypeStruct((members, local, width), jnp.bfloat16),
        in_specs=[
            pl.BlockSpec((experts, 1, 1, local), lambda b, n: (0, b, 0, 0)),
            pl.BlockSpec((1, experts, CAP, half), lambda b, n: (b, 0, 0, n)),
        ],
        out_specs=pl.BlockSpec((1, local, half), lambda b, n: (b, 0, n)),
        compiler_params=pltpu.CompilerParams(vmem_limit_bytes=VMEM),
        cost_estimate=pl.CostEstimate(
            flops=2 * members * local * experts * CAP * width, bytes_accessed=2 * rows.size, transcendentals=0
        ),
        name=name,
    )(rank, rows)


def rows_of(chunks):
    return chunks.reshape(chunks.shape[0], -1, 128)

def per_device(
    tokens,
    cotangent,
    pack_order,
    doc_lengths,
    doc_sets,
    routes,
    attention_gain,
    query_gain,
    key_gain,
    feed_gain,
    qkv_weight,
    out_weight,
    router_weight,
    gate_weight,
    up_weight,
    down_weight,
    qkv_enter,
    qkv_leave,
    out_enter,
    out_leave,
    router_enter,
    router_leave,
    gate_enter,
    gate_leave,
    up_enter,
    up_leave,
    down_enter,
    down_leave,
):
    members = lax.axis_size("ep")
    packs = lax.axis_size("grp")
    pack = lax.axis_index("grp")
    member = lax.axis_index("ep")
    local, width = tokens.shape
    group_len = local * members
    slice_width = width // members
    heads_here = slice_width // HEAD_DIM
    experts_here = gate_weight.shape[0]
    own_cols = member * slice_width
    f32, bf16 = (jnp.float32, jnp.bfloat16)
    slot = jnp.sum(jnp.where(pack_order == pack, jnp.arange(packs, dtype=jnp.int32), 0))
    named = jnp.sum(jnp.left_shift(jnp.int32(1), routes), axis=1)
    documents_here = jnp.concatenate([doc_lengths[0], doc_sets[0]])
    info = jnp.concatenate([named, jnp.pad(documents_here, (0, 128 - documents_here.shape[0]))])
    info = jnp.stack(gather_parts(info, "grp"))
    info = lax.dynamic_index_in_dim(info, slot ^ pack, 0, keepdims=False)
    blocks = [member ^ j for j in range(members)]
    info = jnp.stack(gather_parts(info, "ep"))
    named_all = info[:, :local]
    docs = doc_lengths.shape[1]
    lengths, sets = (info[0, local : local + docs], info[0, local + docs : local + 2 * docs])
    block_ids = jnp.stack(blocks)
    rows = (block_ids[:, None] * local + jnp.arange(local, dtype=jnp.int32)[None, :]).reshape(-1)
    ends = jnp.cumsum(lengths)
    doc_index = jnp.sum((rows[:, None] >= ends[None, :]).astype(jnp.int32), axis=1)
    member_of = doc_index[:, None] == jnp.arange(docs, dtype=jnp.int32)[None, :]
    position = rows - jnp.sum(jnp.where(member_of, (ends - lengths)[None, :], 0), axis=1)
    chosen = jnp.sum(jnp.where(member_of, sets[None, :], 0), axis=1)
    columns = jnp.arange(SETS * RANK, dtype=jnp.int32) // RANK
    selector = (columns[None, :] == chosen[:, None]).astype(f32)
    own_selector = selector[:local]
    cosine, sine = angles(position)

    token_parts = gather_parts(tokens, "ep")
    upstream_parts = gather_parts(cotangent, "ep")
    gain_one = attention_gain.astype(f32)
    resid = tokens.astype(f32)
    scale_one = rms_scale(resid)
    normed_all = jnp.concatenate(
        [(part.astype(f32) * rms_scale(part.astype(f32)) * gain_one).astype(bf16) for part in token_parts]
    )
    low_all = jnp.einsum("td,kdc->ktc", normed_all, qkv_enter, preferred_element_type=f32)
    low_all = (low_all * selector[None]).astype(bf16)
    projected = jnp.einsum("td,kde->kte", normed_all, qkv_weight, preferred_element_type=f32)
    projected = projected + SCALE * jnp.einsum("ktc,kce->kte", low_all, qkv_leave, preferred_element_type=f32)
    squares = sum_relative(jnp.sum(projected[:2] * projected[:2], axis=-1), "ep", local)
    inverse = lax.rsqrt(squares / width + EPS)[:, :, None]
    gain_query = lax.dynamic_slice_in_dim(query_gain, own_cols, slice_width, 0).astype(f32)
    gain_key = lax.dynamic_slice_in_dim(key_gain, own_cols, slice_width, 0).astype(f32)
    shape = (group_len, heads_here, HEAD_DIM)
    query_norm = (projected[0] * inverse[0] * gain_query).reshape(shape)
    key_norm = (projected[1] * inverse[1] * gain_key).reshape(shape)
    queries = rotate(query_norm, cosine, sine).astype(bf16)
    keys = rotate(key_norm, cosine, sine).astype(bf16)
    values = projected[2].reshape(shape).astype(bf16)
    scale_attn = HEAD_DIM ** (-0.5)
    allowed = (doc_index[:, None] == doc_index[None, :]) & (rows[None, :] <= rows[:, None])
    scores = jnp.einsum("qhd,khd->hqk", queries, keys, preferred_element_type=f32) * scale_attn
    probs = jax.nn.softmax(jnp.where(allowed[None], scores, NEG), axis=-1)
    rounded_probs = probs.astype(bf16)
    attended = jnp.einsum("hqk,khd->qhd", rounded_probs, values, preferred_element_type=f32)
    attended = attended.reshape(group_len, slice_width).astype(bf16)
    out_part = jnp.dot(attended, out_weight, preferred_element_type=f32).astype(bf16)
    low_part = jnp.dot(attended, out_enter, preferred_element_type=f32).astype(bf16)
    cut = lambda value: [value[j * local : (j + 1) * local] for j in range(members)]
    out_sum = scatter_parts(cut(out_part), "ep")
    low_sum = scatter_parts(cut(low_part), "ep")
    low_out = (low_sum * own_selector).astype(bf16)
    hidden_state = resid + out_sum + SCALE * jnp.dot(low_out, out_leave, preferred_element_type=f32)
    scale_two = rms_scale(hidden_state)
    gain_two = feed_gain.astype(f32)
    normed_two = (hidden_state * scale_two * gain_two).astype(bf16)

    normed_two_parts = gather_parts(normed_two, "ep")
    normed_two_all = jnp.concatenate(normed_two_parts)
    upstream_all = jnp.concatenate(upstream_parts)
    low_router = jnp.dot(normed_two_all, router_enter, preferred_element_type=f32)
    low_router = (low_router * selector).astype(bf16)
    logits = jnp.dot(normed_two_all, router_weight, preferred_element_type=f32)
    logits = logits + SCALE * jnp.dot(low_router, router_leave, preferred_element_type=f32)
    probs_router = jax.nn.softmax(logits, axis=-1)
    expert_ids = jnp.arange(EXPERTS, dtype=jnp.int32)[None, :, None]
    hot = (jnp.right_shift(named_all[:, None, :], expert_ids) & 1).astype(f32)
    before = jnp.triu(jnp.ones((local, local), bf16), 1)
    rank = jnp.where(hot > 0, dot_nn(hot.astype(bf16), before), -1.0)
    first = member * experts_here
    of_here = lambda value: lax.dynamic_slice_in_dim(value, first, experts_here, 1).transpose(1, 0, 2)[:, :, None, :]
    rank_here = of_here(rank)
    weight_here = of_here(probs_router.reshape(members, local, EXPERTS).transpose(0, 2, 1))
    inner = packs // LINE
    chunk_ids = jnp.arange(packs, dtype=jnp.int32)
    place = jnp.stack([(chunk_ids // inner - pack // inner) % LINE, (chunk_ids % inner - pack % inner) % inner])
    mixed_rows, grad_rows, row_scores, *expert_sums = run_experts(
        rank_here,
        weight_here,
        normed_two_all,
        upstream_all,
        selector.astype(bf16),
        place,
        inner,
        gate_weight,
        up_weight,
        down_weight,
        gate_enter,
        gate_leave,
        up_enter,
        up_leave,
        down_enter,
        down_leave,
    )
    grad_mixed = combine(rank_here, grad_rows, "combine_grad")
    mixed_out = combine(rank_here, mixed_rows, "combine_out")
    expert_sum = sum_packs(expert_sums)
    wide = width // packs

    mixed_sum = scatter_parts([mixed_out[j] for j in range(members)], "ep")
    layer_out = (hidden_state + mixed_sum).astype(bf16)

    dot = lambda spec, a, b: jnp.einsum(spec, a, b, preferred_element_type=f32)
    grad_probs_all = jnp.zeros((EXPERTS, group_len), f32)
    grad_probs_here = row_scores.reshape(experts_here, group_len)
    grad_probs_all = lax.dynamic_update_slice_in_dim(grad_probs_all, grad_probs_here, first, 0)
    grad_probs_all = sum_relative(grad_probs_all, "ep", local).T
    grad_logits = probs_router * (grad_probs_all - jnp.sum(probs_router * grad_probs_all, axis=-1, keepdims=True))
    grad_logits = grad_logits.astype(bf16)
    grad_low_router = (dot("te,ce->tc", grad_logits, router_leave) * SCALE * selector).astype(bf16)
    slice_of = lambda value: lax.dynamic_slice_in_dim(value, own_cols, slice_width, 1)
    grad_router_enter = dot("tc,td->cd", grad_low_router, slice_of(normed_two_all))
    grad_router_leave = SCALE * dot("tc,te->ce", low_router, grad_logits)
    grad_normed_two = scatter_parts([grad_mixed[j] for j in range(members)], "ep")
    grad_normed_two = grad_normed_two + dot("te,de->td", grad_logits[:local], router_weight)
    grad_normed_two = grad_normed_two + dot("tc,dc->td", grad_low_router[:local], router_enter)
    grad_out = cotangent.astype(f32)
    weighted_two = gain_two * grad_normed_two
    grad_hidden_state = (
        grad_out
        + scale_two * weighted_two
        - hidden_state * scale_two**3 * jnp.mean(hidden_state * weighted_two, axis=-1, keepdims=True)
    )
    grad_branch = grad_hidden_state.astype(bf16)
    branch_all = jnp.concatenate(gather_parts(grad_branch, "ep"))
    low_out_all = jnp.concatenate(gather_parts(low_out, "ep"))
    low_grad_all = (dot("td,cd->tc", branch_all, out_leave) * SCALE * selector).astype(bf16)
    grad_att = dot("td,ed->te", branch_all, out_weight) + dot("tc,ec->te", low_grad_all, out_enter)
    grad_att = grad_att.astype(bf16).reshape(shape)
    grad_out_enter = dot("tc,te->ce", low_grad_all, attended)
    grad_out_leave = SCALE * dot("tc,td->cd", low_out_all, slice_of(branch_all))

    grad_probs_att = dot("qhd,khd->hqk", grad_att, values)
    inner = jnp.sum(probs * grad_probs_att, axis=-1, keepdims=True)
    grad_scores = (probs * (grad_probs_att - inner) * scale_attn).astype(bf16)
    grad_queries = dot("hqk,khd->qhd", grad_scores, keys)
    grad_keys = dot("hqk,qhd->khd", grad_scores, queries)
    grad_values = dot("hqk,qhd->khd", rounded_probs, grad_att)
    grad_query_norm = rotate_back(grad_queries, cosine, sine).reshape(group_len, slice_width)
    grad_key_norm = rotate_back(grad_keys, cosine, sine).reshape(group_len, slice_width)
    terms = jnp.stack(
        [
            jnp.sum(projected[0] * gain_query * grad_query_norm, axis=-1),
            jnp.sum(projected[1] * gain_key * grad_key_norm, axis=-1),
        ]
    )
    terms = sum_relative(terms, "ep", local)
    grad_query_proj = inverse[0] * gain_query * grad_query_norm - projected[0] * inverse[0] ** 3 * (terms[0] / width)[:, None]
    grad_key_proj = inverse[1] * gain_key * grad_key_norm - projected[1] * inverse[1] ** 3 * (terms[1] / width)[:, None]
    grad_proj = jnp.stack([grad_query_proj, grad_key_proj, grad_values.reshape(group_len, slice_width)]).astype(bf16)
    grad_qkv_leave = SCALE * dot("ktc,kte->kce", low_all, grad_proj)
    part_input = dot("kte,kde->td", grad_proj, qkv_weight).astype(bf16)
    part_low = (SCALE * dot("kte,kce->tkc", grad_proj, qkv_leave) * selector[:, None, :]).astype(bf16)
    part_low = part_low.reshape(group_len, -1)
    low_own = scatter_parts(cut(part_low), "ep").astype(bf16)
    low_grads = jnp.concatenate(gather_parts(low_own, "ep"))
    grad_qkv_enter = dot("tc,te->ce", low_grads, slice_of(normed_all)).reshape(3, -1, slice_width)
    input_part = scatter_parts(cut(part_input), "ep")
    grad_normed_one = input_part + dot("tkc,kdc->td", low_own.reshape(local, 3, -1), qkv_enter)
    weighted_one = gain_one * grad_normed_one
    grad_input = (
        grad_hidden_state
        + scale_one * weighted_one
        - resid * scale_one**3 * jnp.mean(resid * weighted_one, axis=-1, keepdims=True)
    )
    grad_input = grad_input.astype(bf16)

    by_rows = lambda value: rows_of(value.astype(bf16).reshape(value.shape[0], packs, -1).transpose(1, 0, 2).reshape(packs, -1))
    leave_rows = lax.dynamic_slice_in_dim(grad_router_leave, member * (SETS * RANK // members), SETS * RANK // members, 0)
    leave_chunks = leave_rows.reshape(leave_rows.shape[0], packs, -1).transpose(1, 0, 2).reshape(packs, -1)
    leave_size = leave_chunks.shape[1]
    leave_chunks = jnp.pad(leave_chunks, ((0, 0), (0, 128 - leave_size))).astype(bf16)
    rest = [grad_out_enter[None], grad_out_leave[None], grad_router_enter[None], grad_qkv_enter, grad_qkv_leave]
    pieces = [by_rows(value.reshape(value.shape[0], -1)) for value in rest]
    pieces.append(leave_chunks[:, None, :])
    summed = sum_packs(by_place(jnp.concatenate(pieces, axis=1)))
    outs, at = ([], 0)
    for value, piece in zip(rest, pieces):
        size = piece.shape[1]
        outs.append(summed[at : at + size].reshape(value.shape[0], -1, slice_width))
        at += size
    router_leave_out = summed[at, :leave_size].reshape(SETS * RANK // members, -1)
    low = SETS * RANK
    turn = lambda value: jnp.swapaxes(value, -1, -2)
    return (
        layer_out,
        grad_input,
        turn(outs[3]),
        outs[4],
        turn(outs[0][0]),
        outs[1][0],
        turn(outs[2][0]),
        router_leave_out,
        turn(expert_sum[:, :low, :wide]),
        expert_sum[:, :low, wide:],
        turn(expert_sum[:, low : 2 * low, :wide]),
        expert_sum[:, low : 2 * low, wide:],
        turn(expert_sum[:, 2 * low :, wide:]),
        expert_sum[:, 2 * low :, :wide],
    )


def solution(mesh):
    in_specs = (
        P(("grp", "ep"), None),
        P(("grp", "ep"), None),
        P(),
        P("grp", None),
        P("grp", None),
        P(("grp", "ep"), None),
        P(),
        P(),
        P(),
        P(),
        P(None, None, "ep"),
        P("ep", None),
        P(),
        P("ep", None, None),
        P("ep", None, None),
        P("ep", None, None),
        P(),
        P(None, None, "ep"),
        P("ep", None),
        P(),
        P(),
        P(),
        P("ep", None, None),
        P("ep", None, None),
        P("ep", None, None),
        P("ep", None, None),
        P("ep", None, None),
        P("ep", None, None),
    )
    out_specs = (
        P(("grp", "ep"), None),
        P(("grp", "ep"), None),
        P(None, "ep", "grp"),
        P(None, "grp", "ep"),
        P("ep", "grp"),
        P("grp", "ep"),
        P("ep", "grp"),
        P("ep", "grp"),
        P("ep", "grp", None),
        P("ep", None, "grp"),
        P("ep", "grp", None),
        P("ep", None, "grp"),
        P("ep", "grp", None),
        P("ep", None, "grp"),
    )
    return jax.shard_map(
        per_device, mesh=mesh, in_specs=in_specs, out_specs=out_specs, check_vma=False
    )
```

time: 2370 us -> 686 us (0.29)
  waiting for transfers between devices: 1360 us -> 212 us
  matrix products: 444 us -> 144 us
  blocking collectives: 177 us -> 0 us
  local copies, waits for them, and re-layouts: 203 us -> 41.3 us
  Pallas kernels: 0 us -> 143 us
  other arithmetic: 128 us -> 76.2 us
  starting transfers between devices: 23 us -> 61.3 us
    reduce_scatter x14 -> x0, waiting for transfers between devices: 595 us -> none  [the longest x1 74.3 us: per_device(): lax.psum_scatter(out_part, 'ep', scatter_dimension=0, tiled=True)]
    all_gather x6 -> x0, waiting for transfers between devices: 417 us -> none  [the longest x1 127 us: per_device(): lax.all_gather(tokens, 'grp', axis=0, tiled=True)]
    dot_general x61 -> x29, matrix products: 433 us -> 118 us  [the longest x19 94.4 us: per_device(): dot = lambda spec, a, b: jnp.einsum(spec, a, b, preferred_element_type=f32)]
    ppermute x0 -> x66, waiting for transfers between devices: none -> 212 us  [the longest x52 146 us: swap(): return lax.ppermute(value, axis, [(i, i ^ bit) for i in range(count)])]
    unnamed x28 -> x0, waiting for transfers between devices: 203 us -> none
    all_to_all x4 -> x0, waiting for transfers between devices: 145 us -> none  [the longest x1 71 us: per_device(): lax.all_to_all(grad_rows_in, 'ep', split_axis=0, concat_axis=0, tiled=True)]
    pallas_call x0 -> x3, Pallas kernels: none -> 143 us  [the longest x1 124 us: run_experts(): pl.pallas_call(functools.partial(expert_kernel, line), grid=(experts, tur...]
    all_to_all x1 -> x0, blocking collectives: 112 us -> none  [per_device(): lax.all_to_all(send_rows, 'ep', split_axis=0, concat_axis=0, tiled=True)]
  transfers between devices with their start and end apart: 28 -> 66, of which waited for: 23 -> 28; matrix products, arithmetic and copies ran while one was open for 26% -> 26% of each run, Pallas kernels for 0% -> 1%
where the time goes in v1:
time: 686 us; the launch traced here: 682 us
  waiting for transfers between devices  212 us (31%)
  matrix products  144 us (21%)
  Pallas kernels  143 us (21%)
  other arithmetic  76.2 us (11%)
  starting transfers between devices  61.3 us (9%)
  local copies, waits for them, and re-layouts  41.3 us (6%)
    ppermute x52, waiting for transfers between devices, swap(): return lax.ppermute(value, axis, [(i, i ^ bit) for i in range(count)])  146 us
    pallas_call x1, Pallas kernels, run_experts(): pl.pallas_call(functools.partial(expert_kernel, line), grid=(experts, tur...  124 us
    dot_general x19, matrix products, per_device(): dot = lambda spec, a, b: jnp.einsum(spec, a, b, preferred_element_type=f32)  94.4 us
    ppermute x6, waiting for transfers between devices, line_scatter(): lax.ppermute(total[length - step].astype(jnp.bfloat16), axis, up)  46.8 us
    ppermute x52, starting transfers between devices, swap(): return lax.ppermute(value, axis, [(i, i ^ bit) for i in range(count)])  32.6 us
    pallas_call x2, Pallas kernels, combine(): pl.pallas_call(combine_kernel, grid=(members, 2), out_shape=jax.ShapeDtyp...  19.7 us
    ppermute x6, waiting for transfers between devices, line_scatter(): from_above = lax.ppermute(total[step].astype(jnp.bfloat16), axis, down)  19 us
    ppermute x6, starting transfers between devices, line_scatter(): lax.ppermute(total[length - step].astype(jnp.bfloat16), axis, up)  18.6 us
  transfers between devices with their start and end apart: 66, of which 28 were waited for; matrix products, arithmetic and copies ran while one was open for 26% of the time, Pallas kernels for 1%

profile of v1, /device:TPU:0, one launch (start us, length us, event | category | flops | bytes accessed | tf_op | source)
XLA Modules:
  0.0 681.8 jit_solution(6724540218279368938)
XLA Ops:
  2.9 4.0 collective-permute-start.6
  24.0 2.1 compare_and_fusion
  26.1 8.2 %collective-permute-done.1 = bf16[256,2048]{1,0:T(8,128)(2,1)S(1)} collective-permute-done((bf16[256,2048]{1,0:T(8,128)(2,1)}, bf16[256,2048]{1,0:T(8,128)(2,1)S(1)}, u32[]{:S(2)}, u32[]{:S(2)}) %collective-permute-start.1) | collective-permute-done | bytes 1048608 | tf_op jit(solution)/shard_map/ppermute | solution.py:56
  38.2 2.3 fusion.40
  40.6 5.3 fusion.69
  46.8 3.6 fusion.169
  50.4 13.8 %bitcast_add_fusion = f32[3,1024,512]{1,2,0:T(8,128)S(1)} fusion(f32[3,1024,512]{1,2,0:T(8,128)} %fusion.169, bf16[3,2048,512]{2,1,0:T(8,128)(2,1)} %param.38, bf16[256,2048]{1,0:T(8,128)(2,1)} %copy-done.28, bf16[256,2048]{1,0:T(8,128)(2,1)} %copy-done.27, bf16[256,2048]{1,0:T(8,128)(2,1)} %copy-done.26, bf16[256,2048]{1,0:T(8,128)(2,1)} %copy-done.24), kind=kOutput, calls=%fused_computation.14 | convolution fusion | flops 6462373888 | bytes 23068672 | tf_op jit(solution)/shard_map/td,kde->kte/dot_general | solution.py:432
  71.6 1.9 fusion.49
  73.5 12.3 %fusion.165 = (f32[4,1024]{1,0:T(4,128)S(1)}, f32[4,1024,1024]{1,2,0:T(8,128)}) fusion(pred[1024,1024]{0,1:T(8,128)(4,1)} %compare_and_fusion, bf16[1024,4,128]{0,2,1:T(8,128)(2,1)} %get-tuple-element.130, bf16[1024,4,128]{0,2,1:T(8,128)(2,1)} %get-tuple-element.129), kind=kOutput, calls=%fused_computation.350 | convolution fusion | flops 1090520064 | bytes 19939328 | tf_op jit(solution)/shard_map/sub | solution.py:447
  85.9 7.2 %fusion.62 = bf16[4,128,1024]{2,1,0:T(8,128)(2,1)S(1)} fusion(bf16[1024,4,128]{0,2,1:T(8,128)(2,1)S(1)} %bitcast.250, f32[4,1024,1024]{1,2,0:T(8,128)} %get-tuple-element.193, f32[4,1024]{1,0:T(4,128)S(1)} %get-tuple-element.192), kind=kOutput, calls=%fused_computation.117 | convolution fusion | flops 1082654720 | bytes 18890752 | tf_op jit(solution)/shard_map/hqk,khd->qhd/dot_general | solution.py:449
  93.2 2.4 convolution_convert_fusion
  96.4 2.1 collective-permute-done.13
  104.4 21.9 %collective-permute-done.17 = bf16[256,128]{1,0:T(8,128)(2,1)S(1)} collective-permute-done((bf16[256,128]{1,0:T(8,128)(2,1)S(1)}, bf16[256,128]{1,0:T(8,128)(2,1)S(1)}, u32[]{:S(2)}, u32[]{:S(2)}) %collective-permute-start.17) | collective-permute-done | bytes 65568 | tf_op jit(solution)/shard_map/ppermute | solution.py:56
  128.0 1.8 multiply_reduce_fusion.4
  133.6 15.4 %collective-permute-done.25 = bf16[256,2048]{1,0:T(8,128)(2,1)} collective-permute-done((bf16[256,2048]{1,0:T(8,128)(2,1)}, bf16[256,2048]{1,0:T(8,128)(2,1)}, u32[]{:S(2)}, u32[]{:S(2)}) %collective-permute-start.25) | collective-permute-done | bytes 1048608 | tf_op jit(solution)/shard_map/ppermute | solution.py:56
  149.6 21.1 %collective-permute-done.19 = s32[384]{0:T(512)S(1)} collective-permute-done((s32[384]{0:T(512)S(1)}, s32[384]{0:T(512)S(1)}, u32[]{:S(2)}, u32[]{:S(2)}) %collective-permute-start.19) | collective-permute-done | bytes 1568 | tf_op jit(solution)/shard_map/ppermute | solution.py:56
  173.3 3.8 pad_maximum_fusion.2.upstream_ref
  177.0 6.1 pad_maximum_fusion.1.normed_ref
  187.1 123.6 %experts.1 = (bf16[4,4,144,2048]{3,2,1,0:T(8,128)(2,1)}, bf16[4,4,144,2048]{3,2,1,0:T(8,128)(2,1)}, f32[4,4,1,256]{3,2,1,0:T(1,128)}, bf16[4,4,384,384]{3,2,1,0:T(8,128)(2,1)}, bf16[4,4,384,384]{3,2,1,0:T(8,128)(2,1)}) custom-call(f32[4,4,1,256]{3,2,1,0:T(1,128)} %broadcast_in_dim.141.rank_ref, f32[4,4,1,256]{3,2,1,0:T(1,128)} %broadcast_in_dim.142.weight_ref, ...), custom_call_target="tpu_custom_call" | custom-call | flops 74289512448 | bytes 60000000 | tf_op jit(solution)/shard_map/experts/pallas_call | solution.py:286
  310.7 9.9 %combine_grad.1 = bf16[4,256,2048]{2,1,0:T(8,128)(2,1)} custom-call(f32[4,4,1,256]{3,2,1,0:T(1,128)} %broadcast_in_dim.141.rank_ref, bf16[4,4,144,2048]{3,2,1,0:T(8,128)(2,1)} %get-tuple-element.20.rows_ref), custom_call_target="tpu_custom_call" | custom-call | flops 2415919104 | bytes 9437184 | tf_op jit(solution)/shard_map/combine_grad/pallas_call | solution.py:338
  320.6 3.1 slice_bitcast_fusion.6
  325.2 9.8 %combine_out.1 = bf16[4,256,2048]{2,1,0:T(8,128)(2,1)} custom-call(f32[4,4,1,256]{3,2,1,0:T(1,128)} %broadcast_in_dim.141.rank_ref, bf16[4,4,144,2048]{3,2,1,0:T(8,128)(2,1)} %get-tuple-element.19.rows_ref), custom_call_target="tpu_custom_call" | custom-call | flops 2415919104 | bytes 9437184 | tf_op jit(solution)/shard_map/combine_out/pallas_call | solution.py:338
  337.8 1.7 slice_bitcast_fusion.10
  346.4 20.7 %collective-permute-done.32 = bf16[256,2048]{1,0:T(8,128)(2,1)S(1)} collective-permute-done((bf16[256,2048]{1,0:T(8,128)(2,1)S(1)}, bf16[256,2048]{1,0:T(8,128)(2,1)S(1)}, u32[]{:S(2)}, u32[]{:S(2)}) %collective-permute-start.32) | collective-permute-done | bytes 1048608 | tf_op jit(solution)/shard_map/ppermute | solution.py:56
  368.2 20.5 %collective-permute-done.29 = bf16[256,2048]{1,0:T(8,128)(2,1)S(1)} collective-permute-done((bf16[256,2048]{1,0:T(8,128)(2,1)S(1)}, bf16[256,2048]{1,0:T(8,128)(2,1)S(1)}, u32[]{:S(2)}, u32[]{:S(2)}) %collective-permute-start.29) | collective-permute-done | bytes 1048608 | tf_op jit(solution)/shard_map/ppermute | solution.py:56
  388.7 4.6 fusion.146
  395.3 3.6 pad_maximum_fusion
  398.8 18.9 %collective-permute-done.36 = bf16[256,2048]{1,0:T(8,128)(2,1)} collective-permute-done((bf16[256,2048]{1,0:T(8,128)(2,1)}, bf16[256,2048]{1,0:T(8,128)(2,1)}, u32[]{:S(2)}, u32[]{:S(2)}) %collective-permute-start.36) | collective-permute-done | bytes 1048608 | tf_op jit(solution)/shard_map/ppermute | solution.py:56
  419.5 3.7 collective-permute-done.47
  426.4 2.3 pad_maximum_fusion.3
  431.8 2.4 add_convert_fusion.5
  434.3 8.1 %fusion.171 = f32[4,1024,1024]{1,2,0:T(8,128)} fusion(bf16[1024,4,128]{0,2,1:T(8,128)(2,1)S(1)} %bitcast.255, bf16[1024,4,128]{0,2,1:T(8,128)(2,1)S(1)} %bitcast.251), kind=kOutput, calls=%fused_computation.354 | convolution fusion | flops 1073741824 | bytes 18874368 | tf_op jit(solution)/shard_map/qhd,khd->hqk/dot_general | solution.py:507
  442.4 23.8 %fusion.10 = f32[4,128,1024]{2,1,0:T(8,128)} fusion(bf16[1024,4,128]{0,2,1:T(8,128)(2,1)} %get-tuple-element.130, f32[4,1024,1024]{1,2,0:T(8,128)} %fusion.171, f32[4,1024,1024]{1,2,0:T(8,128)} %get-tuple-element.193, f32[4,1024]{1,0:T(4,128)S(1)} %copy-done.84), kind=kOutput, calls=%fused_computation.15 | convolution fusion | flops 1103107072 | bytes 36716544 | tf_op jit(solution)/shard_map/hqk,qhd->khd/dot_general | solution.py:507
  466.3 25.7 %bitcast_multiply_fusion.4 = (f32[1024,4,128]{0,2,1:T(8,128)}, f32[1024,4,128]{0,2,1:T(8,128)}, f32[4,128,1024]{2,1,0:T(8,128)}) fusion(f32[1024,128]{0,1:T(8,128)S(1)} %copy-done.31, f32[4,128,1024]{2,1,0:T(8,128)} %fusion.10, bf16[1024,4,128]{0,2,1:T(8,128)(2,1)} %get-tuple-element.129, f32[4,1024,1024]{1,2,0:T(8,128)} %fusion.171, ...), kind=kOutput, calls=%fused_computation.96 | convolution fusion | flops 1104155648 | bytes 43532288 | tf_op jit(solution)/shard_map/hqk,khd->qhd/dot_general | solution.py:507
  491.9 1.9 fusion.152
  493.9 1.9 fusion.153
  496.9 2.5 multiply_reduce_fusion.2
  499.8 8.8 %fusion.65 = bf16[4,128,1024]{2,1,0:T(8,128)(2,1)S(1)} fusion(bf16[1024,4,128]{0,2,1:T(8,128)(2,1)S(1)} %bitcast.256, f32[4,1024,1024]{1,2,0:T(8,128)} %get-tuple-element.193, f32[4,1024]{1,0:T(4,128)S(1)} %copy-done.85), kind=kOutput, calls=%fused_computation.118 | convolution fusion | flops 1082654720 | bytes 18890752 | tf_op jit(solution)/shard_map/hqk,qhd->khd/dot_general | solution.py:507
  510.2 2.2 collective-permute-done.39
  515.2 1.7 fusion.78
  521.1 5.1 collective-permute-done.45
  526.7 11.4 %bitcast_convert_fusion = bf16[1024,2048]{1,0:T(8,128)(2,1)} fusion(bf16[3,2048,512]{2,1,0:T(8,128)(2,1)} %param.38, bf16[1,1024,512]{1,2,0:T(8,128)(2,1)S(1)} %bitcast.290, bf16[1,1024,512]{1,2,0:T(8,128)(2,1)S(1)} %copy-done.33, bf16[1,1024,512]{1,2,0:T(8,128)(2,1)S(1)} %get-tuple-element.90), kind=kOutput, calls=%fused_computation.9 | convolution fusion | flops 6447693824 | bytes 13631488 | tf_op jit(solution)/shard_map/kte,kde->td/dot_general | solution.py:507
  540.9 2.0 convolution_convert_fusion.1
  549.6 5.2 add_convert_fusion
  554.9 1.6 slice_bitcast_fusion
  556.5 1.9 copy-done.8
  558.4 3.5 collective-permute-start.60
  563.6 4.3 collective-permute-start.53
  570.7 18.7 %collective-permute-done.53 = bf16[577,128]{1,0:T(8,128)(2,1)S(1)} collective-permute-done((bf16[577,128]{1,0:T(8,128)(2,1)S(1)}, bf16[577,128]{1,0:T(8,128)(2,1)S(1)}, u32[]{:S(2)}, u32[]{:S(2)}) %collective-permute-start.53) | collective-permute-done | bytes 147744 | tf_op jit(solution)/shard_map/ppermute | solution.py:103
  589.5 5.2 collective-permute-done.54
  598.9 4.5 collective-permute-done.57
  604.4 2.2 collective-permute-start.56
  607.9 3.6 fusion.27
  611.5 5.6 collective-permute-start.62
  618.4 2.9 add_convert_fusion.3
  621.3 1.7 collective-permute-start.42
  627.1 12.3 %collective-permute-done.62 = bf16[4,384,384]{2,1,0:T(8,128)(2,1)} collective-permute-done((bf16[4,384,384]{2,1,0:T(8,128)(2,1)}, bf16[4,384,384]{2,1,0:T(8,128)(2,1)}, u32[]{:S(2)}, u32[]{:S(2)}) %collective-permute-start.62) | collective-permute-done | bytes 1179680 | tf_op jit(solution)/shard_map/ppermute | solution.py:103
  639.4 5.1 collective-permute-done.64
  644.5 3.0 add_convert_fusion.2
  650.8 2.4 fusion.45
  653.2 3.2 fusion.44
  656.4 14.5 %collective-permute-done.63 = bf16[4,384,384]{2,1,0:T(8,128)(2,1)S(1)} collective-permute-done((bf16[4,384,384]{2,1,0:T(8,128)(2,1)S(1)}, bf16[4,384,384]{2,1,0:T(8,128)(2,1)S(1)}, u32[]{:S(2)}, u32[]{:S(2)}) %collective-permute-start.63) | collective-permute-done | bytes 1179680 | tf_op jit(solution)/shard_map/ppermute | solution.py:103
  670.9 4.2 collective-permute-done.65
  675.1 1.8 fusion.28
  (443 shorter events, 115.2 us)
Async XLA Ops:
  2.9 12.3 %collective-permute-start.6 = (s32[384]{0:T(512)S(1)}, s32[384]{0:T(512)S(1)}, u32[]{:S(2)}, u32[]{:S(2)}) collective-permute-start(s32[384]{0:T(512)S(1)} %pad_add_fusion.3), channel_id=1, source_target_pairs={{0,16},{4,20},{8,24},{12,28},{16,0},{20,4},{24,8},{28,12},{1,17},{... | collective-permute-start | bytes 4616 | tf_op jit(solution)/shard_map/ppermute | solution.py:56
  6.9 9.3 %collective-permute-start.4 = (s32[384]{0:T(512)S(1)}, s32[384]{0:T(512)S(1)}, u32[]{:S(2)}, u32[]{:S(2)}) collective-permute-start(s32[384]{0:T(512)S(1)} %pad_add_fusion.3), channel_id=1, source_target_pairs={{0,8},{4,12},{8,0},{12,4},{16,24},{20,28},{24,16},{28,20},{1,9},{5... | collective-permute-start | bytes 4616 | tf_op jit(solution)/shard_map/ppermute | solution.py:56
  8.5 12.2 %collective-permute-start.3 = (s32[384]{0:T(512)S(1)}, s32[384]{0:T(512)S(1)}, u32[]{:S(2)}, u32[]{:S(2)}) collective-permute-start(s32[384]{0:T(512)S(1)} %pad_add_fusion.3), channel_id=1, source_target_pairs={{0,4},{4,0},{8,12},{12,8},{16,20},{20,16},{24,28},{28,24},{1,5},{5... | collective-permute-start | bytes 4616 | tf_op jit(solution)/shard_map/ppermute | solution.py:56
  10.0 24.3 %collective-permute-start.1 = (bf16[256,2048]{1,0:T(8,128)(2,1)}, bf16[256,2048]{1,0:T(8,128)(2,1)S(1)}, u32[]{:S(2)}, u32[]{:S(2)}) collective-permute-start(bf16[256,2048]{1,0:T(8,128)(2,1)} %param.28), channel_id=1, source_target_pairs={{0,2},{1,3},{2,0},{3,1},{4,6},{5,7},{6,4},{7,5},{8,10},{9,11},{10,... | collective-permute-start | bytes 3145736 | tf_op jit(solution)/shard_map/ppermute | solution.py:56
  15.2 3.7 collective-permute-start.8
  15.7 5.1 collective-permute-start.7
  16.2 4.7 collective-permute-start.5
  18.9 3.6 collective-permute-start.9
  20.8 15.6 %collective-permute-start = (bf16[256,2048]{1,0:T(8,128)(2,1)}, bf16[256,2048]{1,0:T(8,128)(2,1)}, u32[]{:S(2)}, u32[]{:S(2)}) collective-permute-start(bf16[256,2048]{1,0:T(8,128)(2,1)} %param.28), channel_id=1, source_target_pairs={{0,1},{1,0},{2,3},{3,2},{4,5},{5,4},{6,7},{7,6},{8,9},{9,8},{10,11... | collective-permute-start | bytes 3145736 | tf_op jit(solution)/shard_map/ppermute | solution.py:56
  34.3 3.6 collective-permute-start.2
  64.6 1.4 collective-permute-start.10
  66.0 3.7 collective-permute-start.11
  95.8 2.7 collective-permute-start.13
  95.9 32.1 %collective-permute-start.12 = (bf16[256,2048]{1,0:T(8,128)(2,1)S(1)}, bf16[256,2048]{1,0:T(8,128)(2,1)S(1)}, u32[]{:S(2)}, u32[]{:S(2)}) collective-permute-start(bf16[256,2048]{1,0:T(8,128)(2,1)S(1)} %get-tuple-element.104), channel_id=1, source_target_pairs={{0,1},{1,0},{2,3},{3,2},{4,5},{5,4},{6,7},{7,6},{8,9},{9,8},{10,11... | collective-permute-start | bytes 3145736 | tf_op jit(solution)/shard_map/ppermute | solution.py:56
  98.9 29.1 %collective-permute-start.14 = (bf16[256,2048]{1,0:T(8,128)(2,1)S(1)}, bf16[256,2048]{1,0:T(8,128)(2,1)S(1)}, u32[]{:S(2)}, u32[]{:S(2)}) collective-permute-start(bf16[256,2048]{1,0:T(8,128)(2,1)S(1)} %add_convert_fusion.7), channel_id=1, source_target_pairs={{0,2},{1,3},{2,0},{3,1},{4,6},{5,7},{6,4},{7,5},{8,10},{9,11},{10,... | collective-permute-start | bytes 3145736 | tf_op jit(solution)/shard_map/ppermute | solution.py:56
  101.1 3.4 collective-permute-start.15
  102.3 24.0 %collective-permute-start.17 = (bf16[256,128]{1,0:T(8,128)(2,1)S(1)}, bf16[256,128]{1,0:T(8,128)(2,1)S(1)}, u32[]{:S(2)}, u32[]{:S(2)}) collective-permute-start(bf16[256,128]{1,0:T(8,128)(2,1)S(1)} %add_convert_fusion.13), channel_id=1, source_target_pairs={{0,2},{1,3},{2,0},{3,1},{4,6},{5,7},{6,4},{7,5},{8,10},{9,11},{10,... | collective-permute-start | bytes 196616 | tf_op jit(solution)/shard_map/ppermute | solution.py:56
  102.9 46.0 %collective-permute-start.25 = (bf16[256,2048]{1,0:T(8,128)(2,1)}, bf16[256,2048]{1,0:T(8,128)(2,1)}, u32[]{:S(2)}, u32[]{:S(2)}) collective-permute-start(bf16[256,2048]{1,0:T(8,128)(2,1)} %param.29), channel_id=1, source_target_pairs={{0,2},{1,3},{2,0},{3,1},{4,6},{5,7},{6,4},{7,5},{8,10},{9,11},{10,... | collective-permute-start | bytes 3145736 | tf_op jit(solution)/shard_map/ppermute | solution.py:56
  131.4 40.7 %collective-permute-start.22 = (bf16[256,2048]{1,0:T(8,128)(2,1)S(1)}, bf16[256,2048]{1,0:T(8,128)(2,1)}, u32[]{:S(2)}, u32[]{:S(2)}) collective-permute-start(bf16[256,2048]{1,0:T(8,128)(2,1)S(1)} %multiply_convert_fusion.1), channel_id=1, source_target_pairs={{0,2},{1,3},{2,0},{3,1},{4,6},{5,7},{6,4},{7,5},{8,10},{9,11},{10,... | collective-permute-start | bytes 3145736 | tf_op jit(solution)/shard_map/ppermute | solution.py:56
  133.0 40.3 %collective-permute-start.24 = (bf16[256,2048]{1,0:T(8,128)(2,1)}, bf16[256,2048]{1,0:T(8,128)(2,1)}, u32[]{:S(2)}, u32[]{:S(2)}) collective-permute-start(bf16[256,2048]{1,0:T(8,128)(2,1)} %param.29), channel_id=1, source_target_pairs={{0,1},{1,0},{2,3},{3,2},{4,5},{5,4},{6,7},{7,6},{8,9},{9,8},{10,11... | collective-permute-start | bytes 3145736 | tf_op jit(solution)/shard_map/ppermute | solution.py:56
  133.0 37.7 %collective-permute-start.19 = (s32[384]{0:T(512)S(1)}, s32[384]{0:T(512)S(1)}, u32[]{:S(2)}, u32[]{:S(2)}) collective-permute-start(s32[384]{0:T(512)S(1)} %get-tuple-element.88), channel_id=1, source_target_pairs={{0,2},{1,3},{2,0},{3,1},{4,6},{5,7},{6,4},{7,5},{8,10},{9,11},{10,... | collective-permute-start | bytes 4616 | tf_op jit(solution)/shard_map/ppermute | solution.py:56
  149.0 24.3 %collective-permute-start.26 = (bf16[256,2048]{1,0:T(8,128)(2,1)}, bf16[256,2048]{1,0:T(8,128)(2,1)}, u32[]{:S(2)}, u32[]{:S(2)}) collective-permute-start(bf16[256,2048]{1,0:T(8,128)(2,1)} %collective-permute-done.25), channel_id=1, source_target_pairs={{0,1},{1,0},{2,3},{3,2},{4,5},{5,4},{6,7},{7,6},{8,9},{9,8},{10,11... | collective-permute-start | bytes 3145736 | tf_op jit(solution)/shard_map/ppermute | solution.py:56
  149.0 22.2 %collective-permute-start.18 = (s32[384]{0:T(512)S(1)}, s32[384]{0:T(512)S(1)}, u32[]{:S(2)}, u32[]{:S(2)}) collective-permute-start(s32[384]{0:T(512)S(1)} %get-tuple-element.88), channel_id=1, source_target_pairs={{0,1},{1,0},{2,3},{3,2},{4,5},{5,4},{6,7},{7,6},{8,9},{9,8},{10,11... | collective-permute-start | bytes 4616 | tf_op jit(solution)/shard_map/ppermute | solution.py:56
  171.8 5.2 collective-permute-start.21
  172.1 5.0 collective-permute-start.23
  325.0 10.3 %collective-permute-start.33 = (f32[16,1024]{1,0:T(8,128)}, f32[16,1024]{1,0:T(8,128)}, u32[]{:S(2)}, u32[]{:S(2)}) collective-permute-start(f32[16,1024]{1,0:T(8,128)} %constant_dynamic-update-slice_fusion.6), channel_id=1, source_target_pairs={{0,1},{1,0},{2,3},{3,2},{4,5},{5,4},{6,7},{7,6},{8,9},{9,8},{10,11... | collective-permute-start | bytes 196616 | tf_op jit(solution)/shard_map/ppermute | solution.py:56
  335.0 5.6 collective-permute-start.31
  336.2 4.3 collective-permute-start.34
  339.4 3.4 collective-permute-start.28
  339.5 6.6 collective-permute-start.30
  340.0 28.2 %collective-permute-start.27 = (bf16[256,2048]{1,0:T(8,128)(2,1)S(1)}, bf16[256,2048]{1,0:T(8,128)(2,1)S(1)}, u32[]{:S(2)}, u32[]{:S(2)}) collective-permute-start(bf16[256,2048]{1,0:T(8,128)(2,1)S(1)} %get-tuple-element.102), channel_id=1, source_target_pairs={{0,1},{1,0},{2,3},{3,2},{4,5},{5,4},{6,7},{7,6},{8,9},{9,8},{10,11... | collective-permute-start | bytes 3145736 | tf_op jit(solution)/shard_map/ppermute | solution.py:56
  341.1 26.1 %collective-permute-start.32 = (bf16[256,2048]{1,0:T(8,128)(2,1)S(1)}, bf16[256,2048]{1,0:T(8,128)(2,1)S(1)}, u32[]{:S(2)}, u32[]{:S(2)}) collective-permute-start(bf16[256,2048]{1,0:T(8,128)(2,1)S(1)} %fusion.50), channel_id=1, source_target_pairs={{0,2},{1,3},{2,0},{3,1},{4,6},{5,7},{6,4},{7,5},{8,10},{9,11},{10,... | collective-permute-start | bytes 3145736 | tf_op jit(solution)/shard_map/ppermute | solution.py:56
  344.5 44.2 %collective-permute-start.29 = (bf16[256,2048]{1,0:T(8,128)(2,1)S(1)}, bf16[256,2048]{1,0:T(8,128)(2,1)S(1)}, u32[]{:S(2)}, u32[]{:S(2)}) collective-permute-start(bf16[256,2048]{1,0:T(8,128)(2,1)S(1)} %fusion.52), channel_id=1, source_target_pairs={{0,2},{1,3},{2,0},{3,1},{4,6},{5,7},{6,4},{7,5},{8,10},{9,11},{10,... | collective-permute-start | bytes 3145736 | tf_op jit(solution)/shard_map/ppermute | solution.py:56
  393.2 24.5 %collective-permute-start.36 = (bf16[256,2048]{1,0:T(8,128)(2,1)}, bf16[256,2048]{1,0:T(8,128)(2,1)}, u32[]{:S(2)}, u32[]{:S(2)}) collective-permute-start(bf16[256,2048]{1,0:T(8,128)(2,1)} %get-tuple-element.86), channel_id=1, source_target_pairs={{0,2},{1,3},{2,0},{3,1},{4,6},{5,7},{6,4},{7,5},{8,10},{9,11},{10,... | collective-permute-start | bytes 3145736 | tf_op jit(solution)/shard_map/ppermute | solution.py:56
  398.8 27.6 %collective-permute-start.35 = (bf16[256,2048]{1,0:T(8,128)(2,1)}, bf16[256,2048]{1,0:T(8,128)(2,1)S(1)}, u32[]{:S(2)}, u32[]{:S(2)}) collective-permute-start(bf16[256,2048]{1,0:T(8,128)(2,1)} %get-tuple-element.86), channel_id=1, source_target_pairs={{0,1},{1,0},{2,3},{3,2},{4,5},{5,4},{6,7},{7,6},{8,9},{9,8},{10,11... | collective-permute-start | bytes 3145736 | tf_op jit(solution)/shard_map/ppermute | solution.py:56
  417.8 8.6 %collective-permute-start.37 = (bf16[256,2048]{1,0:T(8,128)(2,1)}, bf16[256,2048]{1,0:T(8,128)(2,1)}, u32[]{:S(2)}, u32[]{:S(2)}) collective-permute-start(bf16[256,2048]{1,0:T(8,128)(2,1)} %collective-permute-done.36), channel_id=1, source_target_pairs={{0,1},{1,0},{2,3},{3,2},{4,5},{5,4},{6,7},{7,6},{8,9},{9,8},{10,11... | collective-permute-start | bytes 3145736 | tf_op jit(solution)/shard_map/ppermute | solution.py:56
  418.4 4.8 collective-permute-start.47
  419.2 96.0 %collective-permute-start.46 = (bf16[256,128]{1,0:T(8,128)(2,1)}, bf16[256,128]{1,0:T(8,128)(2,1)}, u32[]{:S(2)}, u32[]{:S(2)}) collective-permute-start(bf16[256,128]{1,0:T(8,128)(2,1)} %fusion.106), channel_id=1, source_target_pairs={{0,1},{1,0},{2,3},{3,2},{4,5},{5,4},{6,7},{7,6},{8,9},{9,8},{10,11... | collective-permute-start | bytes 196616 | tf_op jit(solution)/shard_map/ppermute | solution.py:56
  423.2 92.0 %collective-permute-start.48 = (bf16[256,128]{1,0:T(8,128)(2,1)}, bf16[256,128]{1,0:T(8,128)(2,1)}, u32[]{:S(2)}, u32[]{:S(2)}) collective-permute-start(bf16[256,128]{1,0:T(8,128)(2,1)} %collective-permute-done.47), channel_id=1, source_target_pairs={{0,1},{1,0},{2,3},{3,2},{4,5},{5,4},{6,7},{7,6},{8,9},{9,8},{10,11... | collective-permute-start | bytes 196616 | tf_op jit(solution)/shard_map/ppermute | solution.py:56
  423.2 126.4 %collective-permute-start.59 = (bf16[4,4,384,384]{3,2,1,0:T(8,128)(2,1)}, bf16[4,4,384,384]{3,2,1,0:T(8,128)(2,1)}, u32[]{:S(2)}, u32[]{:S(2)}) collective-permute-start(bf16[4,4,384,384]{3,2,1,0:T(8,128)(2,1)} %get-tuple-element.23), channel_id=1, source_target_pairs={{0,4},{8,12},{16,20},{24,28},{4,0},{12,8},{20,16},{28,24},{1,5},{9... | collective-permute-start | bytes 14155784 | tf_op jit(solution)/shard_map/ppermute | solution.py:101
  499.5 9.1 %collective-permute-start.38 = (f32[2,1024]{1,0:T(2,128)S(1)}, f32[2,1024]{1,0:T(2,128)S(1)}, u32[]{:S(2)}, u32[]{:S(2)}) collective-permute-start(f32[2,1024]{1,0:T(2,128)S(1)} %pad_maximum_fusion.9), channel_id=1, source_target_pairs={{0,1},{1,0},{2,3},{3,2},{4,5},{5,4},{6,7},{7,6},{8,9},{9,8},{10,11... | collective-permute-start | bytes 24584 | tf_op jit(solution)/shard_map/ppermute | solution.py:56
  508.7 3.7 collective-permute-start.39
  515.2 3.1 collective-permute-start.44
  517.8 3.2 collective-permute-start.43
  519.3 6.9 %collective-permute-start.45 = (bf16[256,384]{0,1:T(8,128)(2,1)S(1)}, bf16[256,384]{0,1:T(8,128)(2,1)S(1)}, u32[]{:S(2)}, u32[]{:S(2)}) collective-permute-start(bf16[256,384]{0,1:T(8,128)(2,1)S(1)} %fusion.89), channel_id=1, source_target_pairs={{0,2},{1,3},{2,0},{3,1},{4,6},{5,7},{6,4},{7,5},{8,10},{9,11},{10,... | collective-permute-start | bytes 589832 | tf_op jit(solution)/shard_map/ppermute | solution.py:56
  526.3 11.8 %collective-permute-start.50 = (bf16[256,384]{0,1:T(8,128)(2,1)S(1)}, bf16[256,384]{0,1:T(8,128)(2,1)S(1)}, u32[]{:S(2)}, u32[]{:S(2)}) collective-permute-start(bf16[256,384]{0,1:T(8,128)(2,1)S(1)} %add_convert_fusion.10), channel_id=1, source_target_pairs={{0,2},{1,3},{2,0},{3,1},{4,6},{5,7},{6,4},{7,5},{8,10},{9,11},{10,... | collective-permute-start | bytes 589832 | tf_op jit(solution)/shard_map/ppermute | solution.py:56
  538.1 2.8 collective-permute-start.49
  538.2 2.8 collective-permute-start.51
  548.0 15.4 %collective-permute-start.52 = (bf16[4,577,128]{2,0,1:T(4,128)(2,1)S(1)}, bf16[4,577,128]{2,0,1:T(4,128)(2,1)S(1)}, u32[]{:S(2)}, u32[]{:S(2)}) collective-permute-start(bf16[4,577,128]{2,0,1:T(4,128)(2,1)S(1)} %copy.145), channel_id=1, source_target_pairs={{0,4},{8,12},{16,20},{24,28},{4,0},{12,8},{20,16},{28,24},{1,5},{9... | collective-permute-start | bytes 1772552 | tf_op jit(solution)/shard_map/ppermute | solution.py:101
  558.4 48.2 %collective-permute-start.60 = (bf16[4,384,384]{2,1,0:T(8,128)(2,1)}, bf16[4,384,384]{2,1,0:T(8,128)(2,1)}, u32[]{:S(2)}, u32[]{:S(2)}) collective-permute-start(bf16[4,384,384]{2,1,0:T(8,128)(2,1)} %get-tuple-element.96), channel_id=1, source_target_pairs={{0,8},{4,12},{8,16},{12,20},{16,24},{20,28},{1,9},{5,13},{9,17},{1... | collective-permute-start | bytes 3538952 | tf_op jit(solution)/shard_map/ppermute | solution.py:103
  561.9 46.0 %collective-permute-start.61 = (bf16[4,384,384]{2,1,0:T(8,128)(2,1)}, bf16[4,384,384]{2,1,0:T(8,128)(2,1)}, u32[]{:S(2)}, u32[]{:S(2)}) collective-permute-start(bf16[4,384,384]{2,1,0:T(8,128)(2,1)} %get-tuple-element.97), channel_id=1, source_target_pairs={{8,0},{12,4},{16,8},{20,12},{24,16},{28,20},{9,1},{13,5},{17,9},{2... | collective-permute-start | bytes 3538952 | tf_op jit(solution)/shard_map/ppermute | solution.py:104
  563.6 25.8 %collective-permute-start.53 = (bf16[577,128]{1,0:T(8,128)(2,1)S(1)}, bf16[577,128]{1,0:T(8,128)(2,1)S(1)}, u32[]{:S(2)}, u32[]{:S(2)}) collective-permute-start(bf16[577,128]{1,0:T(8,128)(2,1)S(1)} %get-tuple-element.137), channel_id=1, source_target_pairs={{0,8},{4,12},{8,16},{12,20},{16,24},{20,28},{1,9},{5,13},{9,17},{1... | collective-permute-start | bytes 443144 | tf_op jit(solution)/shard_map/ppermute | solution.py:103
  568.0 26.7 %collective-permute-start.54 = (bf16[577,128]{1,0:T(8,128)(2,1)S(1)}, bf16[577,128]{1,0:T(8,128)(2,1)S(1)}, u32[]{:S(2)}, u32[]{:S(2)}) collective-permute-start(bf16[577,128]{1,0:T(8,128)(2,1)S(1)} %get-tuple-element.138), channel_id=1, source_target_pairs={{8,0},{12,4},{16,8},{20,12},{24,16},{28,20},{9,1},{13,5},{17,9},{2... | collective-permute-start | bytes 443144 | tf_op jit(solution)/shard_map/ppermute | solution.py:104
  570.7 46.4 %collective-permute-start.41 = (bf16[256,2048]{1,0:T(8,128)(2,1)}, bf16[256,2048]{1,0:T(8,128)(2,1)}, u32[]{:S(2)}, u32[]{:S(2)}) collective-permute-start(bf16[256,2048]{1,0:T(8,128)(2,1)} %get-tuple-element.99), channel_id=1, source_target_pairs={{0,1},{1,0},{2,3},{3,2},{4,5},{5,4},{6,7},{7,6},{8,9},{9,8},{10,11... | collective-permute-start | bytes 3145736 | tf_op jit(solution)/shard_map/ppermute | solution.py:56
  594.7 4.1 collective-permute-start.55
  596.2 7.2 %collective-permute-start.57 = (bf16[577,128]{1,0:T(8,128)(2,1)S(1)}, bf16[577,128]{1,0:T(8,128)(2,1)}, u32[]{:S(2)}, u32[]{:S(2)}) collective-permute-start(bf16[577,128]{1,0:T(8,128)(2,1)S(1)} %fusion.92), channel_id=1, source_target_pairs={{8,0},{12,4},{16,8},{20,12},{24,16},{28,20},{9,1},{13,5},{17,9},{2... | collective-permute-start | bytes 443144 | tf_op jit(solution)/shard_map/ppermute | solution.py:104
  598.9 51.8 %collective-permute-start.40 = (bf16[256,2048]{1,0:T(8,128)(2,1)}, bf16[256,2048]{1,0:T(8,128)(2,1)S(1)}, u32[]{:S(2)}, u32[]{:S(2)}) collective-permute-start(bf16[256,2048]{1,0:T(8,128)(2,1)} %get-tuple-element.98), channel_id=1, source_target_pairs={{0,1},{1,0},{2,3},{3,2},{4,5},{5,4},{6,7},{7,6},{8,9},{9,8},{10,11... | collective-permute-start | bytes 3145736 | tf_op jit(solution)/shard_map/ppermute | solution.py:56
  604.4 16.9 %collective-permute-start.56 = (bf16[577,128]{1,0:T(8,128)(2,1)S(1)}, bf16[577,128]{1,0:T(8,128)(2,1)S(1)}, u32[]{:S(2)}, u32[]{:S(2)}) collective-permute-start(bf16[577,128]{1,0:T(8,128)(2,1)S(1)} %get-tuple-element.135), channel_id=1, source_target_pairs={{0,8},{4,12},{8,16},{12,20},{16,24},{20,28},{1,9},{5,13},{9,17},{1... | collective-permute-start | bytes 443144 | tf_op jit(solution)/shard_map/ppermute | solution.py:103
  606.6 16.4 %collective-permute-start.58 = (bf16[577,128]{1,0:T(8,128)(2,1)S(1)}, bf16[577,128]{1,0:T(8,128)(2,1)S(1)}, u32[]{:S(2)}, u32[]{:S(2)}) collective-permute-start(bf16[577,128]{1,0:T(8,128)(2,1)S(1)} %get-tuple-element.136), channel_id=1, source_target_pairs={{8,0},{12,4},{16,8},{20,12},{24,16},{28,20},{9,1},{13,5},{17,9},{2... | collective-permute-start | bytes 443144 | tf_op jit(solution)/shard_map/ppermute | solution.py:104
  611.5 27.8 %collective-permute-start.62 = (bf16[4,384,384]{2,1,0:T(8,128)(2,1)}, bf16[4,384,384]{2,1,0:T(8,128)(2,1)}, u32[]{:S(2)}, u32[]{:S(2)}) collective-permute-start(bf16[4,384,384]{2,1,0:T(8,128)(2,1)} %fusion.27), channel_id=1, source_target_pairs={{0,8},{4,12},{8,16},{12,20},{16,24},{20,28},{1,9},{5,13},{9,17},{1... | collective-permute-start | bytes 3538952 | tf_op jit(solution)/shard_map/ppermute | solution.py:103
  617.1 27.4 %collective-permute-start.64 = (bf16[4,384,384]{2,1,0:T(8,128)(2,1)}, bf16[4,384,384]{2,1,0:T(8,128)(2,1)}, u32[]{:S(2)}, u32[]{:S(2)}) collective-permute-start(bf16[4,384,384]{2,1,0:T(8,128)(2,1)} %fusion.27), channel_id=1, source_target_pairs={{8,0},{12,4},{16,8},{20,12},{24,16},{28,20},{9,1},{13,5},{17,9},{2... | collective-permute-start | bytes 3538952 | tf_op jit(solution)/shard_map/ppermute | solution.py:104
  621.3 29.4 %collective-permute-start.42 = (bf16[256,2048]{1,0:T(8,128)(2,1)}, bf16[256,2048]{1,0:T(8,128)(2,1)}, u32[]{:S(2)}, u32[]{:S(2)}) collective-permute-start(bf16[256,2048]{1,0:T(8,128)(2,1)} %add_convert_fusion.3), channel_id=1, source_target_pairs={{0,2},{1,3},{2,0},{3,1},{4,6},{5,7},{6,4},{7,5},{8,10},{9,11},{10,... | collective-permute-start | bytes 3145736 | tf_op jit(solution)/shard_map/ppermute | solution.py:56
  647.6 23.4 %collective-permute-start.63 = (bf16[4,384,384]{2,1,0:T(8,128)(2,1)S(1)}, bf16[4,384,384]{2,1,0:T(8,128)(2,1)S(1)}, u32[]{:S(2)}, u32[]{:S(2)}) collective-permute-start(bf16[4,384,384]{2,1,0:T(8,128)(2,1)S(1)} %get-tuple-element.94), channel_id=1, source_target_pairs={{0,8},{4,12},{8,16},{12,20},{16,24},{20,28},{1,9},{5,13},{9,17},{1... | collective-permute-start | bytes 3538952 | tf_op jit(solution)/shard_map/ppermute | solution.py:103
  649.1 26.0 %collective-permute-start.65 = (bf16[4,384,384]{2,1,0:T(8,128)(2,1)S(1)}, bf16[4,384,384]{2,1,0:T(8,128)(2,1)S(1)}, u32[]{:S(2)}, u32[]{:S(2)}) collective-permute-start(bf16[4,384,384]{2,1,0:T(8,128)(2,1)S(1)} %get-tuple-element.95), channel_id=1, source_target_pairs={{8,0},{12,4},{16,8},{20,12},{24,16},{28,20},{9,1},{13,5},{17,9},{2... | collective-permute-start | bytes 3538952 | tf_op jit(solution)/shard_map/ppermute | solution.py:104
  (90 other events, 2302.6 us)

commit v2 on v1

v2 whole, which is shorter than its diff:
```python
import functools

import jax
import jax.numpy as jnp
from jax import lax
from jax.experimental import pallas as pl
from jax.experimental.pallas import tpu as pltpu
from jax.sharding import PartitionSpec as P

HEAD_DIM = 128
EXPERTS = 16
TOP = 8
SETS = 8
RANK = 16
CAP = 144


EPS = 1e-05
SCALE = 2.0
THETA = 10000.0
NEG = -1e30


def rms_scale(value):
    return lax.rsqrt(jnp.mean(value * value, axis=-1, keepdims=True) + EPS)


def angles(position):
    half = HEAD_DIM // 2
    freq = THETA ** (-(jnp.arange(half, dtype=jnp.float32) * 2.0) / HEAD_DIM)
    phase = position.astype(jnp.float32)[:, None] * freq[None, :]
    cosine, sine = (jnp.cos(phase), jnp.sin(phase))
    return (jnp.concatenate([cosine, cosine], axis=-1), jnp.concatenate([-sine, sine], axis=-1))


LINE = 4
VMEM = 62 * 1024 * 1024


def swap(value, axis, bit):
    count = lax.axis_size(axis)
    return lax.ppermute(value, axis, [(i, i ^ bit) for i in range(count)])


def gather_parts(value, axis, bit=None):
    parts, bit = ({0: value}, (bit or lax.axis_size(axis)) // 2)
    while bit >= 1:
        for j in list(parts):
            parts[j ^ bit] = swap(parts[j], axis, bit)
        bit //= 2
    return [parts[j] for j in range(len(parts))]


def gather_near(value, axis):
    return gather_parts(value, axis, lax.axis_size(axis) // 2)


def gather_far(value, axis, *deps):
    far = swap(value, axis, lax.axis_size(axis) // 2)
    return gather_near(fence(far, *deps) if deps else far, axis)


def scatter_even(parts, axis):
    parts, bit = ({2 * i: part for i, part in enumerate(parts)}, 2)
    while bit < lax.axis_size(axis) // 2:
        got = {j: swap(parts[j ^ bit], axis, bit) for j in parts if not j & bit}
        parts = {j: (parts[j].astype(jnp.float32) + got[j].astype(jnp.float32)).astype(jnp.bfloat16) for j in got}
        bit *= 2
    return parts[0]


def reduce_scatter(make, axis, *deps):
    members = lax.axis_size(axis)
    top = members // 2
    odd = {}
    for j in range(members - 1, 0, -2):
        part, mark = make(j, None, *deps)
        odd[j - 1], deps = (swap(part, axis, 1), (mark,))
    sums = {}
    for j in range(members - 2, top - 1, -2):
        sums[j], mark = make(j, odd[j], *deps)
        deps = (mark,)
    far = scatter_even([sums[j] for j in range(top, members, 2)], axis)
    deps = (far,)
    for j in range(top - 2, -1, -2):
        sums[j], mark = make(j, odd[j], *deps)
        deps = (mark,)
    return scatter_even([sums[j] for j in range(0, top, 2)], axis), swap(far, axis, top)


def fence_kernel(*refs):
    pass


def fence(value, *deps):
    return pl.pallas_call(
        fence_kernel,
        out_shape=jax.ShapeDtypeStruct(value.shape, value.dtype),
        in_specs=[pl.BlockSpec(memory_space=pl.ANY)] * (1 + len(deps)),
        out_specs=pl.BlockSpec(memory_space=pl.ANY),
        input_output_aliases={0: 0},
        name="fence",
    )(value, *deps)


def sum_relative(value, axis, local):
    count, bit = (lax.axis_size(axis), 1)
    while bit < count:
        got = swap(value, axis, bit)
        got = [got[..., (j ^ bit) * local : ((j ^ bit) + 1) * local] for j in range(count)]
        value = value + jnp.concatenate(got, axis=-1)
        bit *= 2
    return value


class LineSum:
    def __init__(self, parts, axis, length, stride):
        count = lax.axis_size(axis)
        place = lambda i: i // stride % length
        self.axis, self.length, self.at = (axis, length, place(lax.axis_index(axis)))
        self.up = [(i, i + stride) for i in range(count) if place(i) + 1 < length]
        self.down = [(i + stride, i) for i in range(count) if place(i) + 1 < length]
        self.total = [part.astype(jnp.float32) for part in parts]

    def ready(self, step):
        return [self.total[p].astype(jnp.bfloat16) for p in (self.length - step, step)]

    def send(self, step, ready=None):
        up, down = ready or self.ready(step)
        return lax.ppermute(up, self.axis, self.up), lax.ppermute(down, self.axis, self.down)

    def add(self, step, got):
        left = self.length - step - 1
        below, above = (value.astype(jnp.float32) for value in got)
        good = (self.at >= 1) & (self.at + left < self.length)
        self.total[left] = self.total[left] + jnp.where(good, below, 0.0)
        good = (self.at + 1 < self.length) & (self.at - left >= 0)
        high = (step + 1) % self.length
        self.total[high] = self.total[high] + jnp.where(good, above, 0.0)


def line_scatter(parts, axis, length, stride):
    line = LineSum(parts, axis, length, stride)
    for step in range(1, length):
        line.add(step, line.send(step))
    return line.total[0]


def direct_scatter(parts, axis, length, stride, *deps):
    count = lax.axis_size(axis)
    got = []
    for p in range(1, length):
        moves = [(i, i + ((i // stride % length + p) % length - i // stride % length) * stride) for i in range(count)]
        got.append(lax.ppermute(parts[p], axis, moves))
    total = (fence(parts[0], *deps) if deps else parts[0]).astype(jnp.float32)
    for value in got:
        total = total + value.astype(jnp.float32)
    return total


def by_place(chunks):
    inner = chunks.shape[0] // LINE
    index = lax.axis_index("grp")
    parts = []
    for q in range(inner):
        group = []
        for p in range(LINE):
            chunk = (index // inner + p) % LINE * inner + (index % inner + q) % inner
            group.append(lax.dynamic_index_in_dim(chunks, chunk, 0, keepdims=False))
        parts.append(jnp.stack(group))
    return parts


def sum_packs(parts, *deps):
    inner = len(parts)
    mine = direct_scatter(parts, "grp", inner, 1).astype(jnp.bfloat16) if inner > 1 else parts[0]
    return direct_scatter([mine[p] for p in range(LINE)], "grp", LINE, inner, *deps)


def widen_kernel(docs, line, sets_ref, kept_ref, got_ref, *refs):
    f32 = jnp.float32
    out_refs = refs[-line:]
    experts, rows = got_ref.shape[1:3]
    for p in range(line):
        out_refs[p][...] = kept_ref[p]
        for e in range(experts):
            for g in range(rows // (docs * RANK)):
                for d in range(docs):
                    there = pl.ds(pl.multiple_of(g * SETS * RANK + sets_ref[d] * RANK, RANK), RANK)
                    piece = got_ref[p, e, (g * docs + d) * RANK : (g * docs + d + 1) * RANK]
                    out_refs[p][e, there] = (out_refs[p][e, there].astype(f32) + piece.astype(f32)).astype(kept_ref.dtype)


def widen(docs, sets, kept, got, *deps):
    line = kept.shape[0]
    return pl.pallas_call(
        functools.partial(widen_kernel, docs, line),
        out_shape=(jax.ShapeDtypeStruct(kept.shape[1:], kept.dtype),) * line,
        in_specs=[full(SMEM), full(), full()] + [full(pl.ANY)] * len(deps),
        out_specs=(full(),) * line,
        compiler_params=params(),
        name="widen",
    )(sets, kept, got, *deps)


def sum_experts(docs, sets, parts, *deps):
    inner = len(parts)
    if inner == 2:
        return widen(docs, sets, parts[0], swap(parts[1], "grp", 1), *deps)
    mine = line_scatter(parts, "grp", inner, 1).astype(jnp.bfloat16) if inner > 1 else parts[0]
    return [mine[p] for p in range(LINE)]


def dot_nn(a, b):
    return jnp.dot(a, b, preferred_element_type=jnp.float32)


def dot_nt(a, b):
    return lax.dot_general(a, b, (((1,), (1,)), ((), ())), preferred_element_type=jnp.float32)


def dot_tn(a, b):
    return lax.dot_general(a, b, (((0,), (0,)), ((), ())), preferred_element_type=jnp.float32)


def column(row):
    return jnp.broadcast_to(row, (128, row.shape[1])).T


def as_row(value):
    return jnp.broadcast_to(value, (value.shape[0], 128)).T[:1]


def doc_sum(scal_ref, rows, docs, at):
    value = jnp.full(rows.shape, scal_ref[at], jnp.int32)
    for k in range(1, docs):
        value = jnp.where(rows >= scal_ref[k], scal_ref[at + k], value)
    return value


def block_marks(scal_ref, docs, block, local):
    rows = block * local + lax.broadcasted_iota(jnp.int32, (local, SETS * RANK), 0)
    lanes = lax.broadcasted_iota(jnp.int32, (local, SETS * RANK), 1) // RANK
    return (doc_sum(scal_ref, rows, docs, 1 + docs) == lanes).astype(jnp.float32)


def params(**kinds):
    return pltpu.CompilerParams(vmem_limit_bytes=VMEM, **kinds)


def cost(flops, moved, exps=0):
    return pl.CostEstimate(flops=int(flops) // 8, bytes_accessed=int(moved) // 8, transcendentals=int(exps) // 8)


def full(memory=pltpu.VMEM):
    return pl.BlockSpec(memory_space=memory)


SMEM = pltpu.SMEM


def project_kernel(docs, half, parts, scal_ref, *refs):
    f32, bf16 = (jnp.float32, jnp.bfloat16)
    x_refs, (gain_ref, w_ref, enter_ref, leave_ref) = (refs[:parts], refs[parts : parts + 4])
    normed_ref, low_ref, p_ref, v_ref, square_ref = refs[-5:]
    local = x_refs[0].shape[0]
    rank = SETS * RANK
    which = pl.program_id(0)

    @pl.when(which == 0)
    def _():
        enter = jnp.concatenate([enter_ref[i] for i in range(3)], axis=1)
        for b in range(parts):
            x = x_refs[b][...].astype(f32)
            here = slice(b * local, (b + 1) * local)
            normed_ref[here] = (x * rms_scale(x) * gain_ref[...].astype(f32)).astype(bf16)
            mark = block_marks(scal_ref, docs, scal_ref[0] ^ (half * parts + b), local)
            low = dot_nn(normed_ref[here], enter)
            for i in range(3):
                low_ref[i, here] = (low[:, i * rank : (i + 1) * rank] * mark).astype(bf16) * SCALE

    value = dot_nn(normed_ref[...], w_ref[0]) + dot_nn(low_ref[which], leave_ref[0])

    @pl.when(which < 2)
    def _():
        p_ref[0] = value
        square_ref[pl.ds(which, 1)] = as_row(jnp.sum(value * value, axis=1, keepdims=True))

    @pl.when(which == 2)
    def _():
        v_ref[...] = value.astype(bf16)


def project(docs, half, scal, x_parts, gain, weight, enter, leave, kept):
    parts = len(x_parts)
    local, width = x_parts[0].shape
    slice_width = weight.shape[2]
    rows, rank = (parts * local, enter.shape[2])
    f32, bf16 = (jnp.float32, jnp.bfloat16)
    outs = (
        jax.ShapeDtypeStruct((2 * rows, width), bf16),
        jax.ShapeDtypeStruct((3, 2 * rows, rank), bf16),
        jax.ShapeDtypeStruct((2, 2 * rows, slice_width), f32),
        jax.ShapeDtypeStruct((2 * rows, slice_width), bf16),
        jax.ShapeDtypeStruct((2, 2 * rows), f32),
    )
    extra = () if kept is None else kept
    first = 5 + parts
    return pl.pallas_call(
        functools.partial(project_kernel, docs, half, parts),
        grid=(3,),
        out_shape=outs,
        in_specs=[full(SMEM)]
        + [full()] * parts
        + [
            full(),
            pl.BlockSpec((1, width, slice_width), lambda i: (i, 0, 0)),
            full(),
            pl.BlockSpec((1, rank, slice_width), lambda i: (i, 0, 0)),
        ]
        + [full(pl.ANY)] * len(extra),
        out_specs=(
            pl.BlockSpec((rows, width), lambda i: (half, 0)),
            pl.BlockSpec((3, rows, rank), lambda i: (0, half, 0)),
            pl.BlockSpec((1, rows, slice_width), lambda i: (jnp.minimum(i, 1), half, 0)),
            pl.BlockSpec((rows, slice_width), lambda i: (half, 0)),
            pl.BlockSpec((2, rows), lambda i: (0, half)),
        ),
        input_output_aliases={first + i: i for i in range(len(extra))},
        compiler_params=params(),
        cost_estimate=cost(2 * rows * width * (3 * slice_width + 3 * rank), 14_000_000),
        name="project",
    )(scal, *x_parts, gain, weight, enter, leave, *extra)


def prepare_kernel(width, p_ref, square_ref, gains_ref, cos_ref, sin_ref, q_ref, k_ref):
    inverse = lax.rsqrt(square_ref[...] / width + EPS)
    for i, out_ref in ((0, q_ref), (1, k_ref)):
        scale = column(inverse[i : i + 1])
        for at in range(0, p_ref.shape[2], HEAD_DIM):
            cut = slice(at, at + HEAD_DIM)
            value = p_ref[i, :, cut] * scale * gains_ref[i : i + 1, cut]
            value = value * cos_ref[...] + pltpu.roll(value, HEAD_DIM // 2, 1) * sin_ref[...]
            out_ref[:, cut] = value.astype(jnp.bfloat16)


def prepare(width, p, squares, gains, cosine, sine, local, *deps):
    _, rows, slice_width = p.shape
    out = jax.ShapeDtypeStruct((rows, slice_width), jnp.bfloat16)
    return pl.pallas_call(
        lambda *refs: prepare_kernel(width, *refs[:5], *refs[5 + len(deps) :]),
        grid=(rows // local,),
        out_shape=(out, out),
        in_specs=[
            pl.BlockSpec((2, local, slice_width), lambda i: (0, i, 0)),
            pl.BlockSpec((2, local), lambda i: (0, i)),
            full(),
            pl.BlockSpec((local, HEAD_DIM), lambda i: (i, 0)),
            pl.BlockSpec((local, HEAD_DIM), lambda i: (i, 0)),
        ]
        + [full(pl.ANY)] * len(deps),
        out_specs=(pl.BlockSpec((local, slice_width), lambda i: (i, 0)),) * 2,
        compiler_params=params(),
        cost_estimate=cost(10 * p.size, 8 * p.size),
        name="prepare",
    )(p, squares, gains, cosine, sine, *deps)


def attend_kernel(docs, place, local, added, scal_ref, q_ref, k_ref, v_ref, w_ref, enter_ref, *refs):
    f32, bf16 = (jnp.float32, jnp.bfloat16)
    att_ref, part_ref, log_ref = refs[-3:]
    members = q_ref.shape[0] // local
    heads = q_ref.shape[1] // HEAD_DIM
    width = w_ref.shape[1]
    member = scal_ref[0]
    block = member ^ place
    queries = slice(place * local, (place + 1) * local)

    def run(last):
        rows = last * local + lax.broadcasted_iota(jnp.int32, (local, local), 0)
        begin = doc_sum(scal_ref, rows, docs, 1 + 2 * docs)
        lanes = lax.broadcasted_iota(jnp.int32, (local, local), 1)
        logs = jnp.zeros((8, local), f32)
        for h in range(heads):
            cut = slice(h * HEAD_DIM, (h + 1) * HEAD_DIM)
            query = q_ref[queries, cut]
            scores, values = ([], [])
            for b in range(last + 1):
                there = pl.ds(pl.multiple_of((member ^ b) * local, local), local)
                score = dot_nt(query, k_ref[there, cut]) * HEAD_DIM ** (-0.5)
                good = lanes + b * local >= begin
                if b == last:
                    good = good & (lanes + b * local <= rows)
                scores.append(jnp.where(good, score, NEG))
                values.append(v_ref[there, cut])
            peak = functools.reduce(jnp.maximum, [jnp.max(score, axis=1, keepdims=True) for score in scores])
            expo = [jnp.exp(score - peak) for score in scores]
            total = functools.reduce(jnp.add, [jnp.sum(e, axis=1, keepdims=True) for e in expo])
            share = 1.0 / total
            mixed = functools.reduce(jnp.add, [dot_nn((e * share).astype(bf16), v) for e, v in zip(expo, values)])
            att_ref[:, cut] = mixed.astype(bf16)
            head_row = lax.broadcasted_iota(jnp.int32, (8, local), 0) == h
            logs = jnp.where(head_row, as_row(peak + jnp.log(total)), logs)
        log_ref[...] = logs

    for last in range(members):
        pl.when(block == last)(functools.partial(run, last))
    for cut, value_ref in ((slice(0, width), w_ref), (slice(width, None), enter_ref)):
        value = dot_nn(att_ref[...], value_ref[...])
        if added:
            value = value + refs[0][:, cut].astype(f32)
        part_ref[:, cut] = value.astype(bf16)


def attend(docs, place, local, scal, q, k, v, weight, enter, addend, *deps):
    slice_width = q.shape[1]
    width, rank = (weight.shape[1], enter.shape[1])
    f32, bf16 = (jnp.float32, jnp.bfloat16)
    assert slice_width // HEAD_DIM <= 8
    return pl.pallas_call(
        functools.partial(attend_kernel, docs, place, local, addend is not None),
        out_shape=(
            jax.ShapeDtypeStruct((local, slice_width), bf16),
            jax.ShapeDtypeStruct((local, width + rank), bf16),
            jax.ShapeDtypeStruct((8, local), f32),
        ),
        in_specs=[full(SMEM)] + [full()] * (5 + (addend is not None)) + [full(pl.ANY)] * len(deps),
        out_specs=(full(),) * 3,
        compiler_params=params(),
        cost_estimate=cost(2_200_000_000, 4_000_000, 350_000),
        name="attend",
    )(scal, q, k, v, weight, enter, *(() if addend is None else (addend,)), *deps)


def middle_kernel(
    docs, scal_ref, x_ref, oa_ref, ob_ref, leave_ref, gain_ref, route_ref, route_enter, route_leave, h_ref, normed_ref, route_low, probs_ref
):
    f32, bf16 = (jnp.float32, jnp.bfloat16)
    width = x_ref.shape[1]
    mark = block_marks(scal_ref, docs, scal_ref[0], x_ref.shape[0])
    low = ((oa_ref[:, width:].astype(f32) + ob_ref[:, width:].astype(f32)) * mark).astype(bf16)
    normed_ref[:, width:] = low
    h = x_ref[...].astype(f32) + (oa_ref[:, :width].astype(f32) + ob_ref[:, :width].astype(f32))
    h = h + SCALE * dot_nn(low, leave_ref[...])
    h_ref[...] = h
    normed = (h * rms_scale(h) * gain_ref[...].astype(f32)).astype(bf16)
    normed_ref[:, :width] = normed
    low, probs = router(normed, mark, route_ref, route_enter, route_leave)
    route_low[...] = low
    probs_ref[...] = probs


def router(normed, mark, route_ref, route_enter, route_leave):
    low = (dot_nn(normed, route_enter[...]) * mark).astype(jnp.bfloat16)
    logits = dot_nt(route_ref[...], normed) + SCALE * dot_nt(route_leave[...], low)
    expo = jnp.exp(logits - jnp.max(logits, axis=0, keepdims=True))
    return low, expo / jnp.sum(expo, axis=0, keepdims=True)


def middle(docs, scal, x, outs, leave, gain, route, route_enter, route_leave):
    local, width = x.shape
    rank = leave.shape[0]
    f32, bf16 = (jnp.float32, jnp.bfloat16)
    return pl.pallas_call(
        functools.partial(middle_kernel, docs),
        out_shape=(
            jax.ShapeDtypeStruct((local, width), f32),
            jax.ShapeDtypeStruct((local, width + rank), bf16),
            jax.ShapeDtypeStruct((local, rank), bf16),
            jax.ShapeDtypeStruct((route.shape[0], local), f32),
        ),
        in_specs=[full(SMEM)] + [full()] * 8,
        out_specs=(full(),) * 4,
        compiler_params=params(),
        cost_estimate=cost(4 * local * width * rank, 8_000_000),
        name="middle",
    )(scal, x, *outs, leave, gain, route, route_enter, route_leave)


def middle_back_kernel(
    docs, scal_ref, ga_ref, gb_ref, probs_ref, h_ref, up_ref, route_low, gain_ref, route_ref, route_enter, route_leave, dh_ref, dhb_ref, leave_ref
):
    f32, bf16 = (jnp.float32, jnp.bfloat16)
    width = h_ref.shape[1]
    mark = block_marks(scal_ref, docs, scal_ref[0], h_ref.shape[0])
    probs = probs_ref[...]
    experts = probs.shape[0]
    scores = (ga_ref[:, width:].astype(f32) + gb_ref[:, width:].astype(f32)).T
    dprobs = scores[:experts] + scores[experts : 2 * experts]
    dlogits = (probs * (dprobs - jnp.sum(probs * dprobs, axis=0, keepdims=True))).astype(bf16)
    dlow = (dot_tn(dlogits, route_leave[...]) * SCALE * mark).astype(bf16)
    dhb_ref[:, width:] = dlow
    leave_ref[...] = SCALE * dot_nn(dlogits, route_low[...])
    back = ga_ref[:, :width].astype(f32) + gb_ref[:, :width].astype(f32)
    back = back + dot_tn(dlogits, route_ref[...]) + dot_nt(dlow, route_enter[...])
    back = back * gain_ref[...].astype(f32)
    h = h_ref[...]
    scale = rms_scale(h)
    dh = up_ref[...].astype(f32) + scale * back - h * scale**3 * jnp.mean(h * back, axis=-1, keepdims=True)
    dh_ref[...] = dh
    dhb_ref[:, :width] = dh.astype(bf16)


def middle_back(docs, scal, grads, probs, h, upstream, route_low, gain, route, route_enter, route_leave):
    local, width = h.shape
    rank = route_enter.shape[1]
    f32, bf16 = (jnp.float32, jnp.bfloat16)
    return pl.pallas_call(
        functools.partial(middle_back_kernel, docs),
        out_shape=(
            jax.ShapeDtypeStruct((local, width), f32),
            jax.ShapeDtypeStruct((local, width + rank), bf16),
            jax.ShapeDtypeStruct((route.shape[0], rank), f32),
        ),
        in_specs=[full(SMEM)] + [full()] * 10,
        out_specs=(full(),) * 3,
        compiler_params=params(),
        cost_estimate=cost(4 * local * width * rank, 10_000_000),
        name="middle_back",
    )(scal, *grads, probs, h, upstream, route_low, gain, route, route_enter, route_leave)


def attend_back_kernel(docs, half, local, scal_ref, *refs):
    f32, bf16 = (jnp.float32, jnp.bfloat16)
    q_ref = refs[0]
    members = q_ref.shape[0] // local
    count = members // 2
    heads = q_ref.shape[1] // HEAD_DIM
    q_ref, k_ref, v_ref, w_ref, enter_ref, leave_ref = refs[:6]
    refs = refs[6:]
    grad_refs, att_refs, log_refs, normed_refs, refs = (*(refs[i * count : (i + 1) * count] for i in range(4)), refs[4 * count :])
    before, refs = (refs[: 5 * half], refs[5 * half + half :])
    dq_ref, dk_ref, dv_ref, enter_grad, leave_grad, route_grad, *rest = refs
    term_refs, (grad, datt, att, logs, normed) = (rest[:-5], rest[-5:])
    width = w_ref.shape[1]
    step = pl.program_id(0)
    place = half * count + step
    member = scal_ref[0]
    block = member ^ place
    queries = pl.ds(pl.multiple_of(place * local, local), local)
    mine = pl.ds(pl.multiple_of(member * q_ref.shape[1], 128), q_ref.shape[1])

    @pl.when(step == 0)
    def _():
        for i, ref in enumerate((dk_ref, dv_ref, enter_grad, leave_grad, route_grad)):
            ref[...] = before[i][...] if half else jnp.zeros_like(ref)

    for i in range(count):

        @pl.when(step == i)
        def _():
            grad[...] = grad_refs[i][...]
            att[...] = att_refs[i][...]
            logs[...] = log_refs[i][...]
            normed[:, : mine.size] = normed_refs[i][:, mine]
            normed[:, mine.size :] = normed_refs[i][:, width:]

    mark = block_marks(scal_ref, docs, block, local)
    low = (dot_nt(grad[:, :width], leave_ref[...]) * SCALE * mark).astype(bf16)
    datt[...] = (dot_nt(grad[:, :width], w_ref[...]) + dot_nt(low, enter_ref[...])).astype(bf16)
    enter_grad[...] += dot_tn(low, att[...])
    leave_grad[...] += SCALE * dot_tn(normed[:, mine.size :], grad[:, mine])
    route_grad[...] += dot_tn(grad[:, width:], normed[:, : mine.size])

    def run(last):
        rows = last * local + lax.broadcasted_iota(jnp.int32, (local, local), 1)
        begin = doc_sum(scal_ref, rows, docs, 1 + 2 * docs)
        down = lax.broadcasted_iota(jnp.int32, (local, local), 0)
        term = jnp.zeros((local, 1), f32)
        for h in range(heads):
            cut = slice(h * HEAD_DIM, (h + 1) * HEAD_DIM)
            query, dout = (q_ref[queries, cut], datt[:, cut])
            log = logs[h : h + 1]
            shares, pushes = ([], [])
            for b in range(last + 1):
                there = pl.ds(pl.multiple_of((member ^ b) * local, local), local)
                score = dot_nt(k_ref[there, cut], query) * HEAD_DIM ** (-0.5)
                good = down + b * local >= begin
                if b == last:
                    good = good & (down + b * local <= rows)
                share = jnp.where(good, jnp.exp(score - log), 0.0)
                shares.append(share)
                pushes.append(dot_nt(v_ref[there, cut], dout))
            inner = functools.reduce(jnp.add, [jnp.sum(s * d, axis=0, keepdims=True) for s, d in zip(shares, pushes)])
            dquery = jnp.zeros((local, HEAD_DIM), f32)
            for b in range(last + 1):
                there = pl.ds(pl.multiple_of((member ^ b) * local, local), local)
                dscore = (shares[b] * (pushes[b] - inner) * HEAD_DIM ** (-0.5)).astype(bf16)
                dquery = dquery + dot_tn(dscore, k_ref[there, cut])
                dk_ref[there, cut] += dot_nn(dscore, query)
                dv_ref[there, cut] += dot_nn(shares[b].astype(bf16), dout)
            dq_ref[:, cut] = dquery
            term = term + jnp.sum(dquery * query.astype(f32), axis=1, keepdims=True)
        term_refs[0][...] = as_row(term)

    for last in range(members):
        pl.when(block == last)(functools.partial(run, last))

    if half:

        @pl.when(step == count - 1)
        def _():
            for b in range(members):
                here = slice(b * local, (b + 1) * local)
                value = jnp.sum(dk_ref[here] * k_ref[here].astype(f32), axis=1, keepdims=True)
                term_refs[1][:, here] = as_row(value)


def attend_back(docs, half, scal, q, k, v, weight, enter, leave, grads, atts, logs, normed, before, *deps):
    group_len, slice_width = q.shape
    local = grads[0].shape[0]
    width, rank = (weight.shape[1], enter.shape[1])
    count = len(grads)
    f32, bf16 = (jnp.float32, jnp.bfloat16)
    low_grad = jax.ShapeDtypeStruct((rank, slice_width), f32)
    outs = (
        jax.ShapeDtypeStruct((count * local, slice_width), f32),
        jax.ShapeDtypeStruct((group_len, slice_width), f32),
        jax.ShapeDtypeStruct((group_len, slice_width), f32),
        low_grad,
        low_grad,
        low_grad,
        jax.ShapeDtypeStruct((1, count * local), f32),
    ) + ((jax.ShapeDtypeStruct((1, group_len), f32),) if half else ())
    return pl.pallas_call(
        functools.partial(attend_back_kernel, docs, half, local),
        grid=(count,),
        out_shape=outs,
        in_specs=[full(SMEM)] + [full()] * (6 + 4 * count + len(before)) + [full(pl.ANY)] * len(deps),
        out_specs=(pl.BlockSpec((local, slice_width), lambda i: (i, 0)),)
        + (full(),) * 5
        + (pl.BlockSpec((1, local), lambda i: (0, i)),)
        + ((full(),) if half else ()),
        scratch_shapes=[
            pltpu.VMEM((local, width + rank), bf16),
            pltpu.VMEM((local, slice_width), bf16),
            pltpu.VMEM((local, slice_width), bf16),
            pltpu.VMEM((8, local), f32),
            pltpu.VMEM((local, slice_width + rank), bf16),
        ],
        compiler_params=params(),
        cost_estimate=cost(8_000_000_000, 14_000_000, 700_000),
        name="attend_back",
    )(scal, q, k, v, weight, enter, leave, *grads, *atts, *logs, *normed, *before, *deps)


def project_back_kernel(docs, local, scal_ref, *refs):
    f32, bf16 = (jnp.float32, jnp.bfloat16)
    near_ref, far_ref, dk_ref, dv_ref, p_ref, square_ref, term_ref, gains_ref, cos_ref, sin_ref, normed_ref, low_ref = refs[:12]
    w_ref, enter_ref, leave_ref, route_ref, *refs = refs[12:]
    *dx_refs, enter_grad, leave_grad, dp_ref, dlow_ref, turned = refs
    rows, slice_width = near_ref.shape
    rank = SETS * RANK
    member = scal_ref[0]
    step = pl.program_id(0)
    members = pl.num_programs(0)
    width = slice_width * members
    count = rows // local

    @pl.when(step == 0)
    def _():
        inverse = lax.rsqrt(square_ref[...] / width + EPS)
        biases = inverse * inverse * term_ref[...] / width
        for i in range(2):
            for half in range(2):
                here = slice(half * rows, (half + 1) * rows)
                scale, bias = (column(inverse[i : i + 1, here]), column(biases[i : i + 1, here]))
                for at in range(0, slice_width, HEAD_DIM):
                    cut = slice(at, at + HEAD_DIM)
                    value = dk_ref[here, cut] if i else (far_ref if half else near_ref)[:, cut]
                    value = value * cos_ref[here] - pltpu.roll(value, HEAD_DIM // 2, 1) * sin_ref[here]
                    value = value * gains_ref[i : i + 1, cut] * scale - p_ref[i, here, cut] * bias
                    dp_ref[i, here, cut] = value.astype(bf16)
        dp_ref[2] = dv_ref[...].astype(bf16)
        for b in range(2 * count):
            here = slice(b * local, (b + 1) * local)
            mark = block_marks(scal_ref, docs, member ^ b, local)
            for i in range(3):
                value = dot_nt(dp_ref[i, here], leave_ref[i]) * SCALE * mark
                dlow_ref[here, i * rank : (i + 1) * rank] = value.astype(bf16)
                turned[i * rank : (i + 1) * rank, here] = value.T.astype(bf16)
        for i in range(3):
            leave_grad[i] = dot_tn(low_ref[i], dp_ref[i])

    enter_grad[0, : 3 * rank] = dot_nn(turned[...], normed_ref[...]).astype(bf16)
    enter_grad[0, 3 * rank :] = route_ref[0]
    spread_back(dx_refs, [dp_ref[i, rows:] for i in range(3)], dlow_ref[rows:], w_ref, enter_ref)


def spread_back(dx_refs, grads, low, w_ref, enter_ref):
    value = dot_nt(grads[0], w_ref[0]) + dot_nt(grads[1], w_ref[1]) + dot_nt(grads[2], w_ref[2])
    value = value + dot_nt(low, jnp.concatenate([enter_ref[i] for i in range(3)], axis=1))
    value = value.astype(jnp.bfloat16)
    local = dx_refs[0].shape[0]
    for b, dx_ref in enumerate(dx_refs):
        dx_ref[...] = value[b * local : (b + 1) * local]


def project_back(docs, local, scal, near, far, dk, dv, p, squares, terms, gains, cosine, sine, normed, low, weight, enter, leave, route_grad, *deps):
    rows, slice_width = near.shape
    width, rank = (normed.shape[1], enter.shape[2])
    members, count = (2 * rows // local, rows // local)
    tall = 3 * rank + route_grad.shape[1]
    f32, bf16 = (jnp.float32, jnp.bfloat16)
    pick = lambda i, scal: scal[0] ^ i
    sums = pl.BlockSpec((1, tall, slice_width), lambda i, scal: (i, 0, 0))
    in_specs = [full()] * 10 + [
        pl.BlockSpec((2 * rows, slice_width), lambda i, scal: (0, pick(i, scal))),
        full(),
        pl.BlockSpec((3, slice_width, slice_width), lambda i, scal: (0, pick(i, scal), 0)),
        pl.BlockSpec((3, slice_width, rank), lambda i, scal: (0, pick(i, scal), 0)),
        full(),
        pl.BlockSpec((1, tall - 3 * rank, slice_width), lambda i, scal: (i, 0, 0)),
    ] + [full(pl.ANY)] * len(deps)
    return pl.pallas_call(
        lambda *refs: project_back_kernel(docs, local, *refs[:17], *refs[17 + len(deps) :]),
        out_shape=(jax.ShapeDtypeStruct((local, width), bf16),) * count
        + (
            jax.ShapeDtypeStruct((members, tall, slice_width), bf16),
            jax.ShapeDtypeStruct((3, rank, slice_width), f32),
            jax.ShapeDtypeStruct((3, 2 * rows, slice_width), bf16),
            jax.ShapeDtypeStruct((2 * rows, 3 * rank), bf16),
        ),
        grid_spec=pltpu.PrefetchScalarGridSpec(
            num_scalar_prefetch=1,
            grid=(members,),
            in_specs=in_specs,
            out_specs=(pl.BlockSpec((local, slice_width), lambda i, scal: (0, pick(i, scal))),) * count
            + (sums, full(), full(), full()),
            scratch_shapes=[pltpu.VMEM((3 * rank, 2 * rows), bf16)],
        ),
        compiler_params=params(),
        cost_estimate=cost(2 * rows * (width * 3 * slice_width + 6 * rank * width), 20_000_000),
        name="project_back",
    )(scal, near, far, dk, dv, p, squares, terms, gains, cosine, sine, normed, low, weight, enter, leave, route_grad, *deps)


def project_near(local, grads, low, weight, enter, *deps):
    _, group_len, slice_width = grads.shape
    rows, width, rank = (group_len // 2, weight.shape[1], enter.shape[2])
    count = rows // local
    step = slice_width
    out = jax.ShapeDtypeStruct((local, width), jnp.bfloat16)

    def kernel(grads_ref, low_ref, w_ref, enter_ref, *refs):
        spread_back(refs[-count:], [grads_ref[i] for i in range(3)], low_ref[...], w_ref, enter_ref)

    return pl.pallas_call(
        kernel,
        grid=(width // step,),
        out_shape=(out,) * count,
        in_specs=[
            pl.BlockSpec((3, rows, slice_width), lambda i: (0, 0, 0)),
            pl.BlockSpec((rows, 3 * rank), lambda i: (0, 0)),
            pl.BlockSpec((3, step, slice_width), lambda i: (0, i, 0)),
            pl.BlockSpec((3, step, rank), lambda i: (0, i, 0)),
        ]
        + [full(pl.ANY)] * len(deps),
        out_specs=(pl.BlockSpec((local, step), lambda i: (0, i)),) * count,
        compiler_params=params(),
        cost_estimate=cost(2 * rows * (width * 3 * slice_width), 10_000_000),
        name="project_near",
    )(grads, low, weight, enter, *deps)


def finish_kernel(*refs):
    f32 = jnp.float32
    *parts, dh_ref, x_ref, gain_ref, out_ref = refs
    x = x_ref[...].astype(f32)
    back = functools.reduce(jnp.add, [part[...].astype(f32) for part in parts]) * gain_ref[...].astype(f32)
    scale = rms_scale(x)
    out = dh_ref[...] + scale * back - x * scale**3 * jnp.mean(x * back, axis=-1, keepdims=True)
    out_ref[...] = out.astype(out_ref.dtype)


def finish(grads, dh, x, gain):
    return pl.pallas_call(
        finish_kernel,
        out_shape=jax.ShapeDtypeStruct(x.shape, jnp.bfloat16),
        in_specs=[full()] * (3 + len(grads)),
        out_specs=full(),
        compiler_params=params(),
        cost_estimate=cost(10 * x.size, 12 * x.size),
        name="finish",
    )(*grads, dh, x, gain)


def upstream_kernel(scal_ref, named_ref, *refs):
    blocks = named_ref.shape[0]
    f32, bf16 = (jnp.float32, jnp.bfloat16)
    upstream_refs, (down_w, down_leave, rank_ref, rows_ref, back_ref, low_ref, places) = (refs[:blocks], refs[-7:])
    experts, local = places.shape[1:]
    cap = rows_ref.shape[1] // blocks

    @pl.when((pl.program_id(0) == 0) | (pl.num_programs(1) > 1))
    def _():
        earlier = lax.broadcasted_iota(jnp.int32, (local, local), 0) < lax.broadcasted_iota(jnp.int32, (local, local), 1)
        bits = lax.broadcasted_iota(jnp.int32, (experts, local), 0)
        for b in range(blocks):
            hot = (jnp.right_shift(named_ref[b], bits) & 1).astype(f32)
            rank = dot_nn(hot.astype(bf16), earlier.astype(f32).astype(bf16))
            places[b] = jnp.where(hot > 0.0, rank, -1.0)

    mine = pl.ds(scal_ref[0] * pl.num_programs(0) + pl.program_id(0), 1)
    slots = lax.broadcasted_iota(jnp.int32, (cap, local), 0).astype(f32)
    for b in range(blocks):
        rank_ref[0, b] = places[b, mine]
        pick = (places[b, mine] == slots).astype(bf16)
        rows_ref[0, b * cap : (b + 1) * cap] = dot_nn(pick, upstream_refs[b][...]).astype(bf16)
    back_ref[0] = dot_nt(rows_ref[0], down_w[0]).astype(bf16)
    low_ref[0] = dot_nt(rows_ref[0], down_leave[0])


def run_upstream(scal, named, upstream, down, down_leave, *deps):
    members, _, local = named.shape
    experts, ff, width = down.shape
    low = down_leave.shape[1]
    blocks = min(members, 4)
    turns = members // blocks
    count = blocks * CAP
    f32, bf16 = (jnp.float32, jnp.bfloat16)
    rows = lambda wide: pl.BlockSpec((1, count, wide), lambda e, r: (e, r, 0))
    return pl.pallas_call(
        lambda *refs: upstream_kernel(*refs[: 4 + blocks], *refs[4 + blocks + len(deps) :]),
        grid=(experts, turns),
        out_shape=(
            jax.ShapeDtypeStruct((experts, members, 1, local), f32),
            jax.ShapeDtypeStruct((experts, members * CAP, width), bf16),
            jax.ShapeDtypeStruct((experts, members * CAP, ff), bf16),
            jax.ShapeDtypeStruct((experts, members * CAP, low), f32),
        ),
        in_specs=[full(SMEM), pl.BlockSpec((blocks, 1, local), lambda e, r: (r, 0, 0))]
        + [pl.BlockSpec((local, width), lambda e, r: (r, 0), pipeline_mode=pl.Buffered(1))] * blocks
        + [pl.BlockSpec((1, ff, width), lambda e, r: (e, 0, 0)), pl.BlockSpec((1, low, width), lambda e, r: (e, 0, 0))]
        + [full(pl.ANY)] * len(deps),
        out_specs=(pl.BlockSpec((1, blocks, 1, local), lambda e, r: (e, r, 0, 0)), rows(width), rows(ff), rows(low)),
        scratch_shapes=[pltpu.VMEM((blocks, EXPERTS, local), f32)],
        compiler_params=params(),
        cost_estimate=cost(2 * experts * members * CAP * width * ff, 40_000_000),
        name="upstream",
    )(scal, named, *by_block(upstream, blocks), down, down_leave, *deps)


def by_block(parts, blocks):
    return [jnp.concatenate(parts[b::blocks]) if len(parts) > blocks else parts[b] for b in range(blocks)]


def expert_kernel(line, docs, scal_ref, rank_ref, grads_ref, back_ref, low_ref, route_ref, route_enter, route_leave, *refs):
    blocks = rank_ref.shape[1]
    normed_refs, refs, probs = (refs[:blocks], refs[blocks:-1], refs[-1])
    width = grads_ref.shape[2]
    turn = pl.program_id(1)
    local = rank_ref.shape[3]

    @pl.when((pl.program_id(0) == 0) | (pl.num_programs(1) > 1))
    def _():
        for b in range(blocks):
            mark = block_marks(scal_ref, docs, scal_ref[0] ^ (turn * blocks + b), local)
            probs[b] = router(normed_refs[b][:, :width], mark, route_ref, route_enter, route_leave)[1]

    mine = pl.ds(scal_ref[0] * pl.num_programs(0) + pl.program_id(0), 1)
    weights = [probs[b, mine] for b in range(blocks)]
    expert_rows(line, docs, scal_ref, rank_ref, weights, normed_refs, grads_ref.at[0], back_ref.at[0], low_ref.at[0], *refs)


def expert_rows(
    line,
    docs,
    scal_ref,
    rank_ref,
    weight_rows,
    normed_refs,
    grads_in,
    back_in,
    low_in,
    gate_w,
    up_w,
    down_w,
    gate_enter,
    gate_leave,
    up_enter,
    up_leave,
    down_enter,
    down_leave,
    place_ref,
    mixed_ref,
    grad_ref,
    score_ref,
    *rest,
):
    inner = len(rest) - 9
    sums, (rows_in, hidden, grad_gate, grad_up, marks, out_tile, back_tile, done, full_rows) = (rest[:inner], rest[inner:])
    f32, bf16 = (jnp.float32, jnp.bfloat16)
    blocks, local, width = (rank_ref.shape[1], rank_ref.shape[3], grads_in.shape[1])
    cap = mixed_ref.shape[2]
    expert, turn = (pl.program_id(0), pl.program_id(1))
    count = blocks * cap
    ff = hidden.shape[1]
    slots = lax.broadcasted_iota(jnp.int32, (cap, local), 0).astype(f32)
    weights = []
    for b in range(blocks):
        hit = rank_ref[0, b] == slots
        pick = hit.astype(bf16)
        weights.append(jnp.sum(jnp.where(hit, weight_rows[b], 0.0), axis=1, keepdims=True))
        here = slice(b * cap, (b + 1) * cap)
        mark = block_marks(scal_ref, docs, scal_ref[0] ^ (turn * blocks + b), local).astype(bf16)
        rows_in[here, :] = dot_nn(pick, normed_refs[b][:, :width]).astype(bf16)
        marks[here, :] = dot_nn(pick, mark)
    weight = jnp.concatenate(weights, axis=0)
    mark = marks[...]
    rank = mark.shape[1]
    low = dot_nn(rows_in[...], jnp.concatenate([gate_enter[0], up_enter[0]], axis=1))
    low_gate = (low[:, :rank] * mark).astype(bf16) * SCALE
    low_up = (low[:, rank:] * mark).astype(bf16) * SCALE
    grad_low_down = (low_in[...] * (SCALE * weight) * mark).astype(bf16)
    step = min(256, ff)
    for at in range(0, ff, step):
        cut = slice(at, at + step)
        gate = dot_nn(rows_in[...], gate_w[0, :, cut]) + dot_nn(low_gate, gate_leave[0, :, cut])
        up = dot_nn(rows_in[...], up_w[0, :, cut]) + dot_nn(low_up, up_leave[0, :, cut])
        back = back_in[:, cut].astype(f32) * weight + dot_nt(grad_low_down, down_enter[0, cut, :])
        sigma = 1.0 / (1.0 + jnp.exp(-gate))
        silu = gate * sigma
        hidden[:, cut] = (silu * up).astype(bf16)
        grad_gate[:, cut] = (back * up * sigma * (1.0 + gate * (1.0 - sigma))).astype(bf16)
        grad_up[:, cut] = (back * silu).astype(bf16)
    low_down = (dot_nn(hidden[...], down_enter[0]) * mark).astype(bf16) * SCALE
    grad_low_gate = (dot_nt(grad_gate[...], gate_leave[0]) * SCALE * mark).astype(bf16)
    grad_low_up = (dot_nt(grad_up[...], up_leave[0]) * SCALE * mark).astype(bf16)
    grad_low = jnp.concatenate([grad_low_gate, grad_low_up], axis=1)
    step = out_tile.shape[3]
    sent = []

    def send(slot, cut):
        there = pl.ds(turn * blocks, blocks)
        copies = [
            pltpu.make_async_copy(out_tile.at[slot], mixed_ref.at[there, expert, :, cut], done.at[0, slot]),
            pltpu.make_async_copy(back_tile.at[slot], grad_ref.at[there, expert, :, cut], done.at[1, slot]),
        ]
        for copy in copies:
            copy.start()
        sent.append(copies)

    score = jnp.zeros((count, 1), f32)
    for at in range(0, width, step):
        cut = slice(at, at + step)
        out = dot_nn(hidden[...], down_w[0, :, cut]) + dot_nn(low_down, down_leave[0, :, cut])
        score = score + jnp.sum(out * grads_in[:, cut].astype(f32), axis=1, keepdims=True)
        back = dot_nt(grad_gate[...], gate_w[0, cut, :]) + dot_nt(grad_up[...], up_w[0, cut, :])
        back = back + dot_nt(grad_low, jnp.concatenate([gate_enter[0, cut, :], up_enter[0, cut, :]], axis=1))
        out = (out * weight).astype(bf16)
        back = back.astype(bf16)
        slot = len(sent) % 2
        if len(sent) >= 2:
            for copy in sent[-2]:
                copy.wait()
        for b in range(blocks):
            out_tile[slot, b] = out[b * cap : (b + 1) * cap]
            back_tile[slot, b] = back[b * cap : (b + 1) * cap]
        send(slot, pl.ds(at, step))
    for b in range(blocks):
        hit = rank_ref[0, b] == slots
        score_ref[0, b] = jnp.sum(jnp.where(hit, score[b * cap : (b + 1) * cap], 0.0), axis=0, keepdims=True)

    def keep(value, row, ref_at):
        piece = value.shape[1] // (line * inner)
        value = value.astype(bf16)
        full_rows[: value.shape[0], : value.shape[1]] = value
        columns = slice(ref_at, ref_at + piece)
        for c in range(line * inner):
            part = slice(c * piece, (c + 1) * piece)
            for q in range(inner):

                @pl.when(place_ref[1, c] == q)
                def _():
                    for at in range(0, value.shape[0], rank):
                        if inner != 2 or q == 0:
                            source = full_rows[at : at + rank, part]
                            target = sums[q].at[place_ref[0, c], 0, slice(row + at, row + at + rank), columns]
                            if pl.num_programs(1) > 1:
                                old = jnp.where(turn > 0, target[...].astype(f32), 0.0)
                                source = (old + source.astype(f32)).astype(bf16)
                            target[...] = source
                            continue
                        for d in range(docs):
                            there = pl.ds(pl.multiple_of(at + scal_ref[1 + docs + d] * RANK, RANK), RANK)
                            source = full_rows[there, part]
                            for d2 in range(d):
                                repeated = scal_ref[1 + docs + d2] == scal_ref[1 + docs + d]
                                source = jnp.where(repeated, jnp.zeros_like(source), source)
                            to = ((row + at) // rank * docs + d) * RANK
                            target = sums[q].at[place_ref[0, c], 0, slice(to, to + RANK), columns]
                            if pl.num_programs(1) > 1:
                                old = jnp.where(turn > 0, target[...].astype(f32), 0.0)
                                source = (old + source.astype(f32)).astype(bf16)
                            target[...] = source

    wide = width // (line * inner)
    keep(dot_tn(grad_low, rows_in[...]), 0, 0)
    keep(dot_tn((low_down.astype(f32) * weight).astype(bf16), grads_in[...]), 2 * rank, 0)
    keep(dot_tn(low_gate, grad_gate[...]), 0, wide)
    keep(dot_tn(low_up, grad_up[...]), rank, wide)
    keep(dot_tn(grad_low_down, hidden[...]), 2 * rank, wide)
    for copies in sent[-2:]:
        for copy in copies:
            copy.wait()


def run_experts(docs, scal, ranks, grads, back, low_back, route, route_enter, route_leave, normed, place, inner, *weights):
    experts, members, _, local = ranks.shape
    width = grads.shape[2]
    ff = back.shape[2]
    low = SETS * RANK
    blocks = min(members, 4)
    turns = members // blocks
    packs = place.shape[1]
    line = packs // inner
    bf16 = jnp.bfloat16
    count = blocks * CAP
    tile = min(512, width)
    by_turn = lambda e, r: (e, r, 0, 0)
    rows = lambda wide: pl.BlockSpec((1, count, wide), lambda e, r: (e, r, 0))
    once = lambda wide: [pl.BlockSpec((local, wide), lambda e, r: (r, 0), pipeline_mode=pl.Buffered(1))] * blocks
    per_expert = lambda value: pl.BlockSpec((1,) + value.shape[1:], lambda e, r: (e, 0, 0))
    packed = docs * RANK if inner == 2 else low
    sums = [jax.ShapeDtypeStruct((line, experts, 3 * (packed if q else low), (width + ff) // packs), bf16) for q in range(inner)]
    rows_out = jax.ShapeDtypeStruct((members, experts, CAP, width), bf16)
    return pl.pallas_call(
        functools.partial(expert_kernel, line, docs),
        grid=(experts, turns),
        out_shape=(rows_out, rows_out, jax.ShapeDtypeStruct(ranks.shape, jnp.float32), *sums),
        in_specs=[full(SMEM), pl.BlockSpec((1, blocks, 1, local), by_turn), rows(width), rows(ff), rows(low)]
        + [full()] * 3
        + once(width + low)
        + [per_expert(value) for value in weights]
        + [full(SMEM)],
        out_specs=(full(pl.ANY), full(pl.ANY), pl.BlockSpec((1, blocks, 1, local), by_turn))
        + tuple(pl.BlockSpec((line, 1) + value.shape[2:], lambda e, r: (0, e, 0, 0)) for value in sums),
        scratch_shapes=[
            pltpu.VMEM((count, width), bf16),
            pltpu.VMEM((count, ff), bf16),
            pltpu.VMEM((count, ff), bf16),
            pltpu.VMEM((count, ff), bf16),
            pltpu.VMEM((count, low), jnp.float32),
            pltpu.VMEM((2, blocks, CAP, tile), bf16),
            pltpu.VMEM((2, blocks, CAP, tile), bf16),
            pltpu.SemaphoreType.DMA((2, 2)),
            pltpu.VMEM((2 * low, width), bf16),
            pltpu.VMEM((blocks, EXPERTS, local), jnp.float32),
        ],
        compiler_params=params(),
        cost_estimate=cost(2 * experts * members * CAP * (width * ff * 5 + 9 * low * (width + ff)), 60_000_000),
        name="experts",
    )(scal, ranks, grads, back, low_back, route, route_enter, route_leave, *by_block(normed, blocks), *weights, place)


def mix(rank_ref, rows_ref, pick_ref, step):
    experts, cap, local = (rows_ref.shape[1], rows_ref.shape[2], rank_ref.shape[3])

    @pl.when(step == 0)
    def _():
        slots = lax.broadcasted_iota(jnp.int32, (cap, local), 0).astype(jnp.float32)
        pick = jnp.concatenate([(rank_ref[e, 0] == slots).astype(jnp.float32) for e in range(experts)], axis=0)
        pick_ref[...] = pick.T.astype(jnp.bfloat16)

    rows = jnp.concatenate([rows_ref[0, e] for e in range(experts)], axis=0)
    return dot_nn(pick_ref[...], rows)


def mix_grads(scal_ref, rank_ref, score_ref, rows_ref, added_ref, back_ref, pick_ref, step):
    f32, bf16 = (jnp.float32, jnp.bfloat16)
    experts, local = (rows_ref.shape[1], rank_ref.shape[3])
    piece, low = (rows_ref.shape[3], SETS * RANK)
    width = back_ref.shape[1] - low
    columns = pl.ds(pl.multiple_of(step * piece, 128), piece)
    value = mix(rank_ref, rows_ref, pick_ref, step)
    if added_ref is not None:
        value = value + added_ref[:, columns].astype(f32)
    back_ref[:, columns] = value.astype(bf16)

    @pl.when(step == 0)
    def _():
        lines = lax.broadcasted_iota(jnp.int32, (low, local), 0)
        table = jnp.zeros((low, local), f32)
        for e in range(experts):
            score = score_ref[e, 0]
            whole = score.astype(bf16).astype(f32)
            at = scal_ref[0] * experts + e
            table = jnp.where(lines == at, whole, table)
            table = jnp.where(lines == at + EXPERTS, score - whole, table)
        table = table.T
        if added_ref is not None:
            table = table + added_ref[:, width:].astype(f32)
        back_ref[:, width:] = table.astype(bf16)


def combine_kernel(added, scal_ref, rank_ref, score_ref, rows_ref, *refs):
    back_ref, pick_ref = refs[-2:]
    mix_grads(scal_ref, rank_ref, score_ref, rows_ref, refs[0] if added else None, back_ref, pick_ref, pl.program_id(0))


def combine(scal, ranks, scores, rows, place, addend, *deps):
    experts, members, _, local = ranks.shape
    width = rows.shape[3]
    piece = width // 2
    low = SETS * RANK
    one = pl.BlockSpec((experts, 1, 1, local), lambda n: (0, place, 0, 0))
    more = () if addend is None else (addend,)
    return pl.pallas_call(
        functools.partial(combine_kernel, addend is not None),
        grid=(2,),
        out_shape=jax.ShapeDtypeStruct((local, width + low), jnp.bfloat16),
        in_specs=[full(SMEM), one, one, pl.BlockSpec((1, experts, CAP, piece), lambda n: (place, 0, 0, n))]
        + [full()] * len(more)
        + [full(pl.ANY)] * len(deps),
        out_specs=full(),
        scratch_shapes=[pltpu.VMEM((local, experts * CAP), jnp.bfloat16)],
        compiler_params=params(),
        cost_estimate=cost(2 * local * experts * CAP * width, 2 * experts * CAP * width),
        name="combine",
    )(scal, ranks, scores, rows, *more, *deps)


def combine_last_kernel(scal_ref, rank_ref, score_ref, grads_ref, rows_ref, added_ref, *refs):
    members = pl.num_programs(0)
    out_refs, (back_ref, pick_ref) = (refs[-2 - members : -2], refs[-2:])
    block, step = (pl.program_id(0), pl.program_id(1))
    piece = rows_ref.shape[3]
    columns = pl.ds(pl.multiple_of(step * piece, 128), piece)
    value = mix(rank_ref, rows_ref, pick_ref, step).astype(jnp.bfloat16)
    for b in range(members):

        @pl.when(block == b)
        def _():
            out_refs[b][:, columns] = value

    @pl.when(block == 0)
    def _():
        mix_grads(scal_ref, rank_ref, score_ref, grads_ref, added_ref, back_ref, pick_ref, step)


def combine_last(scal, ranks, scores, grads, mixed, addend, *deps):
    experts, members, _, local = ranks.shape
    width = grads.shape[3]
    piece = width // 2
    low = SETS * RANK
    out = jax.ShapeDtypeStruct((local, width), jnp.bfloat16)
    one = pl.BlockSpec((experts, 1, 1, local), lambda b, n: (0, b, 0, 0))
    first = lambda b, n: (0, 0, 0, jnp.where(b == 0, n, 1))
    return pl.pallas_call(
        lambda *refs: combine_last_kernel(*refs[:6], *refs[6 + len(deps) :]),
        grid=(members, 2),
        out_shape=(out,) * members + (jax.ShapeDtypeStruct((local, width + low), jnp.bfloat16),),
        in_specs=[full(SMEM), one, one]
        + [pl.BlockSpec((1, experts, CAP, piece), first), pl.BlockSpec((1, experts, CAP, piece), lambda b, n: (b, 0, 0, n))]
        + [full()]
        + [full(pl.ANY)] * len(deps),
        out_specs=(full(),) * (members + 1),
        scratch_shapes=[pltpu.VMEM((local, experts * CAP), jnp.bfloat16)],
        compiler_params=params(),
        cost_estimate=cost(2 * 5 * local * experts * CAP * width, 10 * experts * CAP * width),
        name="combine_last",
    )(scal, ranks, scores, grads, mixed, addend, *deps)


def per_device(
    tokens,
    cotangent,
    pack_order,
    doc_lengths,
    doc_sets,
    routes,
    attention_gain,
    query_gain,
    key_gain,
    feed_gain,
    qkv_weight,
    out_weight,
    router_weight,
    gate_weight,
    up_weight,
    down_weight,
    qkv_enter,
    qkv_leave,
    out_enter,
    out_leave,
    router_enter,
    router_leave,
    gate_enter,
    gate_leave,
    up_enter,
    up_leave,
    down_enter,
    down_leave,
):
    members = lax.axis_size("ep")
    packs = lax.axis_size("grp")
    pack = lax.axis_index("grp")
    member = lax.axis_index("ep")
    local, width = tokens.shape
    slice_width = width // members
    experts_here = gate_weight.shape[0]
    own_cols = member * slice_width
    count = members // 2
    low = SETS * RANK
    f32, bf16 = (jnp.float32, jnp.bfloat16)
    slot = jnp.sum(jnp.where(pack_order == pack, jnp.arange(packs, dtype=jnp.int32), 0))
    named = jnp.sum(jnp.left_shift(jnp.int32(1), routes), axis=1)
    documents_here = jnp.concatenate([doc_lengths[0], doc_sets[0]])
    info = jnp.concatenate([named, jnp.pad(documents_here, (0, 128 - documents_here.shape[0]))])
    info = jnp.stack(gather_parts(info, "grp"))
    other = jnp.sum(jnp.where(pack_order == pack ^ 1, jnp.arange(packs, dtype=jnp.int32), 0))
    other = lax.dynamic_index_in_dim(info, other ^ pack, 0, keepdims=False)
    info = lax.dynamic_index_in_dim(info, slot ^ pack, 0, keepdims=False)
    blocks = [member ^ j for j in range(members)]
    named = info[:local]
    docs = doc_lengths.shape[1]
    lengths, sets = (info[local : local + docs], info[local + docs : local + 2 * docs])
    ends = jnp.cumsum(lengths)
    starts = ends - lengths
    scal = jnp.concatenate([member[None].astype(jnp.int32), ends, sets, starts])
    gain_one, gain_two = (attention_gain[None], feed_gain[None])
    route, route_leave = (router_weight.T, router_leave.T)
    adapters = (gain_one, qkv_weight, qkv_enter, qkv_leave)
    kept = project(docs, 0, scal, gather_near(tokens, "ep"), *adapters, None)
    token_parts = gather_far(tokens, "ep", kept[4])
    named_all = jnp.stack(gather_parts(named.reshape(1, local), "ep"))
    kept = project(docs, 1, scal, token_parts, *adapters, kept)
    normed_all, low_all, projected, values, squares = kept
    late = fence(scal, values)
    ends, starts = (late[1 : 1 + docs], late[1 + 2 * docs :])
    rows = (jnp.stack(blocks)[:, None] * local + jnp.arange(local, dtype=jnp.int32)[None, :]).reshape(-1)
    begin = starts[0]
    for k in range(1, docs):
        begin = jnp.where(rows >= ends[k - 1], starts[k], begin)
    cosine, sine = angles(rows - begin)
    upstream_far = gather_near(swap(fence(cotangent, token_parts[0], named_all), "ep", members // 2), "ep")
    upstream_parts = gather_near(cotangent, "ep") + upstream_far
    squares = sum_relative(squares, "ep", local)
    own_gain = lambda gain: lax.dynamic_slice_in_dim(gain, own_cols, slice_width, 0)
    gains = jnp.stack([own_gain(query_gain), own_gain(key_gain)]).astype(f32)
    queries, keys = prepare(width, projected, squares, gains, cosine, sine, local, upstream_parts[-1], named_all)
    heads = [None] * members

    def attend_place(place, addend, *deps):
        heads[place] = attend(docs, place, local, scal, queries, keys, values, out_weight, out_enter, addend, *deps)
        return heads[place][1], heads[place][2]

    top = members // 2
    outs = reduce_scatter(attend_place, "ep")
    hidden_state, normed_two, low_router, probs = middle(
        docs, scal, tokens, outs, out_leave, gain_two, route, router_enter, route_leave
    )

    upstream_rows = run_upstream(scal, named_all, upstream_parts, down_weight, down_leave, normed_two)
    normed_two_parts = gather_near(normed_two, "ep") + gather_far(normed_two, "ep", upstream_rows[0])
    inner = packs // LINE
    chunk_ids = jnp.arange(packs, dtype=jnp.int32)
    place = jnp.stack([(chunk_ids // inner - pack // inner) % LINE, (chunk_ids % inner - pack % inner) % inner])
    ranks = upstream_rows[0]
    mixed_rows, grad_rows, scores, *expert_sums = run_experts(
        docs,
        scal,
        *upstream_rows,
        route,
        router_enter,
        route_leave,
        normed_two_parts,
        place,
        inner,
        gate_weight,
        up_weight,
        down_weight,
        gate_enter,
        gate_leave,
        up_enter,
        up_leave,
        down_enter,
        down_leave,
    )
    mixed = []

    def combine_place(place, addend, *deps):
        if place:
            part = combine(scal, ranks, scores, grad_rows, place, addend, *deps)
        else:
            *parts, part = combine_last(scal, ranks, scores, grad_rows, mixed_rows, addend, *deps)
            mixed.extend(parts)
        return part, part

    grads = reduce_scatter(combine_place, "ep")
    grad_hidden, grad_branch, grad_router_leave = middle_back(
        docs, scal, grads, probs, hidden_state, cotangent, low_router, gain_two, route, router_enter, route_leave
    )
    pair = lambda a, b: (a.astype(f32) + b.astype(f32)).astype(bf16)
    mixed = [pair(mixed[j], swap(mixed[j + 1], "ep", 1)) for j in range(0, members, 2)]
    mixed_near, mixed_far = (scatter_even(mixed[: top // 2], "ep"), scatter_even(mixed[top // 2 :], "ep"))

    inside = (queries, keys, values, out_weight, out_enter, out_leave)

    def attend_half_back(half, branch, before, *deps):
        part = slice(half * count, (half + 1) * count)
        atts, logs = ([head[i] for head in heads[part]] for i in (0, 2))
        return attend_back(docs, half, scal, *inside, branch, atts, logs, normed_two_parts[part], before, *deps)

    near = attend_half_back(0, gather_near(grad_branch, "ep"), ())
    branch_far = gather_far(grad_branch, "ep", near[6])
    other_sets = other[local + docs : local + 2 * docs]
    line_sums = sum_experts(docs, other_sets, expert_sums, near[6])
    far = attend_half_back(1, branch_far, near[1:6], line_sums[0])
    mixed_got = swap(fence(mixed_far, branch_far[0]), "ep", top)
    grad_keys, grad_values, *low_grads = far[1:6]
    terms = jnp.concatenate([jnp.concatenate([near[6], far[6]], axis=1), far[7]])
    line = LineSum(line_sums, "grp", LINE, inner)
    got = line.send(1)
    terms = sum_relative(fence(terms, *got, mixed_got), "ep", local)
    line.add(1, got)
    leave_rows = low // members
    leave_parts = jnp.stack([lax.dynamic_slice_in_dim(grad_router_leave, b * leave_rows, leave_rows, 1) for b in blocks])
    leave_parts = jnp.pad(leave_parts.astype(bf16), ((0, 0), (0, 0), (0, slice_width - leave_rows)))
    shared = (projected, squares, terms, gains, cosine, sine, normed_all, low_all, qkv_weight, qkv_enter, qkv_leave)
    ready = line.ready(2)
    *far_parts, enter_sums, leave_sums, projected_grads, low_grad = project_back(
        docs, local, scal, near[0], far[0], grad_keys, grad_values, *shared, leave_parts, *ready
    )
    got = line.send(2, ready)
    line.add(2, got)
    *far_parts, enter_sums, leave_sums = (fence(value, *got) for value in (*far_parts, enter_sums, leave_sums))
    input_far = scatter_even([pair(far_parts[j], swap(far_parts[j + 1], "ep", 1)) for j in range(0, count, 2)], "ep")
    near_parts = project_near(local, projected_grads, low_grad, qkv_weight, qkv_enter, input_far)
    input_got = swap(input_far, "ep", top)
    if count == 2:
        inputs = (near_parts[0], swap(near_parts[1], "ep", 1), input_got)
    else:
        inputs = [pair(near_parts[j], swap(near_parts[j + 1], "ep", 1)) for j in range(0, count, 2)]
        inputs = (scatter_even(inputs, "ep"), input_got)
    grad_input = finish(inputs, grad_hidden, tokens, gain_one)
    layer_out = (hidden_state + (mixed_near.astype(f32) + mixed_got.astype(f32))).astype(bf16)

    got = line.send(3)
    line.add(3, got)
    expert_sum = line.total[0]
    by_rows = lambda value: value.astype(bf16).reshape(-1, packs, value.shape[-2] // packs, slice_width).transpose(1, 0, 2, 3)
    joined = jnp.concatenate([by_rows(value) for value in (*low_grads, leave_sums)], axis=1)
    joined = sum_packs(by_place(fence(joined, input_far)), input_got)
    enter_sums = [pair(enter_sums[j], swap(enter_sums[j + 1], "ep", 1)) for j in range(0, members, 2)]
    enter_far = swap(scatter_even(enter_sums[top // 2 :], "ep"), "ep", top)
    enter_sum = fence(pair(scatter_even(enter_sums[: top // 2], "ep"), enter_far), input_got, *got, joined)
    enter_chunks = by_rows(enter_sum[: 3 * low].reshape(3, low, slice_width)).reshape(packs, -1, slice_width)
    leave_chunks = by_rows(enter_sum[3 * low :]).reshape(packs, -1, slice_width)
    enter_sum = sum_packs(by_place(jnp.concatenate([enter_chunks, leave_chunks], axis=1)))
    enter_rows = 3 * low // packs
    wide = width // packs
    turn = lambda value: jnp.swapaxes(value, -1, -2)
    return (
        layer_out,
        grad_input,
        turn(enter_sum[:enter_rows].reshape(3, -1, slice_width)),
        joined[3:],
        turn(joined[0]),
        joined[1],
        turn(joined[2]),
        turn(enter_sum[enter_rows:, :leave_rows]),
        turn(expert_sum[:, :low, :wide]),
        expert_sum[:, :low, wide:],
        turn(expert_sum[:, low : 2 * low, :wide]),
        expert_sum[:, low : 2 * low, wide:],
        turn(expert_sum[:, 2 * low :, wide:]),
        expert_sum[:, 2 * low :, :wide],
    )


def solution(mesh):
    in_specs = (
        P(("grp", "ep"), None),
        P(("grp", "ep"), None),
        P(),
        P("grp", None),
        P("grp", None),
        P(("grp", "ep"), None),
        P(),
        P(),
        P(),
        P(),
        P(None, None, "ep"),
        P("ep", None),
        P(),
        P("ep", None, None),
        P("ep", None, None),
        P("ep", None, None),
        P(),
        P(None, None, "ep"),
        P("ep", None),
        P(),
        P(),
        P(),
        P("ep", None, None),
        P("ep", None, None),
        P("ep", None, None),
        P("ep", None, None),
        P("ep", None, None),
        P("ep", None, None),
    )
    out_specs = (
        P(("grp", "ep"), None),
        P(("grp", "ep"), None),
        P(None, "ep", "grp"),
        P(None, "grp", "ep"),
        P("ep", "grp"),
        P("grp", "ep"),
        P("ep", "grp"),
        P("ep", "grp"),
        P("ep", "grp", None),
        P("ep", None, "grp"),
        P("ep", "grp", None),
        P("ep", None, "grp"),
        P("ep", "grp", None),
        P("ep", None, "grp"),
    )
    return jax.shard_map(
        per_device, mesh=mesh, in_specs=in_specs, out_specs=out_specs, check_vma=False
    )
```

time: 686 us -> 514 us (0.75)
  waiting for transfers between devices: 212 us -> 63.5 us
  Pallas kernels: 143 us -> 289 us
  matrix products: 144 us -> 0 us
  other arithmetic: 76.2 us -> 47.7 us
    pallas_call x3 -> x35, Pallas kernels: 143 us -> 289 us  [the longest x1 104 us: run_experts(): pl.pallas_call(functools.partial(expert_kernel, line, docs), grid=(expert...]
    dot_general x30 -> x0, matrix products: 132 us -> none  [the longest x19 94.4 us: per_device(): dot = lambda spec, a, b: jnp.einsum(spec, a, b, preferred_element_type=f32)]
    ppermute x52 -> x42, waiting for transfers between devices: 146 us -> 50.7 us  [swap(): return lax.ppermute(value, axis, [(i, i ^ bit) for i in range(count)])]
    ppermute x14, waiting for transfers between devices: 66 us -> 12.8 us  [the longest x3 5.37 us: send(): lax.ppermute(up, self.axis, self.up)]
    sub x1 -> x0, matrix products: 12.3 us -> none  [per_device(): probs = jax.nn.softmax(jnp.where(allowed[None], scores, NEG), axis=-1)]
    concatenate x7, other arithmetic: 16.7 us -> 4.95 us  [the longest x1 1.31 us: per_device(): jnp.concatenate([jnp.concatenate([near[6], far[6]], axis=1), far[7]])]
    convert_element_type x25 -> x15, other arithmetic: 36.3 us -> 24.9 us  [the longest x3 8.63 us: ready(): self.total[p].astype(jnp.bfloat16)]
    unnamed x187 -> x64, local copies, waits for them, and re-layouts: 15.8 us -> 18.1 us
  transfers between devices with their start and end apart: 66 -> 56, of which waited for: 28 -> 21; matrix products, arithmetic and copies ran while one was open for 26% -> 14% of each run, Pallas kernels for 1% -> 34%
where the time goes in v2:
time: 514 us; the launch traced here: 504 us
  Pallas kernels  289 us (56%)
  starting transfers between devices  65.7 us (13%)
  waiting for transfers between devices  63.5 us (12%)
  other arithmetic  47.7 us (9%)
  local copies, waits for them, and re-layouts  35.1 us (7%)
    pallas_call x1, Pallas kernels, run_experts(): pl.pallas_call(functools.partial(expert_kernel, line, docs), grid=(expert...  104 us
    ppermute x42, waiting for transfers between devices, swap(): return lax.ppermute(value, axis, [(i, i ^ bit) for i in range(count)])  50.7 us
    pallas_call x2, Pallas kernels, attend_back(): pl.pallas_call(functools.partial(attend_back_kernel, docs, half, local),...  35.9 us
    ppermute x42, starting transfers between devices, swap(): return lax.ppermute(value, axis, [(i, i ^ bit) for i in range(count)])  34.6 us
    pallas_call x4, Pallas kernels, attend(): pl.pallas_call(functools.partial(attend_kernel, docs, place, local, adden...  26.9 us
    pallas_call x2, Pallas kernels, project(): pl.pallas_call(functools.partial(project_kernel, docs, half, parts), grid...  22.9 us
    pallas_call x1, Pallas kernels, run_upstream(): pl.pallas_call(lambda *refs: upstream_kernel(*refs[:4 + blocks], *refs[4...  21.3 us
    unnamed x64, local copies, waits for them, and re-layouts  18.1 us
  transfers between devices with their start and end apart: 56, of which 21 were waited for; matrix products, arithmetic and copies ran while one was open for 14% of the time, Pallas kernels for 34%

profile of v2, /device:TPU:0, one launch (start us, length us, event | category | flops | bytes accessed | tf_op | source)
XLA Modules:
  0.0 504.1 jit_solution(1828932363543468108)
XLA Ops:
  1.2 2.6 collective-permute-start.7
  5.8 2.6 collective-permute-start.3
  8.4 1.6 collective-permute-start.1
  20.3 11.5 %project.2 = (bf16[1024,2048]{1,0:T(8,128)(2,1)}, bf16[3,1024,128]{2,1,0:T(8,128)(2,1)}, f32[2,1024,512]{2,1,0:T(8,128)}, bf16[1024,512]{1,0:T(8,128)(2,1)}, f32[2,1024]{1,0:T(2,128)}) custom-call(s32[13]{0:T(128)} %pad_add_fusion.4.scal_ref.refs_0_, bf16[256,2048]{1,0:T(8,128)(2,1)} %refs_4_.11, bf16[256,2048]{1,0:T(8,128)(2,1)} %collective-permute-done.8.refs_1_, ...), custom_call_target="tpu_custom_call" | custom-call | flops 503316480 | bytes 1750000 | tf_op jit(solution)/shard_map/project/pallas_call | solution.py:309
  33.4 2.3 copy.80.refs_0_
  42.9 11.4 %project.3 = (bf16[1024,2048]{1,0:T(8,128)(2,1)}, bf16[3,1024,128]{2,1,0:T(8,128)(2,1)}, f32[2,1024,512]{2,1,0:T(8,128)}, bf16[1024,512]{1,0:T(8,128)(2,1)}, f32[2,1024]{1,0:T(2,128)}) custom-call(s32[13]{0:T(128)} %pad_add_fusion.4.scal_ref.refs_0_, ...), custom_call_target="tpu_custom_call", output_to_operand_aliasing={{0}: (7, {}), {1}: (8, {}), {2}: (9, {}), {3}: (10, {}), {4... | custom-call | flops 503316480 | bytes 1750000 | tf_op jit(solution)/shard_map/project/pallas_call | solution.py:309
  56.0 4.5 subtract_convert_fusion
  60.5 1.9 fusion.2
  70.0 5.0 prepare.1
  75.0 7.5 %attend.4 = (bf16[256,512]{1,0:T(8,128)(2,1)}, bf16[256,2176]{1,0:T(8,128)(2,1)}, f32[8,256]{1,0:T(8,128)}) custom-call(s32[13]{0:T(128)} %pad_add_fusion.4.scal_ref.refs_0_, bf16[1024,512]{1,0:T(8,128)(2,1)} %get-tuple-element.94.q_ref.refs_0_, bf16[1024,512]{1,0:T(8,128)(2,1)} %get-tuple-element.95.k_ref.refs_1_, ...), custom_call_target="tpu_custom_call" | custom-call | flops 275000000 | bytes 500000 | tf_op jit(solution)/shard_map/attend/pallas_call | solution.py:420
  82.5 6.2 %attend.5 = (bf16[256,512]{1,0:T(8,128)(2,1)}, bf16[256,2176]{1,0:T(8,128)(2,1)}, f32[8,256]{1,0:T(8,128)}) custom-call(s32[13]{0:T(128)} %pad_add_fusion.4.scal_ref.refs_0_, bf16[1024,512]{1,0:T(8,128)(2,1)} %get-tuple-element.94.q_ref.refs_0_, bf16[1024,512]{1,0:T(8,128)(2,1)} %get-tuple-element.95.k_ref.refs_1_, ...), custom_call_target="tpu_custom_call" | custom-call | flops 275000000 | bytes 500000 | tf_op jit(solution)/shard_map/attend/pallas_call | solution.py:420
  89.7 7.0 %attend.6 = (bf16[256,512]{1,0:T(8,128)(2,1)}, bf16[256,2176]{1,0:T(8,128)(2,1)}, f32[8,256]{1,0:T(8,128)}) custom-call(s32[13]{0:T(128)} %pad_add_fusion.4.scal_ref.refs_0_, bf16[1024,512]{1,0:T(8,128)(2,1)} %get-tuple-element.94.q_ref.refs_0_, bf16[1024,512]{1,0:T(8,128)(2,1)} %get-tuple-element.95.k_ref.refs_1_, ...), custom_call_target="tpu_custom_call" | custom-call | flops 275000000 | bytes 500000 | tf_op jit(solution)/shard_map/attend/pallas_call | solution.py:420
  96.7 2.0 collective-permute-start.19
  100.3 6.2 %attend.7 = (bf16[256,512]{1,0:T(8,128)(2,1)}, bf16[256,2176]{1,0:T(8,128)(2,1)}, f32[8,256]{1,0:T(8,128)}) custom-call(s32[13]{0:T(128)} %pad_add_fusion.4.scal_ref.refs_0_, bf16[1024,512]{1,0:T(8,128)(2,1)} %get-tuple-element.94.q_ref.refs_0_, bf16[1024,512]{1,0:T(8,128)(2,1)} %get-tuple-element.95.k_ref.refs_1_, ...), custom_call_target="tpu_custom_call" | custom-call | flops 275000000 | bytes 500000 | tf_op jit(solution)/shard_map/attend/pallas_call | solution.py:420
  106.5 17.6 %collective-permute-done.19.ob_ref = bf16[256,2176]{1,0:T(8,128)(2,1)S(1)} collective-permute-done((bf16[256,2176]{1,0:T(8,128)(2,1)}, bf16[256,2176]{1,0:T(8,128)(2,1)S(1)}, u32[]{:S(2)}, u32[]{:S(2)}) %collective-permute-start.19) | collective-permute-done | bytes 1114144 | tf_op jit(solution)/shard_map/ppermute | solution.py:42
  125.1 4.6 middle.1
  129.7 2.2 collective-permute-start.22
  131.9 21.3 %upstream.1 = (f32[4,4,1,256]{3,2,1,0:T(1,128)}, bf16[4,576,2048]{2,1,0:T(8,128)(2,1)}, bf16[4,576,1024]{2,1,0:T(8,128)(2,1)}, f32[4,576,128]{2,1,0:T(8,128)}) custom-call(s32[13]{0:T(128)} %pad_add_fusion.4.scal_ref.refs_0_, s32[4,1,256]{2,1,0:T(1,128)} %pad_add_fusion.refs_2_.refs_6_.refs_1_, bf16[256,2048]{1,0:T(8,128)(2,1)} %up_ref.1, ...), custom_call_target="tpu_custom_call" | custom-call | flops 1207959552 | bytes 5000000 | tf_op jit(solution)/shard_map/upstream/pallas_call | solution.py:823
  153.2 3.7 collective-permute-done.22.refs_0_
  158.6 2.4 collective-permute-done.23.refs_3_.refs_13_
  162.0 104.1 %experts.1 = (bf16[4,4,144,2048]{3,2,1,0:T(8,128)(2,1)}, bf16[4,4,144,2048]{3,2,1,0:T(8,128)(2,1)}, f32[4,4,1,256]{3,2,1,0:T(1,128)}, bf16[4,4,384,384]{3,2,1,0:T(8,128)(2,1)}, bf16[4,4,192,384]{3,2,1,0:T(8,128)(2,1)}) custom-call(s32[13]{0:T(128)} %pad_add_fusion.4.scal_ref.refs_0_, f32[4,4,1,256]{3,2,1,0:T(1,128)} %get-tuple-element.104.refs_1_.rank_ref, ...), custom_call_target="tpu_custom_call" | custom-call | flops 8078229504 | bytes 7500000 | tf_op jit(solution)/shard_map/experts/pallas_call | solution.py:1028
  266.1 3.8 combine.3.refs_0_
  270.0 3.8 combine.4.refs_1_
  274.2 4.1 combine.5.refs_6_
  278.3 1.8 collective-permute-start.28
  282.4 13.5 %combine_last.1 = (bf16[256,2048]{1,0:T(8,128)(2,1)}, bf16[256,2048]{1,0:T(8,128)(2,1)}, bf16[256,2048]{1,0:T(8,128)(2,1)}, bf16[256,2048]{1,0:T(8,128)(2,1)}, bf16[256,2176]{1,0:T(8,128)(2,1)}) custom-call(s32[13]{0:T(128)} %pad_add_fusion.4.scal_ref.refs_0_, f32[4,4,1,256]{3,2,1,0:T(1,128)} %get-tuple-element.104.refs_1_.rank_ref, ...), custom_call_target="tpu_custom_call" | custom-call | flops 377487360 | bytes 1474560 | tf_op jit(solution)/shard_map/combine_last/pallas_call | solution.py:1150
  295.8 9.4 %collective-permute-done.28.gb_ref = bf16[256,2176]{1,0:T(8,128)(2,1)} collective-permute-done((bf16[256,2176]{1,0:T(8,128)(2,1)}, bf16[256,2176]{1,0:T(8,128)(2,1)}, u32[]{:S(2)}, u32[]{:S(2)}) %collective-permute-start.28) | collective-permute-done | bytes 1114144 | tf_op jit(solution)/shard_map/ppermute | solution.py:42
  305.3 6.0 %middle_back.1 = (f32[256,2048]{1,0:T(8,128)}, bf16[256,2176]{1,0:T(8,128)(2,1)}, f32[16,128]{1,0:T(8,128)}) custom-call(s32[13]{0:T(128)} %pad_add_fusion.4.scal_ref.refs_0_, bf16[256,2176]{1,0:T(8,128)(2,1)} %get-tuple-element.115.ga_ref, bf16[256,2176]{1,0:T(8,128)(2,1)} %collective-permute-done.28.gb_ref, f32[16,256]{1,0:T(8,128)} %get-tuple-element.116.probs_ref, ...), custom_call_target="tpu_custom_call" | custom-call | flops 33554432 | bytes 1250000 | tf_op jit(solution)/shard_map/middle_back/pallas_call | solution.py:508
  311.2 1.7 collective-permute-start.29
  314.3 15.1 %attend_back.2 = (f32[512,512]{1,0:T(8,128)}, f32[1024,512]{1,0:T(8,128)}, f32[1024,512]{1,0:T(8,128)}, f32[128,512]{1,0:T(8,128)}, f32[128,512]{1,0:T(8,128)}, /*index=5*/f32[128,512]{1,0:T(8,128)}, f32[1,512]{1,0:T(1,128)}) custom-call(s32[13]{0:T(128)} %pad_add_fusion.4.scal_ref.refs_0_, bf16[1024,512]{1,0:T(8,128)(2,1)} %get-tuple-element.94.q_ref.refs_0_, ...), custom_call_target="tpu_custom_call" | custom-call | flops 1000000000 | bytes 1750000 | tf_op jit(solution)/shard_map/attend_back/pallas_call | solution.py:625
  329.4 9.0 %collective-permute-done.29.refs_0_ = bf16[256,2176]{1,0:T(8,128)(2,1)S(1)} collective-permute-done((bf16[256,2176]{1,0:T(8,128)(2,1)}, bf16[256,2176]{1,0:T(8,128)(2,1)S(1)}, u32[]{:S(2)}, u32[]{:S(2)}) %collective-permute-start.29) | collective-permute-done | bytes 1114144 | tf_op jit(solution)/shard_map/ppermute | solution.py:42
  339.4 5.9 %widen.1 = (bf16[4,384,384]{2,1,0:T(8,128)(2,1)}, bf16[4,384,384]{2,1,0:T(8,128)(2,1)}, bf16[4,384,384]{2,1,0:T(8,128)(2,1)}, bf16[4,384,384]{2,1,0:T(8,128)(2,1)}) custom-call(s32[4]{0:T(128)} %get-tuple-element.222.sets_ref, bf16[4,4,384,384]{3,2,1,0:T(8,128)(2,1)} %get-tuple-element.132.kept_ref, ...), custom_call_target="tpu_custom_call" | custom-call | tf_op jit(solution)/shard_map/widen/pallas_call | solution.py:196
  345.4 3.1 collective-permute-start.34
  349.8 2.9 add_convert_fusion.5.refs_0_
  352.7 1.7 collective-permute-start.31
  354.5 20.8 %attend_back.3 = (f32[512,512]{1,0:T(8,128)}, f32[1024,512]{1,0:T(8,128)}, f32[1024,512]{1,0:T(8,128)}, f32[128,512]{1,0:T(8,128)}, f32[128,512]{1,0:T(8,128)}, ...) custom-call(s32[13]{0:T(128)} %pad_add_fusion.4.scal_ref.refs_0_, ...), custom_call_target="tpu_custom_call" | custom-call | flops 1000000000 | bytes 1750000 | tf_op jit(solution)/shard_map/attend_back/pallas_call | solution.py:625
  376.6 2.2 collective-permute-done.35.refs_2_
  378.8 3.3 add_convert_fusion.2.refs_17_.refs_18_
  383.5 5.6 %collective-permute-start.38 = (bf16[4,384,384]{2,1,0:T(8,128)(2,1)}, bf16[4,384,384]{2,1,0:T(8,128)(2,1)}, u32[]{:S(2)}, u32[]{:S(2)}) collective-permute-start(bf16[4,384,384]{2,1,0:T(8,128)(2,1)} %add_convert_fusion.2.refs_17_.refs_18_), channel_id=1, source_target_pairs={{0,8},{4,12},{8,16},{12,20},{16,24},{20,28},{1,9},{5,13},{9,17},{1... | collective-permute-start | bytes 3538952 | tf_op jit(solution)/shard_map/ppermute | solution.py:130
  391.2 1.7 collective-permute-start.37
  395.4 17.8 %project_back.1 = (bf16[256,2048]{1,0:T(8,128)(2,1)}, bf16[256,2048]{1,0:T(8,128)(2,1)}, bf16[4,400,512]{2,1,0:T(8,128)(2,1)}, f32[3,128,512]{2,1,0:T(8,128)}, b...) custom-call(s32[13]{0:T(128)} %pad_add_fusion.4.scal_ref.refs_0_, f32[512,512]{1,0:T(8,128)} %get-tuple-element.123.refs_1_, ...), custom_call_target="tpu_custom_call" | custom-call | flops 603979776 | bytes 2500000 | tf_op jit(solution)/shard_map/project_back/pallas_call | solution.py:715
  414.3 2.2 slice_bitcast_fusion.4
  416.5 3.8 add_convert_fusion.4
  421.7 2.7 add_convert_fusion
  426.2 1.9 fusion
  428.1 1.7 collective-permute-start.45
  429.8 2.7 add_convert_fusion.1
  432.5 5.3 %collective-permute-start.46 = (bf16[4,384,384]{2,1,0:T(8,128)(2,1)}, bf16[4,384,384]{2,1,0:T(8,128)(2,1)}, u32[]{:S(2)}, u32[]{:S(2)}) collective-permute-start(bf16[4,384,384]{2,1,0:T(8,128)(2,1)} %add_convert_fusion.1), channel_id=1, source_target_pairs={{0,8},{4,12},{8,16},{12,20},{16,24},{20,28},{1,9},{5,13},{9,17},{1... | collective-permute-start | bytes 3538952 | tf_op jit(solution)/shard_map/ppermute | solution.py:130
  440.1 2.0 add_convert_fusion.7.refs_0_
  442.1 1.6 add_convert_fusion.3.refs_0_.refs_1_
  443.7 1.6 collective-permute-start.42
  445.3 2.0 constant_dynamic-slice_fusion.7
  449.1 8.4 %project_near.1 = (bf16[256,2048]{1,0:T(8,128)(2,1)}, bf16[256,2048]{1,0:T(8,128)(2,1)}) custom-call(bf16[3,1024,512]{2,1,0:T(8,128)(2,1)} %get-tuple-element.146.grads_ref, bf16[1024,384]{1,0:T(8,128)(2,1)} %get-tuple-element.147.low_ref, bf16[3,2048,512]{2,1,0:T(8,128)(2,1)} %w_ref.9, bf16[3,2048,128]{2,1,0:T(8,128)(2,1)} %enter_ref.9, ...), custom_call_target="tpu_custom_call" | custom-call | flops 402653184 | bytes 1250000 | tf_op jit(solution)/shard_map/project_near/pallas_call | solution.py:748
  457.6 4.9 collective-permute-done.46.refs_2_
  462.5 2.5 select_add_fusion
  466.9 2.5 collective-permute-start.49
  469.4 2.8 collective-permute-start.50
  474.0 2.0 copy.67
  476.0 2.0 copy.68
  478.7 1.8 convert_add_fusion.2.refs_4_
  485.2 4.6 collective-permute-done.52
  490.8 2.8 collective-permute-start.53
  493.8 2.2 collective-permute-start.55
  497.3 5.4 %finish.1 = bf16[256,2048]{1,0:T(8,128)(2,1)} custom-call(bf16[256,2048]{1,0:T(8,128)(2,1)} %get-tuple-element.150.refs_0_, bf16[256,2048]{1,0:T(8,128)(2,1)} %collective-permute-done.41.refs_1_, bf16[256,2048]{1,0:T(8,128)(2,1)} %collective-permute-done.42.refs_2_.refs_1_, f32[256,2048]{1,0:T(8,128)} %get-tuple-element.152.refs_3_, ...), custom_call_target="tpu_custom_call" | custom-call | flops 655360 | bytes 786432 | tf_op jit(solution)/shard_map/finish/pallas_call | solution.py:777
  (231 shorter events, 70.5 us)
Async XLA Ops:
  0.6 19.6 %collective-permute-start.8 = (bf16[256,2048]{1,0:T(8,128)(2,1)}, bf16[256,2048]{1,0:T(8,128)(2,1)}, u32[]{:S(2)}, u32[]{:S(2)}) collective-permute-start(bf16[256,2048]{1,0:T(8,128)(2,1)} %refs_4_.11), channel_id=1, source_target_pairs={{0,1},{1,0},{2,3},{3,2},{4,5},{5,4},{6,7},{7,6},{8,9},{9,8},{10,11... | collective-permute-start | bytes 3145736 | tf_op jit(solution)/shard_map/ppermute | solution.py:42
  1.2 30.6 %collective-permute-start.7 = (bf16[256,2048]{1,0:T(8,128)(2,1)}, bf16[256,2048]{1,0:T(8,128)(2,1)S(1)}, u32[]{:S(2)}, u32[]{:S(2)}) collective-permute-start(bf16[256,2048]{1,0:T(8,128)(2,1)} %refs_4_.11), channel_id=1, source_target_pairs={{0,2},{1,3},{2,0},{3,1},{4,6},{5,7},{6,4},{7,5},{8,10},{9,11},{10,... | collective-permute-start | bytes 3145736 | tf_op jit(solution)/shard_map/ppermute | solution.py:42
  5.8 5.7 %collective-permute-start.3 = (s32[384]{0:T(512)S(1)}, s32[384]{0:T(512)S(1)}, u32[]{:S(2)}, u32[]{:S(2)}) collective-permute-start(s32[384]{0:T(512)S(1)} %pad_add_fusion.1), channel_id=1, source_target_pairs={{0,16},{4,20},{8,24},{12,28},{16,0},{20,4},{24,8},{28,12},{1,17},{... | collective-permute-start | bytes 4616 | tf_op jit(solution)/shard_map/ppermute | solution.py:42
  8.4 3.6 collective-permute-start.1
  10.0 3.6 collective-permute-start
  11.5 3.6 collective-permute-start.5
  12.0 6.2 %collective-permute-start.4 = (s32[384]{0:T(512)S(1)}, s32[384]{0:T(512)S(1)}, u32[]{:S(2)}, u32[]{:S(2)}) collective-permute-start(s32[384]{0:T(512)S(1)} %collective-permute-done.3), channel_id=1, source_target_pairs={{0,4},{4,0},{8,12},{12,8},{16,20},{20,16},{24,28},{28,24},{1,5},{5... | collective-permute-start | bytes 4616 | tf_op jit(solution)/shard_map/ppermute | solution.py:42
  13.6 4.7 collective-permute-start.2
  15.1 3.6 collective-permute-start.6
  32.7 9.2 %collective-permute-start.9 = (bf16[256,2048]{1,0:T(8,128)(2,1)}, bf16[256,2048]{1,0:T(8,128)(2,1)S(1)}, u32[]{:S(2)}, u32[]{:S(2)}) collective-permute-start(bf16[256,2048]{1,0:T(8,128)(2,1)} %fence.14.refs_0_.refs_1_), channel_id=1, source_target_pairs={{0,1},{1,0},{2,3},{3,2},{4,5},{5,4},{6,7},{7,6},{8,9},{9,8},{10,11... | collective-permute-start | bytes 3145736 | tf_op jit(solution)/shard_map/ppermute | solution.py:42
  32.7 3.6 collective-permute-start.13
  35.8 1.1 collective-permute-start.12
  36.4 1.1 collective-permute-start.14
  38.1 25.6 %collective-permute-start.15 = (bf16[256,2048]{1,0:T(8,128)(2,1)}, bf16[256,2048]{1,0:T(8,128)(2,1)}, u32[]{:S(2)}, u32[]{:S(2)}) collective-permute-start(bf16[256,2048]{1,0:T(8,128)(2,1)} %fence.16), channel_id=1, source_target_pairs={{0,2},{1,3},{2,0},{3,1},{4,6},{5,7},{6,4},{7,5},{8,10},{9,11},{10,... | collective-permute-start | bytes 3145736 | tf_op jit(solution)/shard_map/ppermute | solution.py:42
  54.3 10.4 %copy-start.25 = (f32[2,1024]{1,0:T(2,128)S(1)}, f32[2,1024]{1,0:T(2,128)}, u32[]{:S(2)}) copy-start(f32[2,1024]{1,0:T(2,128)} %get-tuple-element.92) | copy-start | bytes 24580
  54.3 10.4 %collective-permute-start.10 = (f32[2,1024]{1,0:T(2,128)}, f32[2,1024]{1,0:T(2,128)S(1)}, u32[]{:S(2)}, u32[]{:S(2)}) collective-permute-start(f32[2,1024]{1,0:T(2,128)} %get-tuple-element.92), channel_id=1, source_target_pairs={{0,1},{1,0},{2,3},{3,2},{4,5},{5,4},{6,7},{7,6},{8,9},{9,8},{10,11... | collective-permute-start | bytes 24584 | tf_op jit(solution)/shard_map/ppermute | solution.py:42
  63.7 5.4 %collective-permute-start.16 = (bf16[256,2048]{1,0:T(8,128)(2,1)}, bf16[256,2048]{1,0:T(8,128)(2,1)S(1)}, u32[]{:S(2)}, u32[]{:S(2)}) collective-permute-start(bf16[256,2048]{1,0:T(8,128)(2,1)} %collective-permute-done.15.refs_4_), channel_id=1, source_target_pairs={{0,1},{1,0},{2,3},{3,2},{4,5},{5,4},{6,7},{7,6},{8,9},{9,8},{10,11... | collective-permute-start | bytes 3145736 | tf_op jit(solution)/shard_map/ppermute | solution.py:42
  64.7 3.7 collective-permute-start.11
  82.5 6.2 %collective-permute-start.18 = (bf16[256,2176]{1,0:T(8,128)(2,1)}, bf16[256,2176]{1,0:T(8,128)(2,1)S(1)}, u32[]{:S(2)}, u32[]{:S(2)}) collective-permute-start(bf16[256,2176]{1,0:T(8,128)(2,1)} %get-tuple-element.98), channel_id=1, source_target_pairs={{0,1},{1,0},{2,3},{3,2},{4,5},{5,4},{6,7},{7,6},{8,9},{9,8},{10,11... | collective-permute-start | bytes 3342344 | tf_op jit(solution)/shard_map/ppermute | solution.py:42
  88.7 11.6 %collective-permute-start.17 = (bf16[256,2176]{1,0:T(8,128)(2,1)}, bf16[256,2176]{1,0:T(8,128)(2,1)}, u32[]{:S(2)}, u32[]{:S(2)}) collective-permute-start(bf16[256,2176]{1,0:T(8,128)(2,1)} %get-tuple-element.97), channel_id=1, source_target_pairs={{0,1},{1,0},{2,3},{3,2},{4,5},{5,4},{6,7},{7,6},{8,9},{9,8},{10,11... | collective-permute-start | bytes 3342344 | tf_op jit(solution)/shard_map/ppermute | solution.py:42
  89.7 9.9 %copy-start.28 = (bf16[2048]{0:T(1024)(128)(2,1)S(1)}, bf16[2048]{0:T(1024)(128)(2,1)}, u32[]{:S(2)}) copy-start(bf16[2048]{0:T(1024)(128)(2,1)} %param.37) | copy-start | bytes 12292
  96.7 27.3 %collective-permute-start.19 = (bf16[256,2176]{1,0:T(8,128)(2,1)}, bf16[256,2176]{1,0:T(8,128)(2,1)S(1)}, u32[]{:S(2)}, u32[]{:S(2)}) collective-permute-start(bf16[256,2176]{1,0:T(8,128)(2,1)} %get-tuple-element.100.refs_1_), channel_id=1, source_target_pairs={{0,2},{1,3},{2,0},{3,1},{4,6},{5,7},{6,4},{7,5},{8,10},{9,11},{10,... | collective-permute-start | bytes 3342344 | tf_op jit(solution)/shard_map/ppermute | solution.py:42
  98.8 33.1 %collective-permute-start.20 = (bf16[256,2048]{1,0:T(8,128)(2,1)}, bf16[256,2048]{1,0:T(8,128)(2,1)}, u32[]{:S(2)}, u32[]{:S(2)}) collective-permute-start(bf16[256,2048]{1,0:T(8,128)(2,1)} %up_ref.1), channel_id=1, source_target_pairs={{0,1},{1,0},{2,3},{3,2},{4,5},{5,4},{6,7},{7,6},{8,9},{9,8},{10,11... | collective-permute-start | bytes 3145736 | tf_op jit(solution)/shard_map/ppermute | solution.py:42
  129.7 27.3 %collective-permute-start.22 = (bf16[256,2176]{1,0:T(8,128)(2,1)}, bf16[256,2176]{1,0:T(8,128)(2,1)S(1)}, u32[]{:S(2)}, u32[]{:S(2)}) collective-permute-start(bf16[256,2176]{1,0:T(8,128)(2,1)} %get-tuple-element.103.refs_8_.refs_0_.refs_12_), channel_id=1, source_target_pairs={{0,2},{1,3},{2,0},{3,1},{4,6},{5,7},{6,4},{7,5},{8,10},{9,11},{10,... | collective-permute-start | bytes 3342344 | tf_op jit(solution)/shard_map/ppermute | solution.py:42
  131.9 26.7 %collective-permute-start.21 = (bf16[256,2176]{1,0:T(8,128)(2,1)}, bf16[256,2176]{1,0:T(8,128)(2,1)}, u32[]{:S(2)}, u32[]{:S(2)}) collective-permute-start(bf16[256,2176]{1,0:T(8,128)(2,1)} %get-tuple-element.103.refs_8_.refs_0_.refs_12_), channel_id=1, source_target_pairs={{0,1},{1,0},{2,3},{3,2},{4,5},{5,4},{6,7},{7,6},{8,9},{9,8},{10,11... | collective-permute-start | bytes 3342344 | tf_op jit(solution)/shard_map/ppermute | solution.py:42
  158.0 3.0 collective-permute-start.23
  269.9 4.3 collective-permute-start.25
  273.8 7.6 %collective-permute-start.24 = (bf16[256,2176]{1,0:T(8,128)(2,1)}, bf16[256,2176]{1,0:T(8,128)(2,1)S(1)}, u32[]{:S(2)}, u32[]{:S(2)}) collective-permute-start(bf16[256,2176]{1,0:T(8,128)(2,1)} %combine.4.refs_1_), channel_id=1, source_target_pairs={{0,1},{1,0},{2,3},{3,2},{4,5},{5,4},{6,7},{7,6},{8,9},{9,8},{10,11... | collective-permute-start | bytes 3342344 | tf_op jit(solution)/shard_map/ppermute | solution.py:42
  278.3 26.9 %collective-permute-start.28 = (bf16[256,2176]{1,0:T(8,128)(2,1)}, bf16[256,2176]{1,0:T(8,128)(2,1)}, u32[]{:S(2)}, u32[]{:S(2)}) collective-permute-start(bf16[256,2176]{1,0:T(8,128)(2,1)} %combine.5.refs_6_), channel_id=1, source_target_pairs={{0,2},{1,3},{2,0},{3,1},{4,6},{5,7},{6,4},{7,5},{8,10},{9,11},{10,... | collective-permute-start | bytes 3342344 | tf_op jit(solution)/shard_map/ppermute | solution.py:42
  280.1 59.3 %collective-permute-start.33 = (bf16[4,4,192,384]{3,2,1,0:T(8,128)(2,1)}, bf16[4,4,192,384]{3,2,1,0:T(8,128)(2,1)}, u32[]{:S(2)}, u32[]{:S(2)}) collective-permute-start(bf16[4,4,192,384]{3,2,1,0:T(8,128)(2,1)} %get-tuple-element.133), channel_id=1, source_target_pairs={{0,4},{4,0},{8,12},{12,8},{16,20},{20,16},{24,28},{28,24},{1,5},{5... | collective-permute-start | bytes 7077896 | tf_op jit(solution)/shard_map/ppermute | solution.py:42
  311.2 3.1 collective-permute-start.30
  311.2 27.2 %collective-permute-start.29 = (bf16[256,2176]{1,0:T(8,128)(2,1)}, bf16[256,2176]{1,0:T(8,128)(2,1)S(1)}, u32[]{:S(2)}, u32[]{:S(2)}) collective-permute-start(bf16[256,2176]{1,0:T(8,128)(2,1)} %get-tuple-element.118.refs_6_), channel_id=1, source_target_pairs={{0,2},{1,3},{2,0},{3,1},{4,6},{5,7},{6,4},{7,5},{8,10},{9,11},{10,... | collective-permute-start | bytes 3342344 | tf_op jit(solution)/shard_map/ppermute | solution.py:42
  313.0 36.8 %collective-permute-start.27 = (bf16[256,2048]{1,0:T(8,128)(2,1)}, bf16[256,2048]{1,0:T(8,128)(2,1)}, u32[]{:S(2)}, u32[]{:S(2)}) collective-permute-start(bf16[256,2048]{1,0:T(8,128)(2,1)} %get-tuple-element.114), channel_id=1, source_target_pairs={{0,1},{1,0},{2,3},{3,2},{4,5},{5,4},{6,7},{7,6},{8,9},{9,8},{10,11... | collective-permute-start | bytes 3145736 | tf_op jit(solution)/shard_map/ppermute | solution.py:42
  339.4 15.1 %collective-permute-start.32 = (bf16[256,2176]{1,0:T(8,128)(2,1)}, bf16[256,2176]{1,0:T(8,128)(2,1)}, u32[]{:S(2)}, u32[]{:S(2)}) collective-permute-start(bf16[256,2176]{1,0:T(8,128)(2,1)} %fence.18.refs_1_.refs_6_), channel_id=1, source_target_pairs={{0,1},{1,0},{2,3},{3,2},{4,5},{5,4},{6,7},{7,6},{8,9},{9,8},{10,11... | collective-permute-start | bytes 3342344 | tf_op jit(solution)/shard_map/ppermute | solution.py:42
  345.4 31.3 %collective-permute-start.34 = (bf16[4,384,384]{2,1,0:T(8,128)(2,1)}, bf16[4,384,384]{2,1,0:T(8,128)(2,1)S(1)}, u32[]{:S(2)}, u32[]{:S(2)}) collective-permute-start(bf16[4,384,384]{2,1,0:T(8,128)(2,1)} %get-tuple-element.140), channel_id=1, source_target_pairs={{0,8},{4,12},{8,16},{12,20},{16,24},{20,28},{1,9},{5,13},{9,17},{1... | collective-permute-start | bytes 3538952 | tf_op jit(solution)/shard_map/ppermute | solution.py:130
  348.5 30.3 %collective-permute-start.35 = (bf16[4,384,384]{2,1,0:T(8,128)(2,1)}, bf16[4,384,384]{2,1,0:T(8,128)(2,1)}, u32[]{:S(2)}, u32[]{:S(2)}) collective-permute-start(bf16[4,384,384]{2,1,0:T(8,128)(2,1)} %get-tuple-element.141), channel_id=1, source_target_pairs={{8,0},{12,4},{16,8},{20,12},{24,16},{28,20},{9,1},{13,5},{17,9},{2... | collective-permute-start | bytes 3538952 | tf_op jit(solution)/shard_map/ppermute | solution.py:130
  352.7 36.3 %collective-permute-start.31 = (bf16[256,2048]{1,0:T(8,128)(2,1)}, bf16[256,2048]{1,0:T(8,128)(2,1)}, u32[]{:S(2)}, u32[]{:S(2)}) collective-permute-start(bf16[256,2048]{1,0:T(8,128)(2,1)} %fence.19), channel_id=1, source_target_pairs={{0,2},{1,3},{2,0},{3,1},{4,6},{5,7},{6,4},{7,5},{8,10},{9,11},{10,... | collective-permute-start | bytes 3145736 | tf_op jit(solution)/shard_map/ppermute | solution.py:42
  354.5 62.0 %collective-permute-start.26 = (bf16[256,2048]{1,0:T(8,128)(2,1)}, bf16[256,2048]{1,0:T(8,128)(2,1)}, u32[]{:S(2)}, u32[]{:S(2)}) collective-permute-start(bf16[256,2048]{1,0:T(8,128)(2,1)} %get-tuple-element.112), channel_id=1, source_target_pairs={{0,1},{1,0},{2,3},{3,2},{4,5},{5,4},{6,7},{7,6},{8,9},{9,8},{10,11... | collective-permute-start | bytes 3145736 | tf_op jit(solution)/shard_map/ppermute | solution.py:42
  354.5 20.8 %copy-start.27 = (f32[1,512]{1,0:T(1,128)S(1)}, f32[1,512]{1,0:T(1,128)}, u32[]{:S(2)}) copy-start(f32[1,512]{1,0:T(1,128)} %get-tuple-element.122.refs_1_.refs_0_) | copy-start | bytes 6148
  382.1 31.2 %collective-permute-start.39 = (bf16[4,384,384]{2,1,0:T(8,128)(2,1)}, bf16[4,384,384]{2,1,0:T(8,128)(2,1)S(1)}, u32[]{:S(2)}, u32[]{:S(2)}) collective-permute-start(bf16[4,384,384]{2,1,0:T(8,128)(2,1)} %add_convert_fusion.2.refs_17_.refs_18_), channel_id=1, source_target_pairs={{8,0},{12,4},{16,8},{20,12},{24,16},{28,20},{9,1},{13,5},{17,9},{2... | collective-permute-start | bytes 3538952 | tf_op jit(solution)/shard_map/ppermute | solution.py:130
  383.5 30.2 %collective-permute-start.38 = (bf16[4,384,384]{2,1,0:T(8,128)(2,1)}, bf16[4,384,384]{2,1,0:T(8,128)(2,1)}, u32[]{:S(2)}, u32[]{:S(2)}) collective-permute-start(bf16[4,384,384]{2,1,0:T(8,128)(2,1)} %add_convert_fusion.2.refs_17_.refs_18_), channel_id=1, source_target_pairs={{0,8},{4,12},{8,16},{12,20},{16,24},{20,28},{1,9},{5,13},{9,17},{1... | collective-permute-start | bytes 3538952 | tf_op jit(solution)/shard_map/ppermute | solution.py:130
  389.1 1.4 collective-permute-start.36
  391.2 3.7 collective-permute-start.37
  416.5 9.8 %collective-permute-start.44 = (bf16[400,512]{1,0:T(8,128)(2,1)}, bf16[400,512]{1,0:T(8,128)(2,1)}, u32[]{:S(2)}, u32[]{:S(2)}) collective-permute-start(bf16[400,512]{1,0:T(8,128)(2,1)} %get-tuple-element.195), channel_id=1, source_target_pairs={{0,1},{1,0},{2,3},{3,2},{4,5},{5,4},{6,7},{7,6},{8,9},{9,8},{10,11... | collective-permute-start | bytes 1228808 | tf_op jit(solution)/shard_map/ppermute | solution.py:42
  420.5 9.4 %copy-start.12 = (bf16[4,384,384]{2,1,0:T(8,128)(2,1)S(1)}, bf16[4,384,384]{2,1,0:T(8,128)(2,1)}, u32[]{:S(2)}) copy-start(bf16[4,384,384]{2,1,0:T(8,128)(2,1)} %get-tuple-element.141) | copy-start | bytes 3538948
  420.5 21.6 %collective-permute-start.40 = (bf16[256,2048]{1,0:T(8,128)(2,1)}, bf16[256,2048]{1,0:T(8,128)(2,1)}, u32[]{:S(2)}, u32[]{:S(2)}) collective-permute-start(bf16[256,2048]{1,0:T(8,128)(2,1)} %fence.22), channel_id=1, source_target_pairs={{0,1},{1,0},{2,3},{3,2},{4,5},{5,4},{6,7},{7,6},{8,9},{9,8},{10,11... | collective-permute-start | bytes 3145736 | tf_op jit(solution)/shard_map/ppermute | solution.py:42
  424.4 33.2 %collective-permute-start.47 = (bf16[4,384,384]{2,1,0:T(8,128)(2,1)}, bf16[4,384,384]{2,1,0:T(8,128)(2,1)}, u32[]{:S(2)}, u32[]{:S(2)}) collective-permute-start(bf16[4,384,384]{2,1,0:T(8,128)(2,1)} %add_convert_fusion), channel_id=1, source_target_pairs={{8,0},{12,4},{16,8},{20,12},{24,16},{28,20},{9,1},{13,5},{17,9},{2... | collective-permute-start | bytes 3538952 | tf_op jit(solution)/shard_map/ppermute | solution.py:130
  425.7 14.4 %collective-permute-start.43 = (bf16[400,512]{1,0:T(8,128)(2,1)}, bf16[400,512]{1,0:T(8,128)(2,1)}, u32[]{:S(2)}, u32[]{:S(2)}) collective-permute-start(bf16[400,512]{1,0:T(8,128)(2,1)} %get-tuple-element.194), channel_id=1, source_target_pairs={{0,1},{1,0},{2,3},{3,2},{4,5},{5,4},{6,7},{7,6},{8,9},{9,8},{10,11... | collective-permute-start | bytes 1228808 | tf_op jit(solution)/shard_map/ppermute | solution.py:42
  428.1 12.0 %collective-permute-start.45 = (bf16[400,512]{1,0:T(8,128)(2,1)}, bf16[400,512]{1,0:T(8,128)(2,1)}, u32[]{:S(2)}, u32[]{:S(2)}) collective-permute-start(bf16[400,512]{1,0:T(8,128)(2,1)} %fusion), channel_id=1, source_target_pairs={{0,2},{1,3},{2,0},{3,1},{4,6},{5,7},{6,4},{7,5},{8,10},{9,11},{10,... | collective-permute-start | bytes 1228808 | tf_op jit(solution)/shard_map/ppermute | solution.py:42
  432.5 30.0 %collective-permute-start.46 = (bf16[4,384,384]{2,1,0:T(8,128)(2,1)}, bf16[4,384,384]{2,1,0:T(8,128)(2,1)}, u32[]{:S(2)}, u32[]{:S(2)}) collective-permute-start(bf16[4,384,384]{2,1,0:T(8,128)(2,1)} %add_convert_fusion.1), channel_id=1, source_target_pairs={{0,8},{4,12},{8,16},{12,20},{16,24},{20,28},{1,9},{5,13},{9,17},{1... | collective-permute-start | bytes 3538952 | tf_op jit(solution)/shard_map/ppermute | solution.py:130
  443.7 34.3 %collective-permute-start.42 = (bf16[256,2048]{1,0:T(8,128)(2,1)S(1)}, bf16[256,2048]{1,0:T(8,128)(2,1)}, u32[]{:S(2)}, u32[]{:S(2)}) collective-permute-start(bf16[256,2048]{1,0:T(8,128)(2,1)S(1)} %add_convert_fusion.3.refs_0_.refs_1_), channel_id=1, source_target_pairs={{0,2},{1,3},{2,0},{3,1},{4,6},{5,7},{6,4},{7,5},{8,10},{9,11},{10,... | collective-permute-start | bytes 3145736 | tf_op jit(solution)/shard_map/ppermute | solution.py:42
  448.1 17.0 %collective-permute-start.48 = (bf16[4,6,16,512]{3,2,1,0:T(8,128)(2,1)}, bf16[4,6,16,512]{3,2,1,0:T(8,128)(2,1)}, u32[]{:S(2)}, u32[]{:S(2)}) collective-permute-start(bf16[4,6,16,512]{3,2,1,0:T(8,128)(2,1)} %pad_maximum_fusion.3), channel_id=1, source_target_pairs={{0,4},{4,0},{8,12},{12,8},{16,20},{20,16},{24,28},{28,24},{1,5},{5... | collective-permute-start | bytes 1179656 | tf_op jit(solution)/shard_map/ppermute | solution.py:154
  457.5 7.6 %copy-start.18 = (bf16[1,6,16,512]{3,2,1,0:T(8,128)(2,1)S(1)}, bf16[1,6,16,512]{3,2,1,0:T(8,128)(2,1)}, u32[]{:S(2)}) copy-start(bf16[1,6,16,512]{3,2,1,0:T(8,128)(2,1)} %get-tuple-element.201) | copy-start | bytes 294916
  457.5 7.6 %copy-start.19 = (bf16[1,6,16,512]{3,2,1,0:T(8,128)(2,1)S(1)}, bf16[1,6,16,512]{3,2,1,0:T(8,128)(2,1)}, u32[]{:S(2)}) copy-start(bf16[1,6,16,512]{3,2,1,0:T(8,128)(2,1)} %get-tuple-element.202) | copy-start | bytes 294916
  457.5 7.6 %copy-start.20 = (bf16[1,6,16,512]{3,2,1,0:T(8,128)(2,1)S(1)}, bf16[1,6,16,512]{3,2,1,0:T(8,128)(2,1)}, u32[]{:S(2)}) copy-start(bf16[1,6,16,512]{3,2,1,0:T(8,128)(2,1)} %get-tuple-element.203) | copy-start | bytes 294916
  457.5 39.8 %collective-permute-start.41 = (bf16[256,2048]{1,0:T(8,128)(2,1)}, bf16[256,2048]{1,0:T(8,128)(2,1)}, u32[]{:S(2)}, u32[]{:S(2)}) collective-permute-start(bf16[256,2048]{1,0:T(8,128)(2,1)} %get-tuple-element.151), channel_id=1, source_target_pairs={{0,1},{1,0},{2,3},{3,2},{4,5},{5,4},{6,7},{7,6},{8,9},{9,8},{10,11... | collective-permute-start | bytes 3145736 | tf_op jit(solution)/shard_map/ppermute | solution.py:42
  466.9 11.2 %collective-permute-start.49 = (bf16[6,16,512]{2,1,0:T(8,128)(2,1)}, bf16[6,16,512]{2,1,0:T(8,128)(2,1)}, u32[]{:S(2)}, u32[]{:S(2)}) collective-permute-start(bf16[6,16,512]{2,1,0:T(8,128)(2,1)} %get-tuple-element.215), channel_id=1, source_target_pairs={{0,8},{4,12},{8,16},{12,20},{16,24},{20,28},{24,0},{28,4},{1,9},{5... | collective-permute-start | bytes 294920 | tf_op jit(solution)/shard_map/ppermute | solution.py:154
  469.4 9.1 %collective-permute-start.50 = (bf16[6,16,512]{2,1,0:T(8,128)(2,1)}, bf16[6,16,512]{2,1,0:T(8,128)(2,1)}, u32[]{:S(2)}, u32[]{:S(2)}) collective-permute-start(bf16[6,16,512]{2,1,0:T(8,128)(2,1)} %get-tuple-element.214), channel_id=1, source_target_pairs={{0,16},{4,20},{8,24},{12,28},{16,0},{20,4},{24,8},{28,12},{1,17},{... | collective-permute-start | bytes 294920 | tf_op jit(solution)/shard_map/ppermute | solution.py:154
  472.2 6.5 %collective-permute-start.51 = (bf16[6,16,512]{2,1,0:T(8,128)(2,1)S(1)}, bf16[6,16,512]{2,1,0:T(8,128)(2,1)}, u32[]{:S(2)}, u32[]{:S(2)}) collective-permute-start(bf16[6,16,512]{2,1,0:T(8,128)(2,1)S(1)} %get-tuple-element.213), channel_id=1, source_target_pairs={{0,24},{4,28},{8,0},{12,4},{16,8},{20,12},{24,16},{28,20},{1,25},{... | collective-permute-start | bytes 294920 | tf_op jit(solution)/shard_map/ppermute | solution.py:154
  482.3 13.7 %copy-start.11 = (f32[6,16,512]{2,1,0:T(8,128)S(1)}, f32[6,16,512]{2,1,0:T(8,128)}, u32[]{:S(2)}) copy-start(f32[6,16,512]{2,1,0:T(8,128)} %convert_add_fusion.2.refs_4_) | copy-start | bytes 589828
  482.4 7.4 %collective-permute-start.52 = (bf16[4,50,512]{2,1,0:T(8,128)(2,1)S(1)}, bf16[4,50,512]{2,1,0:T(8,128)(2,1)}, u32[]{:S(2)}, u32[]{:S(2)}) collective-permute-start(bf16[4,50,512]{2,1,0:T(8,128)(2,1)S(1)} %pad_maximum_fusion.4), channel_id=1, source_target_pairs={{0,4},{4,0},{8,12},{12,8},{16,20},{20,16},{24,28},{28,24},{1,5},{5... | collective-permute-start | bytes 614408 | tf_op jit(solution)/shard_map/ppermute | solution.py:154
  490.8 11.9 %collective-permute-start.53 = (bf16[50,512]{1,0:T(8,128)(2,1)S(1)}, bf16[50,512]{1,0:T(8,128)(2,1)S(1)}, u32[]{:S(2)}, u32[]{:S(2)}) collective-permute-start(bf16[50,512]{1,0:T(8,128)(2,1)S(1)} %get-tuple-element.216), channel_id=1, source_target_pairs={{0,8},{4,12},{8,16},{12,20},{16,24},{20,28},{24,0},{28,4},{1,9},{5... | collective-permute-start | bytes 153608 | tf_op jit(solution)/shard_map/ppermute | solution.py:154
  493.5 9.2 %collective-permute-start.54 = (bf16[50,512]{1,0:T(8,128)(2,1)S(1)}, bf16[50,512]{1,0:T(8,128)(2,1)S(1)}, u32[]{:S(2)}, u32[]{:S(2)}) collective-permute-start(bf16[50,512]{1,0:T(8,128)(2,1)S(1)} %get-tuple-element.218), channel_id=1, source_target_pairs={{0,16},{4,20},{8,24},{12,28},{16,0},{20,4},{24,8},{28,12},{1,17},{... | collective-permute-start | bytes 153608 | tf_op jit(solution)/shard_map/ppermute | solution.py:154
  493.8 8.9 %collective-permute-start.55 = (bf16[50,512]{1,0:T(8,128)(2,1)S(1)}, bf16[50,512]{1,0:T(8,128)(2,1)S(1)}, u32[]{:S(2)}, u32[]{:S(2)}) collective-permute-start(bf16[50,512]{1,0:T(8,128)(2,1)S(1)} %get-tuple-element.217), channel_id=1, source_target_pairs={{0,24},{4,28},{8,0},{12,4},{16,8},{20,12},{24,16},{28,20},{1,25},{... | collective-permute-start | bytes 153608 | tf_op jit(solution)/shard_map/ppermute | solution.py:154
  (21 other events, 50.4 us)

commit v3 on v2

--- a/solution.py
+++ b/solution.py
@@ -291,7 +291,7 @@
         v_ref[...] = value.astype(bf16)
 
 
-def project(docs, half, scal, x_parts, gain, weight, enter, leave, kept):
+def project(docs, half, scal, x_parts, gain, weight, enter, leave, kept, *deps):
     parts = len(x_parts)
     local, width = x_parts[0].shape
     slice_width = weight.shape[2]
@@ -318,7 +318,7 @@
             full(),
             pl.BlockSpec((1, rank, slice_width), lambda i: (i, 0, 0)),
         ]
-        + [full(pl.ANY)] * len(extra),
+        + [full(pl.ANY)] * (len(extra) + len(deps)),
         out_specs=(
             pl.BlockSpec((rows, width), lambda i: (half, 0)),
             pl.BlockSpec((3, rows, rank), lambda i: (0, half, 0)),
@@ -330,7 +330,7 @@
         compiler_params=params(),
         cost_estimate=cost(2 * rows * width * (3 * slice_width + 3 * rank), 14_000_000),
         name="project",
-    )(scal, *x_parts, gain, weight, enter, leave, *extra)
+    )(scal, *x_parts, gain, weight, enter, leave, *extra, *deps)
 
 
 def prepare_kernel(width, p_ref, square_ref, gains_ref, cos_ref, sin_ref, q_ref, k_ref):
@@ -457,24 +457,24 @@
     return low, expo / jnp.sum(expo, axis=0, keepdims=True)
 
 
-def middle(docs, scal, x, outs, leave, gain, route, route_enter, route_leave):
+def middle(docs, scal, x, outs, leave, gain, route, route_enter, route_leave, *deps):
     local, width = x.shape
     rank = leave.shape[0]
     f32, bf16 = (jnp.float32, jnp.bfloat16)
     return pl.pallas_call(
-        functools.partial(middle_kernel, docs),
+        lambda *refs: middle_kernel(docs, *refs[:9], *refs[9 + len(deps) :]),
         out_shape=(
             jax.ShapeDtypeStruct((local, width), f32),
             jax.ShapeDtypeStruct((local, width + rank), bf16),
             jax.ShapeDtypeStruct((local, rank), bf16),
             jax.ShapeDtypeStruct((route.shape[0], local), f32),
         ),
-        in_specs=[full(SMEM)] + [full()] * 8,
+        in_specs=[full(SMEM)] + [full()] * 8 + [full(pl.ANY)] * len(deps),
         out_specs=(full(),) * 4,
         compiler_params=params(),
         cost_estimate=cost(4 * local * width * rank, 8_000_000),
         name="middle",
-    )(scal, x, *outs, leave, gain, route, route_enter, route_leave)
+    )(scal, x, *outs, leave, gain, route, route_enter, route_leave, *deps)
 
 
 def middle_back_kernel(
@@ -845,8 +845,98 @@
     return [jnp.concatenate(parts[b::blocks]) if len(parts) > blocks else parts[b] for b in range(blocks)]
 
 
-def expert_kernel(line, docs, scal_ref, rank_ref, grads_ref, back_ref, low_ref, route_ref, route_enter, route_leave, *refs):
+def dispatch(docs, scal_ref, place, rank_rows, weight_rows, normed_refs, rows_in, marks):
+    local, low = (rank_rows[0].shape[1], marks.shape[1])
+    cap = rows_in.shape[0] // len(rank_rows)
+    slots = lax.broadcasted_iota(jnp.int32, (cap, local), 0).astype(jnp.float32)
+    weights = []
+    for b, rank_row in enumerate(rank_rows):
+        hit = rank_row == slots
+        pick = hit.astype(jnp.bfloat16)
+        weights.append(jnp.sum(jnp.where(hit, weight_rows[b], 0.0), axis=1, keepdims=True))
+        here = slice(b * cap, (b + 1) * cap)
+        mark = block_marks(scal_ref, docs, scal_ref[0] ^ (place + b), local).astype(jnp.bfloat16)
+        rows_in[here, :] = dot_nn(pick, normed_refs[b][:, : rows_in.shape[1]]).astype(jnp.bfloat16)
+        marks[here, :] = dot_nn(pick, mark)
+    return jnp.concatenate(weights, axis=0)
+
+
+def inner_rows(
+    first, rows_in, mark, weight, low_in, back_in, gate_w, up_w, gate_enter, gate_leave, up_enter, up_leave, down_enter, hidden, grad_gate, grad_up
+):
+    f32, bf16 = (jnp.float32, jnp.bfloat16)
+    rank, ff = (mark.shape[1], hidden.shape[1])
+    rows = rows_in[first:]
+    low = dot_nn(rows, jnp.concatenate([gate_enter[0], up_enter[0]], axis=1))
+    low_gate = (low[:, :rank] * mark).astype(bf16) * SCALE
+    low_up = (low[:, rank:] * mark).astype(bf16) * SCALE
+    grad_low_down = (low_in[...] * (SCALE * weight) * mark).astype(bf16)
+    step = min(256, ff)
+    for at in range(0, ff, step):
+        cut = slice(at, at + step)
+        gate = dot_nn(rows, gate_w[0, :, cut]) + dot_nn(low_gate, gate_leave[0, :, cut])
+        up = dot_nn(rows, up_w[0, :, cut]) + dot_nn(low_up, up_leave[0, :, cut])
+        back = back_in[:, cut].astype(f32) * weight + dot_nt(grad_low_down, down_enter[0, cut, :])
+        sigma = 1.0 / (1.0 + jnp.exp(-gate))
+        silu = gate * sigma
+        hidden[first:, cut] = (silu * up).astype(bf16)
+        grad_gate[first:, cut] = (back * up * sigma * (1.0 + gate * (1.0 - sigma))).astype(bf16)
+        grad_up[first:, cut] = (back * silu).astype(bf16)
+    return low_gate, low_up, grad_low_down
+
+
+def near_kernel(docs, scal_ref, rank_ref, back_ref, low_ref, route_ref, route_enter, route_leave, *refs):
+    count = len(refs) - 14
+    normed_refs, refs = (refs[:count], refs[count:])
+    weights, (hidden, grad_gate, grad_up, lows, rows_in, marks, probs) = (refs[:7], refs[7:])
+    width = rows_in.shape[1]
+    local = rank_ref.shape[3]
+
+    @pl.when(pl.program_id(0) == 0)
+    def _():
+        for b in range(count):
+            mark = block_marks(scal_ref, docs, scal_ref[0] ^ b, local)
+            probs[b] = router(normed_refs[b][:, :width], mark, route_ref, route_enter, route_leave)[1]
+
+    mine = pl.ds(scal_ref[0] * pl.num_programs(0) + pl.program_id(0), 1)
+    rank_rows, weight_rows = ([rank_ref[0, b] for b in range(count)], [probs[b, mine] for b in range(count)])
+    weight = dispatch(docs, scal_ref, 0, rank_rows, weight_rows, normed_refs, rows_in, marks)
+    made = inner_rows(
+        0, rows_in, marks[...], weight, low_ref.at[0], back_ref.at[0], *weights, hidden.at[0], grad_gate.at[0], grad_up.at[0]
+    )
+    lows[0] = jnp.concatenate(made, axis=1)
+
+
+def run_near(docs, scal, ranks, back, low_back, route, route_enter, route_leave, normed, *weights):
+    experts, members, _, local = ranks.shape
+    ff, low = (back.shape[2], low_back.shape[2])
+    width = normed[0].shape[1] - low
+    rows = len(normed) * CAP
+    bf16 = jnp.bfloat16
+    near = lambda wide: pl.BlockSpec((1, rows, wide), lambda e: (e, 0, 0))
+    hidden = jax.ShapeDtypeStruct((experts, rows, ff), bf16)
+    return pl.pallas_call(
+        functools.partial(near_kernel, docs),
+        grid=(experts,),
+        out_shape=(hidden, hidden, hidden, jax.ShapeDtypeStruct((experts, rows, 3 * low), bf16)),
+        in_specs=[full(SMEM), pl.BlockSpec((1, members, 1, local), lambda e: (e, 0, 0, 0)), near(ff), near(low)]
+        + [full()] * (3 + len(normed))
+        + [pl.BlockSpec((1,) + value.shape[1:], lambda e: (e, 0, 0)) for value in weights],
+        out_specs=(near(ff), near(ff), near(ff), near(3 * low)),
+        scratch_shapes=[
+            pltpu.VMEM((rows, width), bf16),
+            pltpu.VMEM((rows, low), jnp.float32),
+            pltpu.VMEM((len(normed), EXPERTS, local), jnp.float32),
+        ],
+        compiler_params=params(),
+        cost_estimate=cost(4 * experts * rows * width * ff, 40_000_000),
+        name="near",
+    )(scal, ranks, back, low_back, route, route_enter, route_leave, *normed, *weights)
+
+
+def expert_kernel(line, docs, made, scal_ref, rank_ref, grads_ref, back_ref, low_ref, route_ref, route_enter, route_leave, *refs):
     blocks = rank_ref.shape[1]
+    ahead, refs = (refs[:made], refs[made:])
     normed_refs, refs, probs = (refs[:blocks], refs[blocks:-1], refs[-1])
     width = grads_ref.shape[2]
     turn = pl.program_id(1)
@@ -860,12 +950,13 @@
 
     mine = pl.ds(scal_ref[0] * pl.num_programs(0) + pl.program_id(0), 1)
     weights = [probs[b, mine] for b in range(blocks)]
-    expert_rows(line, docs, scal_ref, rank_ref, weights, normed_refs, grads_ref.at[0], back_ref.at[0], low_ref.at[0], *refs)
+    expert_rows(line, docs, ahead, scal_ref, rank_ref, weights, normed_refs, grads_ref.at[0], back_ref.at[0], low_ref.at[0], *refs)
 
 
 def expert_rows(
     line,
     docs,
+    ahead,
     scal_ref,
     rank_ref,
     weight_rows,
@@ -897,33 +988,20 @@
     count = blocks * cap
     ff = hidden.shape[1]
     slots = lax.broadcasted_iota(jnp.int32, (cap, local), 0).astype(f32)
-    weights = []
-    for b in range(blocks):
-        hit = rank_ref[0, b] == slots
-        pick = hit.astype(bf16)
-        weights.append(jnp.sum(jnp.where(hit, weight_rows[b], 0.0), axis=1, keepdims=True))
-        here = slice(b * cap, (b + 1) * cap)
-        mark = block_marks(scal_ref, docs, scal_ref[0] ^ (turn * blocks + b), local).astype(bf16)
-        rows_in[here, :] = dot_nn(pick, normed_refs[b][:, :width]).astype(bf16)
-        marks[here, :] = dot_nn(pick, mark)
-    weight = jnp.concatenate(weights, axis=0)
+    rank_rows = [rank_ref[0, b] for b in range(blocks)]
+    weight = dispatch(docs, scal_ref, turn * blocks, rank_rows, weight_rows, normed_refs, rows_in, marks)
     mark = marks[...]
     rank = mark.shape[1]
-    low = dot_nn(rows_in[...], jnp.concatenate([gate_enter[0], up_enter[0]], axis=1))
-    low_gate = (low[:, :rank] * mark).astype(bf16) * SCALE
-    low_up = (low[:, rank:] * mark).astype(bf16) * SCALE
-    grad_low_down = (low_in[...] * (SCALE * weight) * mark).astype(bf16)
-    step = min(256, ff)
-    for at in range(0, ff, step):
-        cut = slice(at, at + step)
-        gate = dot_nn(rows_in[...], gate_w[0, :, cut]) + dot_nn(low_gate, gate_leave[0, :, cut])
-        up = dot_nn(rows_in[...], up_w[0, :, cut]) + dot_nn(low_up, up_leave[0, :, cut])
-        back = back_in[:, cut].astype(f32) * weight + dot_nt(grad_low_down, down_enter[0, cut, :])
-        sigma = 1.0 / (1.0 + jnp.exp(-gate))
-        silu = gate * sigma
-        hidden[:, cut] = (silu * up).astype(bf16)
-        grad_gate[:, cut] = (back * up * sigma * (1.0 + gate * (1.0 - sigma))).astype(bf16)
-        grad_up[:, cut] = (back * silu).astype(bf16)
+    first = ahead[0].shape[1] if ahead else 0
+    lows = inner_rows(
+        first, rows_in, mark[first:], weight[first:], low_in, back_in, gate_w, up_w, gate_enter, gate_leave, up_enter, up_leave, down_enter,
+        hidden, grad_gate, grad_up
+    )
+    if ahead:
+        for to, of in zip((hidden, grad_gate, grad_up), ahead):
+            to[:first] = of[0]
+        lows = [jnp.concatenate([ahead[3][0, :, i * rank : (i + 1) * rank], value], axis=0) for i, value in enumerate(lows)]
+    low_gate, low_up, grad_low_down = lows
     low_down = (dot_nn(hidden[...], down_enter[0]) * mark).astype(bf16) * SCALE
     grad_low_gate = (dot_nt(grad_gate[...], gate_leave[0]) * SCALE * mark).astype(bf16)
     grad_low_up = (dot_nt(grad_up[...], up_leave[0]) * SCALE * mark).astype(bf16)
@@ -1006,7 +1084,7 @@
             copy.wait()
 
 
-def run_experts(docs, scal, ranks, grads, back, low_back, route, route_enter, route_leave, normed, place, inner, *weights):
+def run_experts(docs, scal, ranks, grads, back, low_back, route, route_enter, route_leave, ahead, normed, place, inner, *weights):
     experts, members, _, local = ranks.shape
     width = grads.shape[2]
     ff = back.shape[2]
@@ -1020,17 +1098,20 @@
     tile = min(512, width)
     by_turn = lambda e, r: (e, r, 0, 0)
     rows = lambda wide: pl.BlockSpec((1, count, wide), lambda e, r: (e, r, 0))
+    half = count // 2
+    back_rows = lambda wide: pl.BlockSpec((1, half, wide), lambda e, r: (e, 1, 0)) if ahead else rows(wide)
     once = lambda wide: [pl.BlockSpec((local, wide), lambda e, r: (r, 0), pipeline_mode=pl.Buffered(1))] * blocks
     per_expert = lambda value: pl.BlockSpec((1,) + value.shape[1:], lambda e, r: (e, 0, 0))
     packed = docs * RANK if inner == 2 else low
     sums = [jax.ShapeDtypeStruct((line, experts, 3 * (packed if q else low), (width + ff) // packs), bf16) for q in range(inner)]
     rows_out = jax.ShapeDtypeStruct((members, experts, CAP, width), bf16)
     return pl.pallas_call(
-        functools.partial(expert_kernel, line, docs),
+        functools.partial(expert_kernel, line, docs, len(ahead)),
         grid=(experts, turns),
         out_shape=(rows_out, rows_out, jax.ShapeDtypeStruct(ranks.shape, jnp.float32), *sums),
-        in_specs=[full(SMEM), pl.BlockSpec((1, blocks, 1, local), by_turn), rows(width), rows(ff), rows(low)]
+        in_specs=[full(SMEM), pl.BlockSpec((1, blocks, 1, local), by_turn), rows(width), back_rows(ff), back_rows(low)]
         + [full()] * 3
+        + [pl.BlockSpec((1,) + value.shape[1:], lambda e, r: (e, 0, 0)) for value in ahead]
         + once(width + low)
         + [per_expert(value) for value in weights]
         + [full(SMEM)],
@@ -1051,7 +1132,7 @@
         compiler_params=params(),
         cost_estimate=cost(2 * experts * members * CAP * (width * ff * 5 + 9 * low * (width + ff)), 60_000_000),
         name="experts",
-    )(scal, ranks, grads, back, low_back, route, route_enter, route_leave, *by_block(normed, blocks), *weights, place)
+    )(scal, ranks, grads, back, low_back, route, route_enter, route_leave, *ahead, *by_block(normed, blocks), *weights, place)
 
 
 def mix(rank_ref, rows_ref, pick_ref, step):
@@ -1222,9 +1303,14 @@
     gain_one, gain_two = (attention_gain[None], feed_gain[None])
     route, route_leave = (router_weight.T, router_leave.T)
     adapters = (gain_one, qkv_weight, qkv_enter, qkv_leave)
-    kept = project(docs, 0, scal, gather_near(tokens, "ep"), *adapters, None)
+    named_all = named.reshape(1, 1, local)
+    named_all = jnp.concatenate([named_all, swap(named_all, "ep", 1)])
+    kept = project(docs, 0, scal, gather_near(tokens, "ep"), *adapters, None, named_all)
     token_parts = gather_far(tokens, "ep", kept[4])
-    named_all = jnp.stack(gather_parts(named.reshape(1, local), "ep"))
+    bit = 2
+    while bit < members:
+        named_all = jnp.concatenate([named_all, swap(named_all, "ep", bit)])
+        bit *= 2
     kept = project(docs, 1, scal, token_parts, *adapters, kept)
     normed_all, low_all, projected, values, squares = kept
     late = fence(scal, values)
@@ -1248,23 +1334,30 @@
 
     top = members // 2
     outs = reduce_scatter(attend_place, "ep")
+    upstream_rows = run_upstream(scal, named_all, upstream_parts, down_weight, down_leave, heads[0][2])
     hidden_state, normed_two, low_router, probs = middle(
-        docs, scal, tokens, outs, out_leave, gain_two, route, router_enter, route_leave
+        docs, scal, tokens, outs, out_leave, gain_two, route, router_enter, route_leave, upstream_rows[0]
     )
 
-    upstream_rows = run_upstream(scal, named_all, upstream_parts, down_weight, down_leave, normed_two)
-    normed_two_parts = gather_near(normed_two, "ep") + gather_far(normed_two, "ep", upstream_rows[0])
+    ranks, _, *backs = upstream_rows
+    routers = (route, router_enter, route_leave)
+    normed_two_parts = gather_near(normed_two, "ep")
+    ahead = ()
+    if members <= 4:
+        ahead = run_near(
+            docs, scal, ranks, *backs, *routers, normed_two_parts, gate_weight, up_weight, gate_enter, gate_leave, up_enter, up_leave,
+            down_enter
+        )
+    normed_two_parts = normed_two_parts + gather_far(normed_two, "ep", *ahead[3:])
     inner = packs // LINE
     chunk_ids = jnp.arange(packs, dtype=jnp.int32)
     place = jnp.stack([(chunk_ids // inner - pack // inner) % LINE, (chunk_ids % inner - pack % inner) % inner])
-    ranks = upstream_rows[0]
     mixed_rows, grad_rows, scores, *expert_sums = run_experts(
         docs,
         scal,
         *upstream_rows,
-        route,
-        router_enter,
-        route_leave,
+        *routers,
+        ahead,
         normed_two_parts,
         place,
         inner,
@@ -1337,12 +1430,13 @@
     grad_input = finish(inputs, grad_hidden, tokens, gain_one)
     layer_out = (hidden_state + (mixed_near.astype(f32) + mixed_got.astype(f32))).astype(bf16)
 
-    got = line.send(3)
+    got = [fence(value, input_got) for value in line.send(3)]
     line.add(3, got)
     expert_sum = line.total[0]
     by_rows = lambda value: value.astype(bf16).reshape(-1, packs, value.shape[-2] // packs, slice_width).transpose(1, 0, 2, 3)
     joined = jnp.concatenate([by_rows(value) for value in (*low_grads, leave_sums)], axis=1)
     joined = sum_packs(by_place(fence(joined, input_far)), input_got)
+    enter_sums = fence(enter_sums, input_far)
     enter_sums = [pair(enter_sums[j], swap(enter_sums[j + 1], "ep", 1)) for j in range(0, members, 2)]
     enter_far = swap(scatter_even(enter_sums[top // 2 :], "ep"), "ep", top)
     enter_sum = fence(pair(scatter_even(enter_sums[: top // 2], "ep"), enter_far), input_got, *got, joined)

time: 514 us -> 505 us (0.982)
  Pallas kernels: 289 us -> 309 us
  waiting for transfers between devices: 63.5 us -> 48.6 us
  starting transfers between devices: 65.7 us -> 58.5 us
    pallas_call x2 -> x3, Pallas kernels: 109 us -> 128 us  [the longest x1 95.7 us: run_experts(): pl.pallas_call(functools.partial(expert_kernel, line, docs, len(ahead)),...]
    ppermute x42 -> x41, waiting for transfers between devices: 50.7 us -> 40.6 us  [swap(): return lax.ppermute(value, axis, [(i, i ^ bit) for i in range(count)])]
    ppermute x3, waiting for transfers between devices: 5.37 us -> 0.01 us  [send(): lax.ppermute(up, self.axis, self.up)]
    ppermute x42 -> x41, starting transfers between devices: 34.6 us -> 30.6 us  [swap(): return lax.ppermute(value, axis, [(i, i ^ bit) for i in range(count)])]
    unnamed x64 -> x60, local copies, waits for them, and re-layouts: 18.1 us -> 15.4 us
  transfers between devices with their start and end apart: 56 -> 55, of which waited for: 21 -> 17; matrix products, arithmetic and copies ran while one was open for 14% -> 13% of each run, Pallas kernels for 34% -> 39%
where the time goes in v3:
time: 505 us; the launch traced here: 495 us
  Pallas kernels  309 us (61%)
  starting transfers between devices  58.5 us (12%)
  waiting for transfers between devices  48.6 us (10%)
  other arithmetic  45.8 us (9%)
  local copies, waits for them, and re-layouts  31.1 us (6%)
    pallas_call x1, Pallas kernels, run_experts(): pl.pallas_call(functools.partial(expert_kernel, line, docs, len(ahead)),...  95.7 us
    ppermute x41, waiting for transfers between devices, swap(): return lax.ppermute(value, axis, [(i, i ^ bit) for i in range(count)])  40.6 us
    pallas_call x2, Pallas kernels, attend_back(): pl.pallas_call(functools.partial(attend_back_kernel, docs, half, local),...  35.9 us
    ppermute x41, starting transfers between devices, swap(): return lax.ppermute(value, axis, [(i, i ^ bit) for i in range(count)])  30.6 us
    pallas_call x1, Pallas kernels, run_near(): pl.pallas_call(functools.partial(near_kernel, docs), grid=(experts,), out...  27.5 us
    pallas_call x4, Pallas kernels, attend(): pl.pallas_call(functools.partial(attend_kernel, docs, place, local, adden...  26.9 us
    pallas_call x2, Pallas kernels, project(): pl.pallas_call(functools.partial(project_kernel, docs, half, parts), grid...  22.9 us
    pallas_call x1, Pallas kernels, run_upstream(): pl.pallas_call(lambda *refs: upstream_kernel(*refs[:4 + blocks], *refs[4...  21.3 us
  transfers between devices with their start and end apart: 55, of which 17 were waited for; matrix products, arithmetic and copies ran while one was open for 13% of the time, Pallas kernels for 39%

profile of v3, /device:TPU:0, one launch (start us, length us, event | category | flops | bytes accessed | tf_op | source)
XLA Modules:
  0.0 495.5 jit_solution(316960779630529922)
XLA Ops:
  1.2 2.6 collective-permute-start.7
  4.4 1.4 fusion.28
  5.8 2.6 collective-permute-start.3
  8.4 1.6 collective-permute-start.1
  10.0 1.5 collective-permute-start
  12.0 1.5 collective-permute-start.4
  13.6 1.5 collective-permute-start.2
  21.2 11.5 %project.2 = (bf16[1024,2048]{1,0:T(8,128)(2,1)}, bf16[3,1024,128]{2,1,0:T(8,128)(2,1)}, f32[2,1024,512]{2,1,0:T(8,128)}, bf16[1024,512]{1,0:T(8,128)(2,1)}, f32[2,1024]{1,0:T(2,128)}) custom-call(s32[13]{0:T(128)} %pad_add_fusion.5.scal_ref.refs_0_, bf16[256,2048]{1,0:T(8,128)(2,1)} %refs_4_.13, bf16[256,2048]{1,0:T(8,128)(2,1)} %collective-permute-done.8.refs_1_, ...), custom_call_target="tpu_custom_call" | custom-call | flops 503316480 | bytes 1750000 | tf_op jit(solution)/shard_map/project/pallas_call | solution.py:309
  35.5 2.0 collective-permute-done.13
  42.3 11.4 %project.3 = (bf16[1024,2048]{1,0:T(8,128)(2,1)}, bf16[3,1024,128]{2,1,0:T(8,128)(2,1)}, f32[2,1024,512]{2,1,0:T(8,128)}, bf16[1024,512]{1,0:T(8,128)(2,1)}, f32[2,1024]{1,0:T(2,128)}) custom-call(s32[13]{0:T(128)} %pad_add_fusion.5.scal_ref.refs_0_, ...), custom_call_target="tpu_custom_call", output_to_operand_aliasing={{0}: (7, {}), {1}: (8, {}), {2}: (9, {}), {3}: (10, {}), {4... | custom-call | flops 503316480 | bytes 1750000 | tf_op jit(solution)/shard_map/project/pallas_call | solution.py:309
  53.9 1.5 fusion.36
  55.4 4.5 subtract_convert_fusion
  60.0 1.9 fusion.2
  63.7 1.3 collective-permute-start.12
  66.0 1.4 collective-permute-done.12
  69.0 5.0 %prepare.1 = (bf16[1024,512]{1,0:T(8,128)(2,1)}, bf16[1024,512]{1,0:T(8,128)(2,1)}) custom-call(f32[2,1024,512]{2,1,0:T(8,128)} %get-tuple-element.95.refs_0_.refs_5_, f32[2,1024]{1,0:T(2,128)} %maximum_add_fusion.1.refs_1_.refs_6_, f32[2,512]{1,0:T(2,128)} %maximum_convert_fusion.refs_2_.refs_8_, f32[1024,128]{1,0:T(8,128)} %pad_maximum_fusion.1.refs_3_.refs_9_, ...), custom_call_target="tpu_custom_call" | custom-call | flops 1310720 | bytes 1048576 | tf_op jit(solution)/shard_map/prepare/pallas_call | solution.py:350
  74.0 7.5 %attend.4 = (bf16[256,512]{1,0:T(8,128)(2,1)}, bf16[256,2176]{1,0:T(8,128)(2,1)}, f32[8,256]{1,0:T(8,128)}) custom-call(s32[13]{0:T(128)} %pad_add_fusion.5.scal_ref.refs_0_, bf16[1024,512]{1,0:T(8,128)(2,1)} %get-tuple-element.98.q_ref.refs_0_, bf16[1024,512]{1,0:T(8,128)(2,1)} %get-tuple-element.99.k_ref.refs_1_, ...), custom_call_target="tpu_custom_call" | custom-call | flops 275000000 | bytes 500000 | tf_op jit(solution)/shard_map/attend/pallas_call | solution.py:420
  81.5 6.3 %attend.5 = (bf16[256,512]{1,0:T(8,128)(2,1)}, bf16[256,2176]{1,0:T(8,128)(2,1)}, f32[8,256]{1,0:T(8,128)}) custom-call(s32[13]{0:T(128)} %pad_add_fusion.5.scal_ref.refs_0_, bf16[1024,512]{1,0:T(8,128)(2,1)} %get-tuple-element.98.q_ref.refs_0_, bf16[1024,512]{1,0:T(8,128)(2,1)} %get-tuple-element.99.k_ref.refs_1_, ...), custom_call_target="tpu_custom_call" | custom-call | flops 275000000 | bytes 500000 | tf_op jit(solution)/shard_map/attend/pallas_call | solution.py:420
  88.3 7.0 %attend.6 = (bf16[256,512]{1,0:T(8,128)(2,1)}, bf16[256,2176]{1,0:T(8,128)(2,1)}, f32[8,256]{1,0:T(8,128)}) custom-call(s32[13]{0:T(128)} %pad_add_fusion.5.scal_ref.refs_0_, bf16[1024,512]{1,0:T(8,128)(2,1)} %get-tuple-element.98.q_ref.refs_0_, bf16[1024,512]{1,0:T(8,128)(2,1)} %get-tuple-element.99.k_ref.refs_1_, ...), custom_call_target="tpu_custom_call" | custom-call | flops 275000000 | bytes 500000 | tf_op jit(solution)/shard_map/attend/pallas_call | solution.py:420
  95.3 2.0 collective-permute-start.18
  97.9 6.2 %attend.7 = (bf16[256,512]{1,0:T(8,128)(2,1)}, bf16[256,2176]{1,0:T(8,128)(2,1)}, f32[8,256]{1,0:T(8,128)}) custom-call(s32[13]{0:T(128)} %pad_add_fusion.5.scal_ref.refs_0_, bf16[1024,512]{1,0:T(8,128)(2,1)} %get-tuple-element.98.q_ref.refs_0_, bf16[1024,512]{1,0:T(8,128)(2,1)} %get-tuple-element.99.k_ref.refs_1_, ...), custom_call_target="tpu_custom_call" | custom-call | flops 275000000 | bytes 500000 | tf_op jit(solution)/shard_map/attend/pallas_call | solution.py:420
  104.1 21.3 %upstream.1 = (f32[4,4,1,256]{3,2,1,0:T(1,128)}, bf16[4,576,2048]{2,1,0:T(8,128)(2,1)}, bf16[4,576,1024]{2,1,0:T(8,128)(2,1)}, f32[4,576,128]{2,1,0:T(8,128)}) custom-call(s32[13]{0:T(128)} %pad_add_fusion.5.scal_ref.refs_0_, s32[4,1,256]{2,1,0:T(1,128)} %pad_add_fusion.refs_2_.refs_6_.refs_1_, bf16[256,2048]{1,0:T(8,128)(2,1)} %up_ref.1, ...), custom_call_target="tpu_custom_call" | custom-call | flops 1207959552 | bytes 5000000 | tf_op jit(solution)/shard_map/upstream/pallas_call | solution.py:823
  125.4 4.6 middle.1
  132.4 1.5 collective-permute-done.20.refs_1_.refs_5_.refs_13_
  133.8 27.5 %near.1 = (bf16[4,288,1024]{2,1,0:T(8,128)(2,1)}, bf16[4,288,1024]{2,1,0:T(8,128)(2,1)}, bf16[4,288,1024]{2,1,0:T(8,128)(2,1)}, bf16[4,288,384]{2,1,0:T(8,128)(2,1)}) custom-call(s32[13]{0:T(128)} %pad_add_fusion.5.scal_ref.refs_0_, f32[4,4,1,256]{3,2,1,0:T(1,128)} %get-tuple-element.107.refs_9_.rank_ref.refs_1_, ...), custom_call_target="tpu_custom_call" | custom-call | flops 1207959552 | bytes 5000000 | tf_op jit(solution)/shard_map/near/pallas_call | solution.py:918
  163.4 2.0 collective-permute-done.22.refs_7_.refs_13_
  166.3 95.7 %experts.1 = (bf16[4,4,144,2048]{3,2,1,0:T(8,128)(2,1)}, bf16[4,4,144,2048]{3,2,1,0:T(8,128)(2,1)}, f32[4,4,1,256]{3,2,1,0:T(1,128)}, bf16[4,4,384,384]{3,2,1,0:T(8,128)(2,1)}, bf16[4,4,192,384]{3,2,1,0:T(8,128)(2,1)}) custom-call(s32[13]{0:T(128)} %pad_add_fusion.5.scal_ref.refs_0_, f32[4,4,1,256]{3,2,1,0:T(1,128)} %get-tuple-element.107.refs_9_.rank_ref.refs_1_, ...), custom_call_target="tpu_custom_call" | custom-call | flops 8078229504 | bytes 7500000 | tf_op jit(solution)/shard_map/experts/pallas_call | solution.py:1108
  262.1 3.8 combine.3.refs_0_
  266.3 3.8 combine.4.refs_1_
  270.2 4.1 combine.5.refs_6_
  277.9 13.5 %combine_last.1 = (bf16[256,2048]{1,0:T(8,128)(2,1)}, bf16[256,2048]{1,0:T(8,128)(2,1)}, bf16[256,2048]{1,0:T(8,128)(2,1)}, bf16[256,2048]{1,0:T(8,128)(2,1)}, bf16[256,2176]{1,0:T(8,128)(2,1)}) custom-call(s32[13]{0:T(128)} %pad_add_fusion.5.scal_ref.refs_0_, f32[4,4,1,256]{3,2,1,0:T(1,128)} %get-tuple-element.107.refs_9_.rank_ref.refs_1_, ...), custom_call_target="tpu_custom_call" | custom-call | flops 377487360 | bytes 1474560 | tf_op jit(solution)/shard_map/combine_last/pallas_call | solution.py:1231
  291.4 10.1 %collective-permute-done.27.gb_ref = bf16[256,2176]{1,0:T(8,128)(2,1)} collective-permute-done((bf16[256,2176]{1,0:T(8,128)(2,1)}, bf16[256,2176]{1,0:T(8,128)(2,1)}, u32[]{:S(2)}, u32[]{:S(2)}) %collective-permute-start.27) | collective-permute-done | bytes 1114144 | tf_op jit(solution)/shard_map/ppermute | solution.py:42
  301.5 6.0 %middle_back.1 = (f32[256,2048]{1,0:T(8,128)}, bf16[256,2176]{1,0:T(8,128)(2,1)}, f32[16,128]{1,0:T(8,128)}) custom-call(s32[13]{0:T(128)} %pad_add_fusion.5.scal_ref.refs_0_, bf16[256,2176]{1,0:T(8,128)(2,1)} %get-tuple-element.124.ga_ref, bf16[256,2176]{1,0:T(8,128)(2,1)} %collective-permute-done.27.gb_ref, f32[16,256]{1,0:T(8,128)} %get-tuple-element.125.probs_ref, ...), custom_call_target="tpu_custom_call" | custom-call | flops 33554432 | bytes 1250000 | tf_op jit(solution)/shard_map/middle_back/pallas_call | solution.py:508
  309.0 1.7 collective-permute-done.29.refs_7_
  310.6 15.1 %attend_back.2 = (f32[512,512]{1,0:T(8,128)}, f32[1024,512]{1,0:T(8,128)}, f32[1024,512]{1,0:T(8,128)}, f32[128,512]{1,0:T(8,128)}, f32[128,512]{1,0:T(8,128)}, /*index=5*/f32[128,512]{1,0:T(8,128)}, f32[1,512]{1,0:T(1,128)}) custom-call(s32[13]{0:T(128)} %pad_add_fusion.5.scal_ref.refs_0_, bf16[1024,512]{1,0:T(8,128)(2,1)} %get-tuple-element.98.q_ref.refs_0_, ...), custom_call_target="tpu_custom_call" | custom-call | flops 1000000000 | bytes 1750000 | tf_op jit(solution)/shard_map/attend_back/pallas_call | solution.py:625
  325.7 9.0 %collective-permute-done.28.refs_0_ = bf16[256,2176]{1,0:T(8,128)(2,1)S(1)} collective-permute-done((bf16[256,2176]{1,0:T(8,128)(2,1)}, bf16[256,2176]{1,0:T(8,128)(2,1)S(1)}, u32[]{:S(2)}, u32[]{:S(2)}) %collective-permute-start.28) | collective-permute-done | bytes 1114144 | tf_op jit(solution)/shard_map/ppermute | solution.py:42
  335.8 6.0 %widen.1 = (bf16[4,384,384]{2,1,0:T(8,128)(2,1)}, bf16[4,384,384]{2,1,0:T(8,128)(2,1)}, bf16[4,384,384]{2,1,0:T(8,128)(2,1)}, bf16[4,384,384]{2,1,0:T(8,128)(2,1)}) custom-call(s32[4]{0:T(128)} %get-tuple-element.230.sets_ref, bf16[4,4,384,384]{3,2,1,0:T(8,128)(2,1)} %get-tuple-element.140.kept_ref, ...), custom_call_target="tpu_custom_call" | custom-call | tf_op jit(solution)/shard_map/widen/pallas_call | solution.py:196
  341.7 3.1 collective-permute-start.33
  344.8 1.3 collective-permute-start.34
  346.1 2.9 add_convert_fusion.5.refs_0_
  350.3 20.8 %attend_back.3 = (f32[512,512]{1,0:T(8,128)}, f32[1024,512]{1,0:T(8,128)}, f32[1024,512]{1,0:T(8,128)}, f32[128,512]{1,0:T(8,128)}, f32[128,512]{1,0:T(8,128)}, ...) custom-call(s32[13]{0:T(128)} %pad_add_fusion.5.scal_ref.refs_0_, ...), custom_call_target="tpu_custom_call" | custom-call | flops 1000000000 | bytes 1750000 | tf_op jit(solution)/shard_map/attend_back/pallas_call | solution.py:625
  371.1 1.3 pad_maximum_fusion.5.refs_0_
  372.4 2.7 collective-permute-done.34.refs_2_
  375.1 3.2 add_convert_fusion.2.refs_17_.refs_18_
  378.4 1.4 collective-permute-start.38
  379.8 5.7 %collective-permute-start.37 = (bf16[4,384,384]{2,1,0:T(8,128)(2,1)}, bf16[4,384,384]{2,1,0:T(8,128)(2,1)}, u32[]{:S(2)}, u32[]{:S(2)}) collective-permute-start(bf16[4,384,384]{2,1,0:T(8,128)(2,1)} %add_convert_fusion.2.refs_17_.refs_18_), channel_id=1, source_target_pairs={{0,8},{4,12},{8,16},{12,20},{16,24},{20,28},{1,9},{5,13},{9,17},{1... | collective-permute-start | bytes 3538952 | tf_op jit(solution)/shard_map/ppermute | solution.py:130
  389.4 1.8 collective-permute-done.36
  391.8 17.7 %project_back.1 = (bf16[256,2048]{1,0:T(8,128)(2,1)}, bf16[256,2048]{1,0:T(8,128)(2,1)}, bf16[4,400,512]{2,1,0:T(8,128)(2,1)}, f32[3,128,512]{2,1,0:T(8,128)}, b...) custom-call(s32[13]{0:T(128)} %pad_add_fusion.5.scal_ref.refs_0_, f32[512,512]{1,0:T(8,128)} %get-tuple-element.131.refs_1_, ...), custom_call_target="tpu_custom_call" | custom-call | flops 603979776 | bytes 2500000 | tf_op jit(solution)/shard_map/project_back/pallas_call | solution.py:715
  412.1 2.7 add_convert_fusion
  416.1 2.7 add_convert_fusion.1
  418.8 5.6 %collective-permute-start.45 = (bf16[4,384,384]{2,1,0:T(8,128)(2,1)}, bf16[4,384,384]{2,1,0:T(8,128)(2,1)}, u32[]{:S(2)}, u32[]{:S(2)}) collective-permute-start(bf16[4,384,384]{2,1,0:T(8,128)(2,1)} %add_convert_fusion.1), channel_id=1, source_target_pairs={{0,8},{4,12},{8,16},{12,20},{16,24},{20,28},{1,9},{5,13},{9,17},{1... | collective-permute-start | bytes 3538952 | tf_op jit(solution)/shard_map/ppermute | solution.py:130
  427.7 1.4 add_convert_fusion.3.refs_0_.refs_1_
  430.3 2.0 constant_dynamic-slice_fusion.7
  435.4 3.7 add_convert_fusion.4
  439.1 8.3 %project_near.1 = (bf16[256,2048]{1,0:T(8,128)(2,1)}, bf16[256,2048]{1,0:T(8,128)(2,1)}) custom-call(bf16[3,1024,512]{2,1,0:T(8,128)(2,1)} %get-tuple-element.154.grads_ref, bf16[1024,384]{1,0:T(8,128)(2,1)} %get-tuple-element.155.low_ref, bf16[3,2048,512]{2,1,0:T(8,128)(2,1)} %w_ref.9, bf16[3,2048,128]{2,1,0:T(8,128)(2,1)} %enter_ref.9, ...), custom_call_target="tpu_custom_call" | custom-call | flops 402653184 | bytes 1250000 | tf_op jit(solution)/shard_map/project_near/pallas_call | solution.py:748
  452.1 1.9 collective-permute-start.49
  454.0 8.1 %collective-permute-done.44 = bf16[400,512]{1,0:T(8,128)(2,1)S(1)} collective-permute-done((bf16[400,512]{1,0:T(8,128)(2,1)S(1)}, bf16[400,512]{1,0:T(8,128)(2,1)S(1)}, u32[]{:S(2)}, u32[]{:S(2)}) %collective-permute-start.44) | collective-permute-done | bytes 409632 | tf_op jit(solution)/shard_map/ppermute | solution.py:42
  463.1 1.9 add_convert_fusion.7.refs_0_
  466.7 1.6 convert_add_fusion.2.refs_4_
  470.3 2.2 select_add_fusion
  475.3 4.6 collective-permute-done.51
  481.0 2.0 collective-permute-start.53
  483.0 1.5 collective-permute-start.54
  488.6 5.4 %finish.1 = bf16[256,2048]{1,0:T(8,128)(2,1)} custom-call(bf16[256,2048]{1,0:T(8,128)(2,1)} %get-tuple-element.158.refs_0_, bf16[256,2048]{1,0:T(8,128)(2,1)} %collective-permute-done.40.refs_1_, bf16[256,2048]{1,0:T(8,128)(2,1)} %copy-done.2, f32[256,2048]{1,0:T(8,128)} %get-tuple-element.160.refs_3_, bf16[256,2048]{1,0:T(8,128)(2,1)} %refs_4_.13, ...), custom_call_target="tpu_custom_call" | custom-call | flops 655360 | bytes 786432 | tf_op jit(solution)/shard_map/finish/pallas_call | solution.py:777
  (229 shorter events, 67.2 us)
Async XLA Ops:
  0.6 20.6 %collective-permute-start.8 = (bf16[256,2048]{1,0:T(8,128)(2,1)}, bf16[256,2048]{1,0:T(8,128)(2,1)}, u32[]{:S(2)}, u32[]{:S(2)}) collective-permute-start(bf16[256,2048]{1,0:T(8,128)(2,1)} %refs_4_.13), channel_id=1, source_target_pairs={{0,1},{1,0},{2,3},{3,2},{4,5},{5,4},{6,7},{7,6},{8,9},{9,8},{10,11... | collective-permute-start | bytes 3145736 | tf_op jit(solution)/shard_map/ppermute | solution.py:42
  1.2 31.6 %collective-permute-start.7 = (bf16[256,2048]{1,0:T(8,128)(2,1)}, bf16[256,2048]{1,0:T(8,128)(2,1)S(1)}, u32[]{:S(2)}, u32[]{:S(2)}) collective-permute-start(bf16[256,2048]{1,0:T(8,128)(2,1)} %refs_4_.13), channel_id=1, source_target_pairs={{0,2},{1,3},{2,0},{3,1},{4,6},{5,7},{6,4},{7,5},{8,10},{9,11},{10,... | collective-permute-start | bytes 3145736 | tf_op jit(solution)/shard_map/ppermute | solution.py:42
  5.8 5.7 %collective-permute-start.3 = (s32[384]{0:T(512)S(1)}, s32[384]{0:T(512)S(1)}, u32[]{:S(2)}, u32[]{:S(2)}) collective-permute-start(s32[384]{0:T(512)S(1)} %pad_add_fusion.1), channel_id=1, source_target_pairs={{0,16},{4,20},{8,24},{12,28},{16,0},{20,4},{24,8},{28,12},{1,17},{... | collective-permute-start | bytes 4616 | tf_op jit(solution)/shard_map/ppermute | solution.py:42
  8.4 3.6 collective-permute-start.1
  10.0 3.6 collective-permute-start
  11.5 3.6 collective-permute-start.5
  12.0 6.2 %collective-permute-start.4 = (s32[384]{0:T(512)S(1)}, s32[384]{0:T(512)S(1)}, u32[]{:S(2)}, u32[]{:S(2)}) collective-permute-start(s32[384]{0:T(512)S(1)} %collective-permute-done.3), channel_id=1, source_target_pairs={{0,4},{4,0},{8,12},{12,8},{16,20},{20,16},{24,28},{28,24},{1,5},{5... | collective-permute-start | bytes 4616 | tf_op jit(solution)/shard_map/ppermute | solution.py:42
  13.6 4.7 collective-permute-start.2
  15.1 3.6 collective-permute-start.6
  19.5 1.2 collective-permute-start.9
  33.7 7.6 %collective-permute-start.10 = (bf16[256,2048]{1,0:T(8,128)(2,1)}, bf16[256,2048]{1,0:T(8,128)(2,1)S(1)}, u32[]{:S(2)}, u32[]{:S(2)}) collective-permute-start(bf16[256,2048]{1,0:T(8,128)(2,1)} %fence.17.refs_0_.refs_1_), channel_id=1, source_target_pairs={{0,1},{1,0},{2,3},{3,2},{4,5},{5,4},{6,7},{7,6},{8,9},{9,8},{10,11... | collective-permute-start | bytes 3145736 | tf_op jit(solution)/shard_map/ppermute | solution.py:42
  33.9 3.6 collective-permute-start.13
  35.5 5.3 %copy-start.21 = (s32[13]{0:T(128)S(1)}, s32[13]{0:T(128)}, u32[]{:S(2)}) copy-start(s32[13]{0:T(128)} %pad_add_fusion.5.scal_ref.refs_0_) | copy-start | bytes 160
  38.1 24.6 %collective-permute-start.14 = (bf16[256,2048]{1,0:T(8,128)(2,1)}, bf16[256,2048]{1,0:T(8,128)(2,1)}, u32[]{:S(2)}, u32[]{:S(2)}) collective-permute-start(bf16[256,2048]{1,0:T(8,128)(2,1)} %fence.19), channel_id=1, source_target_pairs={{0,2},{1,3},{2,0},{3,1},{4,6},{5,7},{6,4},{7,5},{8,10},{9,11},{10,... | collective-permute-start | bytes 3145736 | tf_op jit(solution)/shard_map/ppermute | solution.py:42
  53.8 9.9 %copy-start.22 = (f32[2,1024]{1,0:T(2,128)S(1)}, f32[2,1024]{1,0:T(2,128)}, u32[]{:S(2)}) copy-start(f32[2,1024]{1,0:T(2,128)} %get-tuple-element.96) | copy-start | bytes 24580
  53.8 9.9 %collective-permute-start.11 = (f32[2,1024]{1,0:T(2,128)}, f32[2,1024]{1,0:T(2,128)S(1)}, u32[]{:S(2)}, u32[]{:S(2)}) collective-permute-start(f32[2,1024]{1,0:T(2,128)} %get-tuple-element.96), channel_id=1, source_target_pairs={{0,1},{1,0},{2,3},{3,2},{4,5},{5,4},{6,7},{7,6},{8,9},{9,8},{10,11... | collective-permute-start | bytes 24584 | tf_op jit(solution)/shard_map/ppermute | solution.py:42
  62.7 5.4 %collective-permute-start.15 = (bf16[256,2048]{1,0:T(8,128)(2,1)}, bf16[256,2048]{1,0:T(8,128)(2,1)S(1)}, u32[]{:S(2)}, u32[]{:S(2)}) collective-permute-start(bf16[256,2048]{1,0:T(8,128)(2,1)} %collective-permute-done.14.refs_4_), channel_id=1, source_target_pairs={{0,1},{1,0},{2,3},{3,2},{4,5},{5,4},{6,7},{7,6},{8,9},{9,8},{10,11... | collective-permute-start | bytes 3145736 | tf_op jit(solution)/shard_map/ppermute | solution.py:42
  63.7 3.7 collective-permute-start.12
  81.5 6.8 %collective-permute-start.17 = (bf16[256,2176]{1,0:T(8,128)(2,1)}, bf16[256,2176]{1,0:T(8,128)(2,1)}, u32[]{:S(2)}, u32[]{:S(2)}) collective-permute-start(bf16[256,2176]{1,0:T(8,128)(2,1)} %get-tuple-element.102), channel_id=1, source_target_pairs={{0,1},{1,0},{2,3},{3,2},{4,5},{5,4},{6,7},{7,6},{8,9},{9,8},{10,11... | collective-permute-start | bytes 3342344 | tf_op jit(solution)/shard_map/ppermute | solution.py:42
  81.5 6.3 %copy-start.7 = (bf16[256,2048]{1,0:T(8,128)(2,1)S(1)}, bf16[256,2048]{1,0:T(8,128)(2,1)}, u32[]{:S(2)}) copy-start(bf16[256,2048]{1,0:T(8,128)(2,1)} %up_ref.1) | copy-start | bytes 3145732
  87.8 10.1 %collective-permute-start.16 = (bf16[256,2176]{1,0:T(8,128)(2,1)}, bf16[256,2176]{1,0:T(8,128)(2,1)}, u32[]{:S(2)}, u32[]{:S(2)}) collective-permute-start(bf16[256,2176]{1,0:T(8,128)(2,1)} %get-tuple-element.101), channel_id=1, source_target_pairs={{0,1},{1,0},{2,3},{3,2},{4,5},{5,4},{6,7},{7,6},{8,9},{9,8},{10,11... | collective-permute-start | bytes 3342344 | tf_op jit(solution)/shard_map/ppermute | solution.py:42
  87.8 16.3 %collective-permute-start.19 = (bf16[256,2048]{1,0:T(8,128)(2,1)S(1)}, bf16[256,2048]{1,0:T(8,128)(2,1)}, u32[]{:S(2)}, u32[]{:S(2)}) collective-permute-start(bf16[256,2048]{1,0:T(8,128)(2,1)S(1)} %copy-done.7), channel_id=1, source_target_pairs={{0,1},{1,0},{2,3},{3,2},{4,5},{5,4},{6,7},{7,6},{8,9},{9,8},{10,11... | collective-permute-start | bytes 3145736 | tf_op jit(solution)/shard_map/ppermute | solution.py:42
  88.3 9.0 %copy-start.26 = (bf16[2048]{0:T(1024)(128)(2,1)S(1)}, bf16[2048]{0:T(1024)(128)(2,1)}, u32[]{:S(2)}) copy-start(bf16[2048]{0:T(1024)(128)(2,1)} %param.37) | copy-start | bytes 12292
  95.3 30.2 %collective-permute-start.18 = (bf16[256,2176]{1,0:T(8,128)(2,1)}, bf16[256,2176]{1,0:T(8,128)(2,1)}, u32[]{:S(2)}, u32[]{:S(2)}) collective-permute-start(bf16[256,2176]{1,0:T(8,128)(2,1)} %get-tuple-element.104.refs_1_), channel_id=1, source_target_pairs={{0,2},{1,3},{2,0},{3,1},{4,6},{5,7},{6,4},{7,5},{8,10},{9,11},{10,... | collective-permute-start | bytes 3342344 | tf_op jit(solution)/shard_map/ppermute | solution.py:42
  130.1 3.8 collective-permute-start.20
  131.1 30.2 %collective-permute-start.21 = (bf16[256,2176]{1,0:T(8,128)(2,1)}, bf16[256,2176]{1,0:T(8,128)(2,1)S(1)}, u32[]{:S(2)}, u32[]{:S(2)}) collective-permute-start(bf16[256,2176]{1,0:T(8,128)(2,1)} %get-tuple-element.112.refs_0_.refs_4_.refs_12_), channel_id=1, source_target_pairs={{0,2},{1,3},{2,0},{3,1},{4,6},{5,7},{6,4},{7,5},{8,10},{9,11},{10,... | collective-permute-start | bytes 3342344 | tf_op jit(solution)/shard_map/ppermute | solution.py:42
  162.4 3.0 collective-permute-start.22
  265.9 4.3 collective-permute-start.24
  270.1 6.8 %collective-permute-start.23 = (bf16[256,2176]{1,0:T(8,128)(2,1)}, bf16[256,2176]{1,0:T(8,128)(2,1)S(1)}, u32[]{:S(2)}, u32[]{:S(2)}) collective-permute-start(bf16[256,2176]{1,0:T(8,128)(2,1)} %combine.4.refs_1_), channel_id=1, source_target_pairs={{0,1},{1,0},{2,3},{3,2},{4,5},{5,4},{6,7},{7,6},{8,9},{9,8},{10,11... | collective-permute-start | bytes 3342344 | tf_op jit(solution)/shard_map/ppermute | solution.py:42
  274.3 27.2 %collective-permute-start.27 = (bf16[256,2176]{1,0:T(8,128)(2,1)}, bf16[256,2176]{1,0:T(8,128)(2,1)}, u32[]{:S(2)}, u32[]{:S(2)}) collective-permute-start(bf16[256,2176]{1,0:T(8,128)(2,1)} %combine.5.refs_6_), channel_id=1, source_target_pairs={{0,2},{1,3},{2,0},{3,1},{4,6},{5,7},{6,4},{7,5},{8,10},{9,11},{10,... | collective-permute-start | bytes 3342344 | tf_op jit(solution)/shard_map/ppermute | solution.py:42
  275.6 60.2 %collective-permute-start.32 = (bf16[4,4,192,384]{3,2,1,0:T(8,128)(2,1)}, bf16[4,4,192,384]{3,2,1,0:T(8,128)(2,1)}, u32[]{:S(2)}, u32[]{:S(2)}) collective-permute-start(bf16[4,4,192,384]{3,2,1,0:T(8,128)(2,1)} %get-tuple-element.141), channel_id=1, source_target_pairs={{0,4},{4,0},{8,12},{12,8},{16,20},{20,16},{24,28},{28,24},{1,5},{5... | collective-permute-start | bytes 7077896 | tf_op jit(solution)/shard_map/ppermute | solution.py:42
  307.5 3.1 collective-permute-start.29
  307.5 27.2 %collective-permute-start.28 = (bf16[256,2176]{1,0:T(8,128)(2,1)}, bf16[256,2176]{1,0:T(8,128)(2,1)S(1)}, u32[]{:S(2)}, u32[]{:S(2)}) collective-permute-start(bf16[256,2176]{1,0:T(8,128)(2,1)} %get-tuple-element.127.refs_6_), channel_id=1, source_target_pairs={{0,2},{1,3},{2,0},{3,1},{4,6},{5,7},{6,4},{7,5},{8,10},{9,11},{10,... | collective-permute-start | bytes 3342344 | tf_op jit(solution)/shard_map/ppermute | solution.py:42
  308.7 37.4 %collective-permute-start.26 = (bf16[256,2048]{1,0:T(8,128)(2,1)}, bf16[256,2048]{1,0:T(8,128)(2,1)}, u32[]{:S(2)}, u32[]{:S(2)}) collective-permute-start(bf16[256,2048]{1,0:T(8,128)(2,1)} %get-tuple-element.123), channel_id=1, source_target_pairs={{0,1},{1,0},{2,3},{3,2},{4,5},{5,4},{6,7},{7,6},{8,9},{9,8},{10,11... | collective-permute-start | bytes 3145736 | tf_op jit(solution)/shard_map/ppermute | solution.py:42
  335.8 14.5 %collective-permute-start.31 = (bf16[256,2176]{1,0:T(8,128)(2,1)}, bf16[256,2176]{1,0:T(8,128)(2,1)}, u32[]{:S(2)}, u32[]{:S(2)}) collective-permute-start(bf16[256,2176]{1,0:T(8,128)(2,1)} %fence.21.refs_1_.refs_6_), channel_id=1, source_target_pairs={{0,1},{1,0},{2,3},{3,2},{4,5},{5,4},{6,7},{7,6},{8,9},{9,8},{10,11... | collective-permute-start | bytes 3342344 | tf_op jit(solution)/shard_map/ppermute | solution.py:42
  341.7 30.7 %collective-permute-start.33 = (bf16[4,384,384]{2,1,0:T(8,128)(2,1)}, bf16[4,384,384]{2,1,0:T(8,128)(2,1)S(1)}, u32[]{:S(2)}, u32[]{:S(2)}) collective-permute-start(bf16[4,384,384]{2,1,0:T(8,128)(2,1)} %get-tuple-element.148), channel_id=1, source_target_pairs={{0,8},{4,12},{8,16},{12,20},{16,24},{20,28},{1,9},{5,13},{9,17},{1... | collective-permute-start | bytes 3538952 | tf_op jit(solution)/shard_map/ppermute | solution.py:130
  344.8 30.3 %collective-permute-start.34 = (bf16[4,384,384]{2,1,0:T(8,128)(2,1)}, bf16[4,384,384]{2,1,0:T(8,128)(2,1)}, u32[]{:S(2)}, u32[]{:S(2)}) collective-permute-start(bf16[4,384,384]{2,1,0:T(8,128)(2,1)} %get-tuple-element.149), channel_id=1, source_target_pairs={{8,0},{12,4},{16,8},{20,12},{24,16},{28,20},{9,1},{13,5},{17,9},{2... | collective-permute-start | bytes 3538952 | tf_op jit(solution)/shard_map/ppermute | solution.py:130
  349.1 36.4 %collective-permute-start.30 = (bf16[256,2048]{1,0:T(8,128)(2,1)}, bf16[256,2048]{1,0:T(8,128)(2,1)}, u32[]{:S(2)}, u32[]{:S(2)}) collective-permute-start(bf16[256,2048]{1,0:T(8,128)(2,1)} %fence.22), channel_id=1, source_target_pairs={{0,2},{1,3},{2,0},{3,1},{4,6},{5,7},{6,4},{7,5},{8,10},{9,11},{10,... | collective-permute-start | bytes 3145736 | tf_op jit(solution)/shard_map/ppermute | solution.py:42
  350.3 20.8 %copy-start.24 = (f32[1,512]{1,0:T(1,128)S(1)}, f32[1,512]{1,0:T(1,128)}, u32[]{:S(2)}) copy-start(f32[1,512]{1,0:T(1,128)} %get-tuple-element.130.refs_1_.refs_0_) | copy-start | bytes 6148
  372.4 2.7 copy-start.9
  378.4 7.1 %copy-start.23 = (f32[16,128]{1,0:T(8,128)S(1)}, f32[16,128]{1,0:T(8,128)}, u32[]{:S(2)}) copy-start(f32[16,128]{1,0:T(8,128)} %get-tuple-element.152) | copy-start | bytes 24580
  378.4 31.2 %collective-permute-start.38 = (bf16[4,384,384]{2,1,0:T(8,128)(2,1)}, bf16[4,384,384]{2,1,0:T(8,128)(2,1)S(1)}, u32[]{:S(2)}, u32[]{:S(2)}) collective-permute-start(bf16[4,384,384]{2,1,0:T(8,128)(2,1)} %add_convert_fusion.2.refs_17_.refs_18_), channel_id=1, source_target_pairs={{8,0},{12,4},{16,8},{20,12},{24,16},{28,20},{9,1},{13,5},{17,9},{2... | collective-permute-start | bytes 3538952 | tf_op jit(solution)/shard_map/ppermute | solution.py:130
  379.8 29.8 %collective-permute-start.37 = (bf16[4,384,384]{2,1,0:T(8,128)(2,1)}, bf16[4,384,384]{2,1,0:T(8,128)(2,1)}, u32[]{:S(2)}, u32[]{:S(2)}) collective-permute-start(bf16[4,384,384]{2,1,0:T(8,128)(2,1)} %add_convert_fusion.2.refs_17_.refs_18_), channel_id=1, source_target_pairs={{0,8},{4,12},{8,16},{12,20},{16,24},{20,28},{1,9},{5,13},{9,17},{1... | collective-permute-start | bytes 3538952 | tf_op jit(solution)/shard_map/ppermute | solution.py:130
  385.4 1.4 collective-permute-start.35
  387.5 3.7 collective-permute-start.36
  410.6 15.9 %collective-permute-start.39 = (bf16[256,2048]{1,0:T(8,128)(2,1)}, bf16[256,2048]{1,0:T(8,128)(2,1)S(1)}, u32[]{:S(2)}, u32[]{:S(2)}) collective-permute-start(bf16[256,2048]{1,0:T(8,128)(2,1)} %fence.25), channel_id=1, source_target_pairs={{0,1},{1,0},{2,3},{3,2},{4,5},{5,4},{6,7},{7,6},{8,9},{9,8},{10,11... | collective-permute-start | bytes 3145736 | tf_op jit(solution)/shard_map/ppermute | solution.py:42
  410.8 24.5 %collective-permute-start.25 = (bf16[256,2048]{1,0:T(8,128)(2,1)}, bf16[256,2048]{1,0:T(8,128)(2,1)}, u32[]{:S(2)}, u32[]{:S(2)}) collective-permute-start(bf16[256,2048]{1,0:T(8,128)(2,1)} %get-tuple-element.121), channel_id=1, source_target_pairs={{0,1},{1,0},{2,3},{3,2},{4,5},{5,4},{6,7},{7,6},{8,9},{9,8},{10,11... | collective-permute-start | bytes 3145736 | tf_op jit(solution)/shard_map/ppermute | solution.py:42
  411.6 4.4 copy-start.14
  414.8 37.3 %collective-permute-start.46 = (bf16[4,384,384]{2,1,0:T(8,128)(2,1)}, bf16[4,384,384]{2,1,0:T(8,128)(2,1)}, u32[]{:S(2)}, u32[]{:S(2)}) collective-permute-start(bf16[4,384,384]{2,1,0:T(8,128)(2,1)} %add_convert_fusion), channel_id=1, source_target_pairs={{8,0},{12,4},{16,8},{20,12},{24,16},{28,20},{9,1},{13,5},{17,9},{2... | collective-permute-start | bytes 3538952 | tf_op jit(solution)/shard_map/ppermute | solution.py:130
  418.8 47.3 %collective-permute-start.45 = (bf16[4,384,384]{2,1,0:T(8,128)(2,1)}, bf16[4,384,384]{2,1,0:T(8,128)(2,1)}, u32[]{:S(2)}, u32[]{:S(2)}) collective-permute-start(bf16[4,384,384]{2,1,0:T(8,128)(2,1)} %add_convert_fusion.1), channel_id=1, source_target_pairs={{0,8},{4,12},{8,16},{12,20},{16,24},{20,28},{1,9},{5,13},{9,17},{1... | collective-permute-start | bytes 3538952 | tf_op jit(solution)/shard_map/ppermute | solution.py:130
  429.1 35.9 %collective-permute-start.41 = (bf16[256,2048]{1,0:T(8,128)(2,1)}, bf16[256,2048]{1,0:T(8,128)(2,1)S(1)}, u32[]{:S(2)}, u32[]{:S(2)}) collective-permute-start(bf16[256,2048]{1,0:T(8,128)(2,1)} %add_convert_fusion.3.refs_0_.refs_1_), channel_id=1, source_target_pairs={{0,2},{1,3},{2,0},{3,1},{4,6},{5,7},{6,4},{7,5},{8,10},{9,11},{10,... | collective-permute-start | bytes 3145736 | tf_op jit(solution)/shard_map/ppermute | solution.py:42
  433.0 16.2 %collective-permute-start.47 = (bf16[4,6,16,512]{3,2,1,0:T(8,128)(2,1)}, bf16[4,6,16,512]{3,2,1,0:T(8,128)(2,1)}, u32[]{:S(2)}, u32[]{:S(2)}) collective-permute-start(bf16[4,6,16,512]{3,2,1,0:T(8,128)(2,1)} %pad_maximum_fusion.3), channel_id=1, source_target_pairs={{0,4},{4,0},{8,12},{12,8},{16,20},{20,16},{24,28},{28,24},{1,5},{5... | collective-permute-start | bytes 1179656 | tf_op jit(solution)/shard_map/ppermute | solution.py:154
  435.3 12.2 %collective-permute-start.43 = (bf16[400,512]{1,0:T(8,128)(2,1)S(1)}, bf16[400,512]{1,0:T(8,128)(2,1)}, u32[]{:S(2)}, u32[]{:S(2)}) collective-permute-start(bf16[400,512]{1,0:T(8,128)(2,1)S(1)} %get-tuple-element.203), channel_id=1, source_target_pairs={{0,1},{1,0},{2,3},{3,2},{4,5},{5,4},{6,7},{7,6},{8,9},{9,8},{10,11... | collective-permute-start | bytes 1228808 | tf_op jit(solution)/shard_map/ppermute | solution.py:42
  447.5 4.6 collective-permute-start.42
  449.2 12.8 %collective-permute-start.44 = (bf16[400,512]{1,0:T(8,128)(2,1)S(1)}, bf16[400,512]{1,0:T(8,128)(2,1)S(1)}, u32[]{:S(2)}, u32[]{:S(2)}) collective-permute-start(bf16[400,512]{1,0:T(8,128)(2,1)S(1)} %fusion), channel_id=1, source_target_pairs={{0,2},{1,3},{2,0},{3,1},{4,6},{5,7},{6,4},{7,5},{8,10},{9,11},{10,... | collective-permute-start | bytes 1228808 | tf_op jit(solution)/shard_map/ppermute | solution.py:42
  452.0 14.0 %collective-permute-start.48 = (bf16[6,16,512]{2,1,0:T(8,128)(2,1)S(1)}, bf16[6,16,512]{2,1,0:T(8,128)(2,1)S(1)}, u32[]{:S(2)}, u32[]{:S(2)}) collective-permute-start(bf16[6,16,512]{2,1,0:T(8,128)(2,1)S(1)} %get-tuple-element.223), channel_id=1, source_target_pairs={{0,8},{4,12},{8,16},{12,20},{16,24},{20,28},{24,0},{28,4},{1,9},{5... | collective-permute-start | bytes 294920 | tf_op jit(solution)/shard_map/ppermute | solution.py:154
  452.1 13.9 %collective-permute-start.49 = (bf16[6,16,512]{2,1,0:T(8,128)(2,1)S(1)}, bf16[6,16,512]{2,1,0:T(8,128)(2,1)S(1)}, u32[]{:S(2)}, u32[]{:S(2)}) collective-permute-start(bf16[6,16,512]{2,1,0:T(8,128)(2,1)S(1)} %get-tuple-element.222), channel_id=1, source_target_pairs={{0,16},{4,20},{8,24},{12,28},{16,0},{20,4},{24,8},{28,12},{1,17},{... | collective-permute-start | bytes 294920 | tf_op jit(solution)/shard_map/ppermute | solution.py:154
  462.1 4.6 collective-permute-start.50
  465.0 23.6 %collective-permute-start.40 = (bf16[256,2048]{1,0:T(8,128)(2,1)}, bf16[256,2048]{1,0:T(8,128)(2,1)}, u32[]{:S(2)}, u32[]{:S(2)}) collective-permute-start(bf16[256,2048]{1,0:T(8,128)(2,1)} %get-tuple-element.159), channel_id=1, source_target_pairs={{0,1},{1,0},{2,3},{3,2},{4,5},{5,4},{6,7},{7,6},{8,9},{9,8},{10,11... | collective-permute-start | bytes 3145736 | tf_op jit(solution)/shard_map/ppermute | solution.py:42
  473.4 11.1 %copy-start.13 = (f32[6,16,512]{2,1,0:T(8,128)S(1)}, f32[6,16,512]{2,1,0:T(8,128)}, u32[]{:S(2)}) copy-start(f32[6,16,512]{2,1,0:T(8,128)} %convert_add_fusion.2.refs_4_) | copy-start | bytes 589828
  473.4 6.4 %collective-permute-start.51 = (bf16[4,50,512]{2,1,0:T(8,128)(2,1)S(1)}, bf16[4,50,512]{2,1,0:T(8,128)(2,1)S(1)}, u32[]{:S(2)}, u32[]{:S(2)}) collective-permute-start(bf16[4,50,512]{2,1,0:T(8,128)(2,1)S(1)} %pad_maximum_fusion.4), channel_id=1, source_target_pairs={{0,4},{4,0},{8,12},{12,8},{16,20},{20,16},{24,28},{28,24},{1,5},{5... | collective-permute-start | bytes 614408 | tf_op jit(solution)/shard_map/ppermute | solution.py:154
  480.0 14.1 %collective-permute-start.52 = (bf16[50,512]{1,0:T(8,128)(2,1)S(1)}, bf16[50,512]{1,0:T(8,128)(2,1)S(1)}, u32[]{:S(2)}, u32[]{:S(2)}) collective-permute-start(bf16[50,512]{1,0:T(8,128)(2,1)S(1)} %get-tuple-element.224), channel_id=1, source_target_pairs={{0,8},{4,12},{8,16},{12,20},{16,24},{20,28},{24,0},{28,4},{1,9},{5... | collective-permute-start | bytes 153608 | tf_op jit(solution)/shard_map/ppermute | solution.py:154
  481.0 13.0 %collective-permute-start.53 = (bf16[50,512]{1,0:T(8,128)(2,1)S(1)}, bf16[50,512]{1,0:T(8,128)(2,1)S(1)}, u32[]{:S(2)}, u32[]{:S(2)}) collective-permute-start(bf16[50,512]{1,0:T(8,128)(2,1)S(1)} %get-tuple-element.226), channel_id=1, source_target_pairs={{0,16},{4,20},{8,24},{12,28},{16,0},{20,4},{24,8},{28,12},{1,17},{... | collective-permute-start | bytes 153608 | tf_op jit(solution)/shard_map/ppermute | solution.py:154
  483.0 11.0 %collective-permute-start.54 = (bf16[50,512]{1,0:T(8,128)(2,1)S(1)}, bf16[50,512]{1,0:T(8,128)(2,1)S(1)}, u32[]{:S(2)}, u32[]{:S(2)}) collective-permute-start(bf16[50,512]{1,0:T(8,128)(2,1)S(1)} %get-tuple-element.225), channel_id=1, source_target_pairs={{0,24},{4,28},{8,0},{12,4},{16,8},{20,12},{24,16},{28,20},{1,25},{... | collective-permute-start | bytes 153608 | tf_op jit(solution)/shard_map/ppermute | solution.py:154
  (18 other events, 22.1 us)

commit v4 on v3

--- a/solution.py
+++ b/solution.py
@@ -171,9 +171,11 @@
     return parts
 
 
-def sum_packs(parts, *deps):
+def sum_packs(parts, *deps, last=None):
     inner = len(parts)
     mine = direct_scatter(parts, "grp", inner, 1).astype(jnp.bfloat16) if inner > 1 else parts[0]
+    if last is not None:
+        mine = fence(mine, last)
     return direct_scatter([mine[p] for p in range(LINE)], "grp", LINE, inner, *deps)
 
 
@@ -1417,11 +1419,15 @@
         docs, local, scal, near[0], far[0], grad_keys, grad_values, *shared, leave_parts, *ready
     )
     got = line.send(2, ready)
-    line.add(2, got)
     *far_parts, enter_sums, leave_sums = (fence(value, *got) for value in (*far_parts, enter_sums, leave_sums))
     input_far = scatter_even([pair(far_parts[j], swap(far_parts[j + 1], "ep", 1)) for j in range(0, count, 2)], "ep")
-    near_parts = project_near(local, projected_grads, low_grad, qkv_weight, qkv_enter, input_far)
     input_got = swap(input_far, "ep", top)
+    line.add(2, [fence(value, input_far) for value in got])
+    ready = line.ready(3)
+    enter_sums = fence(enter_sums, input_far)
+    enter_sums = [pair(enter_sums[j], swap(enter_sums[j + 1], "ep", 1)) for j in range(0, members, 2)]
+    enter_far = scatter_even(enter_sums[top // 2 :], "ep")
+    near_parts = project_near(local, projected_grads, low_grad, qkv_weight, qkv_enter, input_far, *ready, enter_far)
     if count == 2:
         inputs = (near_parts[0], swap(near_parts[1], "ep", 1), input_got)
     else:
@@ -1430,19 +1436,17 @@
     grad_input = finish(inputs, grad_hidden, tokens, gain_one)
     layer_out = (hidden_state + (mixed_near.astype(f32) + mixed_got.astype(f32))).astype(bf16)
 
-    got = [fence(value, input_got) for value in line.send(3)]
+    got = [fence(value, input_got) for value in line.send(3, ready)]
     line.add(3, got)
     expert_sum = line.total[0]
     by_rows = lambda value: value.astype(bf16).reshape(-1, packs, value.shape[-2] // packs, slice_width).transpose(1, 0, 2, 3)
     joined = jnp.concatenate([by_rows(value) for value in (*low_grads, leave_sums)], axis=1)
     joined = sum_packs(by_place(fence(joined, input_far)), input_got)
-    enter_sums = fence(enter_sums, input_far)
-    enter_sums = [pair(enter_sums[j], swap(enter_sums[j + 1], "ep", 1)) for j in range(0, members, 2)]
-    enter_far = swap(scatter_even(enter_sums[top // 2 :], "ep"), "ep", top)
+    enter_far = swap(enter_far, "ep", top)
     enter_sum = fence(pair(scatter_even(enter_sums[: top // 2], "ep"), enter_far), input_got, *got, joined)
     enter_chunks = by_rows(enter_sum[: 3 * low].reshape(3, low, slice_width)).reshape(packs, -1, slice_width)
     leave_chunks = by_rows(enter_sum[3 * low :]).reshape(packs, -1, slice_width)
-    enter_sum = sum_packs(by_place(jnp.concatenate([enter_chunks, leave_chunks], axis=1)))
+    enter_sum = sum_packs(by_place(jnp.concatenate([enter_chunks, leave_chunks], axis=1)), last=grad_input)
     enter_rows = 3 * low // packs
     wide = width // packs
     turn = lambda value: jnp.swapaxes(value, -1, -2)

time: 505 us -> 513 us (1.016)
  starting transfers between devices: 58.5 us -> 64.8 us
    ppermute x8, starting transfers between devices: 9.61 us -> 19 us  [direct_scatter(): got.append(lax.ppermute(parts[p], axis, moves))]
    ppermute x41, waiting for transfers between devices: 40.6 us -> 32.5 us  [swap(): return lax.ppermute(value, axis, [(i, i ^ bit) for i in range(count)])]
    unnamed x60 -> x66, local copies, waits for them, and re-layouts: 15.4 us -> 15.6 us
  transfers between devices with their start and end apart: 55 -> 55, of which waited for: 17 -> 20; matrix products, arithmetic and copies ran while one was open for 13% -> 13% of each run, Pallas kernels for 39% -> 37%
where the time goes in v4:
time: 513 us; the launch traced here: 503 us
  Pallas kernels  309 us (60%)
  starting transfers between devices  64.8 us (13%)
  waiting for transfers between devices  48.1 us (9%)
  other arithmetic  46.2 us (9%)
  local copies, waits for them, and re-layouts  32.3 us (6%)
    pallas_call x1, Pallas kernels, run_experts(): pl.pallas_call(functools.partial(expert_kernel, line, docs, len(ahead)),...  95.8 us
    pallas_call x2, Pallas kernels, attend_back(): pl.pallas_call(functools.partial(attend_back_kernel, docs, half, local),...  35.9 us
    ppermute x41, waiting for transfers between devices, swap(): return lax.ppermute(value, axis, [(i, i ^ bit) for i in range(count)])  32.5 us
    ppermute x41, starting transfers between devices, swap(): return lax.ppermute(value, axis, [(i, i ^ bit) for i in range(count)])  29.7 us
    pallas_call x1, Pallas kernels, run_near(): pl.pallas_call(functools.partial(near_kernel, docs), grid=(experts,), out...  27.5 us
    pallas_call x4, Pallas kernels, attend(): pl.pallas_call(functools.partial(attend_kernel, docs, place, local, adden...  27 us
    pallas_call x2, Pallas kernels, project(): pl.pallas_call(functools.partial(project_kernel, docs, half, parts), grid...  22.9 us
    pallas_call x1, Pallas kernels, run_upstream(): pl.pallas_call(lambda *refs: upstream_kernel(*refs[:4 + blocks], *refs[4...  21.3 us
  transfers between devices with their start and end apart: 55, of which 20 were waited for; matrix products, arithmetic and copies ran while one was open for 13% of the time, Pallas kernels for 37%

profile of v4, /device:TPU:0, one launch (start us, length us, event | category | flops | bytes accessed | tf_op | source)
XLA Modules:
  0.0 503.5 jit_solution(1241000499804879861)
XLA Ops:
  1.2 2.6 collective-permute-start.7
  4.4 1.4 fusion.28
  5.8 2.6 collective-permute-start.3
  8.4 1.6 collective-permute-start.1
  10.0 1.5 collective-permute-start
  12.0 1.5 collective-permute-start.4
  13.6 1.5 collective-permute-start.2
  21.3 11.5 %project.2 = (bf16[1024,2048]{1,0:T(8,128)(2,1)}, bf16[3,1024,128]{2,1,0:T(8,128)(2,1)}, f32[2,1024,512]{2,1,0:T(8,128)}, bf16[1024,512]{1,0:T(8,128)(2,1)}, f32[2,1024]{1,0:T(2,128)}) custom-call(s32[13]{0:T(128)} %pad_add_fusion.5.scal_ref.refs_0_, bf16[256,2048]{1,0:T(8,128)(2,1)} %refs_4_.13, bf16[256,2048]{1,0:T(8,128)(2,1)} %collective-permute-done.8.refs_1_, ...), custom_call_target="tpu_custom_call" | custom-call | flops 503316480 | bytes 1750000 | tf_op jit(solution)/shard_map/project/pallas_call | solution.py:311
  35.6 2.0 collective-permute-done.13
  42.4 11.5 %project.3 = (bf16[1024,2048]{1,0:T(8,128)(2,1)}, bf16[3,1024,128]{2,1,0:T(8,128)(2,1)}, f32[2,1024,512]{2,1,0:T(8,128)}, bf16[1024,512]{1,0:T(8,128)(2,1)}, f32[2,1024]{1,0:T(2,128)}) custom-call(s32[13]{0:T(128)} %pad_add_fusion.5.scal_ref.refs_0_, ...), custom_call_target="tpu_custom_call", output_to_operand_aliasing={{0}: (7, {}), {1}: (8, {}), {2}: (9, {}), {3}: (10, {}), {4... | custom-call | flops 503316480 | bytes 1750000 | tf_op jit(solution)/shard_map/project/pallas_call | solution.py:311
  53.9 1.5 fusion.36
  55.4 4.5 subtract_convert_fusion
  60.0 1.9 fusion.2
  63.7 1.3 collective-permute-start.12
  66.0 1.4 collective-permute-done.12
  69.0 5.0 prepare.1
  74.0 7.5 %attend.4 = (bf16[256,512]{1,0:T(8,128)(2,1)}, bf16[256,2176]{1,0:T(8,128)(2,1)}, f32[8,256]{1,0:T(8,128)}) custom-call(s32[13]{0:T(128)} %pad_add_fusion.5.scal_ref.refs_0_, bf16[1024,512]{1,0:T(8,128)(2,1)} %get-tuple-element.98.q_ref.refs_0_, bf16[1024,512]{1,0:T(8,128)(2,1)} %get-tuple-element.99.k_ref.refs_1_, ...), custom_call_target="tpu_custom_call" | custom-call | flops 275000000 | bytes 500000 | tf_op jit(solution)/shard_map/attend/pallas_call | solution.py:422
  81.5 6.3 %attend.5 = (bf16[256,512]{1,0:T(8,128)(2,1)}, bf16[256,2176]{1,0:T(8,128)(2,1)}, f32[8,256]{1,0:T(8,128)}) custom-call(s32[13]{0:T(128)} %pad_add_fusion.5.scal_ref.refs_0_, bf16[1024,512]{1,0:T(8,128)(2,1)} %get-tuple-element.98.q_ref.refs_0_, bf16[1024,512]{1,0:T(8,128)(2,1)} %get-tuple-element.99.k_ref.refs_1_, ...), custom_call_target="tpu_custom_call" | custom-call | flops 275000000 | bytes 500000 | tf_op jit(solution)/shard_map/attend/pallas_call | solution.py:422
  88.4 7.0 %attend.6 = (bf16[256,512]{1,0:T(8,128)(2,1)}, bf16[256,2176]{1,0:T(8,128)(2,1)}, f32[8,256]{1,0:T(8,128)}) custom-call(s32[13]{0:T(128)} %pad_add_fusion.5.scal_ref.refs_0_, bf16[1024,512]{1,0:T(8,128)(2,1)} %get-tuple-element.98.q_ref.refs_0_, bf16[1024,512]{1,0:T(8,128)(2,1)} %get-tuple-element.99.k_ref.refs_1_, ...), custom_call_target="tpu_custom_call" | custom-call | flops 275000000 | bytes 500000 | tf_op jit(solution)/shard_map/attend/pallas_call | solution.py:422
  95.4 2.0 collective-permute-start.18
  98.0 6.2 %attend.7 = (bf16[256,512]{1,0:T(8,128)(2,1)}, bf16[256,2176]{1,0:T(8,128)(2,1)}, f32[8,256]{1,0:T(8,128)}) custom-call(s32[13]{0:T(128)} %pad_add_fusion.5.scal_ref.refs_0_, bf16[1024,512]{1,0:T(8,128)(2,1)} %get-tuple-element.98.q_ref.refs_0_, bf16[1024,512]{1,0:T(8,128)(2,1)} %get-tuple-element.99.k_ref.refs_1_, ...), custom_call_target="tpu_custom_call" | custom-call | flops 275000000 | bytes 500000 | tf_op jit(solution)/shard_map/attend/pallas_call | solution.py:422
  104.2 21.3 %upstream.1 = (f32[4,4,1,256]{3,2,1,0:T(1,128)}, bf16[4,576,2048]{2,1,0:T(8,128)(2,1)}, bf16[4,576,1024]{2,1,0:T(8,128)(2,1)}, f32[4,576,128]{2,1,0:T(8,128)}) custom-call(s32[13]{0:T(128)} %pad_add_fusion.5.scal_ref.refs_0_, s32[4,1,256]{2,1,0:T(1,128)} %pad_add_fusion.refs_2_.refs_6_.refs_1_, bf16[256,2048]{1,0:T(8,128)(2,1)} %up_ref.1, ...), custom_call_target="tpu_custom_call" | custom-call | flops 1207959552 | bytes 5000000 | tf_op jit(solution)/shard_map/upstream/pallas_call | solution.py:825
  125.6 4.7 middle.1
  132.5 1.5 collective-permute-done.20.refs_1_.refs_5_.refs_13_
  134.0 27.5 %near.1 = (bf16[4,288,1024]{2,1,0:T(8,128)(2,1)}, bf16[4,288,1024]{2,1,0:T(8,128)(2,1)}, bf16[4,288,1024]{2,1,0:T(8,128)(2,1)}, bf16[4,288,384]{2,1,0:T(8,128)(2,1)}) custom-call(s32[13]{0:T(128)} %pad_add_fusion.5.scal_ref.refs_0_, f32[4,4,1,256]{3,2,1,0:T(1,128)} %get-tuple-element.107.refs_9_.rank_ref.refs_1_, ...), custom_call_target="tpu_custom_call" | custom-call | flops 1207959552 | bytes 5000000 | tf_op jit(solution)/shard_map/near/pallas_call | solution.py:920
  163.5 2.0 collective-permute-done.22.refs_7_.refs_13_
  166.5 95.8 %experts.1 = (bf16[4,4,144,2048]{3,2,1,0:T(8,128)(2,1)}, bf16[4,4,144,2048]{3,2,1,0:T(8,128)(2,1)}, f32[4,4,1,256]{3,2,1,0:T(1,128)}, bf16[4,4,384,384]{3,2,1,0:T(8,128)(2,1)}, bf16[4,4,192,384]{3,2,1,0:T(8,128)(2,1)}) custom-call(s32[13]{0:T(128)} %pad_add_fusion.5.scal_ref.refs_0_, f32[4,4,1,256]{3,2,1,0:T(1,128)} %get-tuple-element.107.refs_9_.rank_ref.refs_1_, ...), custom_call_target="tpu_custom_call" | custom-call | flops 8078229504 | bytes 7500000 | tf_op jit(solution)/shard_map/experts/pallas_call | solution.py:1110
  262.4 3.8 combine.3.refs_0_
  266.5 3.8 combine.4.refs_1_
  270.4 4.2 combine.5.refs_6_
  278.1 13.5 %combine_last.1 = (bf16[256,2048]{1,0:T(8,128)(2,1)}, bf16[256,2048]{1,0:T(8,128)(2,1)}, bf16[256,2048]{1,0:T(8,128)(2,1)}, bf16[256,2048]{1,0:T(8,128)(2,1)}, bf16[256,2176]{1,0:T(8,128)(2,1)}) custom-call(s32[13]{0:T(128)} %pad_add_fusion.5.scal_ref.refs_0_, f32[4,4,1,256]{3,2,1,0:T(1,128)} %get-tuple-element.107.refs_9_.rank_ref.refs_1_, ...), custom_call_target="tpu_custom_call" | custom-call | flops 377487360 | bytes 1474560 | tf_op jit(solution)/shard_map/combine_last/pallas_call | solution.py:1233
  291.6 10.2 %collective-permute-done.27.gb_ref = bf16[256,2176]{1,0:T(8,128)(2,1)} collective-permute-done((bf16[256,2176]{1,0:T(8,128)(2,1)}, bf16[256,2176]{1,0:T(8,128)(2,1)}, u32[]{:S(2)}, u32[]{:S(2)}) %collective-permute-start.27) | collective-permute-done | bytes 1114144 | tf_op jit(solution)/shard_map/ppermute | solution.py:42
  301.7 6.0 %middle_back.1 = (f32[256,2048]{1,0:T(8,128)}, bf16[256,2176]{1,0:T(8,128)(2,1)}, f32[16,128]{1,0:T(8,128)}) custom-call(s32[13]{0:T(128)} %pad_add_fusion.5.scal_ref.refs_0_, bf16[256,2176]{1,0:T(8,128)(2,1)} %get-tuple-element.124.ga_ref, bf16[256,2176]{1,0:T(8,128)(2,1)} %collective-permute-done.27.gb_ref, f32[16,256]{1,0:T(8,128)} %get-tuple-element.125.probs_ref, ...), custom_call_target="tpu_custom_call" | custom-call | flops 33554432 | bytes 1250000 | tf_op jit(solution)/shard_map/middle_back/pallas_call | solution.py:510
  309.2 1.7 collective-permute-done.29.refs_7_
  310.8 15.1 %attend_back.2 = (f32[512,512]{1,0:T(8,128)}, f32[1024,512]{1,0:T(8,128)}, f32[1024,512]{1,0:T(8,128)}, f32[128,512]{1,0:T(8,128)}, f32[128,512]{1,0:T(8,128)}, /*index=5*/f32[128,512]{1,0:T(8,128)}, f32[1,512]{1,0:T(1,128)}) custom-call(s32[13]{0:T(128)} %pad_add_fusion.5.scal_ref.refs_0_, bf16[1024,512]{1,0:T(8,128)(2,1)} %get-tuple-element.98.q_ref.refs_0_, ...), custom_call_target="tpu_custom_call" | custom-call | flops 1000000000 | bytes 1750000 | tf_op jit(solution)/shard_map/attend_back/pallas_call | solution.py:627
  326.0 9.0 %collective-permute-done.28.refs_0_ = bf16[256,2176]{1,0:T(8,128)(2,1)S(1)} collective-permute-done((bf16[256,2176]{1,0:T(8,128)(2,1)}, bf16[256,2176]{1,0:T(8,128)(2,1)S(1)}, u32[]{:S(2)}, u32[]{:S(2)}) %collective-permute-start.28) | collective-permute-done | bytes 1114144 | tf_op jit(solution)/shard_map/ppermute | solution.py:42
  335.9 5.9 %widen.1 = (bf16[4,384,384]{2,1,0:T(8,128)(2,1)}, bf16[4,384,384]{2,1,0:T(8,128)(2,1)}, bf16[4,384,384]{2,1,0:T(8,128)(2,1)}, bf16[4,384,384]{2,1,0:T(8,128)(2,1)}) custom-call(s32[4]{0:T(128)} %get-tuple-element.230.sets_ref, bf16[4,4,384,384]{3,2,1,0:T(8,128)(2,1)} %get-tuple-element.140.kept_ref, ...), custom_call_target="tpu_custom_call" | custom-call | tf_op jit(solution)/shard_map/widen/pallas_call | solution.py:198
  341.9 3.1 collective-permute-start.33
  346.3 2.9 add_convert_fusion.5.refs_0_
  350.4 20.8 %attend_back.3 = (f32[512,512]{1,0:T(8,128)}, f32[1024,512]{1,0:T(8,128)}, f32[1024,512]{1,0:T(8,128)}, f32[128,512]{1,0:T(8,128)}, f32[128,512]{1,0:T(8,128)}, ...) custom-call(s32[13]{0:T(128)} %pad_add_fusion.5.scal_ref.refs_0_, ...), custom_call_target="tpu_custom_call" | custom-call | flops 1000000000 | bytes 1750000 | tf_op jit(solution)/shard_map/attend_back/pallas_call | solution.py:627
  372.6 2.7 collective-permute-done.34.refs_2_
  375.3 3.3 add_convert_fusion.2.refs_17_.refs_18_
  378.6 3.5 collective-permute-start.37
  387.5 1.8 collective-permute-done.36
  389.9 17.8 %project_back.1 = (bf16[256,2048]{1,0:T(8,128)(2,1)}, bf16[256,2048]{1,0:T(8,128)(2,1)}, bf16[4,400,512]{2,1,0:T(8,128)(2,1)}, f32[3,128,512]{2,1,0:T(8,128)}, b...) custom-call(s32[13]{0:T(128)} %pad_add_fusion.5.scal_ref.refs_0_, f32[512,512]{1,0:T(8,128)} %get-tuple-element.131.refs_1_, ...), custom_call_target="tpu_custom_call" | custom-call | flops 603979776 | bytes 2500000 | tf_op jit(solution)/shard_map/project_back/pallas_call | solution.py:717
  407.8 4.2 collective-permute-done.38.refs_2_.refs_0_
  412.0 4.2 add_convert_fusion.4
  421.7 2.6 add_convert_fusion.refs_2_
  425.7 2.0 slice_bitcast_fusion.2
  430.1 2.6 add_convert_fusion.1.refs_1_
  432.7 5.7 %collective-permute-start.45 = (bf16[4,384,384]{2,1,0:T(8,128)(2,1)}, bf16[4,384,384]{2,1,0:T(8,128)(2,1)}, u32[]{:S(2)}, u32[]{:S(2)}) collective-permute-start(bf16[4,384,384]{2,1,0:T(8,128)(2,1)} %add_convert_fusion.1.refs_1_), channel_id=1, source_target_pairs={{0,8},{4,12},{8,16},{12,20},{16,24},{20,28},{1,9},{5,13},{9,17},{1... | collective-permute-start | bytes 3538952 | tf_op jit(solution)/shard_map/ppermute | solution.py:130
  443.4 8.4 %project_near.1 = (bf16[256,2048]{1,0:T(8,128)(2,1)}, bf16[256,2048]{1,0:T(8,128)(2,1)}) custom-call(bf16[3,1024,512]{2,1,0:T(8,128)(2,1)} %get-tuple-element.154.grads_ref, bf16[1024,384]{1,0:T(8,128)(2,1)} %get-tuple-element.155.low_ref, bf16[3,2048,512]{2,1,0:T(8,128)(2,1)} %w_ref.9, bf16[3,2048,128]{2,1,0:T(8,128)(2,1)} %enter_ref.9, ...), custom_call_target="tpu_custom_call" | custom-call | flops 402653184 | bytes 1250000 | tf_op jit(solution)/shard_map/project_near/pallas_call | solution.py:750
  451.8 2.8 collective-permute-start.48
  454.7 4.2 collective-permute-start.49
  459.2 2.2 add_convert_fusion.7.refs_0_
  461.4 4.8 collective-permute-done.48
  466.2 2.0 collective-permute-done.49
  474.5 2.2 select_add_fusion
  476.7 1.4 copy-done.4
  480.6 5.4 %finish.1.refs_1_ = bf16[256,2048]{1,0:T(8,128)(2,1)} custom-call(bf16[256,2048]{1,0:T(8,128)(2,1)} %get-tuple-element.159.refs_0_, bf16[256,2048]{1,0:T(8,128)(2,1)} %collective-permute-done.41.refs_1_, bf16[256,2048]{1,0:T(8,128)(2,1)} %collective-permute-done.42.refs_2_.refs_1_, f32[256,2048]{1,0:T(8,128)} %get-tuple-element.161.refs_3_, ...), custom_call_target="tpu_custom_call" | custom-call | flops 655360 | bytes 786432 | tf_op jit(solution)/shard_map/finish/pallas_call | solution.py:779
  486.9 4.7 collective-permute-start.52
  491.6 3.1 collective-permute-start.53
  494.8 1.6 collective-permute-start.54
  496.4 2.0 slice_bitcast_fusion.6
  (238 shorter events, 70.2 us)
Async XLA Ops:
  0.6 20.6 %collective-permute-start.8 = (bf16[256,2048]{1,0:T(8,128)(2,1)}, bf16[256,2048]{1,0:T(8,128)(2,1)}, u32[]{:S(2)}, u32[]{:S(2)}) collective-permute-start(bf16[256,2048]{1,0:T(8,128)(2,1)} %refs_4_.13), channel_id=1, source_target_pairs={{0,1},{1,0},{2,3},{3,2},{4,5},{5,4},{6,7},{7,6},{8,9},{9,8},{10,11... | collective-permute-start | bytes 3145736 | tf_op jit(solution)/shard_map/ppermute | solution.py:42
  1.2 31.6 %collective-permute-start.7 = (bf16[256,2048]{1,0:T(8,128)(2,1)}, bf16[256,2048]{1,0:T(8,128)(2,1)S(1)}, u32[]{:S(2)}, u32[]{:S(2)}) collective-permute-start(bf16[256,2048]{1,0:T(8,128)(2,1)} %refs_4_.13), channel_id=1, source_target_pairs={{0,2},{1,3},{2,0},{3,1},{4,6},{5,7},{6,4},{7,5},{8,10},{9,11},{10,... | collective-permute-start | bytes 3145736 | tf_op jit(solution)/shard_map/ppermute | solution.py:42
  5.8 5.7 %collective-permute-start.3 = (s32[384]{0:T(512)S(1)}, s32[384]{0:T(512)S(1)}, u32[]{:S(2)}, u32[]{:S(2)}) collective-permute-start(s32[384]{0:T(512)S(1)} %pad_add_fusion.1), channel_id=1, source_target_pairs={{0,16},{4,20},{8,24},{12,28},{16,0},{20,4},{24,8},{28,12},{1,17},{... | collective-permute-start | bytes 4616 | tf_op jit(solution)/shard_map/ppermute | solution.py:42
  8.4 3.6 collective-permute-start.1
  10.0 3.6 collective-permute-start
  11.5 3.6 collective-permute-start.5
  12.0 6.2 %collective-permute-start.4 = (s32[384]{0:T(512)S(1)}, s32[384]{0:T(512)S(1)}, u32[]{:S(2)}, u32[]{:S(2)}) collective-permute-start(s32[384]{0:T(512)S(1)} %collective-permute-done.3), channel_id=1, source_target_pairs={{0,4},{4,0},{8,12},{12,8},{16,20},{20,16},{24,28},{28,24},{1,5},{5... | collective-permute-start | bytes 4616 | tf_op jit(solution)/shard_map/ppermute | solution.py:42
  13.6 4.7 collective-permute-start.2
  15.1 3.6 collective-permute-start.6
  19.5 1.2 collective-permute-start.9
  33.7 7.6 %collective-permute-start.10 = (bf16[256,2048]{1,0:T(8,128)(2,1)}, bf16[256,2048]{1,0:T(8,128)(2,1)S(1)}, u32[]{:S(2)}, u32[]{:S(2)}) collective-permute-start(bf16[256,2048]{1,0:T(8,128)(2,1)} %fence.20.refs_0_.refs_1_), channel_id=1, source_target_pairs={{0,1},{1,0},{2,3},{3,2},{4,5},{5,4},{6,7},{7,6},{8,9},{9,8},{10,11... | collective-permute-start | bytes 3145736 | tf_op jit(solution)/shard_map/ppermute | solution.py:42
  33.9 3.6 collective-permute-start.13
  35.6 5.3 %copy-start.24 = (s32[13]{0:T(128)S(1)}, s32[13]{0:T(128)}, u32[]{:S(2)}) copy-start(s32[13]{0:T(128)} %pad_add_fusion.5.scal_ref.refs_0_) | copy-start | bytes 160
  38.1 24.6 %collective-permute-start.14 = (bf16[256,2048]{1,0:T(8,128)(2,1)}, bf16[256,2048]{1,0:T(8,128)(2,1)}, u32[]{:S(2)}, u32[]{:S(2)}) collective-permute-start(bf16[256,2048]{1,0:T(8,128)(2,1)} %fence.22), channel_id=1, source_target_pairs={{0,2},{1,3},{2,0},{3,1},{4,6},{5,7},{6,4},{7,5},{8,10},{9,11},{10,... | collective-permute-start | bytes 3145736 | tf_op jit(solution)/shard_map/ppermute | solution.py:42
  53.8 9.9 %copy-start.25 = (f32[2,1024]{1,0:T(2,128)S(1)}, f32[2,1024]{1,0:T(2,128)}, u32[]{:S(2)}) copy-start(f32[2,1024]{1,0:T(2,128)} %get-tuple-element.96) | copy-start | bytes 24580
  53.8 9.8 %collective-permute-start.11 = (f32[2,1024]{1,0:T(2,128)}, f32[2,1024]{1,0:T(2,128)S(1)}, u32[]{:S(2)}, u32[]{:S(2)}) collective-permute-start(f32[2,1024]{1,0:T(2,128)} %get-tuple-element.96), channel_id=1, source_target_pairs={{0,1},{1,0},{2,3},{3,2},{4,5},{5,4},{6,7},{7,6},{8,9},{9,8},{10,11... | collective-permute-start | bytes 24584 | tf_op jit(solution)/shard_map/ppermute | solution.py:42
  62.7 5.4 %collective-permute-start.15 = (bf16[256,2048]{1,0:T(8,128)(2,1)}, bf16[256,2048]{1,0:T(8,128)(2,1)S(1)}, u32[]{:S(2)}, u32[]{:S(2)}) collective-permute-start(bf16[256,2048]{1,0:T(8,128)(2,1)} %collective-permute-done.14.refs_4_), channel_id=1, source_target_pairs={{0,1},{1,0},{2,3},{3,2},{4,5},{5,4},{6,7},{7,6},{8,9},{9,8},{10,11... | collective-permute-start | bytes 3145736 | tf_op jit(solution)/shard_map/ppermute | solution.py:42
  63.7 3.7 collective-permute-start.12
  81.5 6.8 %collective-permute-start.17 = (bf16[256,2176]{1,0:T(8,128)(2,1)}, bf16[256,2176]{1,0:T(8,128)(2,1)}, u32[]{:S(2)}, u32[]{:S(2)}) collective-permute-start(bf16[256,2176]{1,0:T(8,128)(2,1)} %get-tuple-element.102), channel_id=1, source_target_pairs={{0,1},{1,0},{2,3},{3,2},{4,5},{5,4},{6,7},{7,6},{8,9},{9,8},{10,11... | collective-permute-start | bytes 3342344 | tf_op jit(solution)/shard_map/ppermute | solution.py:42
  81.5 6.3 %copy-start.7 = (bf16[256,2048]{1,0:T(8,128)(2,1)S(1)}, bf16[256,2048]{1,0:T(8,128)(2,1)}, u32[]{:S(2)}) copy-start(bf16[256,2048]{1,0:T(8,128)(2,1)} %up_ref.1) | copy-start | bytes 3145732
  87.9 10.2 %collective-permute-start.16 = (bf16[256,2176]{1,0:T(8,128)(2,1)}, bf16[256,2176]{1,0:T(8,128)(2,1)}, u32[]{:S(2)}, u32[]{:S(2)}) collective-permute-start(bf16[256,2176]{1,0:T(8,128)(2,1)} %get-tuple-element.101), channel_id=1, source_target_pairs={{0,1},{1,0},{2,3},{3,2},{4,5},{5,4},{6,7},{7,6},{8,9},{9,8},{10,11... | collective-permute-start | bytes 3342344 | tf_op jit(solution)/shard_map/ppermute | solution.py:42
  87.9 16.4 %collective-permute-start.19 = (bf16[256,2048]{1,0:T(8,128)(2,1)S(1)}, bf16[256,2048]{1,0:T(8,128)(2,1)}, u32[]{:S(2)}, u32[]{:S(2)}) collective-permute-start(bf16[256,2048]{1,0:T(8,128)(2,1)S(1)} %copy-done.7), channel_id=1, source_target_pairs={{0,1},{1,0},{2,3},{3,2},{4,5},{5,4},{6,7},{7,6},{8,9},{9,8},{10,11... | collective-permute-start | bytes 3145736 | tf_op jit(solution)/shard_map/ppermute | solution.py:42
  88.4 9.0 %copy-start.29 = (bf16[2048]{0:T(1024)(128)(2,1)S(1)}, bf16[2048]{0:T(1024)(128)(2,1)}, u32[]{:S(2)}) copy-start(bf16[2048]{0:T(1024)(128)(2,1)} %param.37) | copy-start | bytes 12292
  95.4 30.2 %collective-permute-start.18 = (bf16[256,2176]{1,0:T(8,128)(2,1)}, bf16[256,2176]{1,0:T(8,128)(2,1)}, u32[]{:S(2)}, u32[]{:S(2)}) collective-permute-start(bf16[256,2176]{1,0:T(8,128)(2,1)} %get-tuple-element.104.refs_1_), channel_id=1, source_target_pairs={{0,2},{1,3},{2,0},{3,1},{4,6},{5,7},{6,4},{7,5},{8,10},{9,11},{10,... | collective-permute-start | bytes 3342344 | tf_op jit(solution)/shard_map/ppermute | solution.py:42
  130.2 3.8 collective-permute-start.20
  131.3 30.3 %collective-permute-start.21 = (bf16[256,2176]{1,0:T(8,128)(2,1)}, bf16[256,2176]{1,0:T(8,128)(2,1)S(1)}, u32[]{:S(2)}, u32[]{:S(2)}) collective-permute-start(bf16[256,2176]{1,0:T(8,128)(2,1)} %get-tuple-element.112.refs_0_.refs_4_.refs_12_), channel_id=1, source_target_pairs={{0,2},{1,3},{2,0},{3,1},{4,6},{5,7},{6,4},{7,5},{8,10},{9,11},{10,... | collective-permute-start | bytes 3342344 | tf_op jit(solution)/shard_map/ppermute | solution.py:42
  162.6 3.0 collective-permute-start.22
  266.2 4.3 collective-permute-start.24
  270.3 6.8 %collective-permute-start.23 = (bf16[256,2176]{1,0:T(8,128)(2,1)}, bf16[256,2176]{1,0:T(8,128)(2,1)S(1)}, u32[]{:S(2)}, u32[]{:S(2)}) collective-permute-start(bf16[256,2176]{1,0:T(8,128)(2,1)} %combine.4.refs_1_), channel_id=1, source_target_pairs={{0,1},{1,0},{2,3},{3,2},{4,5},{5,4},{6,7},{7,6},{8,9},{9,8},{10,11... | collective-permute-start | bytes 3342344 | tf_op jit(solution)/shard_map/ppermute | solution.py:42
  274.6 27.2 %collective-permute-start.27 = (bf16[256,2176]{1,0:T(8,128)(2,1)}, bf16[256,2176]{1,0:T(8,128)(2,1)}, u32[]{:S(2)}, u32[]{:S(2)}) collective-permute-start(bf16[256,2176]{1,0:T(8,128)(2,1)} %combine.5.refs_6_), channel_id=1, source_target_pairs={{0,2},{1,3},{2,0},{3,1},{4,6},{5,7},{6,4},{7,5},{8,10},{9,11},{10,... | collective-permute-start | bytes 3342344 | tf_op jit(solution)/shard_map/ppermute | solution.py:42
  275.8 60.1 %collective-permute-start.32 = (bf16[4,4,192,384]{3,2,1,0:T(8,128)(2,1)}, bf16[4,4,192,384]{3,2,1,0:T(8,128)(2,1)}, u32[]{:S(2)}, u32[]{:S(2)}) collective-permute-start(bf16[4,4,192,384]{3,2,1,0:T(8,128)(2,1)} %get-tuple-element.141), channel_id=1, source_target_pairs={{0,4},{4,0},{8,12},{12,8},{16,20},{20,16},{24,28},{28,24},{1,5},{5... | collective-permute-start | bytes 7077896 | tf_op jit(solution)/shard_map/ppermute | solution.py:42
  307.7 3.1 collective-permute-start.29
  307.7 27.2 %collective-permute-start.28 = (bf16[256,2176]{1,0:T(8,128)(2,1)}, bf16[256,2176]{1,0:T(8,128)(2,1)S(1)}, u32[]{:S(2)}, u32[]{:S(2)}) collective-permute-start(bf16[256,2176]{1,0:T(8,128)(2,1)} %get-tuple-element.127.refs_6_), channel_id=1, source_target_pairs={{0,2},{1,3},{2,0},{3,1},{4,6},{5,7},{6,4},{7,5},{8,10},{9,11},{10,... | collective-permute-start | bytes 3342344 | tf_op jit(solution)/shard_map/ppermute | solution.py:42
  308.9 37.4 %collective-permute-start.26 = (bf16[256,2048]{1,0:T(8,128)(2,1)}, bf16[256,2048]{1,0:T(8,128)(2,1)}, u32[]{:S(2)}, u32[]{:S(2)}) collective-permute-start(bf16[256,2048]{1,0:T(8,128)(2,1)} %get-tuple-element.123), channel_id=1, source_target_pairs={{0,1},{1,0},{2,3},{3,2},{4,5},{5,4},{6,7},{7,6},{8,9},{9,8},{10,11... | collective-permute-start | bytes 3145736 | tf_op jit(solution)/shard_map/ppermute | solution.py:42
  335.9 14.5 %collective-permute-start.31 = (bf16[256,2176]{1,0:T(8,128)(2,1)}, bf16[256,2176]{1,0:T(8,128)(2,1)}, u32[]{:S(2)}, u32[]{:S(2)}) collective-permute-start(bf16[256,2176]{1,0:T(8,128)(2,1)} %fence.24.refs_1_.refs_6_), channel_id=1, source_target_pairs={{0,1},{1,0},{2,3},{3,2},{4,5},{5,4},{6,7},{7,6},{8,9},{9,8},{10,11... | collective-permute-start | bytes 3342344 | tf_op jit(solution)/shard_map/ppermute | solution.py:42
  341.9 30.7 %collective-permute-start.33 = (bf16[4,384,384]{2,1,0:T(8,128)(2,1)}, bf16[4,384,384]{2,1,0:T(8,128)(2,1)S(1)}, u32[]{:S(2)}, u32[]{:S(2)}) collective-permute-start(bf16[4,384,384]{2,1,0:T(8,128)(2,1)} %get-tuple-element.148), channel_id=1, source_target_pairs={{0,8},{4,12},{8,16},{12,20},{16,24},{20,28},{1,9},{5,13},{9,17},{1... | collective-permute-start | bytes 3538952 | tf_op jit(solution)/shard_map/ppermute | solution.py:130
  345.0 30.3 %collective-permute-start.34 = (bf16[4,384,384]{2,1,0:T(8,128)(2,1)}, bf16[4,384,384]{2,1,0:T(8,128)(2,1)}, u32[]{:S(2)}, u32[]{:S(2)}) collective-permute-start(bf16[4,384,384]{2,1,0:T(8,128)(2,1)} %get-tuple-element.149), channel_id=1, source_target_pairs={{8,0},{12,4},{16,8},{20,12},{24,16},{28,20},{9,1},{13,5},{17,9},{2... | collective-permute-start | bytes 3538952 | tf_op jit(solution)/shard_map/ppermute | solution.py:130
  349.2 34.2 %collective-permute-start.30 = (bf16[256,2048]{1,0:T(8,128)(2,1)}, bf16[256,2048]{1,0:T(8,128)(2,1)}, u32[]{:S(2)}, u32[]{:S(2)}) collective-permute-start(bf16[256,2048]{1,0:T(8,128)(2,1)} %fence.25), channel_id=1, source_target_pairs={{0,2},{1,3},{2,0},{3,1},{4,6},{5,7},{6,4},{7,5},{8,10},{9,11},{10,... | collective-permute-start | bytes 3145736 | tf_op jit(solution)/shard_map/ppermute | solution.py:42
  350.4 61.6 %collective-permute-start.25 = (bf16[256,2048]{1,0:T(8,128)(2,1)}, bf16[256,2048]{1,0:T(8,128)(2,1)}, u32[]{:S(2)}, u32[]{:S(2)}) collective-permute-start(bf16[256,2048]{1,0:T(8,128)(2,1)} %get-tuple-element.121), channel_id=1, source_target_pairs={{0,1},{1,0},{2,3},{3,2},{4,5},{5,4},{6,7},{7,6},{8,9},{9,8},{10,11... | collective-permute-start | bytes 3145736 | tf_op jit(solution)/shard_map/ppermute | solution.py:42
  350.4 20.8 %copy-start.27 = (f32[1,512]{1,0:T(1,128)S(1)}, f32[1,512]{1,0:T(1,128)}, u32[]{:S(2)}) copy-start(f32[1,512]{1,0:T(1,128)} %get-tuple-element.130.refs_1_.refs_0_) | copy-start | bytes 6148
  378.6 4.9 copy-start.26
  378.6 29.2 %collective-permute-start.37 = (bf16[4,384,384]{2,1,0:T(8,128)(2,1)}, bf16[4,384,384]{2,1,0:T(8,128)(2,1)S(1)}, u32[]{:S(2)}, u32[]{:S(2)}) collective-permute-start(bf16[4,384,384]{2,1,0:T(8,128)(2,1)} %add_convert_fusion.2.refs_17_.refs_18_), channel_id=1, source_target_pairs={{0,8},{4,12},{8,16},{12,20},{16,24},{20,28},{1,9},{5,13},{9,17},{1... | collective-permute-start | bytes 3538952 | tf_op jit(solution)/shard_map/ppermute | solution.py:130
  382.1 29.8 %collective-permute-start.38 = (bf16[4,384,384]{2,1,0:T(8,128)(2,1)}, bf16[4,384,384]{2,1,0:T(8,128)(2,1)}, u32[]{:S(2)}, u32[]{:S(2)}) collective-permute-start(bf16[4,384,384]{2,1,0:T(8,128)(2,1)} %add_convert_fusion.2.refs_17_.refs_18_), channel_id=1, source_target_pairs={{8,0},{12,4},{16,8},{20,12},{24,16},{28,20},{9,1},{13,5},{17,9},{2... | collective-permute-start | bytes 3538952 | tf_op jit(solution)/shard_map/ppermute | solution.py:130
  383.5 1.4 collective-permute-start.35
  385.6 3.7 collective-permute-start.36
  412.0 6.5 %collective-permute-start.39 = (bf16[256,2048]{1,0:T(8,128)(2,1)}, bf16[256,2048]{1,0:T(8,128)(2,1)S(1)}, u32[]{:S(2)}, u32[]{:S(2)}) collective-permute-start(bf16[256,2048]{1,0:T(8,128)(2,1)} %fence.28), channel_id=1, source_target_pairs={{0,1},{1,0},{2,3},{3,2},{4,5},{5,4},{6,7},{7,6},{8,9},{9,8},{10,11... | collective-permute-start | bytes 3145736 | tf_op jit(solution)/shard_map/ppermute | solution.py:42
  412.0 4.2 copy-start.23
  412.0 4.2 copy-start.22
  412.0 4.2 copy-start.21
  419.5 39.4 %collective-permute-start.42 = (bf16[256,2048]{1,0:T(8,128)(2,1)S(1)}, bf16[256,2048]{1,0:T(8,128)(2,1)}, u32[]{:S(2)}, u32[]{:S(2)}) collective-permute-start(bf16[256,2048]{1,0:T(8,128)(2,1)S(1)} %add_convert_fusion.3.refs_1_.refs_0_), channel_id=1, source_target_pairs={{0,2},{1,3},{2,0},{3,1},{4,6},{5,7},{6,4},{7,5},{8,10},{9,11},{10,... | collective-permute-start | bytes 3145736 | tf_op jit(solution)/shard_map/ppermute | solution.py:42
  424.3 47.0 %collective-permute-start.46 = (bf16[4,384,384]{2,1,0:T(8,128)(2,1)}, bf16[4,384,384]{2,1,0:T(8,128)(2,1)}, u32[]{:S(2)}, u32[]{:S(2)}) collective-permute-start(bf16[4,384,384]{2,1,0:T(8,128)(2,1)} %add_convert_fusion.refs_2_), channel_id=1, source_target_pairs={{8,0},{12,4},{16,8},{20,12},{24,16},{28,20},{9,1},{13,5},{17,9},{2... | collective-permute-start | bytes 3538952 | tf_op jit(solution)/shard_map/ppermute | solution.py:130
  427.7 10.8 %collective-permute-start.40 = (bf16[400,512]{1,0:T(8,128)(2,1)}, bf16[400,512]{1,0:T(8,128)(2,1)S(1)}, u32[]{:S(2)}, u32[]{:S(2)}) collective-permute-start(bf16[400,512]{1,0:T(8,128)(2,1)} %get-tuple-element.203), channel_id=1, source_target_pairs={{0,1},{1,0},{2,3},{3,2},{4,5},{5,4},{6,7},{7,6},{8,9},{9,8},{10,11... | collective-permute-start | bytes 1228808 | tf_op jit(solution)/shard_map/ppermute | solution.py:42
  429.0 11.4 %collective-permute-start.47 = (bf16[4,6,16,512]{3,2,1,0:T(8,128)(2,1)}, bf16[4,6,16,512]{3,2,1,0:T(8,128)(2,1)}, u32[]{:S(2)}, u32[]{:S(2)}) collective-permute-start(bf16[4,6,16,512]{3,2,1,0:T(8,128)(2,1)} %pad_maximum_fusion.3), channel_id=1, source_target_pairs={{0,4},{4,0},{8,12},{12,8},{16,20},{20,16},{24,28},{28,24},{1,5},{5... | collective-permute-start | bytes 1179656 | tf_op jit(solution)/shard_map/ppermute | solution.py:154
  432.7 38.7 %collective-permute-start.45 = (bf16[4,384,384]{2,1,0:T(8,128)(2,1)}, bf16[4,384,384]{2,1,0:T(8,128)(2,1)}, u32[]{:S(2)}, u32[]{:S(2)}) collective-permute-start(bf16[4,384,384]{2,1,0:T(8,128)(2,1)} %add_convert_fusion.1.refs_1_), channel_id=1, source_target_pairs={{0,8},{4,12},{8,16},{12,20},{16,24},{20,28},{1,9},{5,13},{9,17},{1... | collective-permute-start | bytes 3538952 | tf_op jit(solution)/shard_map/ppermute | solution.py:130
  439.2 12.6 %collective-permute-start.43 = (bf16[400,512]{1,0:T(8,128)(2,1)S(1)}, bf16[400,512]{1,0:T(8,128)(2,1)}, u32[]{:S(2)}, u32[]{:S(2)}) collective-permute-start(bf16[400,512]{1,0:T(8,128)(2,1)S(1)} %get-tuple-element.202), channel_id=1, source_target_pairs={{0,1},{1,0},{2,3},{3,2},{4,5},{5,4},{6,7},{7,6},{8,9},{9,8},{10,11... | collective-permute-start | bytes 1228808 | tf_op jit(solution)/shard_map/ppermute | solution.py:42
  440.4 14.2 %collective-permute-start.44 = (bf16[400,512]{1,0:T(8,128)(2,1)S(1)}, bf16[400,512]{1,0:T(8,128)(2,1)}, u32[]{:S(2)}, u32[]{:S(2)}) collective-permute-start(bf16[400,512]{1,0:T(8,128)(2,1)S(1)} %fusion.1.refs_3_), channel_id=1, source_target_pairs={{0,2},{1,3},{2,0},{3,1},{4,6},{5,7},{6,4},{7,5},{8,10},{9,11},{10,... | collective-permute-start | bytes 1228808 | tf_op jit(solution)/shard_map/ppermute | solution.py:42
  451.8 14.4 %collective-permute-start.48 = (bf16[6,16,512]{2,1,0:T(8,128)(2,1)}, bf16[6,16,512]{2,1,0:T(8,128)(2,1)S(1)}, u32[]{:S(2)}, u32[]{:S(2)}) collective-permute-start(bf16[6,16,512]{2,1,0:T(8,128)(2,1)} %get-tuple-element.223), channel_id=1, source_target_pairs={{0,8},{4,12},{8,16},{12,20},{16,24},{20,28},{24,0},{28,4},{1,9},{5... | collective-permute-start | bytes 294920 | tf_op jit(solution)/shard_map/ppermute | solution.py:154
  454.7 13.5 %collective-permute-start.49 = (bf16[6,16,512]{2,1,0:T(8,128)(2,1)}, bf16[6,16,512]{2,1,0:T(8,128)(2,1)S(1)}, u32[]{:S(2)}, u32[]{:S(2)}) collective-permute-start(bf16[6,16,512]{2,1,0:T(8,128)(2,1)} %get-tuple-element.222), channel_id=1, source_target_pairs={{0,16},{4,20},{8,24},{12,28},{16,0},{20,4},{24,8},{28,12},{1,17},{... | collective-permute-start | bytes 294920 | tf_op jit(solution)/shard_map/ppermute | solution.py:154
  458.8 10.2 %collective-permute-start.50 = (bf16[6,16,512]{2,1,0:T(8,128)(2,1)S(1)}, bf16[6,16,512]{2,1,0:T(8,128)(2,1)S(1)}, u32[]{:S(2)}, u32[]{:S(2)}) collective-permute-start(bf16[6,16,512]{2,1,0:T(8,128)(2,1)S(1)} %get-tuple-element.221), channel_id=1, source_target_pairs={{0,24},{4,28},{8,0},{12,4},{16,8},{20,12},{24,16},{28,20},{1,25},{... | collective-permute-start | bytes 294920 | tf_op jit(solution)/shard_map/ppermute | solution.py:154
  466.2 14.5 %collective-permute-start.41 = (bf16[256,2048]{1,0:T(8,128)(2,1)}, bf16[256,2048]{1,0:T(8,128)(2,1)}, u32[]{:S(2)}, u32[]{:S(2)}) collective-permute-start(bf16[256,2048]{1,0:T(8,128)(2,1)} %get-tuple-element.160), channel_id=1, source_target_pairs={{0,1},{1,0},{2,3},{3,2},{4,5},{5,4},{6,7},{7,6},{8,9},{9,8},{10,11... | collective-permute-start | bytes 3145736 | tf_op jit(solution)/shard_map/ppermute | solution.py:42
  473.4 6.4 %collective-permute-start.51 = (bf16[4,50,512]{2,1,0:T(8,128)(2,1)S(1)}, bf16[4,50,512]{2,1,0:T(8,128)(2,1)S(1)}, u32[]{:S(2)}, u32[]{:S(2)}) collective-permute-start(bf16[4,50,512]{2,1,0:T(8,128)(2,1)S(1)} %pad_maximum_fusion.4), channel_id=1, source_target_pairs={{0,4},{4,0},{8,12},{12,8},{16,20},{20,16},{24,28},{28,24},{1,5},{5... | collective-permute-start | bytes 614408 | tf_op jit(solution)/shard_map/ppermute | solution.py:154
  486.9 14.2 %collective-permute-start.52 = (bf16[50,512]{1,0:T(8,128)(2,1)S(1)}, bf16[50,512]{1,0:T(8,128)(2,1)S(1)}, u32[]{:S(2)}, u32[]{:S(2)}) collective-permute-start(bf16[50,512]{1,0:T(8,128)(2,1)S(1)} %get-tuple-element.224), channel_id=1, source_target_pairs={{0,8},{4,12},{8,16},{12,20},{16,24},{20,28},{24,0},{28,4},{1,9},{5... | collective-permute-start | bytes 153608 | tf_op jit(solution)/shard_map/ppermute | solution.py:154
  491.6 9.5 %collective-permute-start.53 = (bf16[50,512]{1,0:T(8,128)(2,1)S(1)}, bf16[50,512]{1,0:T(8,128)(2,1)S(1)}, u32[]{:S(2)}, u32[]{:S(2)}) collective-permute-start(bf16[50,512]{1,0:T(8,128)(2,1)S(1)} %get-tuple-element.226), channel_id=1, source_target_pairs={{0,16},{4,20},{8,24},{12,28},{16,0},{20,4},{24,8},{28,12},{1,17},{... | collective-permute-start | bytes 153608 | tf_op jit(solution)/shard_map/ppermute | solution.py:154
  494.8 6.4 %collective-permute-start.54 = (bf16[50,512]{1,0:T(8,128)(2,1)S(1)}, bf16[50,512]{1,0:T(8,128)(2,1)S(1)}, u32[]{:S(2)}, u32[]{:S(2)}) collective-permute-start(bf16[50,512]{1,0:T(8,128)(2,1)S(1)} %get-tuple-element.225), channel_id=1, source_target_pairs={{0,24},{4,28},{8,0},{12,4},{16,8},{20,12},{24,16},{28,20},{1,25},{... | collective-permute-start | bytes 153608 | tf_op jit(solution)/shard_map/ppermute | solution.py:154
  (21 other events, 34.5 us)

commit v5 on v3

--- a/solution.py
+++ b/solution.py
@@ -171,9 +171,11 @@
     return parts
 
 
-def sum_packs(parts, *deps):
+def sum_packs(parts, *deps, last=None):
     inner = len(parts)
     mine = direct_scatter(parts, "grp", inner, 1).astype(jnp.bfloat16) if inner > 1 else parts[0]
+    if last is not None:
+        mine = fence(mine, last)
     return direct_scatter([mine[p] for p in range(LINE)], "grp", LINE, inner, *deps)
 
 
@@ -1442,7 +1444,7 @@
     enter_sum = fence(pair(scatter_even(enter_sums[: top // 2], "ep"), enter_far), input_got, *got, joined)
     enter_chunks = by_rows(enter_sum[: 3 * low].reshape(3, low, slice_width)).reshape(packs, -1, slice_width)
     leave_chunks = by_rows(enter_sum[3 * low :]).reshape(packs, -1, slice_width)
-    enter_sum = sum_packs(by_place(jnp.concatenate([enter_chunks, leave_chunks], axis=1)))
+    enter_sum = sum_packs(by_place(jnp.concatenate([enter_chunks, leave_chunks], axis=1)), last=grad_input)
     enter_rows = 3 * low // packs
     wide = width // packs
     turn = lambda value: jnp.swapaxes(value, -1, -2)

time: 505 us -> 509 us (level)
  starting transfers between devices: 58.5 us -> 64.2 us
    ppermute x8, starting transfers between devices: 9.61 us -> 16.6 us  [direct_scatter(): got.append(lax.ppermute(parts[p], axis, moves))]
    unnamed x60 -> x64, local copies, waits for them, and re-layouts: 15.4 us -> 14.2 us
  transfers between devices with their start and end apart: 55 -> 55, of which waited for: 17 -> 19; matrix products, arithmetic and copies ran while one was open for 13% -> 13% of each run, Pallas kernels for 39% -> 38%
where the time goes in v5:
time: 509 us; the launch traced here: 500 us
  Pallas kernels  309 us (61%)
  starting transfers between devices  64.2 us (13%)
  other arithmetic  46.5 us (9%)
  waiting for transfers between devices  45.6 us (9%)
  local copies, waits for them, and re-layouts  31.6 us (6%)
    pallas_call x1, Pallas kernels, run_experts(): pl.pallas_call(functools.partial(expert_kernel, line, docs, len(ahead)),...  95.8 us
    ppermute x41, waiting for transfers between devices, swap(): return lax.ppermute(value, axis, [(i, i ^ bit) for i in range(count)])  40.9 us
    pallas_call x2, Pallas kernels, attend_back(): pl.pallas_call(functools.partial(attend_back_kernel, docs, half, local),...  35.9 us
    ppermute x41, starting transfers between devices, swap(): return lax.ppermute(value, axis, [(i, i ^ bit) for i in range(count)])  29.9 us
    pallas_call x1, Pallas kernels, run_near(): pl.pallas_call(functools.partial(near_kernel, docs), grid=(experts,), out...  27.5 us
    pallas_call x4, Pallas kernels, attend(): pl.pallas_call(functools.partial(attend_kernel, docs, place, local, adden...  27 us
    pallas_call x2, Pallas kernels, project(): pl.pallas_call(functools.partial(project_kernel, docs, half, parts), grid...  22.9 us
    pallas_call x1, Pallas kernels, run_upstream(): pl.pallas_call(lambda *refs: upstream_kernel(*refs[:4 + blocks], *refs[4...  21.3 us
  transfers between devices with their start and end apart: 55, of which 19 were waited for; matrix products, arithmetic and copies ran while one was open for 13% of the time, Pallas kernels for 38%

profile of v5, /device:TPU:0, one launch (start us, length us, event | category | flops | bytes accessed | tf_op | source)
XLA Modules:
  0.0 499.6 jit_solution(5969363959057184506)
XLA Ops:
  1.2 2.6 collective-permute-start.7
  4.4 1.4 fusion.28
  5.8 2.6 collective-permute-start.3
  8.4 1.6 collective-permute-start.1
  10.0 1.5 collective-permute-start
  12.0 1.5 collective-permute-start.4
  13.6 1.5 collective-permute-start.2
  21.3 11.5 %project.2 = (bf16[1024,2048]{1,0:T(8,128)(2,1)}, bf16[3,1024,128]{2,1,0:T(8,128)(2,1)}, f32[2,1024,512]{2,1,0:T(8,128)}, bf16[1024,512]{1,0:T(8,128)(2,1)}, f32[2,1024]{1,0:T(2,128)}) custom-call(s32[13]{0:T(128)} %pad_add_fusion.5.scal_ref.refs_0_, bf16[256,2048]{1,0:T(8,128)(2,1)} %refs_4_.13, bf16[256,2048]{1,0:T(8,128)(2,1)} %collective-permute-done.8.refs_1_, ...), custom_call_target="tpu_custom_call" | custom-call | flops 503316480 | bytes 1750000 | tf_op jit(solution)/shard_map/project/pallas_call | solution.py:311
  35.6 2.0 collective-permute-done.13
  42.4 11.4 %project.3 = (bf16[1024,2048]{1,0:T(8,128)(2,1)}, bf16[3,1024,128]{2,1,0:T(8,128)(2,1)}, f32[2,1024,512]{2,1,0:T(8,128)}, bf16[1024,512]{1,0:T(8,128)(2,1)}, f32[2,1024]{1,0:T(2,128)}) custom-call(s32[13]{0:T(128)} %pad_add_fusion.5.scal_ref.refs_0_, ...), custom_call_target="tpu_custom_call", output_to_operand_aliasing={{0}: (7, {}), {1}: (8, {}), {2}: (9, {}), {3}: (10, {}), {4... | custom-call | flops 503316480 | bytes 1750000 | tf_op jit(solution)/shard_map/project/pallas_call | solution.py:311
  53.9 1.5 fusion.36
  55.4 4.5 subtract_convert_fusion
  60.0 1.9 fusion.2
  66.0 1.4 collective-permute-done.12
  69.0 5.0 %prepare.1 = (bf16[1024,512]{1,0:T(8,128)(2,1)}, bf16[1024,512]{1,0:T(8,128)(2,1)}) custom-call(f32[2,1024,512]{2,1,0:T(8,128)} %get-tuple-element.95.refs_0_.refs_5_, f32[2,1024]{1,0:T(2,128)} %maximum_add_fusion.1.refs_1_.refs_6_, f32[2,512]{1,0:T(2,128)} %maximum_convert_fusion.refs_2_.refs_8_, f32[1024,128]{1,0:T(8,128)} %pad_maximum_fusion.1.refs_3_.refs_9_, ...), custom_call_target="tpu_custom_call" | custom-call | flops 1310720 | bytes 1048576 | tf_op jit(solution)/shard_map/prepare/pallas_call | solution.py:352
  74.0 7.5 %attend.4 = (bf16[256,512]{1,0:T(8,128)(2,1)}, bf16[256,2176]{1,0:T(8,128)(2,1)}, f32[8,256]{1,0:T(8,128)}) custom-call(s32[13]{0:T(128)} %pad_add_fusion.5.scal_ref.refs_0_, bf16[1024,512]{1,0:T(8,128)(2,1)} %get-tuple-element.98.q_ref.refs_0_, bf16[1024,512]{1,0:T(8,128)(2,1)} %get-tuple-element.99.k_ref.refs_1_, ...), custom_call_target="tpu_custom_call" | custom-call | flops 275000000 | bytes 500000 | tf_op jit(solution)/shard_map/attend/pallas_call | solution.py:422
  81.6 6.3 %attend.5 = (bf16[256,512]{1,0:T(8,128)(2,1)}, bf16[256,2176]{1,0:T(8,128)(2,1)}, f32[8,256]{1,0:T(8,128)}) custom-call(s32[13]{0:T(128)} %pad_add_fusion.5.scal_ref.refs_0_, bf16[1024,512]{1,0:T(8,128)(2,1)} %get-tuple-element.98.q_ref.refs_0_, bf16[1024,512]{1,0:T(8,128)(2,1)} %get-tuple-element.99.k_ref.refs_1_, ...), custom_call_target="tpu_custom_call" | custom-call | flops 275000000 | bytes 500000 | tf_op jit(solution)/shard_map/attend/pallas_call | solution.py:422
  88.4 7.0 %attend.6 = (bf16[256,512]{1,0:T(8,128)(2,1)}, bf16[256,2176]{1,0:T(8,128)(2,1)}, f32[8,256]{1,0:T(8,128)}) custom-call(s32[13]{0:T(128)} %pad_add_fusion.5.scal_ref.refs_0_, bf16[1024,512]{1,0:T(8,128)(2,1)} %get-tuple-element.98.q_ref.refs_0_, bf16[1024,512]{1,0:T(8,128)(2,1)} %get-tuple-element.99.k_ref.refs_1_, ...), custom_call_target="tpu_custom_call" | custom-call | flops 275000000 | bytes 500000 | tf_op jit(solution)/shard_map/attend/pallas_call | solution.py:422
  95.4 2.0 collective-permute-start.18
  98.0 6.2 %attend.7 = (bf16[256,512]{1,0:T(8,128)(2,1)}, bf16[256,2176]{1,0:T(8,128)(2,1)}, f32[8,256]{1,0:T(8,128)}) custom-call(s32[13]{0:T(128)} %pad_add_fusion.5.scal_ref.refs_0_, bf16[1024,512]{1,0:T(8,128)(2,1)} %get-tuple-element.98.q_ref.refs_0_, bf16[1024,512]{1,0:T(8,128)(2,1)} %get-tuple-element.99.k_ref.refs_1_, ...), custom_call_target="tpu_custom_call" | custom-call | flops 275000000 | bytes 500000 | tf_op jit(solution)/shard_map/attend/pallas_call | solution.py:422
  104.2 21.3 %upstream.1 = (f32[4,4,1,256]{3,2,1,0:T(1,128)}, bf16[4,576,2048]{2,1,0:T(8,128)(2,1)}, bf16[4,576,1024]{2,1,0:T(8,128)(2,1)}, f32[4,576,128]{2,1,0:T(8,128)}) custom-call(s32[13]{0:T(128)} %pad_add_fusion.5.scal_ref.refs_0_, s32[4,1,256]{2,1,0:T(1,128)} %pad_add_fusion.refs_2_.refs_6_.refs_1_, bf16[256,2048]{1,0:T(8,128)(2,1)} %up_ref.1, ...), custom_call_target="tpu_custom_call" | custom-call | flops 1207959552 | bytes 5000000 | tf_op jit(solution)/shard_map/upstream/pallas_call | solution.py:825
  125.5 4.6 middle.1
  132.4 1.5 collective-permute-done.20.refs_1_.refs_5_.refs_13_
  133.9 27.5 %near.1 = (bf16[4,288,1024]{2,1,0:T(8,128)(2,1)}, bf16[4,288,1024]{2,1,0:T(8,128)(2,1)}, bf16[4,288,1024]{2,1,0:T(8,128)(2,1)}, bf16[4,288,384]{2,1,0:T(8,128)(2,1)}) custom-call(s32[13]{0:T(128)} %pad_add_fusion.5.scal_ref.refs_0_, f32[4,4,1,256]{3,2,1,0:T(1,128)} %get-tuple-element.107.refs_9_.rank_ref.refs_1_, ...), custom_call_target="tpu_custom_call" | custom-call | flops 1207959552 | bytes 5000000 | tf_op jit(solution)/shard_map/near/pallas_call | solution.py:920
  163.5 2.0 collective-permute-done.22.refs_7_.refs_13_
  166.5 95.8 %experts.1 = (bf16[4,4,144,2048]{3,2,1,0:T(8,128)(2,1)}, bf16[4,4,144,2048]{3,2,1,0:T(8,128)(2,1)}, f32[4,4,1,256]{3,2,1,0:T(1,128)}, bf16[4,4,384,384]{3,2,1,0:T(8,128)(2,1)}, bf16[4,4,192,384]{3,2,1,0:T(8,128)(2,1)}) custom-call(s32[13]{0:T(128)} %pad_add_fusion.5.scal_ref.refs_0_, f32[4,4,1,256]{3,2,1,0:T(1,128)} %get-tuple-element.107.refs_9_.rank_ref.refs_1_, ...), custom_call_target="tpu_custom_call" | custom-call | flops 8078229504 | bytes 7500000 | tf_op jit(solution)/shard_map/experts/pallas_call | solution.py:1110
  262.2 3.8 combine.3.refs_0_
  266.5 3.8 combine.4.refs_1_
  270.3 4.2 combine.5.refs_6_
  274.5 1.3 collective-permute-start.27
  278.1 13.5 %combine_last.1 = (bf16[256,2048]{1,0:T(8,128)(2,1)}, bf16[256,2048]{1,0:T(8,128)(2,1)}, bf16[256,2048]{1,0:T(8,128)(2,1)}, bf16[256,2048]{1,0:T(8,128)(2,1)}, bf16[256,2176]{1,0:T(8,128)(2,1)}) custom-call(s32[13]{0:T(128)} %pad_add_fusion.5.scal_ref.refs_0_, f32[4,4,1,256]{3,2,1,0:T(1,128)} %get-tuple-element.107.refs_9_.rank_ref.refs_1_, ...), custom_call_target="tpu_custom_call" | custom-call | flops 377487360 | bytes 1474560 | tf_op jit(solution)/shard_map/combine_last/pallas_call | solution.py:1233
  291.6 10.1 %collective-permute-done.27.gb_ref = bf16[256,2176]{1,0:T(8,128)(2,1)} collective-permute-done((bf16[256,2176]{1,0:T(8,128)(2,1)}, bf16[256,2176]{1,0:T(8,128)(2,1)}, u32[]{:S(2)}, u32[]{:S(2)}) %collective-permute-start.27) | collective-permute-done | bytes 1114144 | tf_op jit(solution)/shard_map/ppermute | solution.py:42
  301.7 6.0 %middle_back.1 = (f32[256,2048]{1,0:T(8,128)}, bf16[256,2176]{1,0:T(8,128)(2,1)}, f32[16,128]{1,0:T(8,128)}) custom-call(s32[13]{0:T(128)} %pad_add_fusion.5.scal_ref.refs_0_, bf16[256,2176]{1,0:T(8,128)(2,1)} %get-tuple-element.124.ga_ref, bf16[256,2176]{1,0:T(8,128)(2,1)} %collective-permute-done.27.gb_ref, f32[16,256]{1,0:T(8,128)} %get-tuple-element.125.probs_ref, ...), custom_call_target="tpu_custom_call" | custom-call | flops 33554432 | bytes 1250000 | tf_op jit(solution)/shard_map/middle_back/pallas_call | solution.py:510
  309.1 1.7 collective-permute-done.29.refs_7_
  310.8 15.1 %attend_back.2 = (f32[512,512]{1,0:T(8,128)}, f32[1024,512]{1,0:T(8,128)}, f32[1024,512]{1,0:T(8,128)}, f32[128,512]{1,0:T(8,128)}, f32[128,512]{1,0:T(8,128)}, /*index=5*/f32[128,512]{1,0:T(8,128)}, f32[1,512]{1,0:T(1,128)}) custom-call(s32[13]{0:T(128)} %pad_add_fusion.5.scal_ref.refs_0_, bf16[1024,512]{1,0:T(8,128)(2,1)} %get-tuple-element.98.q_ref.refs_0_, ...), custom_call_target="tpu_custom_call" | custom-call | flops 1000000000 | bytes 1750000 | tf_op jit(solution)/shard_map/attend_back/pallas_call | solution.py:627
  325.9 9.0 %collective-permute-done.28.refs_0_ = bf16[256,2176]{1,0:T(8,128)(2,1)S(1)} collective-permute-done((bf16[256,2176]{1,0:T(8,128)(2,1)}, bf16[256,2176]{1,0:T(8,128)(2,1)S(1)}, u32[]{:S(2)}, u32[]{:S(2)}) %collective-permute-start.28) | collective-permute-done | bytes 1114144 | tf_op jit(solution)/shard_map/ppermute | solution.py:42
  335.9 5.9 %widen.1 = (bf16[4,384,384]{2,1,0:T(8,128)(2,1)}, bf16[4,384,384]{2,1,0:T(8,128)(2,1)}, bf16[4,384,384]{2,1,0:T(8,128)(2,1)}, bf16[4,384,384]{2,1,0:T(8,128)(2,1)}) custom-call(s32[4]{0:T(128)} %get-tuple-element.230.sets_ref, bf16[4,4,384,384]{3,2,1,0:T(8,128)(2,1)} %get-tuple-element.140.kept_ref, ...), custom_call_target="tpu_custom_call" | custom-call | tf_op jit(solution)/shard_map/widen/pallas_call | solution.py:198
  341.8 3.1 collective-permute-start.33
  346.3 2.9 add_convert_fusion.5.refs_0_
  350.4 20.8 %attend_back.3 = (f32[512,512]{1,0:T(8,128)}, f32[1024,512]{1,0:T(8,128)}, f32[1024,512]{1,0:T(8,128)}, f32[128,512]{1,0:T(8,128)}, f32[128,512]{1,0:T(8,128)}, ...) custom-call(s32[13]{0:T(128)} %pad_add_fusion.5.scal_ref.refs_0_, ...), custom_call_target="tpu_custom_call" | custom-call | flops 1000000000 | bytes 1750000 | tf_op jit(solution)/shard_map/attend_back/pallas_call | solution.py:627
  372.6 2.7 collective-permute-done.34.refs_2_
  375.3 3.2 add_convert_fusion.2.refs_17_.refs_18_
  378.5 1.4 collective-permute-start.38
  379.9 4.6 collective-permute-start.37
  388.6 1.8 collective-permute-done.36
  391.0 17.8 %project_back.1 = (bf16[256,2048]{1,0:T(8,128)(2,1)}, bf16[256,2048]{1,0:T(8,128)(2,1)}, bf16[4,400,512]{2,1,0:T(8,128)(2,1)}, f32[3,128,512]{2,1,0:T(8,128)}, b...) custom-call(s32[13]{0:T(128)} %pad_add_fusion.5.scal_ref.refs_0_, f32[512,512]{1,0:T(8,128)} %get-tuple-element.131.refs_1_, ...), custom_call_target="tpu_custom_call" | custom-call | flops 603979776 | bytes 2500000 | tf_op jit(solution)/shard_map/project_back/pallas_call | solution.py:717
  410.4 4.2 add_convert_fusion.4
  414.7 2.7 add_convert_fusion
  421.4 1.4 add_convert_fusion.3.refs_0_.refs_1_
  424.0 2.1 slice_bitcast_fusion.4
  428.9 1.5 add_convert_fusion.1
  430.3 5.9 %collective-permute-start.45 = (bf16[4,384,384]{2,1,0:T(8,128)(2,1)}, bf16[4,384,384]{2,1,0:T(8,128)(2,1)}, u32[]{:S(2)}, u32[]{:S(2)}) collective-permute-start(bf16[4,384,384]{2,1,0:T(8,128)(2,1)} %add_convert_fusion.1), channel_id=1, source_target_pairs={{0,8},{4,12},{8,16},{12,20},{16,24},{20,28},{1,9},{5,13},{9,17},{1... | collective-permute-start | bytes 3538952 | tf_op jit(solution)/shard_map/ppermute | solution.py:130
  436.3 8.4 %project_near.1 = (bf16[256,2048]{1,0:T(8,128)(2,1)}, bf16[256,2048]{1,0:T(8,128)(2,1)}) custom-call(bf16[3,1024,512]{2,1,0:T(8,128)(2,1)} %get-tuple-element.154.grads_ref, bf16[1024,384]{1,0:T(8,128)(2,1)} %get-tuple-element.155.low_ref, bf16[3,2048,512]{2,1,0:T(8,128)(2,1)} %w_ref.9, bf16[3,2048,128]{2,1,0:T(8,128)(2,1)} %enter_ref.9, ...), custom_call_target="tpu_custom_call" | custom-call | flops 402653184 | bytes 1250000 | tf_op jit(solution)/shard_map/project_near/pallas_call | solution.py:750
  449.4 8.4 %collective-permute-done.44 = bf16[400,512]{1,0:T(8,128)(2,1)S(1)} collective-permute-done((bf16[400,512]{1,0:T(8,128)(2,1)S(1)}, bf16[400,512]{1,0:T(8,128)(2,1)S(1)}, u32[]{:S(2)}, u32[]{:S(2)}) %collective-permute-start.44) | collective-permute-done | bytes 409632 | tf_op jit(solution)/shard_map/ppermute | solution.py:42
  457.8 3.7 collective-permute-start.49
  461.5 2.4 collective-permute-start.50
  463.9 1.9 add_convert_fusion.7.refs_0_
  467.2 1.6 convert_add_fusion.2.refs_4_
  472.0 2.2 select_add_fusion
  474.1 1.4 copy-done.5
  476.4 5.4 %finish.1.refs_1_ = bf16[256,2048]{1,0:T(8,128)(2,1)} custom-call(bf16[256,2048]{1,0:T(8,128)(2,1)} %get-tuple-element.158.refs_0_, bf16[256,2048]{1,0:T(8,128)(2,1)} %collective-permute-done.40.refs_1_, bf16[256,2048]{1,0:T(8,128)(2,1)} %copy-done.2, f32[256,2048]{1,0:T(8,128)} %get-tuple-element.160.refs_3_, bf16[256,2048]{1,0:T(8,128)(2,1)} %refs_4_.13, ...), custom_call_target="tpu_custom_call" | custom-call | flops 655360 | bytes 786432 | tf_op jit(solution)/shard_map/finish/pallas_call | solution.py:779
  481.8 2.0 slice_bitcast_fusion.6
  485.5 4.1 collective-permute-start.52
  489.6 3.4 collective-permute-start.53
  (234 shorter events, 67.6 us)
Async XLA Ops:
  0.6 20.6 %collective-permute-start.8 = (bf16[256,2048]{1,0:T(8,128)(2,1)}, bf16[256,2048]{1,0:T(8,128)(2,1)}, u32[]{:S(2)}, u32[]{:S(2)}) collective-permute-start(bf16[256,2048]{1,0:T(8,128)(2,1)} %refs_4_.13), channel_id=1, source_target_pairs={{0,1},{1,0},{2,3},{3,2},{4,5},{5,4},{6,7},{7,6},{8,9},{9,8},{10,11... | collective-permute-start | bytes 3145736 | tf_op jit(solution)/shard_map/ppermute | solution.py:42
  1.2 31.6 %collective-permute-start.7 = (bf16[256,2048]{1,0:T(8,128)(2,1)}, bf16[256,2048]{1,0:T(8,128)(2,1)S(1)}, u32[]{:S(2)}, u32[]{:S(2)}) collective-permute-start(bf16[256,2048]{1,0:T(8,128)(2,1)} %refs_4_.13), channel_id=1, source_target_pairs={{0,2},{1,3},{2,0},{3,1},{4,6},{5,7},{6,4},{7,5},{8,10},{9,11},{10,... | collective-permute-start | bytes 3145736 | tf_op jit(solution)/shard_map/ppermute | solution.py:42
  5.8 5.7 %collective-permute-start.3 = (s32[384]{0:T(512)S(1)}, s32[384]{0:T(512)S(1)}, u32[]{:S(2)}, u32[]{:S(2)}) collective-permute-start(s32[384]{0:T(512)S(1)} %pad_add_fusion.1), channel_id=1, source_target_pairs={{0,16},{4,20},{8,24},{12,28},{16,0},{20,4},{24,8},{28,12},{1,17},{... | collective-permute-start | bytes 4616 | tf_op jit(solution)/shard_map/ppermute | solution.py:42
  8.4 3.6 collective-permute-start.1
  10.0 3.6 collective-permute-start
  11.5 3.6 collective-permute-start.5
  12.0 6.2 %collective-permute-start.4 = (s32[384]{0:T(512)S(1)}, s32[384]{0:T(512)S(1)}, u32[]{:S(2)}, u32[]{:S(2)}) collective-permute-start(s32[384]{0:T(512)S(1)} %collective-permute-done.3), channel_id=1, source_target_pairs={{0,4},{4,0},{8,12},{12,8},{16,20},{20,16},{24,28},{28,24},{1,5},{5... | collective-permute-start | bytes 4616 | tf_op jit(solution)/shard_map/ppermute | solution.py:42
  13.6 4.7 collective-permute-start.2
  15.1 3.6 collective-permute-start.6
  19.5 1.2 collective-permute-start.9
  33.8 7.6 %collective-permute-start.10 = (bf16[256,2048]{1,0:T(8,128)(2,1)}, bf16[256,2048]{1,0:T(8,128)(2,1)S(1)}, u32[]{:S(2)}, u32[]{:S(2)}) collective-permute-start(bf16[256,2048]{1,0:T(8,128)(2,1)} %fence.18.refs_0_.refs_1_), channel_id=1, source_target_pairs={{0,1},{1,0},{2,3},{3,2},{4,5},{5,4},{6,7},{7,6},{8,9},{9,8},{10,11... | collective-permute-start | bytes 3145736 | tf_op jit(solution)/shard_map/ppermute | solution.py:42
  34.0 3.6 collective-permute-start.13
  35.6 5.3 %copy-start.23 = (s32[13]{0:T(128)S(1)}, s32[13]{0:T(128)}, u32[]{:S(2)}) copy-start(s32[13]{0:T(128)} %pad_add_fusion.5.scal_ref.refs_0_) | copy-start | bytes 160
  38.1 24.6 %collective-permute-start.14 = (bf16[256,2048]{1,0:T(8,128)(2,1)}, bf16[256,2048]{1,0:T(8,128)(2,1)}, u32[]{:S(2)}, u32[]{:S(2)}) collective-permute-start(bf16[256,2048]{1,0:T(8,128)(2,1)} %fence.20), channel_id=1, source_target_pairs={{0,2},{1,3},{2,0},{3,1},{4,6},{5,7},{6,4},{7,5},{8,10},{9,11},{10,... | collective-permute-start | bytes 3145736 | tf_op jit(solution)/shard_map/ppermute | solution.py:42
  53.8 9.9 %copy-start.24 = (f32[2,1024]{1,0:T(2,128)S(1)}, f32[2,1024]{1,0:T(2,128)}, u32[]{:S(2)}) copy-start(f32[2,1024]{1,0:T(2,128)} %get-tuple-element.96) | copy-start | bytes 24580
  53.8 9.9 %collective-permute-start.11 = (f32[2,1024]{1,0:T(2,128)}, f32[2,1024]{1,0:T(2,128)S(1)}, u32[]{:S(2)}, u32[]{:S(2)}) collective-permute-start(f32[2,1024]{1,0:T(2,128)} %get-tuple-element.96), channel_id=1, source_target_pairs={{0,1},{1,0},{2,3},{3,2},{4,5},{5,4},{6,7},{7,6},{8,9},{9,8},{10,11... | collective-permute-start | bytes 24584 | tf_op jit(solution)/shard_map/ppermute | solution.py:42
  62.7 5.4 %collective-permute-start.15 = (bf16[256,2048]{1,0:T(8,128)(2,1)}, bf16[256,2048]{1,0:T(8,128)(2,1)S(1)}, u32[]{:S(2)}, u32[]{:S(2)}) collective-permute-start(bf16[256,2048]{1,0:T(8,128)(2,1)} %collective-permute-done.14.refs_4_), channel_id=1, source_target_pairs={{0,1},{1,0},{2,3},{3,2},{4,5},{5,4},{6,7},{7,6},{8,9},{9,8},{10,11... | collective-permute-start | bytes 3145736 | tf_op jit(solution)/shard_map/ppermute | solution.py:42
  63.7 3.7 collective-permute-start.12
  81.6 6.8 %collective-permute-start.17 = (bf16[256,2176]{1,0:T(8,128)(2,1)}, bf16[256,2176]{1,0:T(8,128)(2,1)}, u32[]{:S(2)}, u32[]{:S(2)}) collective-permute-start(bf16[256,2176]{1,0:T(8,128)(2,1)} %get-tuple-element.102), channel_id=1, source_target_pairs={{0,1},{1,0},{2,3},{3,2},{4,5},{5,4},{6,7},{7,6},{8,9},{9,8},{10,11... | collective-permute-start | bytes 3342344 | tf_op jit(solution)/shard_map/ppermute | solution.py:42
  81.6 6.3 %copy-start.8 = (bf16[256,2048]{1,0:T(8,128)(2,1)S(1)}, bf16[256,2048]{1,0:T(8,128)(2,1)}, u32[]{:S(2)}) copy-start(bf16[256,2048]{1,0:T(8,128)(2,1)} %up_ref.1) | copy-start | bytes 3145732
  87.9 10.1 %collective-permute-start.16 = (bf16[256,2176]{1,0:T(8,128)(2,1)}, bf16[256,2176]{1,0:T(8,128)(2,1)}, u32[]{:S(2)}, u32[]{:S(2)}) collective-permute-start(bf16[256,2176]{1,0:T(8,128)(2,1)} %get-tuple-element.101), channel_id=1, source_target_pairs={{0,1},{1,0},{2,3},{3,2},{4,5},{5,4},{6,7},{7,6},{8,9},{9,8},{10,11... | collective-permute-start | bytes 3342344 | tf_op jit(solution)/shard_map/ppermute | solution.py:42
  87.9 16.3 %collective-permute-start.19 = (bf16[256,2048]{1,0:T(8,128)(2,1)S(1)}, bf16[256,2048]{1,0:T(8,128)(2,1)}, u32[]{:S(2)}, u32[]{:S(2)}) collective-permute-start(bf16[256,2048]{1,0:T(8,128)(2,1)S(1)} %copy-done.8), channel_id=1, source_target_pairs={{0,1},{1,0},{2,3},{3,2},{4,5},{5,4},{6,7},{7,6},{8,9},{9,8},{10,11... | collective-permute-start | bytes 3145736 | tf_op jit(solution)/shard_map/ppermute | solution.py:42
  88.4 9.0 %copy-start.28 = (bf16[2048]{0:T(1024)(128)(2,1)S(1)}, bf16[2048]{0:T(1024)(128)(2,1)}, u32[]{:S(2)}) copy-start(bf16[2048]{0:T(1024)(128)(2,1)} %param.37) | copy-start | bytes 12292
  95.4 30.1 %collective-permute-start.18 = (bf16[256,2176]{1,0:T(8,128)(2,1)}, bf16[256,2176]{1,0:T(8,128)(2,1)}, u32[]{:S(2)}, u32[]{:S(2)}) collective-permute-start(bf16[256,2176]{1,0:T(8,128)(2,1)} %get-tuple-element.104.refs_1_), channel_id=1, source_target_pairs={{0,2},{1,3},{2,0},{3,1},{4,6},{5,7},{6,4},{7,5},{8,10},{9,11},{10,... | collective-permute-start | bytes 3342344 | tf_op jit(solution)/shard_map/ppermute | solution.py:42
  130.2 3.8 collective-permute-start.20
  131.2 30.3 %collective-permute-start.21 = (bf16[256,2176]{1,0:T(8,128)(2,1)}, bf16[256,2176]{1,0:T(8,128)(2,1)S(1)}, u32[]{:S(2)}, u32[]{:S(2)}) collective-permute-start(bf16[256,2176]{1,0:T(8,128)(2,1)} %get-tuple-element.112.refs_0_.refs_4_.refs_12_), channel_id=1, source_target_pairs={{0,2},{1,3},{2,0},{3,1},{4,6},{5,7},{6,4},{7,5},{8,10},{9,11},{10,... | collective-permute-start | bytes 3342344 | tf_op jit(solution)/shard_map/ppermute | solution.py:42
  162.5 3.0 collective-permute-start.22
  266.0 4.3 collective-permute-start.24
  270.3 6.8 %collective-permute-start.23 = (bf16[256,2176]{1,0:T(8,128)(2,1)}, bf16[256,2176]{1,0:T(8,128)(2,1)S(1)}, u32[]{:S(2)}, u32[]{:S(2)}) collective-permute-start(bf16[256,2176]{1,0:T(8,128)(2,1)} %combine.4.refs_1_), channel_id=1, source_target_pairs={{0,1},{1,0},{2,3},{3,2},{4,5},{5,4},{6,7},{7,6},{8,9},{9,8},{10,11... | collective-permute-start | bytes 3342344 | tf_op jit(solution)/shard_map/ppermute | solution.py:42
  274.5 27.2 %collective-permute-start.27 = (bf16[256,2176]{1,0:T(8,128)(2,1)}, bf16[256,2176]{1,0:T(8,128)(2,1)}, u32[]{:S(2)}, u32[]{:S(2)}) collective-permute-start(bf16[256,2176]{1,0:T(8,128)(2,1)} %combine.5.refs_6_), channel_id=1, source_target_pairs={{0,2},{1,3},{2,0},{3,1},{4,6},{5,7},{6,4},{7,5},{8,10},{9,11},{10,... | collective-permute-start | bytes 3342344 | tf_op jit(solution)/shard_map/ppermute | solution.py:42
  275.8 60.1 %collective-permute-start.32 = (bf16[4,4,192,384]{3,2,1,0:T(8,128)(2,1)}, bf16[4,4,192,384]{3,2,1,0:T(8,128)(2,1)}, u32[]{:S(2)}, u32[]{:S(2)}) collective-permute-start(bf16[4,4,192,384]{3,2,1,0:T(8,128)(2,1)} %get-tuple-element.141), channel_id=1, source_target_pairs={{0,4},{4,0},{8,12},{12,8},{16,20},{20,16},{24,28},{28,24},{1,5},{5... | collective-permute-start | bytes 7077896 | tf_op jit(solution)/shard_map/ppermute | solution.py:42
  307.7 3.1 collective-permute-start.29
  307.7 27.2 %collective-permute-start.28 = (bf16[256,2176]{1,0:T(8,128)(2,1)}, bf16[256,2176]{1,0:T(8,128)(2,1)S(1)}, u32[]{:S(2)}, u32[]{:S(2)}) collective-permute-start(bf16[256,2176]{1,0:T(8,128)(2,1)} %get-tuple-element.127.refs_6_), channel_id=1, source_target_pairs={{0,2},{1,3},{2,0},{3,1},{4,6},{5,7},{6,4},{7,5},{8,10},{9,11},{10,... | collective-permute-start | bytes 3342344 | tf_op jit(solution)/shard_map/ppermute | solution.py:42
  308.9 37.4 %collective-permute-start.26 = (bf16[256,2048]{1,0:T(8,128)(2,1)}, bf16[256,2048]{1,0:T(8,128)(2,1)}, u32[]{:S(2)}, u32[]{:S(2)}) collective-permute-start(bf16[256,2048]{1,0:T(8,128)(2,1)} %get-tuple-element.123), channel_id=1, source_target_pairs={{0,1},{1,0},{2,3},{3,2},{4,5},{5,4},{6,7},{7,6},{8,9},{9,8},{10,11... | collective-permute-start | bytes 3145736 | tf_op jit(solution)/shard_map/ppermute | solution.py:42
  335.9 14.5 %collective-permute-start.31 = (bf16[256,2176]{1,0:T(8,128)(2,1)}, bf16[256,2176]{1,0:T(8,128)(2,1)}, u32[]{:S(2)}, u32[]{:S(2)}) collective-permute-start(bf16[256,2176]{1,0:T(8,128)(2,1)} %fence.22.refs_1_.refs_6_), channel_id=1, source_target_pairs={{0,1},{1,0},{2,3},{3,2},{4,5},{5,4},{6,7},{7,6},{8,9},{9,8},{10,11... | collective-permute-start | bytes 3342344 | tf_op jit(solution)/shard_map/ppermute | solution.py:42
  341.8 30.7 %collective-permute-start.33 = (bf16[4,384,384]{2,1,0:T(8,128)(2,1)}, bf16[4,384,384]{2,1,0:T(8,128)(2,1)S(1)}, u32[]{:S(2)}, u32[]{:S(2)}) collective-permute-start(bf16[4,384,384]{2,1,0:T(8,128)(2,1)} %get-tuple-element.148), channel_id=1, source_target_pairs={{0,8},{4,12},{8,16},{12,20},{16,24},{20,28},{1,9},{5,13},{9,17},{1... | collective-permute-start | bytes 3538952 | tf_op jit(solution)/shard_map/ppermute | solution.py:130
  345.0 30.3 %collective-permute-start.34 = (bf16[4,384,384]{2,1,0:T(8,128)(2,1)}, bf16[4,384,384]{2,1,0:T(8,128)(2,1)}, u32[]{:S(2)}, u32[]{:S(2)}) collective-permute-start(bf16[4,384,384]{2,1,0:T(8,128)(2,1)} %get-tuple-element.149), channel_id=1, source_target_pairs={{8,0},{12,4},{16,8},{20,12},{24,16},{28,20},{9,1},{13,5},{17,9},{2... | collective-permute-start | bytes 3538952 | tf_op jit(solution)/shard_map/ppermute | solution.py:130
  349.2 35.4 %collective-permute-start.30 = (bf16[256,2048]{1,0:T(8,128)(2,1)}, bf16[256,2048]{1,0:T(8,128)(2,1)}, u32[]{:S(2)}, u32[]{:S(2)}) collective-permute-start(bf16[256,2048]{1,0:T(8,128)(2,1)} %fence.23), channel_id=1, source_target_pairs={{0,2},{1,3},{2,0},{3,1},{4,6},{5,7},{6,4},{7,5},{8,10},{9,11},{10,... | collective-permute-start | bytes 3145736 | tf_op jit(solution)/shard_map/ppermute | solution.py:42
  350.4 59.9 %collective-permute-start.25 = (bf16[256,2048]{1,0:T(8,128)(2,1)}, bf16[256,2048]{1,0:T(8,128)(2,1)}, u32[]{:S(2)}, u32[]{:S(2)}) collective-permute-start(bf16[256,2048]{1,0:T(8,128)(2,1)} %get-tuple-element.121), channel_id=1, source_target_pairs={{0,1},{1,0},{2,3},{3,2},{4,5},{5,4},{6,7},{7,6},{8,9},{9,8},{10,11... | collective-permute-start | bytes 3145736 | tf_op jit(solution)/shard_map/ppermute | solution.py:42
  350.4 20.8 %copy-start.26 = (f32[1,512]{1,0:T(1,128)S(1)}, f32[1,512]{1,0:T(1,128)}, u32[]{:S(2)}) copy-start(f32[1,512]{1,0:T(1,128)} %get-tuple-element.130.refs_1_.refs_0_) | copy-start | bytes 6148
  372.6 6.0 %copy-start.11 = (bf16[4,384,384]{2,1,0:T(8,128)(2,1)}, bf16[4,384,384]{2,1,0:T(8,128)(2,1)S(1)}, u32[]{:S(2)}) copy-start(bf16[4,384,384]{2,1,0:T(8,128)(2,1)S(1)} %collective-permute-done.33.refs_1_) | copy-start | bytes 3538948
  378.5 6.2 %copy-start.25 = (f32[16,128]{1,0:T(8,128)S(1)}, f32[16,128]{1,0:T(8,128)}, u32[]{:S(2)}) copy-start(f32[16,128]{1,0:T(8,128)} %get-tuple-element.152) | copy-start | bytes 24580
  378.5 30.3 %collective-permute-start.38 = (bf16[4,384,384]{2,1,0:T(8,128)(2,1)}, bf16[4,384,384]{2,1,0:T(8,128)(2,1)}, u32[]{:S(2)}, u32[]{:S(2)}) collective-permute-start(bf16[4,384,384]{2,1,0:T(8,128)(2,1)} %add_convert_fusion.2.refs_17_.refs_18_), channel_id=1, source_target_pairs={{8,0},{12,4},{16,8},{20,12},{24,16},{28,20},{9,1},{13,5},{17,9},{2... | collective-permute-start | bytes 3538952 | tf_op jit(solution)/shard_map/ppermute | solution.py:130
  379.9 29.4 %collective-permute-start.37 = (bf16[4,384,384]{2,1,0:T(8,128)(2,1)}, bf16[4,384,384]{2,1,0:T(8,128)(2,1)S(1)}, u32[]{:S(2)}, u32[]{:S(2)}) collective-permute-start(bf16[4,384,384]{2,1,0:T(8,128)(2,1)} %add_convert_fusion.2.refs_17_.refs_18_), channel_id=1, source_target_pairs={{0,8},{4,12},{8,16},{12,20},{16,24},{20,28},{1,9},{5,13},{9,17},{1... | collective-permute-start | bytes 3538952 | tf_op jit(solution)/shard_map/ppermute | solution.py:130
  384.6 1.4 collective-permute-start.35
  386.8 3.7 collective-permute-start.36
  410.3 10.6 %collective-permute-start.39 = (bf16[256,2048]{1,0:T(8,128)(2,1)}, bf16[256,2048]{1,0:T(8,128)(2,1)S(1)}, u32[]{:S(2)}, u32[]{:S(2)}) collective-permute-start(bf16[256,2048]{1,0:T(8,128)(2,1)} %fence.26), channel_id=1, source_target_pairs={{0,1},{1,0},{2,3},{3,2},{4,5},{5,4},{6,7},{7,6},{8,9},{9,8},{10,11... | collective-permute-start | bytes 3145736 | tf_op jit(solution)/shard_map/ppermute | solution.py:42
  417.4 51.4 %collective-permute-start.46 = (bf16[4,384,384]{2,1,0:T(8,128)(2,1)}, bf16[4,384,384]{2,1,0:T(8,128)(2,1)}, u32[]{:S(2)}, u32[]{:S(2)}) collective-permute-start(bf16[4,384,384]{2,1,0:T(8,128)(2,1)} %add_convert_fusion), channel_id=1, source_target_pairs={{8,0},{12,4},{16,8},{20,12},{24,16},{28,20},{9,1},{13,5},{17,9},{2... | collective-permute-start | bytes 3538952 | tf_op jit(solution)/shard_map/ppermute | solution.py:130
  422.8 38.7 %collective-permute-start.41 = (bf16[256,2048]{1,0:T(8,128)(2,1)}, bf16[256,2048]{1,0:T(8,128)(2,1)S(1)}, u32[]{:S(2)}, u32[]{:S(2)}) collective-permute-start(bf16[256,2048]{1,0:T(8,128)(2,1)} %add_convert_fusion.3.refs_0_.refs_1_), channel_id=1, source_target_pairs={{0,2},{1,3},{2,0},{3,1},{4,6},{5,7},{6,4},{7,5},{8,10},{9,11},{10,... | collective-permute-start | bytes 3145736 | tf_op jit(solution)/shard_map/ppermute | solution.py:42
  424.0 4.9 copy-start.16
  426.1 18.6 %collective-permute-start.43 = (bf16[400,512]{1,0:T(8,128)(2,1)}, bf16[400,512]{1,0:T(8,128)(2,1)S(1)}, u32[]{:S(2)}, u32[]{:S(2)}) collective-permute-start(bf16[400,512]{1,0:T(8,128)(2,1)} %get-tuple-element.203), channel_id=1, source_target_pairs={{0,1},{1,0},{2,3},{3,2},{4,5},{5,4},{6,7},{7,6},{8,9},{9,8},{10,11... | collective-permute-start | bytes 1228808 | tf_op jit(solution)/shard_map/ppermute | solution.py:42
  427.8 18.0 %collective-permute-start.47 = (bf16[4,6,16,512]{3,2,1,0:T(8,128)(2,1)}, bf16[4,6,16,512]{3,2,1,0:T(8,128)(2,1)}, u32[]{:S(2)}, u32[]{:S(2)}) collective-permute-start(bf16[4,6,16,512]{3,2,1,0:T(8,128)(2,1)} %pad_maximum_fusion.3), channel_id=1, source_target_pairs={{0,4},{4,0},{8,12},{12,8},{16,20},{20,16},{24,28},{28,24},{1,5},{5... | collective-permute-start | bytes 1179656 | tf_op jit(solution)/shard_map/ppermute | solution.py:154
  430.3 38.5 %collective-permute-start.45 = (bf16[4,384,384]{2,1,0:T(8,128)(2,1)}, bf16[4,384,384]{2,1,0:T(8,128)(2,1)}, u32[]{:S(2)}, u32[]{:S(2)}) collective-permute-start(bf16[4,384,384]{2,1,0:T(8,128)(2,1)} %add_convert_fusion.1), channel_id=1, source_target_pairs={{0,8},{4,12},{8,16},{12,20},{16,24},{20,28},{1,9},{5,13},{9,17},{1... | collective-permute-start | bytes 3538952 | tf_op jit(solution)/shard_map/ppermute | solution.py:130
  444.7 4.0 collective-permute-start.42
  445.9 11.9 %collective-permute-start.44 = (bf16[400,512]{1,0:T(8,128)(2,1)S(1)}, bf16[400,512]{1,0:T(8,128)(2,1)S(1)}, u32[]{:S(2)}, u32[]{:S(2)}) collective-permute-start(bf16[400,512]{1,0:T(8,128)(2,1)S(1)} %fusion), channel_id=1, source_target_pairs={{0,2},{1,3},{2,0},{3,1},{4,6},{5,7},{6,4},{7,5},{8,10},{9,11},{10,... | collective-permute-start | bytes 1228808 | tf_op jit(solution)/shard_map/ppermute | solution.py:42
  448.6 17.2 %collective-permute-start.48 = (bf16[6,16,512]{2,1,0:T(8,128)(2,1)S(1)}, bf16[6,16,512]{2,1,0:T(8,128)(2,1)S(1)}, u32[]{:S(2)}, u32[]{:S(2)}) collective-permute-start(bf16[6,16,512]{2,1,0:T(8,128)(2,1)S(1)} %get-tuple-element.223), channel_id=1, source_target_pairs={{0,8},{4,12},{8,16},{12,20},{16,24},{20,28},{24,0},{28,4},{1,9},{5... | collective-permute-start | bytes 294920 | tf_op jit(solution)/shard_map/ppermute | solution.py:154
  457.8 8.3 %collective-permute-start.49 = (bf16[6,16,512]{2,1,0:T(8,128)(2,1)S(1)}, bf16[6,16,512]{2,1,0:T(8,128)(2,1)S(1)}, u32[]{:S(2)}, u32[]{:S(2)}) collective-permute-start(bf16[6,16,512]{2,1,0:T(8,128)(2,1)S(1)} %get-tuple-element.222), channel_id=1, source_target_pairs={{0,16},{4,20},{8,24},{12,28},{16,0},{20,4},{24,8},{28,12},{1,17},{... | collective-permute-start | bytes 294920 | tf_op jit(solution)/shard_map/ppermute | solution.py:154
  461.5 5.7 %collective-permute-start.50 = (bf16[6,16,512]{2,1,0:T(8,128)(2,1)S(1)}, bf16[6,16,512]{2,1,0:T(8,128)(2,1)S(1)}, u32[]{:S(2)}, u32[]{:S(2)}) collective-permute-start(bf16[6,16,512]{2,1,0:T(8,128)(2,1)S(1)} %get-tuple-element.221), channel_id=1, source_target_pairs={{0,24},{4,28},{8,0},{12,4},{16,8},{20,12},{24,16},{28,20},{1,25},{... | collective-permute-start | bytes 294920 | tf_op jit(solution)/shard_map/ppermute | solution.py:154
  465.8 10.6 %collective-permute-start.40 = (bf16[256,2048]{1,0:T(8,128)(2,1)}, bf16[256,2048]{1,0:T(8,128)(2,1)}, u32[]{:S(2)}, u32[]{:S(2)}) collective-permute-start(bf16[256,2048]{1,0:T(8,128)(2,1)} %get-tuple-element.159), channel_id=1, source_target_pairs={{0,1},{1,0},{2,3},{3,2},{4,5},{5,4},{6,7},{7,6},{8,9},{9,8},{10,11... | collective-permute-start | bytes 3145736 | tf_op jit(solution)/shard_map/ppermute | solution.py:42
  470.9 13.0 %collective-permute-start.51 = (bf16[4,50,512]{2,1,0:T(8,128)(2,1)S(1)}, bf16[4,50,512]{2,1,0:T(8,128)(2,1)S(1)}, u32[]{:S(2)}, u32[]{:S(2)}) collective-permute-start(bf16[4,50,512]{2,1,0:T(8,128)(2,1)S(1)} %pad_maximum_fusion.4), channel_id=1, source_target_pairs={{0,4},{4,0},{8,12},{12,8},{16,20},{20,16},{24,28},{28,24},{1,5},{5... | collective-permute-start | bytes 614408 | tf_op jit(solution)/shard_map/ppermute | solution.py:154
  481.8 11.2 %copy-start.15 = (f32[6,16,512]{2,1,0:T(8,128)S(1)}, f32[6,16,512]{2,1,0:T(8,128)}, u32[]{:S(2)}) copy-start(f32[6,16,512]{2,1,0:T(8,128)} %convert_add_fusion.2.refs_4_) | copy-start | bytes 589828
  485.5 11.7 %collective-permute-start.52 = (bf16[50,512]{1,0:T(8,128)(2,1)S(1)}, bf16[50,512]{1,0:T(8,128)(2,1)S(1)}, u32[]{:S(2)}, u32[]{:S(2)}) collective-permute-start(bf16[50,512]{1,0:T(8,128)(2,1)S(1)} %get-tuple-element.224), channel_id=1, source_target_pairs={{0,8},{4,12},{8,16},{12,20},{16,24},{20,28},{24,0},{28,4},{1,9},{5... | collective-permute-start | bytes 153608 | tf_op jit(solution)/shard_map/ppermute | solution.py:154
  489.6 7.6 %collective-permute-start.53 = (bf16[50,512]{1,0:T(8,128)(2,1)S(1)}, bf16[50,512]{1,0:T(8,128)(2,1)S(1)}, u32[]{:S(2)}, u32[]{:S(2)}) collective-permute-start(bf16[50,512]{1,0:T(8,128)(2,1)S(1)} %get-tuple-element.226), channel_id=1, source_target_pairs={{0,16},{4,20},{8,24},{12,28},{16,0},{20,4},{24,8},{28,12},{1,17},{... | collective-permute-start | bytes 153608 | tf_op jit(solution)/shard_map/ppermute | solution.py:154
  493.0 4.3 collective-permute-start.54
  (20 other events, 45.6 us)
